TPU v7x, 32 devices: a whole 2x2x4 slice. The times are simulated.
32 devices in a mesh: rep: 8 (over z, y), shard: 4 (over x, core).
Axes of the slice: x: 2, y: 2, z: 4, core: 2. Of those that a mesh axis runs over, the one named last changes fastest.
Arguments:
- frames: bfloat16 [16, 1024, 768], P('rep', 'shard'), may hold values from -6 to 6
- cotangent: bfloat16 [16, 1024, 768], P('rep', 'shard'), may hold values from -6 to 6
- first_gain: bfloat16 [2, 768], P(None, 'shard'), may hold values from 0.5 to 1.5
- first_shift: bfloat16 [2, 768], P(None, 'shard'), may hold values from -1.75 to 1.75
- query_weight: bfloat16 [2, 768, 768], P(None, 'shard'), may hold values from -0.21875 to 0.21875
- query_bias: bfloat16 [2, 768], P(None, 'shard'), may hold values from -3 to 3
- key_weight: bfloat16 [2, 768, 768], P(None, 'shard'), may hold values from -0.21875 to 0.21875
- value_weight: bfloat16 [2, 768, 768], P(None, 'shard'), may hold values from -0.21875 to 0.21875
- value_bias: bfloat16 [2, 768], P(None, 'shard'), may hold values from -3 to 3
- out_weight: bfloat16 [2, 768, 768], P(None, 'shard'), may hold values from -0.875 to 0.875
- out_bias: bfloat16 [2, 768], P(None, 'shard'), may hold values from -3 to 3
- second_gain: bfloat16 [2, 768], P(None, 'shard'), may hold values from 0.5 to 1.5
- second_shift: bfloat16 [2, 768], P(None, 'shard'), may hold values from -1.75 to 1.75
- up_weight: bfloat16 [2, 768, 3072], P(None, 'shard'), may hold values from -0.21875 to 0.21875
- up_bias: bfloat16 [2, 3072], P(None, 'shard'), may hold values from -3 to 3
- down_weight: bfloat16 [2, 3072, 768], P(None, 'shard'), may hold values from -0.109375 to 0.109375
- down_bias: bfloat16 [2, 768], P(None, 'shard'), may hold values from -1.75 to 1.75
Outputs:
- output: bfloat16 [16, 1024, 768], P('rep', 'shard')
- input_grad: float32 [16, 1024, 768], P('rep', 'shard')
- first_gain_grad: float32 [2, 768], P(None, 'shard')
- first_shift_grad: float32 [2, 768], P(None, 'shard')
- query_weight_grad: float32 [2, 768, 768], P(None, 'shard')
- query_bias_grad: float32 [2, 768], P(None, 'shard')
- key_weight_grad: float32 [2, 768, 768], P(None, 'shard')
- value_weight_grad: float32 [2, 768, 768], P(None, 'shard')
- value_bias_grad: float32 [2, 768], P(None, 'shard')
- out_weight_grad: float32 [2, 768, 768], P(None, 'shard')
- out_bias_grad: float32 [2, 768], P(None, 'shard')
- second_gain_grad: float32 [2, 768], P(None, 'shard')
- second_shift_grad: float32 [2, 768], P(None, 'shard')
- up_weight_grad: float32 [2, 768, 3072], P(None, 'shard')
- up_bias_grad: float32 [2, 3072], P(None, 'shard')
- down_weight_grad: float32 [2, 3072, 768], P(None, 'shard')
- down_bias_grad: float32 [2, 768], P(None, 'shard')
All inputs are finite; a program needn't handle non-finite values.
Results may differ from a plain program's by a relative error of at most 0.02.
Values may be sent and summed in bfloat16 or wider, within the bound.
No kernel may reach another device: no remote copies, remote signals or barrier semaphores. Data moves between devices by JAX's collectives and lax.ppermute only.
A program may use at most 320 MiB of HBM per device.

v0:
```python
import jax
import jax.numpy as jnp
from jax import lax
from jax.sharding import PartitionSpec as P

HEAD = 64
LAYERS = 2


EPSILON = 1e-05


def project(left, right):
    return jnp.einsum("cfd,de->cfe", left, right, preferred_element_type=jnp.float32)


def project_back(left, right):
    return jnp.einsum("cfe,de->cfd", left, right, preferred_element_type=jnp.float32)


def contract(left, right):
    return jnp.einsum("cfd,cfe->de", left, right, preferred_element_type=jnp.float32)


def row_total(values):
    return jnp.sum(values.astype(jnp.float32), axis=(0, 1))


def exact_gelu(values):
    return jax.nn.gelu(values, approximate=False)


def normalize(values, norm_gain, norm_shift):
    average = jnp.mean(values, axis=-1, keepdims=True)
    centered = values - average
    variance = jnp.mean(centered * centered, axis=-1, keepdims=True)
    inverse_scale = lax.rsqrt(variance + EPSILON)
    standard = centered * inverse_scale
    return (
        standard * norm_gain.astype(jnp.float32) + norm_shift.astype(jnp.float32),
        standard,
        inverse_scale,
    )


def norm_back(grad_out, standard, inverse_scale, norm_gain):
    grad_gain = jnp.sum(grad_out * standard, axis=(0, 1))
    grad_shift = jnp.sum(grad_out, axis=(0, 1))
    grad_standard = grad_out * norm_gain.astype(jnp.float32)
    grad_input = inverse_scale * (
        grad_standard
        - jnp.mean(grad_standard, axis=-1, keepdims=True)
        - standard * jnp.mean(grad_standard * standard, axis=-1, keepdims=True)
    )
    return (grad_gain, grad_shift, grad_input)


def score_block(query_heads, key_heads):
    return HEAD ** (-0.5) * jnp.einsum(
        "cqhe,ckhe->chqk", query_heads, key_heads, preferred_element_type=jnp.float32
    )


def forward_layer(stream, gathered):
    (
        gain_one,
        shift_one,
        weight_query,
        bias_query,
        weight_key,
        weight_value,
        bias_value,
        weight_out,
        bias_out,
        gain_two,
        shift_two,
        weight_up,
        bias_up,
        weight_down,
        bias_down,
    ) = gathered
    clip_count, frame_rows, model_width = stream.shape
    head_count = model_width // HEAD
    normed, standard_one, inverse_one = normalize(stream, gain_one, shift_one)
    normed_b = normed.astype(jnp.bfloat16)
    queries_b = (project(normed_b, weight_query) + bias_query.astype(jnp.float32)).astype(
        jnp.bfloat16
    )
    keys_b = project(normed_b, weight_key).astype(jnp.bfloat16)
    values_b = (project(normed_b, weight_value) + bias_value.astype(jnp.float32)).astype(
        jnp.bfloat16
    )
    keys_all, values_all = (
        lax.all_gather(keys_b, "shard", axis=1, tiled=True),
        lax.all_gather(values_b, "shard", axis=1, tiled=True),
    )
    query_heads = queries_b.reshape(clip_count, frame_rows, head_count, HEAD)
    key_heads = keys_all.reshape(clip_count, -1, head_count, HEAD)
    value_heads = values_all.reshape(clip_count, -1, head_count, HEAD)
    scores = score_block(query_heads, key_heads)
    row_peak = jnp.max(scores, axis=-1, keepdims=True)
    log_total = row_peak + jnp.log(jnp.sum(jnp.exp(scores - row_peak), axis=-1, keepdims=True))
    probability_b = jnp.exp(scores - log_total).astype(jnp.bfloat16)
    mixed_b = jnp.einsum(
        "chqk,ckhe->cqhe", probability_b, value_heads, preferred_element_type=jnp.float32
    )
    mixed_b = mixed_b.reshape(clip_count, frame_rows, model_width).astype(jnp.bfloat16)
    attended = stream + project(mixed_b, weight_out) + bias_out.astype(jnp.float32)
    second, standard_two, inverse_two = normalize(attended, gain_two, shift_two)
    second_b = second.astype(jnp.bfloat16)
    hidden = project(second_b, weight_up) + bias_up.astype(jnp.float32)
    activated_b = exact_gelu(hidden).astype(jnp.bfloat16)
    result = attended + project(activated_b, weight_down) + bias_down.astype(jnp.float32)
    stored = (
        normed_b,
        standard_one,
        inverse_one,
        queries_b,
        keys_all,
        values_all,
        log_total,
        mixed_b,
        standard_two,
        inverse_two,
        second_b,
        hidden,
        activated_b,
    )
    return (result, stored)


def backward_layer(upstream, gathered, stored):
    (
        gain_one,
        shift_one,
        weight_query,
        bias_query,
        weight_key,
        weight_value,
        bias_value,
        weight_out,
        bias_out,
        gain_two,
        shift_two,
        weight_up,
        bias_up,
        weight_down,
        bias_down,
    ) = gathered
    (
        normed_b,
        standard_one,
        inverse_one,
        queries_b,
        keys_all,
        values_all,
        log_total,
        mixed_b,
        standard_two,
        inverse_two,
        second_b,
        hidden,
        activated_b,
    ) = stored
    clip_count, frame_rows, model_width = upstream.shape
    head_count = model_width // HEAD
    branch_b = upstream.astype(jnp.bfloat16)
    grad_weight_down = contract(activated_b, branch_b)
    grad_bias_down = row_total(branch_b)
    grad_activated = project_back(branch_b, weight_down)
    unused_value, gelu_pull = jax.vjp(exact_gelu, hidden)
    grad_hidden_b = gelu_pull(grad_activated)[0].astype(jnp.bfloat16)
    grad_weight_up = contract(second_b, grad_hidden_b)
    grad_bias_up = row_total(grad_hidden_b)
    grad_second = project_back(grad_hidden_b, weight_up)
    grad_gain_two, grad_shift_two, grad_from_norm = norm_back(
        grad_second, standard_two, inverse_two, gain_two
    )
    grad_attended = upstream + grad_from_norm
    out_grad_b = grad_attended.astype(jnp.bfloat16)
    grad_weight_out = contract(mixed_b, out_grad_b)
    grad_bias_out = row_total(out_grad_b)
    grad_mixed_b = project_back(out_grad_b, weight_out).astype(jnp.bfloat16)
    query_heads = queries_b.reshape(clip_count, frame_rows, head_count, HEAD)
    key_heads = keys_all.reshape(clip_count, -1, head_count, HEAD)
    value_heads = values_all.reshape(clip_count, -1, head_count, HEAD)
    scores = score_block(query_heads, key_heads)
    probability = jnp.exp(scores - log_total)
    grad_heads = grad_mixed_b.reshape(clip_count, frame_rows, head_count, HEAD)
    grad_probability = jnp.einsum(
        "cqhe,ckhe->chqk", grad_heads, value_heads, preferred_element_type=jnp.float32
    )
    inner_sum = jnp.sum(grad_probability * probability, axis=-1, keepdims=True)
    grad_scores_b = (probability * (grad_probability - inner_sum)).astype(jnp.bfloat16)
    grad_queries_b = HEAD ** (-0.5) * jnp.einsum(
        "chqk,ckhe->cqhe", grad_scores_b, key_heads, preferred_element_type=jnp.float32
    )
    grad_queries_b = grad_queries_b.reshape(clip_count, frame_rows, model_width).astype(
        jnp.bfloat16
    )
    probability_b = probability.astype(jnp.bfloat16)
    value_part = jnp.einsum(
        "chqk,cqhe->ckhe", probability_b, grad_heads, preferred_element_type=jnp.float32
    )
    key_part = HEAD ** (-0.5) * jnp.einsum(
        "chqk,cqhe->ckhe", grad_scores_b, query_heads, preferred_element_type=jnp.float32
    )
    key_sums, value_sums = (
        lax.psum_scatter(
            key_part.reshape(clip_count, -1, model_width).astype(jnp.bfloat16),
            "shard",
            scatter_dimension=1,
            tiled=True,
        ).astype(jnp.float32),
        lax.psum_scatter(
            value_part.reshape(clip_count, -1, model_width).astype(jnp.bfloat16),
            "shard",
            scatter_dimension=1,
            tiled=True,
        ).astype(jnp.float32),
    )
    grad_keys_b = key_sums.astype(jnp.bfloat16)
    grad_values_b = value_sums.astype(jnp.bfloat16)
    grad_weight_query = contract(normed_b, grad_queries_b)
    grad_bias_query = row_total(grad_queries_b)
    grad_weight_key = contract(normed_b, grad_keys_b)
    grad_weight_value = contract(normed_b, grad_values_b)
    grad_bias_value = row_total(grad_values_b)
    grad_normed = (
        project_back(grad_queries_b, weight_query)
        + project_back(grad_keys_b, weight_key)
        + project_back(grad_values_b, weight_value)
    )
    grad_gain_one, grad_shift_one, grad_from_first = norm_back(
        grad_normed, standard_one, inverse_one, gain_one
    )
    partials = (
        grad_gain_one,
        grad_shift_one,
        grad_weight_query,
        grad_bias_query,
        grad_weight_key,
        grad_weight_value,
        grad_bias_value,
        grad_weight_out,
        grad_bias_out,
        grad_gain_two,
        grad_shift_two,
        grad_weight_up,
        grad_bias_up,
        grad_weight_down,
        grad_bias_down,
    )
    return (grad_attended + grad_from_first, partials)


def body(
    frames,
    cotangent,
    first_gain,
    first_shift,
    query_weight,
    query_bias,
    key_weight,
    value_weight,
    value_bias,
    out_weight,
    out_bias,
    second_gain,
    second_shift,
    up_weight,
    up_bias,
    down_weight,
    down_bias,
):
    params = (
        first_gain,
        first_shift,
        query_weight,
        query_bias,
        key_weight,
        value_weight,
        value_bias,
        out_weight,
        out_bias,
        second_gain,
        second_shift,
        up_weight,
        up_bias,
        down_weight,
        down_bias,
    )
    stream = frames.astype(jnp.float32)
    saved = []
    for layer_index in range(LAYERS):
        slices = tuple((entry[layer_index] for entry in params))
        gathered = (
            lax.all_gather(slices[0], "shard", axis=0, tiled=True),
            lax.all_gather(slices[1], "shard", axis=0, tiled=True),
            lax.all_gather(slices[2], "shard", axis=0, tiled=True),
            lax.all_gather(slices[3], "shard", axis=0, tiled=True),
            lax.all_gather(slices[4], "shard", axis=0, tiled=True),
            lax.all_gather(slices[5], "shard", axis=0, tiled=True),
            lax.all_gather(slices[6], "shard", axis=0, tiled=True),
            lax.all_gather(slices[7], "shard", axis=0, tiled=True),
            lax.all_gather(slices[8], "shard", axis=0, tiled=True),
            lax.all_gather(slices[9], "shard", axis=0, tiled=True),
            lax.all_gather(slices[10], "shard", axis=0, tiled=True),
            lax.all_gather(slices[11], "shard", axis=0, tiled=True),
            lax.all_gather(slices[12], "shard", axis=0, tiled=True),
            lax.all_gather(slices[13], "shard", axis=0, tiled=True),
            lax.all_gather(slices[14], "shard", axis=0, tiled=True),
        )
        stream, stored = forward_layer(stream, gathered)
        saved.append((gathered, stored))
    output = stream.astype(jnp.bfloat16)
    gradient = cotangent.astype(jnp.float32)
    owned = [None] * LAYERS
    for layer_index in reversed(range(LAYERS)):
        gathered, stored = saved[layer_index]
        slices = tuple((entry[layer_index] for entry in params))
        gathered = (
            lax.all_gather(slices[0], "shard", axis=0, tiled=True),
            lax.all_gather(slices[1], "shard", axis=0, tiled=True),
            lax.all_gather(slices[2], "shard", axis=0, tiled=True),
            lax.all_gather(slices[3], "shard", axis=0, tiled=True),
            lax.all_gather(slices[4], "shard", axis=0, tiled=True),
            lax.all_gather(slices[5], "shard", axis=0, tiled=True),
            lax.all_gather(slices[6], "shard", axis=0, tiled=True),
            lax.all_gather(slices[7], "shard", axis=0, tiled=True),
            lax.all_gather(slices[8], "shard", axis=0, tiled=True),
            lax.all_gather(slices[9], "shard", axis=0, tiled=True),
            lax.all_gather(slices[10], "shard", axis=0, tiled=True),
            lax.all_gather(slices[11], "shard", axis=0, tiled=True),
            lax.all_gather(slices[12], "shard", axis=0, tiled=True),
            lax.all_gather(slices[13], "shard", axis=0, tiled=True),
            lax.all_gather(slices[14], "shard", axis=0, tiled=True),
        )
        gradient, partials = backward_layer(gradient, gathered, stored)
        shares = (
            lax.psum_scatter(
                partials[0].astype(jnp.bfloat16), "shard", scatter_dimension=0, tiled=True
            ).astype(jnp.float32),
            lax.psum_scatter(
                partials[1].astype(jnp.bfloat16), "shard", scatter_dimension=0, tiled=True
            ).astype(jnp.float32),
            lax.psum_scatter(
                partials[2].astype(jnp.bfloat16), "shard", scatter_dimension=0, tiled=True
            ).astype(jnp.float32),
            lax.psum_scatter(
                partials[3].astype(jnp.bfloat16), "shard", scatter_dimension=0, tiled=True
            ).astype(jnp.float32),
            lax.psum_scatter(
                partials[4].astype(jnp.bfloat16), "shard", scatter_dimension=0, tiled=True
            ).astype(jnp.float32),
            lax.psum_scatter(
                partials[5].astype(jnp.bfloat16), "shard", scatter_dimension=0, tiled=True
            ).astype(jnp.float32),
            lax.psum_scatter(
                partials[6].astype(jnp.bfloat16), "shard", scatter_dimension=0, tiled=True
            ).astype(jnp.float32),
            lax.psum_scatter(
                partials[7].astype(jnp.bfloat16), "shard", scatter_dimension=0, tiled=True
            ).astype(jnp.float32),
            lax.psum_scatter(
                partials[8].astype(jnp.bfloat16), "shard", scatter_dimension=0, tiled=True
            ).astype(jnp.float32),
            lax.psum_scatter(
                partials[9].astype(jnp.bfloat16), "shard", scatter_dimension=0, tiled=True
            ).astype(jnp.float32),
            lax.psum_scatter(
                partials[10].astype(jnp.bfloat16), "shard", scatter_dimension=0, tiled=True
            ).astype(jnp.float32),
            lax.psum_scatter(
                partials[11].astype(jnp.bfloat16), "shard", scatter_dimension=0, tiled=True
            ).astype(jnp.float32),
            lax.psum_scatter(
                partials[12].astype(jnp.bfloat16), "shard", scatter_dimension=0, tiled=True
            ).astype(jnp.float32),
            lax.psum_scatter(
                partials[13].astype(jnp.bfloat16), "shard", scatter_dimension=0, tiled=True
            ).astype(jnp.float32),
            lax.psum_scatter(
                partials[14].astype(jnp.bfloat16), "shard", scatter_dimension=0, tiled=True
            ).astype(jnp.float32),
        )
        owned[layer_index] = shares
    stacked = tuple(
        (jnp.stack([owned[level][position] for level in range(LAYERS)]) for position in range(15))
    )
    stacked = (
        lax.psum(stacked[0].astype(jnp.bfloat16), "rep").astype(jnp.float32),
        lax.psum(stacked[1].astype(jnp.bfloat16), "rep").astype(jnp.float32),
        lax.psum(stacked[2].astype(jnp.bfloat16), "rep").astype(jnp.float32),
        lax.psum(stacked[3].astype(jnp.bfloat16), "rep").astype(jnp.float32),
        lax.psum(stacked[4].astype(jnp.bfloat16), "rep").astype(jnp.float32),
        lax.psum(stacked[5].astype(jnp.bfloat16), "rep").astype(jnp.float32),
        lax.psum(stacked[6].astype(jnp.bfloat16), "rep").astype(jnp.float32),
        lax.psum(stacked[7].astype(jnp.bfloat16), "rep").astype(jnp.float32),
        lax.psum(stacked[8].astype(jnp.bfloat16), "rep").astype(jnp.float32),
        lax.psum(stacked[9].astype(jnp.bfloat16), "rep").astype(jnp.float32),
        lax.psum(stacked[10].astype(jnp.bfloat16), "rep").astype(jnp.float32),
        lax.psum(stacked[11].astype(jnp.bfloat16), "rep").astype(jnp.float32),
        lax.psum(stacked[12].astype(jnp.bfloat16), "rep").astype(jnp.float32),
        lax.psum(stacked[13].astype(jnp.bfloat16), "rep").astype(jnp.float32),
        lax.psum(stacked[14].astype(jnp.bfloat16), "rep").astype(jnp.float32),
    )
    return (
        output,
        gradient,
        stacked[0],
        stacked[1],
        stacked[2],
        stacked[3],
        stacked[4],
        stacked[5],
        stacked[6],
        stacked[7],
        stacked[8],
        stacked[9],
        stacked[10],
        stacked[11],
        stacked[12],
        stacked[13],
        stacked[14],
    )


def solution(mesh):
    return jax.shard_map(
        body,
        mesh=mesh,
        in_specs=(
            P("rep", "shard", None),
            P("rep", "shard", None),
            P(None, "shard"),
            P(None, "shard"),
            P(None, "shard", None),
            P(None, "shard"),
            P(None, "shard", None),
            P(None, "shard", None),
            P(None, "shard"),
            P(None, "shard", None),
            P(None, "shard"),
            P(None, "shard"),
            P(None, "shard"),
            P(None, "shard", None),
            P(None, "shard"),
            P(None, "shard", None),
            P(None, "shard"),
        ),
        out_specs=(
            P("rep", "shard", None),
            P("rep", "shard", None),
            P(None, "shard"),
            P(None, "shard"),
            P(None, "shard", None),
            P(None, "shard"),
            P(None, "shard", None),
            P(None, "shard", None),
            P(None, "shard"),
            P(None, "shard", None),
            P(None, "shard"),
            P(None, "shard"),
            P(None, "shard"),
            P(None, "shard", None),
            P(None, "shard"),
            P(None, "shard", None),
            P(None, "shard"),
        ),
        check_vma=False,
    )
```

profile of v0, /device:TPU:0, one launch (start us, length us, event | category | flops | bytes accessed | tf_op | source)
XLA Modules:
  0.0 1408.4 jit_solution(9612807501176093999)
XLA Ops:
  29.6 13.4 all-reduce.37
  73.3 27.2 %all-gather.49.cloned.1.call-done = bf16[2,1024,768]{2,1,0:T(8,128)(2,1)} async-done(((bf16[2,256,768]{2,1,0:T(8,128)(2,1)}), bf16[2,1024,768]{2,1,0:T(8,128)(2,1)}) %all-gather.49.cloned.1.call-update) | async-done | bytes 3145744 | tf_op jit(solution)/shard_map/all_gather | solution.py:94
  103.7 12.7 multiply_reduce_fusion.3
  116.4 11.0 exponential_reduce_fusion.1
  134.3 12.9 fusion.63
  153.0 36.6 %all-gather.63.cloned.1.call-done = bf16[1,768,3072]{2,1,0:T(8,128)(2,1)} async-done(((bf16[1,192,3072]{2,1,0:T(8,128)(2,1)}), bf16[1,768,3072]{2,1,0:T(8,128)(2,1)}) %all-gather.63.cloned.1.call-update) | async-done | bytes 4718608 | tf_op jit(solution)/shard_map/all_gather | solution.py:309
  189.6 7.0 fusion.57
  199.4 15.8 %multiply_convert_fusion.5 = (bf16[2,256,3072]{2,1,0:T(8,128)(2,1)}, f32[2,256,3072]{2,1,0:T(8,128)}) fusion(f32[2,256,3072]{2,1,0:T(8,128)S(1)} %get-tuple-element.133, f32[3072]{0:T(1024)S(1)} %bitcast.267, u8[256,3072]{1,0:T(8,128)(4,1)S(1)} %get-tuple-element.20, u8[256,3072]{1,0:T(8,128)(4,1)S(1)} %get-tuple-element.19), kind=kLoop, calls=%fused_computation.46 | loop fusion | flops 111673344 | bytes 17313792 | tf_op jit(solution)/shard_map/convert_element_type | solution.py:112
  215.2 14.0 all-gather.65.cloned.1.call-done
  236.7 12.2 all-gather.71.cloned.1.call-done
  251.9 15.9 %all-gather.67.cloned.1.call-done = bf16[1,768,768]{2,1,0:T(8,128)(2,1)} async-done(((bf16[1,192,768]{2,1,0:T(8,128)(2,1)}), bf16[1,768,768]{2,1,0:T(8,128)(2,1)}) %all-gather.67.cloned.1.call-update) | async-done | bytes 1179664 | tf_op jit(solution)/shard_map/all_gather | solution.py:303
  277.7 9.1 all-gather.69.cloned.1.call-done
  290.0 27.3 %all-gather.53.cloned.1.call-done = bf16[2,1024,768]{2,1,0:T(8,128)(2,1)} async-done(((bf16[2,256,768]{2,1,0:T(8,128)(2,1)}), bf16[2,1024,768]{2,1,0:T(8,128)(2,1)}) %all-gather.53.cloned.1.call-update) | async-done | bytes 3145744 | tf_op jit(solution)/shard_map/all_gather | solution.py:94
  321.0 12.1 multiply_reduce_fusion.2
  333.0 11.0 exponential_reduce_fusion
  352.7 12.9 fusion.66
  371.4 35.1 %all-gather.75.cloned.1.call-done = bf16[1,768,3072]{2,1,0:T(8,128)(2,1)} async-done(((bf16[1,192,3072]{2,1,0:T(8,128)(2,1)}), bf16[1,768,3072]{2,1,0:T(8,128)(2,1)}) %all-gather.75.cloned.1.call-update) | async-done | bytes 4718608 | tf_op jit(solution)/shard_map/all_gather | solution.py:309
  406.5 7.4 fusion.58
  416.7 15.9 %multiply_convert_fusion.4 = (bf16[2,256,3072]{2,1,0:T(8,128)(2,1)}, f32[2,256,3072]{2,1,0:T(8,128)}) fusion(f32[2,256,3072]{2,1,0:T(8,128)S(1)} %get-tuple-element.140, f32[3072]{0:T(1024)S(1)} %bitcast.270, u8[256,3072]{1,0:T(8,128)(4,1)S(1)} %get-tuple-element.18, u8[256,3072]{1,0:T(8,128)(4,1)S(1)} %get-tuple-element.17), kind=kLoop, calls=%fused_computation.33 | loop fusion | flops 111673344 | bytes 17313792 | tf_op jit(solution)/shard_map/convert_element_type | solution.py:112
  432.6 13.3 all-gather.77.cloned.1.call-done
  446.0 11.3 fusion.120
  457.3 7.1 multiply_reduce_fusion.4
  471.0 17.7 %multiply_reduce_fusion.1 = (f32[2,12,256]{2,1,0:T(8,128)S(1)}, f32[2,12,256,1024]{3,2,1,0:T(8,128)}) fusion(f32[2,12,256,1024]{3,2,1,0:T(8,128)} %get-tuple-element.137, f32[2,12,256]{2,1,0:T(8,128)S(1)} %log_add_fusion, bf16[2,256,12,64]{1,3,2,0:T(8,128)(2,1)} %bitcast.242, bf16[2,1024,12,64]{1,3,2,0:T(8,128)(2,1)} %bitcast.233), kind=kOutput, calls=%fused_computation.3 | convolution fusion | flops 830466048 | bytes 54312960 | tf_op jit(solution)/shard_map/cqhe,ckhe->chqk/dot_general | solution.py:190
  488.7 16.7 %multiply_convert_fusion.1 = bf16[2,12,256,1024]{3,2,1,0:T(8,128)(2,1)S(1)} fusion(f32[2,12,256,1024]{3,2,1,0:T(8,128)} %get-tuple-element.143, f32[2,12,256,1024]{3,2,1,0:T(8,128)} %get-tuple-element.137, f32[2,12,256]{2,1,0:T(8,128)S(1)} %get-tuple-element.142, f32[2,12,256]{2,1,0:T(8,128)S(1)} %log_add_fusion), kind=kLoop, calls=%fused_computation.2 | loop fusion | flops 31457280 | bytes 62963712 | tf_op jit(solution)/shard_map/convert_element_type | solution.py:194
  515.6 13.6 convolution_convert_fusion.1
  534.2 8.7 fusion.118
  545.8 7.9 reduce-scatter.17.cloned.1.call-done
  556.8 37.4 %reduce-scatter.19.cloned.1.call-done = bf16[2,256,768]{2,1,0:T(8,128)(2,1)} async-done(((bf16[2,1024,768]{2,1,0:T(8,128)(2,1)}), bf16[2,256,768]{2,1,0:T(8,128)(2,1)}) %reduce-scatter.19.cloned.1.call-update) | async-done | bytes 786448 | tf_op jit(solution)/shard_map/reduce_scatter | solution.py:215
  598.7 9.8 fusion.121
  615.4 10.8 convolution_convert_fusion
  630.9 19.1 %multiply_reduce_fusion = (f32[2,12,256]{2,1,0:T(8,128)S(1)}, f32[2,12,256,1024]{3,2,1,0:T(8,128)}) fusion(f32[2,12,256,1024]{3,2,1,0:T(8,128)} %get-tuple-element.130, f32[2,12,256]{2,1,0:T(8,128)S(1)} %copy-done.36, bf16[2,256,12,64]{1,3,2,0:T(8,128)(2,1)} %bitcast.245, bf16[2,1024,12,64]{1,3,2,0:T(8,128)(2,1)S(1)} %bitcast.229), kind=kOutput, calls=%fused_computation.1 | convolution fusion | flops 830466048 | bytes 54312960 | tf_op jit(solution)/shard_map/cqhe,ckhe->chqk/dot_general | solution.py:190
  650.0 16.9 %multiply_convert_fusion = bf16[2,12,256,1024]{3,2,1,0:T(8,128)(2,1)S(1)} fusion(f32[2,12,256,1024]{3,2,1,0:T(8,128)} %get-tuple-element.147, f32[2,12,256,1024]{3,2,1,0:T(8,128)} %get-tuple-element.130, f32[2,12,256]{2,1,0:T(8,128)S(1)} %get-tuple-element.146, f32[2,12,256]{2,1,0:T(8,128)S(1)} %copy-done.36), kind=kLoop, calls=%fused_computation | loop fusion | flops 31457280 | bytes 62963712 | tf_op jit(solution)/shard_map/convert_element_type | solution.py:194
  685.8 8.7 fusion.119
  704.8 8.1 reduce-scatter.21.cloned.1.call-done
  747.1 22.7 %reduce-scatter.37.cloned.1.call-done = bf16[192,768]{1,0:T(8,128)(2,1)} async-done(((bf16[768,768]{1,0:T(8,128)(2,1)}), bf16[192,768]{1,0:T(8,128)(2,1)}) %reduce-scatter.37.cloned.1.call-update) | async-done | bytes 294928 | tf_op jit(solution)/shard_map/reduce_scatter | solution.py:362
  771.6 27.0 %reduce-scatter.27.cloned.1.call-done = bf16[192,768]{1,0:T(8,128)(2,1)} async-done(((bf16[768,768]{1,0:T(8,128)(2,1)}), bf16[192,768]{1,0:T(8,128)(2,1)}) %reduce-scatter.27.cloned.1.call-update) | async-done | bytes 294928 | tf_op jit(solution)/shard_map/reduce_scatter | solution.py:347
  798.6 28.9 %reduce-scatter.25.cloned.1.call-done = bf16[192,768]{1,0:T(8,128)(2,1)} async-done(((bf16[768,768]{1,0:T(8,128)(2,1)}), bf16[192,768]{1,0:T(8,128)(2,1)}) %reduce-scatter.25.cloned.1.call-update) | async-done | bytes 294928 | tf_op jit(solution)/shard_map/reduce_scatter | solution.py:347
  829.5 26.4 %reduce-scatter.35.cloned.1.call-done = bf16[192,768]{1,0:T(8,128)(2,1)} async-done(((bf16[768,768]{1,0:T(8,128)(2,1)}), bf16[192,768]{1,0:T(8,128)(2,1)}) %reduce-scatter.35.cloned.1.call-update) | async-done | bytes 294928 | tf_op jit(solution)/shard_map/reduce_scatter | solution.py:356
  855.8 28.3 %reduce-scatter.33.cloned.1.call-done = bf16[192,768]{1,0:T(8,128)(2,1)} async-done(((bf16[768,768]{1,0:T(8,128)(2,1)}), bf16[192,768]{1,0:T(8,128)(2,1)}) %reduce-scatter.33.cloned.1.call-update) | async-done | bytes 294928 | tf_op jit(solution)/shard_map/reduce_scatter | solution.py:356
  886.1 26.8 %reduce-scatter.31.cloned.1.call-done = bf16[192,768]{1,0:T(8,128)(2,1)} async-done(((bf16[768,768]{1,0:T(8,128)(2,1)}), bf16[192,768]{1,0:T(8,128)(2,1)}) %reduce-scatter.31.cloned.1.call-update) | async-done | bytes 294928 | tf_op jit(solution)/shard_map/reduce_scatter | solution.py:353
  912.9 29.1 %reduce-scatter.29.cloned.1.call-done = bf16[192,768]{1,0:T(8,128)(2,1)} async-done(((bf16[768,768]{1,0:T(8,128)(2,1)}), bf16[192,768]{1,0:T(8,128)(2,1)}) %reduce-scatter.29.cloned.1.call-update) | async-done | bytes 294928 | tf_op jit(solution)/shard_map/reduce_scatter | solution.py:353
  943.9 48.5 %reduce-scatter.47.cloned.1.call-done = bf16[768,768]{1,0:T(8,128)(2,1)} async-done(((bf16[3072,768]{1,0:T(8,128)(2,1)}), bf16[768,768]{1,0:T(8,128)(2,1)}) %reduce-scatter.47.cloned.1.call-update) | async-done | bytes 1179664 | tf_op jit(solution)/shard_map/reduce_scatter | solution.py:380
  992.4 50.4 %reduce-scatter.45.cloned.1.call-done = bf16[768,768]{1,0:T(8,128)(2,1)} async-done(((bf16[3072,768]{1,0:T(8,128)(2,1)}), bf16[768,768]{1,0:T(8,128)(2,1)}) %reduce-scatter.45.cloned.1.call-update) | async-done | bytes 1179664 | tf_op jit(solution)/shard_map/reduce_scatter | solution.py:380
  1046.1 47.7 %reduce-scatter.43.cloned.1.call-done = bf16[192,3072]{1,0:T(8,128)(2,1)} async-done(((bf16[768,3072]{1,0:T(8,128)(2,1)}), bf16[192,3072]{1,0:T(8,128)(2,1)}) %reduce-scatter.43.cloned.1.call-update) | async-done | bytes 1179664 | tf_op jit(solution)/shard_map/reduce_scatter | solution.py:374
  1093.8 51.2 %reduce-scatter.41.cloned.1.call-done = bf16[192,3072]{1,0:T(8,128)(2,1)} async-done(((bf16[768,3072]{1,0:T(8,128)(2,1)}), bf16[192,3072]{1,0:T(8,128)(2,1)}) %reduce-scatter.41.cloned.1.call-update) | async-done | bytes 1179664 | tf_op jit(solution)/shard_map/reduce_scatter | solution.py:374
  1158.6 11.4 all-reduce.36
  1171.7 39.3 %all-reduce.34 = (bf16[2,192]{1,0:T(2,128)(2,1)S(1)}, bf16[2,192]{1,0:T(2,128)(2,1)S(1)}, bf16[2,192]{1,0:T(2,128)(2,1)S(1)}, bf16[2,192]{1,0:T(2,128)(2,1)S(1)}...) all-reduce(bf16[2,192]{1,0:T(2,128)(2,1)S(1)} %pad_maximum_fusion.7, ...), channel_id=1, replica_groups=mesh['rep'=8,'shard'=4] {'rep'}, use_global_device_ids=true, to_apply=%region_30.0 | all-reduce | flops 4608 | bytes 18432 | tf_op jit(solution)/shard_map/psum | solution.py:392
  1225.2 163.8 %all-reduce.40.cloned.1.call-done = (bf16[2,192,768]{2,1,0:T(8,128)(2,1)}, bf16[2,192,768]{2,1,0:T(8,128)(2,1)}, bf16[2,192,768]{2,1,0:T(8,128)(2,1)}, bf16[2,19...) async-done(((bf16[2,192,768]{2,1,0:T(8,128)(2,1)}, bf16[2,192,768]{2,1,0:T(8,128)(2,1)}, bf16[2,192,768]{2,1,0:T(8,128)(2,1)}, ...) | async-done | bytes 7077904 | tf_op jit(solution)/shard_map/psum | solution.py:394
  (486 shorter events, 271.6 us)
Async XLA Ops:
  7.3 35.8 %copy-start.16 = (bf16[2,256,768]{2,1,0:T(8,128)(2,1)S(1)}, bf16[2,256,768]{2,1,0:T(8,128)(2,1)}, u32[]{:S(2)}) copy-start(bf16[2,256,768]{2,1,0:T(8,128)(2,1)} %param.17) | copy-start | bytes 2359300
  7.3 36.4 %all-gather.59.cloned.1.call-start = ((), (), s32[]{:S(2)}) async-start(), calls=%async_computation.38 | async-start | bytes 1474560 | tf_op jit(solution)/shard_map/all_gather | solution.py:302
  9.5 40.7 %all-gather.55.cloned.1.call-start = ((), (), s32[]{:S(2)}) async-start(), calls=%async_computation.36 | async-start | bytes 1474560 | tf_op jit(solution)/shard_map/all_gather | solution.py:303
  11.5 58.5 %all-gather.57.cloned.1.call-start = ((), (), s32[]{:S(2)}) async-start(), calls=%async_computation.37 | async-start | bytes 1474560 | tf_op jit(solution)/shard_map/all_gather | solution.py:300
  12.4 88.1 %all-gather.49.cloned.1.call-start = ((), (), s32[]{:S(2)}) async-start(), calls=%async_computation.17 | async-start | bytes 3932160 | tf_op jit(solution)/shard_map/all_gather | solution.py:94
  43.1 26.9 %copy-start.55 = (f32[768]{0:T(1024)}, f32[768]{0:T(1024)S(1)}, u32[]{:S(2)}) copy-start(f32[768]{0:T(1024)S(1)} %convert_element_type.514) | copy-start | bytes 9220
  46.9 84.2 %all-gather.47.cloned.1.call-start = ((), (), s32[]{:S(2)}) async-start(), calls=%async_computation.16 | async-start | bytes 3932160 | tf_op jit(solution)/shard_map/all_gather | solution.py:95
  53.3 96.7 %all-gather.61.cloned.1.call-start = ((), (), s32[]{:S(2)}) async-start(), calls=%async_computation.39 | async-start | bytes 1474560 | tf_op jit(solution)/shard_map/all_gather | solution.py:305
  55.3 134.3 %all-gather.63.cloned.1.call-start = ((), (), s32[]{:S(2)}) async-start(), calls=%async_computation.40 | async-start | bytes 5898240 | tf_op jit(solution)/shard_map/all_gather | solution.py:309
  56.9 172.3 %all-gather.65.cloned.1.call-start = ((), (), s32[]{:S(2)}) async-start(), calls=%async_computation.41 | async-start | bytes 5898240 | tf_op jit(solution)/shard_map/all_gather | solution.py:311
  60.2 188.6 %all-gather.71.cloned.1.call-start = ((), (), s32[]{:S(2)}) async-start(), calls=%async_computation.44 | async-start | bytes 1474560 | tf_op jit(solution)/shard_map/all_gather | solution.py:302
  61.0 206.8 %all-gather.67.cloned.1.call-start = ((), (), s32[]{:S(2)}) async-start(), calls=%async_computation.42 | async-start | bytes 1474560 | tf_op jit(solution)/shard_map/all_gather | solution.py:303
  61.6 225.3 %all-gather.69.cloned.1.call-start = ((), (), s32[]{:S(2)}) async-start(), calls=%async_computation.43 | async-start | bytes 1474560 | tf_op jit(solution)/shard_map/all_gather | solution.py:300
  62.3 255.1 %all-gather.53.cloned.1.call-start = ((), (), s32[]{:S(2)}) async-start(), calls=%async_computation.19 | async-start | bytes 3932160 | tf_op jit(solution)/shard_map/all_gather | solution.py:94
  62.4 127.2 %copy-start.57 = (f32[768]{0:T(1024)}, f32[768]{0:T(1024)S(1)}, u32[]{:S(2)}) copy-start(f32[768]{0:T(1024)S(1)} %convert_element_type.519) | copy-start | bytes 9220
  62.4 127.2 %copy-start.73 = (f32[768]{0:T(1024)}, f32[768]{0:T(1024)S(1)}, u32[]{:S(2)}) copy-start(f32[768]{0:T(1024)S(1)} %convert_element_type.520) | copy-start | bytes 9220
  152.6 76.6 %copy-start.25 = (f32[2,256,768]{2,1,0:T(8,128)}, f32[2,256,768]{2,1,0:T(8,128)S(1)}, u32[]{:S(2)}) copy-start(f32[2,256,768]{2,1,0:T(8,128)S(1)} %get-tuple-element.132) | copy-start | bytes 4718596
  152.6 44.0 %copy-start.49 = (f32[2,256]{1,0:T(2,128)}, f32[2,256]{1,0:T(2,128)S(1)}, u32[]{:S(2)}) copy-start(f32[2,256]{1,0:T(2,128)S(1)} %broadcast_multiply_fusion.10) | copy-start | bytes 6148
  153.0 43.6 %copy-start.62 = (f32[2,256]{1,0:T(2,128)}, f32[2,256]{1,0:T(2,128)S(1)}, u32[]{:S(2)}) copy-start(f32[2,256]{1,0:T(2,128)S(1)} %add_rsqrt_fusion.2) | copy-start | bytes 6148
  236.7 50.2 %copy-start.42 = (bf16[2,256,768]{2,1,0:T(8,128)(2,1)}, bf16[2,256,768]{2,1,0:T(8,128)(2,1)S(1)}, u32[]{:S(2)}) copy-start(bf16[2,256,768]{2,1,0:T(8,128)(2,1)S(1)} %add_convert_fusion.6) | copy-start | bytes 2359300
  251.8 96.3 %all-gather.51.cloned.1.call-start = ((), (), s32[]{:S(2)}) async-start(), calls=%async_computation.18 | async-start | bytes 3932160 | tf_op jit(solution)/shard_map/all_gather | solution.py:95
  270.7 96.3 %all-gather.73.cloned.1.call-start = ((), (), s32[]{:S(2)}) async-start(), calls=%async_computation.45 | async-start | bytes 1474560 | tf_op jit(solution)/shard_map/all_gather | solution.py:305
  271.3 135.2 %all-gather.75.cloned.1.call-start = ((), (), s32[]{:S(2)}) async-start(), calls=%async_computation.46 | async-start | bytes 5898240 | tf_op jit(solution)/shard_map/all_gather | solution.py:309
  271.9 174.1 %all-gather.77.cloned.1.call-start = ((), (), s32[]{:S(2)}) async-start(), calls=%async_computation.47 | async-start | bytes 5898240 | tf_op jit(solution)/shard_map/all_gather | solution.py:311
  272.5 281.3 %reduce-scatter.17.cloned.1.call-start = ((), (), s32[]{:S(2)}) async-start(), calls=%async_computation.20 | async-start | bytes 3932160 | tf_op jit(solution)/shard_map/reduce_scatter | solution.py:209
  272.5 191.9 %copy-start.59 = (f32[768]{0:T(1024)}, f32[768]{0:T(1024)S(1)}, u32[]{:S(2)}) copy-start(f32[768]{0:T(1024)S(1)} %convert_element_type.527) | copy-start | bytes 9220
  272.5 133.9 %copy-start.75 = (f32[768]{0:T(1024)}, f32[768]{0:T(1024)S(1)}, u32[]{:S(2)}) copy-start(f32[768]{0:T(1024)S(1)} %convert_element_type.528) | copy-start | bytes 9220
  369.9 94.5 %copy-start.53 = (f32[2,256]{1,0:T(2,128)}, f32[2,256]{1,0:T(2,128)S(1)}, u32[]{:S(2)}) copy-start(f32[2,256]{1,0:T(2,128)S(1)} %broadcast_multiply_fusion.8) | copy-start | bytes 6148
  371.4 93.1 %copy-start.68 = (f32[2,256]{1,0:T(2,128)}, f32[2,256]{1,0:T(2,128)S(1)}, u32[]{:S(2)}) copy-start(f32[2,256]{1,0:T(2,128)S(1)} %add_rsqrt_fusion) | copy-start | bytes 6148
  515.6 78.6 %reduce-scatter.19.cloned.1.call-start = ((), (), s32[]{:S(2)}) async-start(), calls=%async_computation.21 | async-start | bytes 3932160 | tf_op jit(solution)/shard_map/reduce_scatter | solution.py:215
  533.9 165.6 %reduce-scatter.23.cloned.1.call-start = ((), (), s32[]{:S(2)}) async-start(), calls=%async_computation.23 | async-start | bytes 3932160 | tf_op jit(solution)/shard_map/reduce_scatter | solution.py:215
  543.8 50.4 %copy-start.7 = (f32[2,256,768]{2,1,0:T(8,128)S(1)}, f32[2,256,768]{2,1,0:T(8,128)}, u32[]{:S(2)}) copy-start(f32[2,256,768]{2,1,0:T(8,128)} %copy-done.6) | copy-start | bytes 4718596
  556.8 41.2 %copy-start.12 = (f32[2,256,768]{2,1,0:T(8,128)S(1)}, f32[2,256,768]{2,1,0:T(8,128)}, u32[]{:S(2)}) copy-start(f32[2,256,768]{2,1,0:T(8,128)} %copy-done.11) | copy-start | bytes 4718596
  629.0 83.9 %reduce-scatter.21.cloned.1.call-start = ((), (), s32[]{:S(2)}) async-start(), calls=%async_computation.22 | async-start | bytes 3932160 | tf_op jit(solution)/shard_map/reduce_scatter | solution.py:209
  674.3 72.8 %reduce-scatter.39.cloned.1.call-start = ((), (), s32[]{:S(2)}) async-start(), calls=%async_computation.31 | async-start | bytes 1474560 | tf_op jit(solution)/shard_map/reduce_scatter | solution.py:362
  678.7 91.0 %reduce-scatter.37.cloned.1.call-start = ((), (), s32[]{:S(2)}) async-start(), calls=%async_computation.30 | async-start | bytes 1474560 | tf_op jit(solution)/shard_map/reduce_scatter | solution.py:362
  681.7 116.9 %reduce-scatter.27.cloned.1.call-start = ((), (), s32[]{:S(2)}) async-start(), calls=%async_computation.25 | async-start | bytes 1474560 | tf_op jit(solution)/shard_map/reduce_scatter | solution.py:347
  685.5 142.0 %reduce-scatter.25.cloned.1.call-start = ((), (), s32[]{:S(2)}) async-start(), calls=%async_computation.24 | async-start | bytes 1474560 | tf_op jit(solution)/shard_map/reduce_scatter | solution.py:347
  697.5 158.3 %reduce-scatter.35.cloned.1.call-start = ((), (), s32[]{:S(2)}) async-start(), calls=%async_computation.29 | async-start | bytes 1474560 | tf_op jit(solution)/shard_map/reduce_scatter | solution.py:356
  699.5 184.7 %reduce-scatter.33.cloned.1.call-start = ((), (), s32[]{:S(2)}) async-start(), calls=%async_computation.28 | async-start | bytes 1474560 | tf_op jit(solution)/shard_map/reduce_scatter | solution.py:356
  702.8 210.1 %reduce-scatter.31.cloned.1.call-start = ((), (), s32[]{:S(2)}) async-start(), calls=%async_computation.27 | async-start | bytes 1474560 | tf_op jit(solution)/shard_map/reduce_scatter | solution.py:353
  704.7 237.3 %reduce-scatter.29.cloned.1.call-start = ((), (), s32[]{:S(2)}) async-start(), calls=%async_computation.26 | async-start | bytes 1474560 | tf_op jit(solution)/shard_map/reduce_scatter | solution.py:353
  716.1 276.3 %reduce-scatter.47.cloned.1.call-start = ((), (), s32[]{:S(2)}) async-start(), calls=%async_computation.35 | async-start | bytes 5898240 | tf_op jit(solution)/shard_map/reduce_scatter | solution.py:380
  722.9 320.0 %reduce-scatter.45.cloned.1.call-start = ((), (), s32[]{:S(2)}) async-start(), calls=%async_computation.34 | async-start | bytes 5898240 | tf_op jit(solution)/shard_map/reduce_scatter | solution.py:380
  731.1 362.7 %reduce-scatter.43.cloned.1.call-start = ((), (), s32[]{:S(2)}) async-start(), calls=%async_computation.33 | async-start | bytes 5898240 | tf_op jit(solution)/shard_map/reduce_scatter | solution.py:374
  739.1 405.9 %reduce-scatter.41.cloned.1.call-start = ((), (), s32[]{:S(2)}) async-start(), calls=%async_computation.32 | async-start | bytes 5898240 | tf_op jit(solution)/shard_map/reduce_scatter | solution.py:374
  747.0 642.1 %all-reduce.40.cloned.1.call-start = ((), (), s32[]{:S(2)}) async-start(), calls=%async_computation.48 | async-start | bytes 14155776 | tf_op jit(solution)/shard_map/psum | solution.py:394
  1156.2 60.1 %copy-start.10 = (f32[2,256,768]{2,1,0:T(8,128)S(1)}, f32[2,256,768]{2,1,0:T(8,128)}, u32[]{:S(2)}) copy-start(f32[2,256,768]{2,1,0:T(8,128)} %copy-done.8) | copy-start | bytes 4718596
  (85 other events, 574.1 us)
Sparse Core Ops, SparseCore 0:
  10.3 20.2 all-gather.58
  32.7 17.4 all-gather.54
  52.3 17.5 all-gather.56
  71.9 28.5 all-gather.48
  102.5 28.5 all-gather.46
  132.5 17.4 all-gather.60
  152.1 37.4 all-gather.62
  191.7 37.4 all-gather.64
  231.4 17.4 all-gather.70
  250.3 17.4 all-gather.66
  269.3 17.4 all-gather.68
  288.8 28.5 all-gather.52
  319.5 28.5 all-gather.50
  349.5 17.4 all-gather.72
  369.0 37.4 all-gather.74
  408.5 37.4 all-gather.76
  515.7 37.9 reduce-scatter.16
  556.3 37.9 reduce-scatter.18
  629.2 37.9 reduce-scatter.22
  674.4 38.4 reduce-scatter.20
  715.5 25.7 reduce-scatter.38
  744.0 25.6 reduce-scatter.36
  772.9 25.7 reduce-scatter.26
  801.8 25.7 reduce-scatter.24
  830.1 25.7 reduce-scatter.34
  858.4 25.7 reduce-scatter.32
  887.2 25.7 reduce-scatter.30
  916.2 25.7 reduce-scatter.28
  944.5 47.8 reduce-scatter.46
  994.9 47.8 reduce-scatter.44
  1045.9 47.8 reduce-scatter.42
  1097.1 47.8 reduce-scatter.40
  1151.0 237.9 all-reduce.39
where the time goes:
time: 1420 us; the launch traced here: 1410 us
  waiting for transfers between devices  816 us (57%)
  matrix products  283 us (20%)
  other arithmetic  127 us (9%)
  local copies, waits for them, and re-layouts  87.4 us (6%)
  blocking collectives  74.7 us (5%)
  between operations  18.6 us (1%)
    psum x1, waiting for transfers between devices, body(): lax.psum(stacked[2].astype(jnp.bfloat16), 'rep').astype(jnp.float32)  164 us
    reduce_scatter x2, waiting for transfers between devices, body(): lax.psum_scatter(partials[11].astype(jnp.bfloat16), 'shard', scatter_dime...  98.9 us
    reduce_scatter x2, waiting for transfers between devices, body(): lax.psum_scatter(partials[13].astype(jnp.bfloat16), 'shard', scatter_dime...  98.9 us
    all_gather x2, waiting for transfers between devices, body(): lax.all_gather(slices[11], 'shard', axis=0, tiled=True)  71.7 us
    reduce_scatter x2, waiting for transfers between devices, body(): lax.psum_scatter(partials[2].astype(jnp.bfloat16), 'shard', scatter_dimen...  55.9 us
    reduce_scatter x2, waiting for transfers between devices, body(): lax.psum_scatter(partials[4].astype(jnp.bfloat16), 'shard', scatter_dimen...  55.9 us
    reduce_scatter x2, waiting for transfers between devices, body(): lax.psum_scatter(partials[5].astype(jnp.bfloat16), 'shard', scatter_dimen...  54.7 us
    all_gather x2, waiting for transfers between devices, forward_layer(): lax.all_gather(keys_b, 'shard', axis=1, tiled=True)  54.5 us
  transfers between devices with their start and end apart: 33, of which 30 were waited for; matrix products, arithmetic and copies ran while one was open for 25% of the time, Pallas kernels for 0%

commit v1 on v0

v1 whole, which is shorter than its diff:
```python
import functools

import jax
import jax.numpy as jnp
from jax import lax
from jax.experimental import pallas as pl
from jax.experimental.pallas import tpu as pltpu
from jax.sharding import Mesh
from jax.sharding import PartitionSpec as P

HEAD = 64
LAYERS = 2
SHARDS = 4
EPSILON = 1e-05
SWAP = [(0, 1), (1, 0)]
F32 = jnp.float32
BF16 = jnp.bfloat16
NN = (((1,), (0,)), ((), ()))
NT = (((1,), (1,)), ((), ()))
TN = (((0,), (0,)), ((), ()))
VMEM_LIMIT = 56 * 1024 * 1024

ATTENTION, UP, DOWN = slice(0, 4), slice(4, 8), slice(8, 12)


def dot(left, right, dims=NN):
    return lax.dot_general(left, right, dims, preferred_element_type=F32)


def swap(values, axis):
    return lax.ppermute(values, axis, SWAP)


def vmem_spec():
    return pl.BlockSpec(memory_space=pltpu.VMEM)


def any_spec():
    return pl.BlockSpec(memory_space=pl.ANY)


def smem_spec():
    return pl.BlockSpec(memory_space=pltpu.SMEM)


def cost(flops, bytes_accessed, transcendentals=0):
    return pl.CostEstimate(
        flops=int(flops), bytes_accessed=int(bytes_accessed), transcendentals=int(transcendentals)
    )


def shaped(shape, dtype):
    return jax.ShapeDtypeStruct(shape, dtype)


def standardize(values):
    average = jnp.mean(values, axis=-1, keepdims=True)
    centered = values - average
    variance = jnp.mean(centered * centered, axis=-1, keepdims=True)
    inverse_scale = lax.rsqrt(variance + EPSILON)
    return centered * inverse_scale, inverse_scale


def norm_input_grad(grad_out, standard, inverse_scale, gain):
    grad_standard = grad_out * gain
    return inverse_scale * (
        grad_standard
        - jnp.mean(grad_standard, axis=-1, keepdims=True)
        - standard * jnp.mean(grad_standard * standard, axis=-1, keepdims=True)
    )


def column_sum(values):
    return jnp.sum(values.astype(F32), axis=0, keepdims=True)


def gelu_parts(hidden):
    density = jnp.exp(-0.5 * hidden * hidden)
    t = 1.0 / (1.0 + (0.3275911 * 0.7071067811865476) * jnp.abs(hidden))
    series = t * (
        0.127414796
        + t * (-0.142248368 + t * (0.7107068705 + t * (-0.7265760135 + t * 0.5307027145)))
    )
    tail = series * density
    phi = jnp.where(hidden >= 0.0, 1.0 - tail, tail)
    return hidden * phi, phi + (hidden * 0.3989422804014327) * density


def share_places(place_ref):
    s, y = place_ref[0], place_ref[1]
    return ((s, None), (s ^ 1, None), (s ^ 2, y), (s ^ 2, 1 - y), (s ^ 3, y), (s ^ 3, 1 - y))


def load_rows(shares, place_ref, blocks, target, sems, rows):
    copies = []
    for index, (share, (shard, half)) in enumerate(zip(shares, share_places(place_ref))):
        start, size = shard * rows, rows
        if half is not None:
            size = rows // 2
            start = start + half * size
        copies.append(
            pltpu.make_async_copy(
                share.at[blocks], target.at[:, pl.ds(pl.multiple_of(start, size), size), :], sems.at[index]
            )
        )
    return copies


def load_blocks(shares, place_ref, blocks, target, sems, rows):
    count = blocks.stop - blocks.start
    copies = []
    for index, (share, (shard, half)) in enumerate(zip(shares, share_places(place_ref))):
        at = pl.ds(shard * count, count)
        place = target.at[at]
        if half is not None:
            size = rows // 2
            place = target.at[at, pl.ds(pl.multiple_of(half * size, size), size)]
        copies.append(pltpu.make_async_copy(share.at[blocks], place, sems.at[index]))
    return copies


def start_all(copies):
    for copy in copies:
        copy.start()


def wait_all(copies):
    for copy in copies:
        copy.wait()


def qkv_kernel(place_ref, stream_ref, vectors_ref, *refs):
    shares, (queries_ref, keys_ref, values_ref, weights, sems) = refs[:6], refs[6:]
    copies = load_rows(shares, place_ref, slice(0, 3), weights, sems, weights.shape[1] // SHARDS)
    start_all(copies)
    standard, _ = standardize(stream_ref[...])
    normed = (standard * vectors_ref[0:1] + vectors_ref[1:2]).astype(BF16)
    wait_all(copies)
    queries = (dot(normed, weights[0]) + vectors_ref[2:3]).astype(BF16)
    queries_ref[...] = queries * jnp.asarray(HEAD ** (-0.5), BF16)
    keys_ref[...] = dot(normed, weights[1]).astype(BF16)
    values_ref[...] = (dot(normed, weights[2]) + vectors_ref[3:4]).astype(BF16)


def project_qkv(place, stream, vectors, shares):
    rows, width = stream.shape
    out = shaped((rows, width), BF16)
    return pl.pallas_call(
        qkv_kernel,
        out_shape=(out, out, out),
        in_specs=[smem_spec(), vmem_spec(), vmem_spec()] + [any_spec()] * 6,
        out_specs=(vmem_spec(),) * 3,
        scratch_shapes=[pltpu.VMEM((3, width, width), BF16), pltpu.SemaphoreType.DMA((6,))],
        compiler_params=pltpu.CompilerParams(vmem_limit_bytes=VMEM_LIMIT),
        cost_estimate=cost(6 * rows * width * width, 10 * rows * width + 6 * width * width),
        name="project_qkv",
    )(place, stream, vectors, *shares)


def attention_kernel(q_ref, ko_ref, kt_ref, vo_ref, vt_ref, mixed_ref, lse_ref):
    queries_t = q_ref[...].T
    row = lax.broadcasted_iota(jnp.int32, queries_t.shape, 0)
    values_t = (vo_ref[...].T, vt_ref[...].T)
    outs = []
    for head in range(2):
        mine = (row >= head * HEAD) & (row < (head + 1) * HEAD)
        q_t = jnp.where(mine, queries_t, jnp.zeros_like(queries_t))
        scores = (dot(ko_ref[...], q_t), dot(kt_ref[...], q_t))
        peak = jnp.maximum(
            jnp.max(scores[0], axis=0, keepdims=True), jnp.max(scores[1], axis=0, keepdims=True)
        )
        weights = tuple(jnp.exp(part - peak) for part in scores)
        total = jnp.sum(weights[0], axis=0, keepdims=True) + jnp.sum(weights[1], axis=0, keepdims=True)
        lse_ref[0, head : head + 1, :] = peak + jnp.log(total)
        at = slice(head * HEAD, (head + 1) * HEAD)
        out = dot(values_t[0][at], weights[0].astype(BF16)) + dot(values_t[1][at], weights[1].astype(BF16))
        outs.append(out / total)
    mixed_ref[...] = jnp.concatenate(outs, axis=0).T.astype(BF16)


def attend(queries, keys, keys_twin, values, values_twin):
    rows, width = queries.shape
    pairs = width // (2 * HEAD)
    block = pl.BlockSpec((rows, 2 * HEAD), lambda pair: (0, pair))
    return pl.pallas_call(
        attention_kernel,
        grid=(pairs,),
        out_shape=(shaped((rows, width), BF16), shaped((pairs, 8, rows), F32)),
        in_specs=[block] * 5,
        out_specs=(block, pl.BlockSpec((1, 8, rows), lambda pair: (pair, 0, 0))),
        compiler_params=pltpu.CompilerParams(vmem_limit_bytes=VMEM_LIMIT),
        cost_estimate=cost(32 * rows * rows * width, 12 * rows * width, 4 * pairs * rows * rows),
        name="attend",
    )(queries, keys, keys_twin, values, values_twin)


def feed_kernel(place_ref, stream_ref, mixed_ref, vectors_ref, up_bias_ref, *refs):
    shares, refs = refs[:6], refs[6:]
    attended_ref, activated_ref, slope_ref, next_ref, out_w, up_w, down_w, sems = refs
    width = stream_ref.shape[1]
    share = width // SHARDS
    out_copies = load_rows(shares, place_ref, slice(3, 4), out_w, sems.at[0], share)
    up_copies = load_rows(shares, place_ref, UP, up_w, sems.at[1], share)
    down_copies = load_blocks(shares, place_ref, DOWN, down_w, sems.at[2], share)
    start_all(out_copies)
    start_all(up_copies)
    start_all(down_copies)
    wait_all(out_copies)
    attended_ref[...] = stream_ref[...] + dot(mixed_ref[...], out_w[0]) + vectors_ref[4:5]
    standard, _ = standardize(attended_ref[...])
    second = (standard * vectors_ref[5:6] + vectors_ref[6:7]).astype(BF16)
    wait_all(up_copies)
    wait_all(down_copies)
    next_ref[...] = attended_ref[...] + vectors_ref[7:8]
    for block in range(SHARDS):
        at = slice(block * width, (block + 1) * width)
        hidden = dot(second, up_w[block]) + up_bias_ref[:, at]
        activated, slope = gelu_parts(hidden)
        activated = activated.astype(BF16)
        activated_ref[:, at] = activated
        slope_ref[:, at] = slope.astype(BF16)
        down = down_w[block * SHARDS : (block + 1) * SHARDS].reshape(width, width)
        next_ref[...] += dot(activated, down)


def feed_forward(place, stream, mixed, vectors, up_bias, shares):
    rows, width = stream.shape
    wide = SHARDS * width
    share = width // SHARDS
    return pl.pallas_call(
        feed_kernel,
        out_shape=(
            shaped((rows, width), F32),
            shaped((rows, wide), BF16),
            shaped((rows, wide), BF16),
            shaped((rows, width), F32),
        ),
        in_specs=[smem_spec()] + [vmem_spec()] * 4 + [any_spec()] * 6,
        out_specs=(vmem_spec(),) * 4,
        scratch_shapes=[
            pltpu.VMEM((1, width, width), BF16),
            pltpu.VMEM((4, width, width), BF16),
            pltpu.VMEM((4 * SHARDS, share, width), BF16),
            pltpu.SemaphoreType.DMA((3, 6)),
        ],
        compiler_params=pltpu.CompilerParams(vmem_limit_bytes=VMEM_LIMIT),
        cost_estimate=cost(18 * rows * width * width, 32 * rows * width + 18 * width * width, rows * wide),
        name="feed_forward",
    )(place, stream, mixed, vectors, up_bias, *shares)


def feed_back_kernel(place_ref, grad_ref, slope_ref, attended_ref, vectors_ref, *refs):
    shares, refs = refs[:6], refs[6:]
    hidden_ref, attended_grad_ref, mixed_grad_ref, sums_ref, up_sums_ref, out_w, up_w, down_w, sems = refs
    width = grad_ref.shape[1]
    share = width // SHARDS
    down_copies = load_blocks(shares, place_ref, DOWN, down_w, sems.at[2], share)
    up_copies = load_rows(shares, place_ref, UP, up_w, sems.at[1], share)
    out_copies = load_rows(shares, place_ref, slice(3, 4), out_w, sems.at[0], share)
    start_all(down_copies)
    start_all(up_copies)
    start_all(out_copies)
    branch = grad_ref[...].astype(BF16)
    sums_ref[...] = jnp.zeros_like(sums_ref)
    sums_ref[7:8] = column_sum(branch)
    wait_all(down_copies)
    wait_all(up_copies)
    second_grad = None
    for block in range(SHARDS):
        at = slice(block * width, (block + 1) * width)
        down = down_w[block * SHARDS : (block + 1) * SHARDS].reshape(width, width)
        hidden_grad = (dot(branch, down, NT) * slope_ref[:, at].astype(F32)).astype(BF16)
        hidden_ref[:, at] = hidden_grad
        up_sums_ref[:, at] = column_sum(hidden_grad)
        part = dot(hidden_grad, up_w[block], NT)
        second_grad = part if second_grad is None else second_grad + part
    standard, inverse = standardize(attended_ref[...])
    sums_ref[5:6] = column_sum(second_grad * standard)
    sums_ref[6:7] = column_sum(second_grad)
    attended_grad = grad_ref[...] + norm_input_grad(second_grad, standard, inverse, vectors_ref[5:6])
    attended_grad_ref[...] = attended_grad
    out_grad = attended_grad.astype(BF16)
    sums_ref[4:5] = column_sum(out_grad)
    wait_all(out_copies)
    mixed_grad_ref[...] = dot(out_grad, out_w[0], NT).astype(BF16)


def feed_back(place, grad, slope, attended, vectors, shares):
    rows, width = grad.shape
    wide = SHARDS * width
    share = width // SHARDS
    return pl.pallas_call(
        feed_back_kernel,
        out_shape=(
            shaped((rows, wide), BF16),
            shaped((rows, width), F32),
            shaped((rows, width), BF16),
            shaped((8, width), F32),
            shaped((1, wide), F32),
        ),
        in_specs=[smem_spec()] + [vmem_spec()] * 4 + [any_spec()] * 6,
        out_specs=(vmem_spec(),) * 5,
        scratch_shapes=[
            pltpu.VMEM((1, width, width), BF16),
            pltpu.VMEM((4, width, width), BF16),
            pltpu.VMEM((4 * SHARDS, share, width), BF16),
            pltpu.SemaphoreType.DMA((3, 6)),
        ],
        compiler_params=pltpu.CompilerParams(vmem_limit_bytes=VMEM_LIMIT),
        cost_estimate=cost(18 * rows * width * width, 30 * rows * width + 18 * width * width),
        name="feed_back",
    )(place, grad, slope, attended, vectors, *shares)


def store_rows(place_ref, work, keep_ref, send_ref, block, sems, rows):
    s = place_ref[0]
    copies = []
    for index, (shard, target) in enumerate(
        ((s, keep_ref.at[0, block]), (s ^ 2, keep_ref.at[1, block]), (s ^ 1, send_ref.at[0, block]), (s ^ 3, send_ref.at[1, block]))
    ):
        source = work.at[pl.ds(pl.multiple_of(shard * rows, rows), rows), :]
        copies.append(pltpu.make_async_copy(source, target, sems.at[index]))
    return copies


def down_grad_kernel(place_ref, activated_ref, grad_ref, out_ref):
    del place_ref
    rows, width = grad_ref.shape
    result = dot(activated_ref[...], grad_ref[...].astype(BF16), TN).astype(BF16)
    out_ref[...] = result.reshape(out_ref.shape)


def down_weight_grad(place, activated, grad):
    rows, width = grad.shape
    share = width // SHARDS

    def shard_of(step, place_ref):
        return place_ref[0] ^ (step // 2 + 2 * (step % 2))

    return pl.pallas_call(
        down_grad_kernel,
        out_shape=shaped((SHARDS, SHARDS, share, width), BF16),
        grid_spec=pltpu.PrefetchScalarGridSpec(
            num_scalar_prefetch=1,
            grid=(SHARDS,),
            in_specs=[
                pl.BlockSpec((rows, width), lambda step, place_ref: (0, shard_of(step, place_ref))),
                pl.BlockSpec((rows, width), lambda step, place_ref: (0, 0)),
            ],
            out_specs=pl.BlockSpec((1, SHARDS, share, width), lambda step, place_ref: (step, 0, 0, 0)),
        ),
        compiler_params=pltpu.CompilerParams(vmem_limit_bytes=VMEM_LIMIT),
        cost_estimate=cost(8 * rows * width * width, 12 * rows * width + 8 * width * width),
        name="down_weight_grad",
    )(place, activated, grad)


def weight_grad_steps(place_ref, keep_ref, send_ref, work, sems, makers):
    pending = [None, None]
    for block, make in enumerate(makers):
        slot = block % 2
        if pending[slot] is not None:
            wait_all(pending[slot])
        work[slot] = make().astype(BF16)
        copies = store_rows(
            place_ref, work.at[slot], keep_ref, send_ref, block, sems.at[slot], work.shape[1] // SHARDS
        )
        start_all(copies)
        pending[slot] = copies
    for copies in pending:
        if copies is not None:
            wait_all(copies)


def feed_weight_grad_kernel(
    place_ref, hidden_ref, attended_ref, attended_grad_ref, mixed_ref, vectors_ref, keep_ref, send_ref, work, sems
):
    width = attended_ref.shape[1]
    standard, _ = standardize(attended_ref[...])
    second = (standard * vectors_ref[5:6] + vectors_ref[6:7]).astype(BF16)
    second_t = second.T

    def up_block(block):
        return lambda: dot(second_t, hidden_ref[:, block * width : (block + 1) * width])

    def out_block():
        return dot(mixed_ref[...], attended_grad_ref[...].astype(BF16), TN)

    makers = [out_block] + [up_block(block) for block in range(SHARDS)]
    weight_grad_steps(place_ref, keep_ref, send_ref, work, sems, makers)


def grad_shapes(count, width):
    share = width // SHARDS
    return (shaped((2, count, share, width), BF16),) * 2


def grad_scratch(width):
    return [pltpu.VMEM((2, width, width), BF16), pltpu.SemaphoreType.DMA((2, 4))]


def feed_weight_grads(place, hidden_grad, attended, attended_grad, mixed, vectors):
    rows, width = attended.shape
    return pl.pallas_call(
        feed_weight_grad_kernel,
        out_shape=grad_shapes(5, width),
        in_specs=[smem_spec()] + [vmem_spec()] * 5,
        out_specs=(any_spec(),) * 2,
        scratch_shapes=grad_scratch(width),
        compiler_params=pltpu.CompilerParams(vmem_limit_bytes=VMEM_LIMIT),
        cost_estimate=cost(10 * rows * width * width, 20 * rows * width + 10 * width * width),
        name="feed_weight_grads",
    )(place, hidden_grad, attended, attended_grad, mixed, vectors)


def qkv_weight_grad_kernel(
    place_ref, stream_ref, vectors_ref, dq_ref, dkv_ref, sums_ref, keep_ref, send_ref, work, sems
):
    standard, _ = standardize(stream_ref[...])
    normed_t = (standard * vectors_ref[0:1] + vectors_ref[1:2]).astype(BF16).T
    sums_ref[...] = jnp.zeros_like(sums_ref)
    sums_ref[2:3] = column_sum(dq_ref[...])
    sums_ref[3:4] = column_sum(dkv_ref[1])
    makers = [
        lambda: dot(normed_t, dq_ref[...]),
        lambda: dot(normed_t, dkv_ref[0]),
        lambda: dot(normed_t, dkv_ref[1]),
    ]
    weight_grad_steps(place_ref, keep_ref, send_ref, work, sems, makers)


def qkv_weight_grads(place, stream, vectors, dq, dkv):
    rows, width = stream.shape
    return pl.pallas_call(
        qkv_weight_grad_kernel,
        out_shape=(shaped((8, width), F32),) + grad_shapes(3, width),
        in_specs=[smem_spec()] + [vmem_spec()] * 4,
        out_specs=(vmem_spec(), any_spec(), any_spec()),
        scratch_shapes=grad_scratch(width),
        compiler_params=pltpu.CompilerParams(vmem_limit_bytes=VMEM_LIMIT),
        cost_estimate=cost(6 * rows * width * width, 10 * rows * width + 6 * width * width),
        name="qkv_weight_grads",
    )(place, stream, vectors, dq, dkv)


def attention_back_kernel(
    q_ref, ko_ref, kt_ref, vo_ref, vt_ref, lse_ref, out_grad_ref, dq_ref, keep_ref, send_ref
):
    queries = q_ref[...]
    out_grad = out_grad_ref[...]
    queries_t, out_grad_t = queries.T, out_grad.T
    row = lax.broadcasted_iota(jnp.int32, queries_t.shape, 0)
    lane = lax.broadcasted_iota(jnp.int32, queries.shape, 1)
    keys, values = (ko_ref, kt_ref), (vo_ref, vt_ref)
    keys_t = tuple(part[...].T for part in keys)
    key_grads, value_grads, query_grads = [None, None], [None, None], []
    for head in range(2):
        low, high = head * HEAD, (head + 1) * HEAD
        mine_t = (row >= low) & (row < high)
        mine = (lane >= low) & (lane < high)
        q_t = jnp.where(mine_t, queries_t, jnp.zeros_like(queries_t))
        o_t = jnp.where(mine_t, out_grad_t, jnp.zeros_like(queries_t))
        q_h = jnp.where(mine, queries, jnp.zeros_like(queries))
        o_h = jnp.where(mine, out_grad, jnp.zeros_like(queries))
        lse = lse_ref[0, head : head + 1, :]
        probability = [jnp.exp(dot(part[...], q_t) - lse) for part in keys]
        probability_grad = [dot(part[...], o_t) for part in values]
        inner = sum(
            jnp.sum(left * right, axis=0, keepdims=True)
            for left, right in zip(probability, probability_grad)
        )
        query_grad = None
        for index in range(2):
            score_grad = (probability[index] * (probability_grad[index] - inner)).astype(BF16)
            value_part = dot(probability[index].astype(BF16), o_h)
            key_part = dot(score_grad, q_h)
            query_part = dot(keys_t[index][low:high], score_grad)
            if head == 0:
                key_grads[index], value_grads[index] = key_part, value_part
            else:
                key_grads[index] += key_part
                value_grads[index] += value_part
            query_grad = query_part if index == 0 else query_grad + query_part
        query_grads.append(query_grad)
    dq_ref[...] = (jnp.concatenate(query_grads, axis=0).T * HEAD ** (-0.5)).astype(BF16)
    keep_ref[0] = key_grads[0].astype(BF16)
    keep_ref[1] = value_grads[0].astype(BF16)
    send_ref[0] = key_grads[1].astype(BF16)
    send_ref[1] = value_grads[1].astype(BF16)


def attend_back(queries, keys, keys_twin, values, values_twin, lse, out_grad):
    rows, width = queries.shape
    pairs = width // (2 * HEAD)
    block = pl.BlockSpec((rows, 2 * HEAD), lambda pair: (0, pair))
    pair_block = pl.BlockSpec((2, rows, 2 * HEAD), lambda pair: (0, 0, pair))
    return pl.pallas_call(
        attention_back_kernel,
        grid=(pairs,),
        out_shape=(
            shaped((rows, width), BF16),
            shaped((2, rows, width), BF16),
            shaped((2, rows, width), BF16),
        ),
        in_specs=[block] * 5 + [pl.BlockSpec((1, 8, rows), lambda pair: (pair, 0, 0)), block],
        out_specs=(block, pair_block, pair_block),
        compiler_params=pltpu.CompilerParams(vmem_limit_bytes=VMEM_LIMIT),
        cost_estimate=cost(80 * rows * rows * width, 24 * rows * width, 4 * pairs * rows * rows),
        name="attend_back",
    )(queries, keys, keys_twin, values, values_twin, lse, out_grad)


def norm_back_kernel(place_ref, stream_ref, vectors_ref, attended_grad_ref, dq_ref, dkv_ref, *refs):
    shares, (grad_ref, sums_ref, weights, sems) = refs[:6], refs[6:]
    copies = load_rows(shares, place_ref, slice(0, 3), weights, sems, weights.shape[1] // SHARDS)
    start_all(copies)
    standard, inverse = standardize(stream_ref[...])
    wait_all(copies)
    normed_grad = (
        dot(dq_ref[...], weights[0], NT) + dot(dkv_ref[0], weights[1], NT) + dot(dkv_ref[1], weights[2], NT)
    )
    sums_ref[...] = jnp.zeros_like(sums_ref)
    sums_ref[0:1] = column_sum(normed_grad * standard)
    sums_ref[1:2] = column_sum(normed_grad)
    grad_ref[...] = attended_grad_ref[...] + norm_input_grad(
        normed_grad, standard, inverse, vectors_ref[0:1]
    )


def norm_back(place, stream, vectors, attended_grad, dq, dkv, shares):
    rows, width = stream.shape
    return pl.pallas_call(
        norm_back_kernel,
        out_shape=(shaped((rows, width), F32), shaped((8, width), F32)),
        in_specs=[smem_spec()] + [vmem_spec()] * 5 + [any_spec()] * 6,
        out_specs=(vmem_spec(),) * 2,
        scratch_shapes=[pltpu.VMEM((3, width, width), BF16), pltpu.SemaphoreType.DMA((6,))],
        compiler_params=pltpu.CompilerParams(vmem_limit_bytes=VMEM_LIMIT),
        cost_estimate=cost(6 * rows * width * width, 18 * rows * width + 6 * width * width),
        name="norm_back",
    )(place, stream, vectors, attended_grad, dq, dkv, *shares)


def half_of(values, half):
    size = values.shape[-2] // 2
    return lax.dynamic_slice_in_dim(values, half * size, size, axis=values.ndim - 2)


def gather_shares(own, y):
    twin = swap(own, "core")
    near = swap(half_of(own, y), "x")
    far = swap(near, "y")
    return (own, twin, near, far, swap(near, "core"), swap(far, "core"))


def add(left, right):
    return (left.astype(F32) + right.astype(F32)).astype(BF16)


def reduce_grads(keep, send, y):
    back = swap(send, "core")
    other = add(keep[1], back[1])
    mine = add(keep[0], back[0])
    share = add(mine, swap(other, "x"))
    part = add(half_of(share, y), swap(half_of(share, 1 - y), "y"))
    part = lax.psum(part, "z")
    rest = swap(part, "y")
    ordered = jnp.where(
        y == 0, jnp.concatenate([part, rest], axis=-2), jnp.concatenate([rest, part], axis=-2)
    )
    return ordered.astype(F32)


def body(
    frames,
    cotangent,
    first_gain,
    first_shift,
    query_weight,
    query_bias,
    key_weight,
    value_weight,
    value_bias,
    out_weight,
    out_bias,
    second_gain,
    second_shift,
    up_weight,
    up_bias,
    down_weight,
    down_bias,
):
    x, y, core = lax.axis_index("x"), lax.axis_index("y"), lax.axis_index("core")
    shard = 2 * x + core
    place = jnp.stack([shard, y]).astype(jnp.int32)
    quarter, width = frames.shape[1:]
    share = width // SHARDS

    def to_clip(values):
        mine = lax.dynamic_index_in_dim(values, x, 0, keepdims=False)
        other = lax.dynamic_index_in_dim(values, 1 - x, 0, keepdims=False)
        return jnp.concatenate([mine, swap(other, "x")], axis=0).astype(F32)

    def from_clip(values):
        mine, other = values[:quarter], swap(values[quarter:], "x")
        return jnp.where(x == 0, jnp.stack([mine, other]), jnp.stack([other, mine]))

    small = jnp.stack(
        [first_gain, first_shift, query_bias, value_bias, out_bias, second_gain, second_shift, down_bias], axis=1
    )
    small = jnp.concatenate([small, up_bias.reshape(LAYERS, SHARDS, share)], axis=1)
    small = lax.all_gather(small, ("x", "core"), axis=0).astype(F32)
    vectors = jnp.transpose(small[:, :, :8], (1, 2, 0, 3)).reshape(LAYERS, 8, width)
    up_biases = jnp.transpose(small[:, :, 8:], (1, 0, 2, 3)).reshape(LAYERS, 1, SHARDS * width)

    stream = to_clip(frames)
    saved = []
    for layer in range(LAYERS):
        pack = jnp.concatenate(
            [
                jnp.stack([query_weight[layer], key_weight[layer], value_weight[layer], out_weight[layer]]),
                jnp.transpose(up_weight[layer].reshape(share, SHARDS, width), (1, 0, 2)),
                down_weight[layer].reshape(SHARDS, share, width),
            ],
            axis=0,
        )
        shares = gather_shares(pack, y)
        queries, keys, values = project_qkv(place, stream, vectors[layer], shares)
        keys_twin, values_twin = swap(keys, "core"), swap(values, "core")
        mixed, lse = attend(queries, keys, keys_twin, values, values_twin)
        attended, activated, slope, following = feed_forward(
            place, stream, mixed, vectors[layer], up_biases[layer], shares
        )
        saved.append(
            (shares, stream, queries, keys, keys_twin, values, values_twin, mixed, lse, attended, activated, slope)
        )
        stream = following
    output = from_clip(stream.astype(BF16))

    gradient = to_clip(cotangent)
    owned, sums = [None] * LAYERS, [None] * LAYERS
    for layer in reversed(range(LAYERS)):
        shares, stream, queries, keys, keys_twin, values, values_twin, mixed, lse, attended, activated, slope = saved[
            layer
        ]
        down = down_weight_grad(place, activated, gradient)
        hidden_grad, attended_grad, mixed_grad, feed_sums, up_sums = feed_back(
            place, gradient, slope, attended, vectors[layer], shares
        )
        feed_keep, feed_send = feed_weight_grads(
            place, hidden_grad, attended, attended_grad, mixed, vectors[layer]
        )
        dq, dkv_keep, dkv_send = attend_back(queries, keys, keys_twin, values, values_twin, lse, mixed_grad)
        dkv = add(dkv_keep, swap(dkv_send, "core"))
        qkv_sums, qkv_keep, qkv_send = qkv_weight_grads(place, stream, vectors[layer], dq, dkv)
        gradient, norm_sums = norm_back(place, stream, vectors[layer], attended_grad, dq, dkv, shares)
        owned[layer] = (
            reduce_grads(down[:2], down[2:], y),
            reduce_grads(feed_keep, feed_send, y),
            reduce_grads(qkv_keep, qkv_send, y),
        )
        sums[layer] = jnp.concatenate(
            [feed_sums + qkv_sums + norm_sums, up_sums.reshape(SHARDS, width)], axis=0
        )
    input_grad = from_clip(gradient.astype(BF16)).astype(F32)

    totals = lax.psum(jnp.stack(sums), ("z", "y", "x", "core"))
    own_vectors = lax.dynamic_slice_in_dim(totals[:, :8], shard * share, share, axis=2)
    own_up = lax.dynamic_slice_in_dim(
        totals[:, 8:].reshape(LAYERS, SHARDS * width), shard * width, width, axis=1
    )

    def both(part, block):
        return jnp.stack([owned[layer][part][block] for layer in range(LAYERS)])

    up_grad = jnp.stack(
        [
            jnp.transpose(owned[layer][1][1:], (1, 0, 2)).reshape(share, SHARDS * width)
            for layer in range(LAYERS)
        ]
    )
    down_grad = jnp.stack([owned[layer][0].reshape(width, width) for layer in range(LAYERS)])
    vector = [own_vectors[:, index] for index in range(8)]
    return (
        output,
        input_grad,
        vector[0],
        vector[1],
        both(2, 0),
        vector[2],
        both(2, 1),
        both(2, 2),
        vector[3],
        both(1, 0),
        vector[4],
        vector[5],
        vector[6],
        up_grad,
        own_up,
        down_grad,
        vector[7],
    )


def solution(mesh):
    groups = mesh.shape["rep"]
    finer = Mesh(mesh.devices.reshape(groups // 2, 2, 2, 2), ("z", "y", "x", "core"))
    rep, shard = ("z", "y"), ("x", "core")
    rows = P(rep, shard, None)
    vector, matrix = P(None, shard), P(None, shard, None)
    parameters = (
        vector,
        vector,
        matrix,
        vector,
        matrix,
        matrix,
        vector,
        matrix,
        vector,
        vector,
        vector,
        matrix,
        vector,
        matrix,
        vector,
    )
    return jax.shard_map(
        body,
        mesh=finer,
        in_specs=(rows, rows) + parameters,
        out_specs=(rows, rows) + parameters,
        check_vma=False,
    )
```

time: 1420 us -> 833 us (0.59)
  waiting for transfers between devices: 816 us -> 414 us
  matrix products: 283 us -> 0 us
  Pallas kernels: 0 us -> 217 us
  other arithmetic: 127 us -> 52.5 us
  blocking collectives: 74.7 us -> 5.23 us
  starting transfers between devices: 2.07 us -> 36 us
    reduce_scatter x16 -> x0, waiting for transfers between devices: 441 us -> none  [the longest x2 98.9 us: body(): lax.psum_scatter(partials[11].astype(jnp.bfloat16), 'shard', scatter_dime...]
    ppermute x0 -> x44, waiting for transfers between devices: none -> 297 us  [swap(): return lax.ppermute(values, axis, SWAP)]
    dot_general x48 -> x0, matrix products: 283 us -> none  [the longest x12 50.8 us: project_back(): jnp.einsum('cfe,de->cfd', left, right, preferred_element_type=jnp.float32)]
    pallas_call x0 -> x18, Pallas kernels: none -> 217 us  [the longest x2 45.6 us: attend_back(): pl.pallas_call(attention_back_kernel, grid=(pairs,), out_shape=(shaped((r...]
    all_gather x16 -> x0, waiting for transfers between devices: 208 us -> none  [the longest x2 71.7 us: body(): lax.all_gather(slices[11], 'shard', axis=0, tiled=True)]
    psum x1 -> x2, waiting for transfers between devices: 164 us -> 117 us  [the longest x1 117 us: reduce_grads(): part = lax.psum(part, 'z')]
    convert_element_type x38 -> x30, other arithmetic: 82.9 us -> 39.2 us  [the longest x20 31.2 us: add(): return (left.astype(F32) + right.astype(F32)).astype(BF16)]
    psum x1 -> x0, blocking collectives: 39.3 us -> none  [body(): lax.psum(stacked[0].astype(jnp.bfloat16), 'rep').astype(jnp.float32)]
  transfers between devices with their start and end apart: 33 -> 46, of which waited for: 30 -> 18; matrix products, arithmetic and copies ran while one was open for 25% -> 11% of each run, Pallas kernels for 0% -> 17%
where the time goes in v1:
time: 833 us; the launch traced here: 825 us
  waiting for transfers between devices  414 us (50%)
  Pallas kernels  217 us (26%)
  local copies, waits for them, and re-layouts  85.2 us (10%)
  other arithmetic  52.5 us (6%)
  starting transfers between devices  36 us (4%)
  between operations  15.1 us (2%)
    ppermute x44, waiting for transfers between devices, swap(): return lax.ppermute(values, axis, SWAP)  297 us
    psum x1, waiting for transfers between devices, reduce_grads(): part = lax.psum(part, 'z')  117 us
    pallas_call x2, Pallas kernels, attend_back(): pl.pallas_call(attention_back_kernel, grid=(pairs,), out_shape=(shaped((r...  45.6 us
    ppermute x44, starting transfers between devices, swap(): return lax.ppermute(values, axis, SWAP)  35.7 us
    pallas_call x2, Pallas kernels, feed_forward(): pl.pallas_call(feed_kernel, out_shape=(shaped((rows, width), F32), shaped...  34.1 us
    convert_element_type x20, other arithmetic, add(): return (left.astype(F32) + right.astype(F32)).astype(BF16)  31.2 us
    pallas_call x2, Pallas kernels, feed_back(): pl.pallas_call(feed_back_kernel, out_shape=(shaped((rows, wide), BF16), s...  30.5 us
    pallas_call x2, Pallas kernels, attend(): pl.pallas_call(attention_kernel, grid=(pairs,), out_shape=(shaped((rows,...  27.8 us
  transfers between devices with their start and end apart: 46, of which 18 were waited for; matrix products, arithmetic and copies ran while one was open for 11% of the time, Pallas kernels for 17%

profile of v1, /device:TPU:0, one launch (start us, length us, event | category | flops | bytes accessed | tf_op | source)
XLA Modules:
  0.0 824.8 jit_solution(1542272919680645347)
XLA Ops:
  9.1 3.2 fusion.24
  12.3 3.5 reshape_squeeze.12
  15.7 3.2 fusion.23
  28.4 2.9 collective-permute-start.2
  31.4 3.5 reshape_squeeze.14
  34.8 35.5 %collective-permute-done.2.refs_2_ = bf16[12,96,768]{2,1,0:T(8,128)(2,1)} collective-permute-done((bf16[12,96,768]{2,1,0:T(8,128)(2,1)}, bf16[12,96,768]{2,1,0:T(8,128)(2,1)}, u32[]{:S(2)}, u32[]{:S(2)}) %collective-permute-start.2) | collective-permute-done | bytes 1769504 | tf_op jit(solution)/shard_map/ppermute | solution.py:31
  78.9 31.5 %collective-permute-done.3.refs_3_ = bf16[12,96,768]{2,1,0:T(8,128)(2,1)} collective-permute-done((bf16[12,96,768]{2,1,0:T(8,128)(2,1)}, bf16[12,96,768]{2,1,0:T(8,128)(2,1)}, u32[]{:S(2)}, u32[]{:S(2)}) %collective-permute-start.3) | collective-permute-done | bytes 1769504 | tf_op jit(solution)/shard_map/ppermute | solution.py:31
  110.4 12.4 %collective-permute-done = bf16[256,768]{1,0:T(8,128)(2,1)S(1)} collective-permute-done((bf16[256,768]{1,0:T(8,128)(2,1)S(1)}, bf16[256,768]{1,0:T(8,128)(2,1)S(1)}, u32[]{:S(2)}, u32[]{:S(2)}) %collective-permute-start) | collective-permute-done | bytes 393248 | tf_op jit(solution)/shard_map/ppermute | solution.py:31
  134.4 5.2 all-gather
  147.9 6.3 project_qkv.2
  155.1 9.0 %collective-permute-done.10.refs_3_ = bf16[12,96,768]{2,1,0:T(8,128)(2,1)} collective-permute-done((bf16[12,96,768]{2,1,0:T(8,128)(2,1)}, bf16[12,96,768]{2,1,0:T(8,128)(2,1)}, u32[]{:S(2)}, u32[]{:S(2)}) %collective-permute-start.10) | collective-permute-done | bytes 1769504 | tf_op jit(solution)/shard_map/ppermute | solution.py:31
  167.7 13.8 %attend.2 = (bf16[512,768]{1,0:T(8,128)(2,1)}, f32[6,8,512]{2,1,0:T(8,128)}) custom-call(bf16[512,768]{1,0:T(8,128)(2,1)} %get-tuple-element.65.q_ref, bf16[512,768]{1,0:T(8,128)(2,1)} %get-tuple-element.66.ko_ref, bf16[512,768]{1,0:T(8,128)(2,1)} %collective-permute-done.6.kt_ref, bf16[512,768]{1,0:T(8,128)(2,1)} %get-tuple-element.67.vo_ref, ...), custom_call_target="tpu_custom_call" | custom-call | flops 6442450944 | bytes 4718592 | tf_op jit(solution)/shard_map/attend/pallas_call | solution.py:185
  181.5 17.0 %feed_forward.2 = (f32[512,768]{1,0:T(8,128)}, bf16[512,3072]{1,0:T(8,128)(2,1)}, bf16[512,3072]{1,0:T(8,128)(2,1)}, f32[512,768]{1,0:T(8,128)}) custom-call(s32[2]{0:T(128)} %pad_add_fusion.place_ref, f32[512,768]{1,0:T(8,128)} %maximum_convert_fusion.1.stream_ref, bf16[512,768]{1,0:T(8,128)(2,1)} %get-tuple-element.68.mixed_ref, ...), custom_call_target="tpu_custom_call" | custom-call | flops 5435817984 | bytes 23199744 | tf_op jit(solution)/shard_map/feed_forward/pallas_call | solution.py:230
  198.5 6.4 project_qkv.3
  207.9 9.3 %collective-permute-done.16 = bf16[256,768]{1,0:T(8,128)(2,1)S(1)} collective-permute-done((bf16[256,768]{1,0:T(8,128)(2,1)S(1)}, bf16[256,768]{1,0:T(8,128)(2,1)S(1)}, u32[]{:S(2)}, u32[]{:S(2)}) %collective-permute-start.16) | collective-permute-done | bytes 393248 | tf_op jit(solution)/shard_map/ppermute | solution.py:31
  219.6 14.0 %attend.3 = (bf16[512,768]{1,0:T(8,128)(2,1)}, f32[6,8,512]{2,1,0:T(8,128)}) custom-call(bf16[512,768]{1,0:T(8,128)(2,1)} %get-tuple-element.70.q_ref, bf16[512,768]{1,0:T(8,128)(2,1)} %get-tuple-element.71.ko_ref, bf16[512,768]{1,0:T(8,128)(2,1)} %copy-done.41, bf16[512,768]{1,0:T(8,128)(2,1)} %get-tuple-element.72.vo_ref, bf16[512,768]{1,0:T(8,128)(2,1)} %copy-done.42), custom_call_target="tpu_custom_call" | custom-call | flops 6442450944 | bytes 4718592 | tf_op jit(solution)/shard_map/attend/pallas_call | solution.py:185
  233.6 17.1 %feed_forward.3 = (f32[512,768]{1,0:T(8,128)}, bf16[512,3072]{1,0:T(8,128)(2,1)}, bf16[512,3072]{1,0:T(8,128)(2,1)}, f32[512,768]{1,0:T(8,128)}) custom-call(s32[2]{0:T(128)} %pad_add_fusion.place_ref, f32[512,768]{1,0:T(8,128)} %get-tuple-element.69.stream_ref, bf16[512,768]{1,0:T(8,128)(2,1)} %get-tuple-element.73.mixed_ref, ...), custom_call_target="tpu_custom_call" | custom-call | flops 5435817984 | bytes 23199744 | tf_op jit(solution)/shard_map/feed_forward/pallas_call | solution.py:230
  250.7 15.3 %feed_back.2 = (bf16[512,3072]{1,0:T(8,128)(2,1)}, f32[512,768]{1,0:T(8,128)}, bf16[512,768]{1,0:T(8,128)(2,1)}, f32[8,768]{1,0:T(8,128)}, f32[1,3072]{1,0:T(1,128)}) custom-call(s32[2]{0:T(128)} %pad_add_fusion.place_ref, f32[512,768]{1,0:T(8,128)} %maximum_convert_fusion.2.grad_ref, bf16[512,3072]{1,0:T(8,128)(2,1)} %get-tuple-element.75.slope_ref, ...), custom_call_target="tpu_custom_call" | custom-call | flops 5435817984 | bytes 22413312 | tf_op jit(solution)/shard_map/feed_back/pallas_call | solution.py:292
  266.0 22.6 %attend_back.2 = (bf16[512,768]{1,0:T(8,128)(2,1)}, bf16[2,512,768]{2,1,0:T(8,128)(2,1)}, bf16[2,512,768]{2,1,0:T(8,128)(2,1)}) custom-call(bf16[512,768]{1,0:T(8,128)(2,1)} %get-tuple-element.70.q_ref, bf16[512,768]{1,0:T(8,128)(2,1)} %get-tuple-element.71.ko_ref, bf16[512,768]{1,0:T(8,128)(2,1)} %copy-done.41, bf16[512,768]{1,0:T(8,128)(2,1)} %get-tuple-element.72.vo_ref, ...), custom_call_target="tpu_custom_call" | custom-call | flops 16106127360 | bytes 9437184 | tf_op jit(solution)/shard_map/attend_back/pallas_call | solution.py:497
  288.7 9.3 %feed_weight_grads.3 = (bf16[2,5,192,768]{3,2,1,0:T(8,128)(2,1)}, bf16[2,5,192,768]{3,2,1,0:T(8,128)(2,1)}) custom-call(s32[2]{0:T(128)} %pad_add_fusion.place_ref, bf16[512,3072]{1,0:T(8,128)(2,1)} %get-tuple-element.108.hidden_ref, f32[512,768]{1,0:T(8,128)} %get-tuple-element.76.attended_ref, f32[512,768]{1,0:T(8,128)} %get-tuple-element.77.attended_grad_ref, ...), custom_call_target="tpu_custom_call" | custom-call | flops 3019898880 | bytes 13762560 | tf_op jit(solution)/shard_map/feed_weight_grads/pallas_call | solution.py:404
  298.5 7.7 down_weight_grad.3
  306.2 3.3 slice.328
  311.1 8.3 %norm_back.2 = (f32[512,768]{1,0:T(8,128)}, f32[8,768]{1,0:T(8,128)}) custom-call(s32[2]{0:T(128)} %pad_add_fusion.place_ref, f32[512,768]{1,0:T(8,128)} %get-tuple-element.69.stream_ref, f32[8,768]{1,0:T(8,128)} %squeeze.41.vectors_ref, f32[512,768]{1,0:T(8,128)} %get-tuple-element.77.attended_grad_ref, bf16[512,768]{1,0:T(8,128)(2,1)} %get-tuple-element.80.dq_ref, ...), custom_call_target="tpu_custom_call" | custom-call | flops 1811939328 | bytes 10616832 | tf_op jit(solution)/shard_map/norm_back/pallas_call | solution.py:532
  319.4 15.2 %feed_back.3 = (bf16[512,3072]{1,0:T(8,128)(2,1)}, f32[512,768]{1,0:T(8,128)}, bf16[512,768]{1,0:T(8,128)(2,1)}, f32[8,768]{1,0:T(8,128)}, f32[1,3072]{1,0:T(1,128)}) custom-call(s32[2]{0:T(128)} %pad_add_fusion.place_ref, f32[512,768]{1,0:T(8,128)} %get-tuple-element.83.grad_ref, bf16[512,3072]{1,0:T(8,128)(2,1)} %get-tuple-element.84.slope_ref, ...), custom_call_target="tpu_custom_call" | custom-call | flops 5435817984 | bytes 22413312 | tf_op jit(solution)/shard_map/feed_back/pallas_call | solution.py:292
  334.7 23.0 %attend_back.3 = (bf16[512,768]{1,0:T(8,128)(2,1)}, bf16[2,512,768]{2,1,0:T(8,128)(2,1)}, bf16[2,512,768]{2,1,0:T(8,128)(2,1)}) custom-call(bf16[512,768]{1,0:T(8,128)(2,1)} %get-tuple-element.65.q_ref, bf16[512,768]{1,0:T(8,128)(2,1)} %get-tuple-element.66.ko_ref, bf16[512,768]{1,0:T(8,128)(2,1)} %collective-permute-done.6.kt_ref, ...), custom_call_target="tpu_custom_call" | custom-call | flops 16106127360 | bytes 9437184 | tf_op jit(solution)/shard_map/attend_back/pallas_call | solution.py:497
  360.8 7.5 qkv_weight_grads.3
  368.4 9.5 %feed_weight_grads.2 = (bf16[2,5,192,768]{3,2,1,0:T(8,128)(2,1)}, bf16[2,5,192,768]{3,2,1,0:T(8,128)(2,1)}) custom-call(s32[2]{0:T(128)} %pad_add_fusion.place_ref, bf16[512,3072]{1,0:T(8,128)(2,1)} %get-tuple-element.105.hidden_ref, f32[512,768]{1,0:T(8,128)} %get-tuple-element.85.attended_ref, f32[512,768]{1,0:T(8,128)} %get-tuple-element.86.attended_grad_ref, ...), custom_call_target="tpu_custom_call" | custom-call | flops 3019898880 | bytes 13762560 | tf_op jit(solution)/shard_map/feed_weight_grads/pallas_call | solution.py:404
  378.4 7.8 down_weight_grad.2
  386.2 3.3 slice.323
  395.4 3.0 add_convert_fusion.dkv_ref
  398.4 7.6 qkv_weight_grads.2
  406.3 8.3 %norm_back.3 = (f32[512,768]{1,0:T(8,128)}, f32[8,768]{1,0:T(8,128)}) custom-call(s32[2]{0:T(128)} %pad_add_fusion.place_ref, f32[512,768]{1,0:T(8,128)} %maximum_convert_fusion.1.stream_ref, f32[8,768]{1,0:T(8,128)} %squeeze.39.vectors_ref, f32[512,768]{1,0:T(8,128)} %get-tuple-element.86.attended_grad_ref, bf16[512,768]{1,0:T(8,128)(2,1)} %get-tuple-element.89.dq_ref, ...), custom_call_target="tpu_custom_call" | custom-call | flops 1811939328 | bytes 10616832 | tf_op jit(solution)/shard_map/norm_back/pallas_call | solution.py:532
  428.6 10.1 %collective-permute-done.42 = bf16[4,96,768]{2,1,0:T(8,128)(2,1)} collective-permute-done((bf16[4,96,768]{2,1,0:T(8,128)(2,1)S(1)}, bf16[4,96,768]{2,1,0:T(8,128)(2,1)}, u32[]{:S(2)}, u32[]{:S(2)}) %collective-permute-start.42) | collective-permute-done | bytes 589856 | tf_op jit(solution)/shard_map/ppermute | solution.py:31
  449.1 23.2 %collective-permute-done.33 = bf16[5,192,768]{2,1,0:T(8,128)(2,1)S(1)} collective-permute-done((bf16[5,192,768]{2,1,0:T(8,128)(2,1)}, bf16[5,192,768]{2,1,0:T(8,128)(2,1)S(1)}, u32[]{:S(2)}, u32[]{:S(2)}) %collective-permute-start.33) | collective-permute-done | bytes 1474592 | tf_op jit(solution)/shard_map/ppermute | solution.py:31
  474.5 23.4 %collective-permute-done.37 = bf16[4,192,768]{2,1,0:T(8,128)(2,1)S(1)} collective-permute-done((bf16[4,192,768]{2,1,0:T(8,128)(2,1)S(1)}, bf16[4,192,768]{2,1,0:T(8,128)(2,1)S(1)}, u32[]{:S(2)}, u32[]{:S(2)}) %collective-permute-start.37) | collective-permute-done | bytes 1179680 | tf_op jit(solution)/shard_map/ppermute | solution.py:31
  500.6 47.9 %collective-permute-done.21 = bf16[3,192,768]{2,1,0:T(8,128)(2,1)S(1)} collective-permute-done((bf16[3,192,768]{2,1,0:T(8,128)(2,1)S(1)}, bf16[3,192,768]{2,1,0:T(8,128)(2,1)S(1)}, u32[]{:S(2)}, u32[]{:S(2)}) %collective-permute-start.21) | collective-permute-done | bytes 884768 | tf_op jit(solution)/shard_map/ppermute | solution.py:31
  555.1 6.9 collective-permute-done.22
  562.9 13.8 %collective-permute-done.30 = bf16[5,96,768]{2,1,0:T(8,128)(2,1)S(1)} collective-permute-done((bf16[5,96,768]{2,1,0:T(8,128)(2,1)S(1)}, bf16[5,96,768]{2,1,0:T(8,128)(2,1)S(1)}, u32[]{:S(2)}, u32[]{:S(2)}) %collective-permute-start.30) | collective-permute-done | bytes 737312 | tf_op jit(solution)/shard_map/ppermute | solution.py:31
  580.8 8.5 %collective-permute-done.15 = bf16[256,768]{1,0:T(8,128)(2,1)S(1)} collective-permute-done((bf16[256,768]{1,0:T(8,128)(2,1)S(1)}, bf16[256,768]{1,0:T(8,128)(2,1)S(1)}, u32[]{:S(2)}, u32[]{:S(2)}) %collective-permute-start.15) | collective-permute-done | bytes 393248 | tf_op jit(solution)/shard_map/ppermute | solution.py:31
  597.0 116.8 %all-reduce.6.cloned.1.call-done = (bf16[3,96,768]{2,1,0:T(8,128)(2,1)}, bf16[3,96,768]{2,1,0:T(8,128)(2,1)}, bf16[5,96,768]{2,1,0:T(8,128)(2,1)}, bf16[5,96,768...) async-done(((bf16[3,96,768]{2,1,0:T(8,128)(2,1)}, bf16[3,96,768]{2,1,0:T(8,128)(2,1)}, bf16[5,96,768]{2,1,0:T(8,128)(2,1)}, ...) | async-done | bytes 3538960 | tf_op jit(solution)/shard_map/psum | solution.py:566
  722.6 4.5 collective-permute-done.27
  730.1 6.5 collective-permute-done.23
  739.5 41.3 %collective-permute-done.43 = bf16[4,96,768]{2,1,0:T(8,128)(2,1)S(1)} collective-permute-done((bf16[4,96,768]{2,1,0:T(8,128)(2,1)}, bf16[4,96,768]{2,1,0:T(8,128)(2,1)S(1)}, u32[]{:S(2)}, u32[]{:S(2)}) %collective-permute-start.43) | collective-permute-done | bytes 589856 | tf_op jit(solution)/shard_map/ppermute | solution.py:31
  781.2 11.0 %collective-permute-done.39 = bf16[4,96,768]{2,1,0:T(8,128)(2,1)S(1)} collective-permute-done((bf16[4,96,768]{2,1,0:T(8,128)(2,1)S(1)}, bf16[4,96,768]{2,1,0:T(8,128)(2,1)S(1)}, u32[]{:S(2)}, u32[]{:S(2)}) %collective-permute-start.39) | collective-permute-done | bytes 589856 | tf_op jit(solution)/shard_map/ppermute | solution.py:31
  800.0 2.9 copy.87
  802.9 4.1 stack_reshape.9
  807.0 3.0 copy.86
  810.0 3.0 stack_reshape.8
  (276 shorter events, 137.7 us)
Async XLA Ops:
  7.2 584.8 %all-reduce.4.cloned.1.call-start = ((), (), s32[]{:S(2)}) async-start(), calls=%async_computation | async-start | bytes 196608 | tf_op jit(solution)/shard_map/psum | solution.py:667
  28.4 41.9 %collective-permute-start.2 = (bf16[12,96,768]{2,1,0:T(8,128)(2,1)}, bf16[12,96,768]{2,1,0:T(8,128)(2,1)}, u32[]{:S(2)}, u32[]{:S(2)}) collective-permute-start(bf16[12,96,768]{2,1,0:T(8,128)(2,1)} %constant_dynamic-slice_fusion.16), channel_id=1, source_target_pairs={{0,2},{2,0},{1,3},{3,1},{4,6},{6,4},{5,7},{7,5},{8,10},{10,8},{9,1... | collective-permute-start | bytes 5308424 | tf_op jit(solution)/shard_map/ppermute | solution.py:31
  31.4 116.5 %collective-permute-start.1 = (bf16[12,192,768]{2,1,0:T(8,128)(2,1)}, bf16[12,192,768]{2,1,0:T(8,128)(2,1)}, u32[]{:S(2)}, u32[]{:S(2)}) collective-permute-start(bf16[12,192,768]{2,1,0:T(8,128)(2,1)} %constant_dynamic-update-slice_fusion.refs_0_), channel_id=1, source_target_pairs={{0,1},{1,0},{2,3},{3,2},{4,5},{5,4},{6,7},{7,6},{8,9},{9,8},{10,11... | collective-permute-start | bytes 10616840 | tf_op jit(solution)/shard_map/ppermute | solution.py:31
  70.3 40.1 %collective-permute-start.3 = (bf16[12,96,768]{2,1,0:T(8,128)(2,1)}, bf16[12,96,768]{2,1,0:T(8,128)(2,1)}, u32[]{:S(2)}, u32[]{:S(2)}) collective-permute-start(bf16[12,96,768]{2,1,0:T(8,128)(2,1)} %collective-permute-done.2.refs_2_), channel_id=1, source_target_pairs={{0,4},{4,0},{1,5},{5,1},{2,6},{6,2},{3,7},{7,3},{8,12},{12,8},{9,1... | collective-permute-start | bytes 5308424 | tf_op jit(solution)/shard_map/ppermute | solution.py:31
  73.6 51.7 %copy-start.40 = (bf16[2,192]{1,0:T(2,128)(2,1)S(1)}, bf16[2,192]{1,0:T(2,128)(2,1)}, u32[]{:S(2)}) copy-start(bf16[2,192]{1,0:T(2,128)(2,1)} %param.22) | copy-start | bytes 2308
  73.6 58.6 %copy-start.37 = (bf16[2,768]{1,0:T(2,128)(2,1)S(1)}, bf16[2,768]{1,0:T(2,128)(2,1)}, u32[]{:S(2)}) copy-start(bf16[2,768]{1,0:T(2,128)(2,1)} %param.31) | copy-start | bytes 9220
  74.9 48.6 %collective-permute-start.9 = (bf16[12,96,768]{2,1,0:T(8,128)(2,1)}, bf16[12,96,768]{2,1,0:T(8,128)(2,1)}, u32[]{:S(2)}, u32[]{:S(2)}) collective-permute-start(bf16[12,96,768]{2,1,0:T(8,128)(2,1)} %constant_dynamic-slice_fusion.15), channel_id=1, source_target_pairs={{0,2},{2,0},{1,3},{3,1},{4,6},{6,4},{5,7},{7,5},{8,10},{10,8},{9,1... | collective-permute-start | bytes 5308424 | tf_op jit(solution)/shard_map/ppermute | solution.py:31
  78.3 44.4 %collective-permute-start = (bf16[256,768]{1,0:T(8,128)(2,1)S(1)}, bf16[256,768]{1,0:T(8,128)(2,1)S(1)}, u32[]{:S(2)}, u32[]{:S(2)}) collective-permute-start(bf16[256,768]{1,0:T(8,128)(2,1)S(1)} %get-tuple-element.138), channel_id=1, source_target_pairs={{0,2},{2,0},{1,3},{3,1},{4,6},{6,4},{5,7},{7,5},{8,10},{10,8},{9,1... | collective-permute-start | bytes 1179656 | tf_op jit(solution)/shard_map/ppermute | solution.py:31
  78.9 69.0 %collective-permute-start.4 = (bf16[12,96,768]{2,1,0:T(8,128)(2,1)}, bf16[12,96,768]{2,1,0:T(8,128)(2,1)}, u32[]{:S(2)}, u32[]{:S(2)}) collective-permute-start(bf16[12,96,768]{2,1,0:T(8,128)(2,1)} %collective-permute-done.2.refs_2_), channel_id=1, source_target_pairs={{0,1},{1,0},{2,3},{3,2},{4,5},{5,4},{6,7},{7,6},{8,9},{9,8},{10,11... | collective-permute-start | bytes 5308424 | tf_op jit(solution)/shard_map/ppermute | solution.py:31
  110.4 37.5 %collective-permute-start.5 = (bf16[12,96,768]{2,1,0:T(8,128)(2,1)}, bf16[12,96,768]{2,1,0:T(8,128)(2,1)}, u32[]{:S(2)}, u32[]{:S(2)}) collective-permute-start(bf16[12,96,768]{2,1,0:T(8,128)(2,1)} %collective-permute-done.3.refs_3_), channel_id=1, source_target_pairs={{0,1},{1,0},{2,3},{3,2},{4,5},{5,4},{6,7},{7,6},{8,9},{9,8},{10,11... | collective-permute-start | bytes 5308424 | tf_op jit(solution)/shard_map/ppermute | solution.py:31
  122.8 75.7 %collective-permute-start.8 = (bf16[12,192,768]{2,1,0:T(8,128)(2,1)S(1)}, bf16[12,192,768]{2,1,0:T(8,128)(2,1)}, u32[]{:S(2)}, u32[]{:S(2)}) collective-permute-start(bf16[12,192,768]{2,1,0:T(8,128)(2,1)S(1)} %constant_dynamic-update-slice_fusion.1.refs_0_), channel_id=1, source_target_pairs={{0,1},{1,0},{2,3},{3,2},{4,5},{5,4},{6,7},{7,6},{8,9},{9,8},{10,11... | collective-permute-start | bytes 10616840 | tf_op jit(solution)/shard_map/ppermute | solution.py:31
  123.5 40.6 %collective-permute-start.10 = (bf16[12,96,768]{2,1,0:T(8,128)(2,1)}, bf16[12,96,768]{2,1,0:T(8,128)(2,1)}, u32[]{:S(2)}, u32[]{:S(2)}) collective-permute-start(bf16[12,96,768]{2,1,0:T(8,128)(2,1)} %collective-permute-done.9.refs_2_), channel_id=1, source_target_pairs={{0,4},{4,0},{1,5},{5,1},{2,6},{6,2},{3,7},{7,3},{8,12},{12,8},{9,1... | collective-permute-start | bytes 5308424 | tf_op jit(solution)/shard_map/ppermute | solution.py:31
  154.2 13.5 %collective-permute-start.6 = (bf16[512,768]{1,0:T(8,128)(2,1)}, bf16[512,768]{1,0:T(8,128)(2,1)}, u32[]{:S(2)}, u32[]{:S(2)}) collective-permute-start(bf16[512,768]{1,0:T(8,128)(2,1)} %get-tuple-element.66.ko_ref), channel_id=1, source_target_pairs={{0,1},{1,0},{2,3},{3,2},{4,5},{5,4},{6,7},{7,6},{8,9},{9,8},{10,11... | collective-permute-start | bytes 2359304 | tf_op jit(solution)/shard_map/ppermute | solution.py:31
  154.6 13.1 %collective-permute-start.7 = (bf16[512,768]{1,0:T(8,128)(2,1)}, bf16[512,768]{1,0:T(8,128)(2,1)}, u32[]{:S(2)}, u32[]{:S(2)}) collective-permute-start(bf16[512,768]{1,0:T(8,128)(2,1)} %get-tuple-element.67.vo_ref), channel_id=1, source_target_pairs={{0,1},{1,0},{2,3},{3,2},{4,5},{5,4},{6,7},{7,6},{8,9},{9,8},{10,11... | collective-permute-start | bytes 2359304 | tf_op jit(solution)/shard_map/ppermute | solution.py:31
  154.8 43.7 %collective-permute-start.11 = (bf16[12,96,768]{2,1,0:T(8,128)(2,1)}, bf16[12,96,768]{2,1,0:T(8,128)(2,1)}, u32[]{:S(2)}, u32[]{:S(2)}) collective-permute-start(bf16[12,96,768]{2,1,0:T(8,128)(2,1)} %collective-permute-done.9.refs_2_), channel_id=1, source_target_pairs={{0,1},{1,0},{2,3},{3,2},{4,5},{5,4},{6,7},{7,6},{8,9},{9,8},{10,11... | collective-permute-start | bytes 5308424 | tf_op jit(solution)/shard_map/ppermute | solution.py:31
  164.1 34.3 %collective-permute-start.12 = (bf16[12,96,768]{2,1,0:T(8,128)(2,1)}, bf16[12,96,768]{2,1,0:T(8,128)(2,1)}, u32[]{:S(2)}, u32[]{:S(2)}) collective-permute-start(bf16[12,96,768]{2,1,0:T(8,128)(2,1)} %collective-permute-done.10.refs_3_), channel_id=1, source_target_pairs={{0,1},{1,0},{2,3},{3,2},{4,5},{5,4},{6,7},{7,6},{8,9},{9,8},{10,11... | collective-permute-start | bytes 5308424 | tf_op jit(solution)/shard_map/ppermute | solution.py:31
  204.9 13.5 %collective-permute-start.13 = (bf16[512,768]{1,0:T(8,128)(2,1)}, bf16[512,768]{1,0:T(8,128)(2,1)S(1)}, u32[]{:S(2)}, u32[]{:S(2)}) collective-permute-start(bf16[512,768]{1,0:T(8,128)(2,1)} %get-tuple-element.71.ko_ref), channel_id=1, source_target_pairs={{0,1},{1,0},{2,3},{3,2},{4,5},{5,4},{6,7},{7,6},{8,9},{9,8},{10,11... | collective-permute-start | bytes 2359304 | tf_op jit(solution)/shard_map/ppermute | solution.py:31
  205.5 12.9 %collective-permute-start.14 = (bf16[512,768]{1,0:T(8,128)(2,1)}, bf16[512,768]{1,0:T(8,128)(2,1)S(1)}, u32[]{:S(2)}, u32[]{:S(2)}) collective-permute-start(bf16[512,768]{1,0:T(8,128)(2,1)} %get-tuple-element.72.vo_ref), channel_id=1, source_target_pairs={{0,1},{1,0},{2,3},{3,2},{4,5},{5,4},{6,7},{7,6},{8,9},{9,8},{10,11... | collective-permute-start | bytes 2359304 | tf_op jit(solution)/shard_map/ppermute | solution.py:31
  205.6 11.5 %collective-permute-start.16 = (bf16[256,768]{1,0:T(8,128)(2,1)S(1)}, bf16[256,768]{1,0:T(8,128)(2,1)S(1)}, u32[]{:S(2)}, u32[]{:S(2)}) collective-permute-start(bf16[256,768]{1,0:T(8,128)(2,1)S(1)} %get-tuple-element.134), channel_id=1, source_target_pairs={{0,2},{2,0},{1,3},{3,1},{4,6},{6,4},{5,7},{7,5},{8,10},{10,8},{9,1... | collective-permute-start | bytes 1179656 | tf_op jit(solution)/shard_map/ppermute | solution.py:31
  288.6 21.0 %collective-permute-start.17 = (bf16[2,512,768]{2,1,0:T(8,128)(2,1)}, bf16[2,512,768]{2,1,0:T(8,128)(2,1)S(1)}, u32[]{:S(2)}, u32[]{:S(2)}) collective-permute-start(bf16[2,512,768]{2,1,0:T(8,128)(2,1)} %get-tuple-element.82), channel_id=1, source_target_pairs={{0,1},{1,0},{2,3},{3,2},{4,5},{5,4},{6,7},{7,6},{8,9},{9,8},{10,11... | collective-permute-start | bytes 4718600 | tf_op jit(solution)/shard_map/ppermute | solution.py:31
  298.0 94.4 %collective-permute-start.32 = (bf16[2,5,192,768]{3,2,1,0:T(8,128)(2,1)}, bf16[2,5,192,768]{3,2,1,0:T(8,128)(2,1)S(1)}, u32[]{:S(2)}, u32[]{:S(2)}) collective-permute-start(bf16[2,5,192,768]{3,2,1,0:T(8,128)(2,1)} %get-tuple-element.110), channel_id=1, source_target_pairs={{0,1},{1,0},{2,3},{3,2},{4,5},{5,4},{6,7},{7,6},{8,9},{9,8},{10,11... | collective-permute-start | bytes 8847368 | tf_op jit(solution)/shard_map/ppermute | solution.py:31
  309.5 80.0 %collective-permute-start.40 = (bf16[2,4,192,768]{3,2,1,0:T(8,128)(2,1)}, bf16[2,4,192,768]{3,2,1,0:T(8,128)(2,1)}, u32[]{:S(2)}, u32[]{:S(2)}) collective-permute-start(bf16[2,4,192,768]{3,2,1,0:T(8,128)(2,1)} %slice.328), channel_id=1, source_target_pairs={{0,1},{1,0},{2,3},{3,2},{4,5},{5,4},{6,7},{7,6},{8,9},{9,8},{10,11... | collective-permute-start | bytes 7077896 | tf_op jit(solution)/shard_map/ppermute | solution.py:31
  357.7 37.7 %collective-permute-start.18 = (bf16[2,512,768]{2,1,0:T(8,128)(2,1)}, bf16[2,512,768]{2,1,0:T(8,128)(2,1)}, u32[]{:S(2)}, u32[]{:S(2)}) collective-permute-start(bf16[2,512,768]{2,1,0:T(8,128)(2,1)} %get-tuple-element.91), channel_id=1, source_target_pairs={{0,1},{1,0},{2,3},{3,2},{4,5},{5,4},{6,7},{7,6},{8,9},{9,8},{10,11... | collective-permute-start | bytes 4718600 | tf_op jit(solution)/shard_map/ppermute | solution.py:31
  368.3 46.3 %collective-permute-start.24 = (bf16[2,3,192,768]{3,2,1,0:T(8,128)(2,1)}, bf16[2,3,192,768]{3,2,1,0:T(8,128)(2,1)}, u32[]{:S(2)}, u32[]{:S(2)}) collective-permute-start(bf16[2,3,192,768]{3,2,1,0:T(8,128)(2,1)} %get-tuple-element.104), channel_id=1, source_target_pairs={{0,1},{1,0},{2,3},{3,2},{4,5},{5,4},{6,7},{7,6},{8,9},{9,8},{10,11... | collective-permute-start | bytes 5308424 | tf_op jit(solution)/shard_map/ppermute | solution.py:31
  377.8 66.9 %collective-permute-start.28 = (bf16[2,5,192,768]{3,2,1,0:T(8,128)(2,1)}, bf16[2,5,192,768]{3,2,1,0:T(8,128)(2,1)}, u32[]{:S(2)}, u32[]{:S(2)}) collective-permute-start(bf16[2,5,192,768]{3,2,1,0:T(8,128)(2,1)} %get-tuple-element.107), channel_id=1, source_target_pairs={{0,1},{1,0},{2,3},{3,2},{4,5},{5,4},{6,7},{7,6},{8,9},{9,8},{10,11... | collective-permute-start | bytes 8847368 | tf_op jit(solution)/shard_map/ppermute | solution.py:31
  389.5 35.6 %collective-permute-start.36 = (bf16[2,4,192,768]{3,2,1,0:T(8,128)(2,1)}, bf16[2,4,192,768]{3,2,1,0:T(8,128)(2,1)}, u32[]{:S(2)}, u32[]{:S(2)}) collective-permute-start(bf16[2,4,192,768]{3,2,1,0:T(8,128)(2,1)} %slice.323), channel_id=1, source_target_pairs={{0,1},{1,0},{2,3},{3,2},{4,5},{5,4},{6,7},{7,6},{8,9},{9,8},{10,11... | collective-permute-start | bytes 7077896 | tf_op jit(solution)/shard_map/ppermute | solution.py:31
  392.3 29.1 %collective-permute-start.41 = (bf16[4,192,768]{2,1,0:T(8,128)(2,1)}, bf16[4,192,768]{2,1,0:T(8,128)(2,1)}, u32[]{:S(2)}, u32[]{:S(2)}) collective-permute-start(bf16[4,192,768]{2,1,0:T(8,128)(2,1)} %fusion.15), channel_id=1, source_target_pairs={{0,2},{2,0},{1,3},{3,1},{4,6},{6,4},{5,7},{7,5},{8,10},{10,8},{9,1... | collective-permute-start | bytes 3538952 | tf_op jit(solution)/shard_map/ppermute | solution.py:31
  405.9 41.4 %collective-permute-start.20 = (bf16[2,3,192,768]{3,2,1,0:T(8,128)(2,1)}, bf16[2,3,192,768]{3,2,1,0:T(8,128)(2,1)S(1)}, u32[]{:S(2)}, u32[]{:S(2)}) collective-permute-start(bf16[2,3,192,768]{3,2,1,0:T(8,128)(2,1)} %get-tuple-element.102), channel_id=1, source_target_pairs={{0,1},{1,0},{2,3},{3,2},{4,5},{5,4},{6,7},{7,6},{8,9},{9,8},{10,11... | collective-permute-start | bytes 5308424 | tf_op jit(solution)/shard_map/ppermute | solution.py:31
  417.2 25.0 %collective-permute-start.25 = (bf16[3,192,768]{2,1,0:T(8,128)(2,1)}, bf16[3,192,768]{2,1,0:T(8,128)(2,1)}, u32[]{:S(2)}, u32[]{:S(2)}) collective-permute-start(bf16[3,192,768]{2,1,0:T(8,128)(2,1)} %fusion.19), channel_id=1, source_target_pairs={{0,2},{2,0},{1,3},{3,1},{4,6},{6,4},{5,7},{7,5},{8,10},{10,8},{9,1... | collective-permute-start | bytes 2654216 | tf_op jit(solution)/shard_map/ppermute | solution.py:31
  423.5 15.1 %collective-permute-start.42 = (bf16[4,96,768]{2,1,0:T(8,128)(2,1)S(1)}, bf16[4,96,768]{2,1,0:T(8,128)(2,1)}, u32[]{:S(2)}, u32[]{:S(2)}) collective-permute-start(bf16[4,96,768]{2,1,0:T(8,128)(2,1)S(1)} %constant_dynamic-slice_fusion.7), channel_id=1, source_target_pairs={{0,4},{4,0},{1,5},{5,1},{2,6},{6,2},{3,7},{7,3},{8,12},{12,8},{9,1... | collective-permute-start | bytes 1769480 | tf_op jit(solution)/shard_map/ppermute | solution.py:31
  424.9 288.9 %all-reduce.6.cloned.1.call-start = ((), (), s32[]{:S(2)}) async-start(), calls=%async_computation.1 | async-start | bytes 7077888 | tf_op jit(solution)/shard_map/psum | solution.py:566
  425.2 47.1 %collective-permute-start.33 = (bf16[5,192,768]{2,1,0:T(8,128)(2,1)}, bf16[5,192,768]{2,1,0:T(8,128)(2,1)S(1)}, u32[]{:S(2)}, u32[]{:S(2)}) collective-permute-start(bf16[5,192,768]{2,1,0:T(8,128)(2,1)} %fusion.9), channel_id=1, source_target_pairs={{0,2},{2,0},{1,3},{3,1},{4,6},{6,4},{5,7},{7,5},{8,10},{10,8},{9,1... | collective-permute-start | bytes 4423688 | tf_op jit(solution)/shard_map/ppermute | solution.py:31
  438.7 59.2 %collective-permute-start.37 = (bf16[4,192,768]{2,1,0:T(8,128)(2,1)S(1)}, bf16[4,192,768]{2,1,0:T(8,128)(2,1)S(1)}, u32[]{:S(2)}, u32[]{:S(2)}) collective-permute-start(bf16[4,192,768]{2,1,0:T(8,128)(2,1)S(1)} %fusion.13), channel_id=1, source_target_pairs={{0,2},{2,0},{1,3},{3,1},{4,6},{6,4},{5,7},{7,5},{8,10},{10,8},{9,1... | collective-permute-start | bytes 3538952 | tf_op jit(solution)/shard_map/ppermute | solution.py:31
  444.2 29.4 %collective-permute-start.26 = (bf16[3,96,768]{2,1,0:T(8,128)(2,1)S(1)}, bf16[3,96,768]{2,1,0:T(8,128)(2,1)S(1)}, u32[]{:S(2)}, u32[]{:S(2)}) collective-permute-start(bf16[3,96,768]{2,1,0:T(8,128)(2,1)S(1)} %constant_dynamic-slice_fusion.12), channel_id=1, source_target_pairs={{0,4},{4,0},{1,5},{5,1},{2,6},{6,2},{3,7},{7,3},{8,12},{12,8},{9,1... | collective-permute-start | bytes 1327112 | tf_op jit(solution)/shard_map/ppermute | solution.py:31
  446.7 102.8 %collective-permute-start.29 = (bf16[5,192,768]{2,1,0:T(8,128)(2,1)S(1)}, bf16[5,192,768]{2,1,0:T(8,128)(2,1)S(1)}, u32[]{:S(2)}, u32[]{:S(2)}) collective-permute-start(bf16[5,192,768]{2,1,0:T(8,128)(2,1)S(1)} %fusion.7), channel_id=1, source_target_pairs={{0,2},{2,0},{1,3},{3,1},{4,6},{6,4},{5,7},{7,5},{8,10},{10,8},{9,1... | collective-permute-start | bytes 4423688 | tf_op jit(solution)/shard_map/ppermute | solution.py:31
  447.6 100.9 %collective-permute-start.21 = (bf16[3,192,768]{2,1,0:T(8,128)(2,1)S(1)}, bf16[3,192,768]{2,1,0:T(8,128)(2,1)S(1)}, u32[]{:S(2)}, u32[]{:S(2)}) collective-permute-start(bf16[3,192,768]{2,1,0:T(8,128)(2,1)S(1)} %fusion.17), channel_id=1, source_target_pairs={{0,2},{2,0},{1,3},{3,1},{4,6},{6,4},{5,7},{7,5},{8,10},{10,8},{9,1... | collective-permute-start | bytes 2654216 | tf_op jit(solution)/shard_map/ppermute | solution.py:31
  473.0 80.1 %collective-permute-start.34 = (bf16[5,96,768]{2,1,0:T(8,128)(2,1)S(1)}, bf16[5,96,768]{2,1,0:T(8,128)(2,1)S(1)}, u32[]{:S(2)}, u32[]{:S(2)}) collective-permute-start(bf16[5,96,768]{2,1,0:T(8,128)(2,1)S(1)} %constant_dynamic-slice_fusion.10), channel_id=1, source_target_pairs={{0,4},{4,0},{1,5},{5,1},{2,6},{6,2},{3,7},{7,3},{8,12},{12,8},{9,1... | collective-permute-start | bytes 2211848 | tf_op jit(solution)/shard_map/ppermute | solution.py:31
  500.0 54.1 %collective-permute-start.38 = (bf16[4,96,768]{2,1,0:T(8,128)(2,1)S(1)}, bf16[4,96,768]{2,1,0:T(8,128)(2,1)S(1)}, u32[]{:S(2)}, u32[]{:S(2)}) collective-permute-start(bf16[4,96,768]{2,1,0:T(8,128)(2,1)S(1)} %constant_dynamic-slice_fusion.8), channel_id=1, source_target_pairs={{0,4},{4,0},{1,5},{5,1},{2,6},{6,2},{3,7},{7,3},{8,12},{12,8},{9,1... | collective-permute-start | bytes 1769480 | tf_op jit(solution)/shard_map/ppermute | solution.py:31
  548.9 13.1 %collective-permute-start.22 = (bf16[3,96,768]{2,1,0:T(8,128)(2,1)S(1)}, bf16[3,96,768]{2,1,0:T(8,128)(2,1)S(1)}, u32[]{:S(2)}, u32[]{:S(2)}) collective-permute-start(bf16[3,96,768]{2,1,0:T(8,128)(2,1)S(1)} %constant_dynamic-slice_fusion.13), channel_id=1, source_target_pairs={{0,4},{4,0},{1,5},{5,1},{2,6},{6,2},{3,7},{7,3},{8,12},{12,8},{9,1... | collective-permute-start | bytes 1327112 | tf_op jit(solution)/shard_map/ppermute | solution.py:31
  551.5 25.1 %collective-permute-start.30 = (bf16[5,96,768]{2,1,0:T(8,128)(2,1)S(1)}, bf16[5,96,768]{2,1,0:T(8,128)(2,1)S(1)}, u32[]{:S(2)}, u32[]{:S(2)}) collective-permute-start(bf16[5,96,768]{2,1,0:T(8,128)(2,1)S(1)} %constant_dynamic-slice_fusion.11), channel_id=1, source_target_pairs={{0,4},{4,0},{1,5},{5,1},{2,6},{6,2},{3,7},{7,3},{8,12},{12,8},{9,1... | collective-permute-start | bytes 2211848 | tf_op jit(solution)/shard_map/ppermute | solution.py:31
  579.3 10.1 %collective-permute-start.15 = (bf16[256,768]{1,0:T(8,128)(2,1)S(1)}, bf16[256,768]{1,0:T(8,128)(2,1)S(1)}, u32[]{:S(2)}, u32[]{:S(2)}) collective-permute-start(bf16[256,768]{1,0:T(8,128)(2,1)S(1)} %get-tuple-element.136), channel_id=1, source_target_pairs={{0,2},{2,0},{1,3},{3,1},{4,6},{6,4},{5,7},{7,5},{8,10},{10,8},{9,1... | collective-permute-start | bytes 1179656 | tf_op jit(solution)/shard_map/ppermute | solution.py:31
  590.5 127.4 %collective-permute-start.19 = (bf16[256,768]{1,0:T(8,128)(2,1)S(1)}, bf16[256,768]{1,0:T(8,128)(2,1)S(1)}, u32[]{:S(2)}, u32[]{:S(2)}) collective-permute-start(bf16[256,768]{1,0:T(8,128)(2,1)S(1)} %get-tuple-element.132), channel_id=1, source_target_pairs={{0,2},{2,0},{1,3},{3,1},{4,6},{6,4},{5,7},{7,5},{8,10},{10,8},{9,1... | collective-permute-start | bytes 1179656 | tf_op jit(solution)/shard_map/ppermute | solution.py:31
  713.8 13.3 %collective-permute-start.27 = (bf16[3,96,768]{2,1,0:T(8,128)(2,1)}, bf16[3,96,768]{2,1,0:T(8,128)(2,1)S(1)}, u32[]{:S(2)}, u32[]{:S(2)}) collective-permute-start(bf16[3,96,768]{2,1,0:T(8,128)(2,1)} %get-tuple-element.115), channel_id=1, source_target_pairs={{0,4},{4,0},{1,5},{5,1},{2,6},{6,2},{3,7},{7,3},{8,12},{12,8},{9,1... | collective-permute-start | bytes 1327112 | tf_op jit(solution)/shard_map/ppermute | solution.py:31
  717.2 19.3 %collective-permute-start.23 = (bf16[3,96,768]{2,1,0:T(8,128)(2,1)}, bf16[3,96,768]{2,1,0:T(8,128)(2,1)S(1)}, u32[]{:S(2)}, u32[]{:S(2)}) collective-permute-start(bf16[3,96,768]{2,1,0:T(8,128)(2,1)} %get-tuple-element.116), channel_id=1, source_target_pairs={{0,4},{4,0},{1,5},{5,1},{2,6},{6,2},{3,7},{7,3},{8,12},{12,8},{9,1... | collective-permute-start | bytes 1327112 | tf_op jit(solution)/shard_map/ppermute | solution.py:31
  719.1 76.0 %collective-permute-start.35 = (bf16[5,96,768]{2,1,0:T(8,128)(2,1)S(1)}, bf16[5,96,768]{2,1,0:T(8,128)(2,1)S(1)}, u32[]{:S(2)}, u32[]{:S(2)}) collective-permute-start(bf16[5,96,768]{2,1,0:T(8,128)(2,1)S(1)} %copy-done.21), channel_id=1, source_target_pairs={{0,4},{4,0},{1,5},{5,1},{2,6},{6,2},{3,7},{7,3},{8,12},{12,8},{9,1... | collective-permute-start | bytes 2211848 | tf_op jit(solution)/shard_map/ppermute | solution.py:31
  720.6 76.6 %collective-permute-start.31 = (bf16[5,96,768]{2,1,0:T(8,128)(2,1)S(1)}, bf16[5,96,768]{2,1,0:T(8,128)(2,1)S(1)}, u32[]{:S(2)}, u32[]{:S(2)}) collective-permute-start(bf16[5,96,768]{2,1,0:T(8,128)(2,1)S(1)} %copy-done.20), channel_id=1, source_target_pairs={{0,4},{4,0},{1,5},{5,1},{2,6},{6,2},{3,7},{7,3},{8,12},{12,8},{9,1... | collective-permute-start | bytes 2211848 | tf_op jit(solution)/shard_map/ppermute | solution.py:31
  721.2 59.6 %collective-permute-start.43 = (bf16[4,96,768]{2,1,0:T(8,128)(2,1)}, bf16[4,96,768]{2,1,0:T(8,128)(2,1)S(1)}, u32[]{:S(2)}, u32[]{:S(2)}) collective-permute-start(bf16[4,96,768]{2,1,0:T(8,128)(2,1)} %get-tuple-element.119), channel_id=1, source_target_pairs={{0,4},{4,0},{1,5},{5,1},{2,6},{6,2},{3,7},{7,3},{8,12},{12,8},{9,1... | collective-permute-start | bytes 1769480 | tf_op jit(solution)/shard_map/ppermute | solution.py:31
  727.0 65.2 %collective-permute-start.39 = (bf16[4,96,768]{2,1,0:T(8,128)(2,1)S(1)}, bf16[4,96,768]{2,1,0:T(8,128)(2,1)S(1)}, u32[]{:S(2)}, u32[]{:S(2)}) collective-permute-start(bf16[4,96,768]{2,1,0:T(8,128)(2,1)S(1)} %copy-done.22), channel_id=1, source_target_pairs={{0,4},{4,0},{1,5},{5,1},{2,6},{6,2},{3,7},{7,3},{8,12},{12,8},{9,1... | collective-permute-start | bytes 1769480 | tf_op jit(solution)/shard_map/ppermute | solution.py:31
  (45 other events, 527.9 us)
Sparse Core Ops, SparseCore 0:
  425.0 122.2 all-reduce.3
  577.9 135.8 all-reduce.5

commit v2 on v1

v2 whole, which is shorter than its diff:
```python
import functools

import jax
import jax.numpy as jnp
from jax import lax
from jax.experimental import pallas as pl
from jax.experimental.pallas import tpu as pltpu
from jax.sharding import Mesh
from jax.sharding import PartitionSpec as P

HEAD = 64
LAYERS = 2
SHARDS = 4
EPSILON = 1e-05
SWAP = [(0, 1), (1, 0)]
F32 = jnp.float32
BF16 = jnp.bfloat16
NN = (((1,), (0,)), ((), ()))
NT = (((1,), (1,)), ((), ()))
TN = (((0,), (0,)), ((), ()))
VMEM_LIMIT = 56 * 1024 * 1024
SCALE = 0.0

QKV = ((0, slice(0, 3), 0),)
OUT = ((0, slice(0, 1), 0),)
UP = (((0, slice(1, 5), 0),), ((0, slice(1, 3), 0), (6, slice(0, 2), 2)))
DOWN = (((0, slice(5, 6), 0), (6, slice(0, 3), 1)), ((-6, slice(0, 4), 0),))


def dot(left, right, dims=NN):
    return lax.dot_general(left, right, dims, preferred_element_type=F32)


def swap(values, axis):
    return lax.ppermute(values, axis, SWAP)


def vmem_spec():
    return pl.BlockSpec(memory_space=pltpu.VMEM)


def any_spec():
    return pl.BlockSpec(memory_space=pl.ANY)


def smem_spec():
    return pl.BlockSpec(memory_space=pltpu.SMEM)


def cost(flops, bytes_accessed, transcendentals=0):
    return pl.CostEstimate(
        flops=int(SCALE * flops), bytes_accessed=int(SCALE * bytes_accessed), transcendentals=0
    )


def shaped(shape, dtype):
    return jax.ShapeDtypeStruct(shape, dtype)


def call(kernel, operands, in_specs, out_shape, out_specs, deps=(), **options):
    first, last = len(operands), len(operands) + len(deps)

    def ordered(*refs):
        kernel(*refs[:first], *refs[last:])

    return pl.pallas_call(
        ordered,
        in_specs=list(in_specs) + [any_spec()] * len(deps),
        out_shape=out_shape,
        out_specs=out_specs,
        compiler_params=pltpu.CompilerParams(vmem_limit_bytes=VMEM_LIMIT),
        **options,
    )(*operands, *deps)


def after(values, *deps):
    if isinstance(values, tuple):
        return lax.optimization_barrier(values + deps)[: len(values)]
    return lax.optimization_barrier((values,) + deps)[0]


def standardize(values):
    average = jnp.mean(values, axis=-1, keepdims=True)
    centered = values - average
    variance = jnp.mean(centered * centered, axis=-1, keepdims=True)
    inverse_scale = lax.rsqrt(variance + EPSILON)
    return centered * inverse_scale, inverse_scale


def norm_input_grad(grad_out, standard, inverse_scale, gain):
    grad_standard = grad_out * gain
    return inverse_scale * (
        grad_standard
        - jnp.mean(grad_standard, axis=-1, keepdims=True)
        - standard * jnp.mean(grad_standard * standard, axis=-1, keepdims=True)
    )


def column_sum(values):
    return jnp.sum(values.astype(F32), axis=0, keepdims=True)


def gelu_parts(hidden):
    density = jnp.exp(-0.5 * hidden * hidden)
    t = 1.0 / (1.0 + (0.3275911 * 0.7071067811865476) * jnp.abs(hidden))
    series = t * (
        0.127414796
        + t * (-0.142248368 + t * (0.7107068705 + t * (-0.7265760135 + t * 0.5307027145)))
    )
    tail = series * density
    phi = jnp.where(hidden >= 0.0, 1.0 - tail, tail)
    return hidden * phi, phi + (hidden * 0.3989422804014327) * density


def pieces_of(place_ref, refs):
    s, y = place_ref[0], place_ref[1]
    places = ((s, None), (s ^ 1, None), (s ^ 2, y), (s ^ 2, 1 - y), (s ^ 3, y), (s ^ 3, 1 - y))
    return [(ref, *place) for ref, place in zip(refs, places)]


def aligned(start, size):
    return pl.ds(start if isinstance(start, int) else pl.multiple_of(start, size), size)


def load_rows(refs, place_ref, groups, target, sems, rows):
    copies = []
    for first, blocks, block in groups:
        for piece, shard, half in pieces_of(place_ref, refs[first:]):
            start, size = shard * rows, rows
            if half is not None:
                size = rows // 2
                start = start + half * size
            place = target.at[pl.ds(block, blocks.stop - blocks.start), aligned(start, size), :]
            copies.append(pltpu.make_async_copy(piece.at[blocks], place, sems.at[len(copies)]))
    return copies


def load_down(refs, place_ref, groups, target, sems, rows):
    copies = []
    for first, blocks, block in groups:
        for piece, shard, half in pieces_of(place_ref, refs[first:]):
            at = pl.ds(shard * SHARDS + block, blocks.stop - blocks.start)
            place = target.at[at]
            if half is not None:
                size = rows // 2
                place = target.at[at, aligned(half * size, size)]
            copies.append(pltpu.make_async_copy(piece.at[blocks], place, sems.at[len(copies)]))
    return copies


def start_all(copies):
    for copy in copies:
        copy.start()


def wait_all(copies):
    for copy in copies:
        copy.wait()


def pack_kernel(jobs, outs_of, slices, place_ref, *refs):
    count = 1 + max(source for _, _, source, _, _ in jobs)
    sources, inputs, refs = refs[:count], refs[count : count + slices], refs[count + slices :]
    outs, picked, work, frames, sems = refs[: -3 - slices], refs[-3 - slices : -3], *refs[-3:]
    loads, stores = [], []
    for index, (chunk, block, source, layer, (rows, columns)) in enumerate(jobs):
        own, half = outs_of[chunk]
        size, width = outs[half].shape[1:]
        whole = sources[source].at[layer, pl.ds(rows, 2 * size), pl.ds(columns, width)]
        part = work.at[index, pl.ds(pl.multiple_of(place_ref[1] * size, size), size)]
        loads.append([pltpu.make_async_copy(whole, work.at[index], sems.at[0, index])])
        stores.append([pltpu.make_async_copy(part, outs[half].at[block], sems.at[1, index])])
        if own is not None:
            stores[-1].append(pltpu.make_async_copy(work.at[index], outs[own].at[block], sems.at[2, index]))
    for index, (source, target) in enumerate(zip(inputs, picked)):
        at = len(jobs) + index
        loads.append([pltpu.make_async_copy(source.at[1 - place_ref[2]], frames.at[index], sems.at[0, at])])
        stores.append([pltpu.make_async_copy(frames.at[index], target, sems.at[1, at])])
    for copies in loads:
        start_all(copies)
    for load, store in zip(loads, stores):
        wait_all(load)
        start_all(store)
    for copies in stores:
        wait_all(copies)


def pack_shares(place, sources, chunks, share, width, clips=(), deps=()):
    jobs = [
        (chunk, block) + place_of
        for chunk, (_, blocks) in enumerate(chunks)
        for block, place_of in enumerate(blocks)
    ]
    out_shape, outs_of = [], []
    for whole, blocks in chunks:
        outs_of.append((len(out_shape) if whole else None, len(out_shape) + whole))
        if whole:
            out_shape.append(shaped((len(blocks), share, width), BF16))
        out_shape.append(shaped((len(blocks), share // 2, width), BF16))
    out_shape += [shaped(clip.shape[1:], BF16) for clip in clips]
    count = len(jobs) + len(clips)
    return call(
        functools.partial(pack_kernel, jobs, outs_of, len(clips)),
        [place, *sources, *clips],
        [smem_spec()] + [any_spec()] * (len(sources) + len(clips)),
        tuple(out_shape),
        (any_spec(),) * len(out_shape),
        deps,
        scratch_shapes=[
            pltpu.VMEM((len(jobs), share, width), BF16),
            pltpu.VMEM((len(clips), clips[0].shape[1], width), BF16),
            pltpu.SemaphoreType.DMA((3, count)),
        ],
        cost_estimate=cost(0, 0),
        name="pack_shares",
    )


def project(layer, standard, vectors_ref, weights, queries_ref, keys_ref, values_ref, ready):
    normed = (standard * vectors_ref[layer, 0:1] + vectors_ref[layer, 1:2]).astype(BF16)
    ready()
    queries = (dot(normed, weights[0]) + vectors_ref[layer, 2:3]).astype(BF16)
    queries_ref[...] = queries * jnp.asarray(HEAD ** (-0.5), BF16)
    keys_ref[...] = dot(normed, weights[1]).astype(BF16)
    values_ref[...] = (dot(normed, weights[2]) + vectors_ref[layer, 3:4]).astype(BF16)


def first_qkv_kernel(place_ref, frames_ref, arrived_ref, vectors_ref, *refs):
    shares, (stream_ref, *outs, weights, sems) = refs[:-6], refs[-6:]
    copies = load_rows(shares, place_ref, QKV, weights, sems, weights.shape[1] // SHARDS)
    start_all(copies)
    quarter = arrived_ref.shape[0]
    stream_ref[:quarter] = frames_ref[place_ref[2]].astype(F32)
    stream_ref[quarter:] = arrived_ref[...].astype(F32)
    standard, _ = standardize(stream_ref[...])
    project(0, standard, vectors_ref, weights, *outs, lambda: wait_all(copies))


def qkv_kernel(layer, place_ref, stream_ref, vectors_ref, *refs):
    shares, (*outs, weights, sems) = refs[:-5], refs[-5:]
    copies = load_rows(shares, place_ref, QKV, weights, sems, weights.shape[1] // SHARDS)
    start_all(copies)
    standard, _ = standardize(stream_ref[...])
    project(layer, standard, vectors_ref, weights, *outs, lambda: wait_all(copies))


def qkv_options(rows, width, name):
    return dict(
        scratch_shapes=[pltpu.VMEM((3, width, width), BF16), pltpu.SemaphoreType.DMA((8,))],
        cost_estimate=cost(6 * rows * width * width, 10 * rows * width + 6 * width * width),
        name=name,
    )


def first_qkv(place, frames, arrived, vectors, shares, deps=()):
    rows, width = 2 * arrived.shape[0], arrived.shape[1]
    return call(
        first_qkv_kernel,
        [place, frames, arrived, vectors, *shares],
        [smem_spec()] + [vmem_spec()] * 3 + [any_spec()] * len(shares),
        (shaped((rows, width), F32),) + (shaped((rows, width), BF16),) * 3,
        (vmem_spec(),) * 4,
        deps,
        **qkv_options(rows, width, "first_qkv"),
    )


def next_qkv(layer, place, stream, vectors, shares, deps=()):
    rows, width = stream.shape
    return call(
        functools.partial(qkv_kernel, layer),
        [place, stream, vectors, *shares],
        [smem_spec()] + [vmem_spec()] * 2 + [any_spec()] * len(shares),
        (shaped((rows, width), BF16),) * 3,
        (vmem_spec(),) * 3,
        deps,
        **qkv_options(rows, width, "next_qkv"),
    )


def attention_kernel(q_ref, ko_ref, kt_ref, vo_ref, vt_ref, mixed_ref, lse_ref):
    queries_t = q_ref[...].T
    row = lax.broadcasted_iota(jnp.int32, queries_t.shape, 0)
    values_t = (vo_ref[...].T, vt_ref[...].T)
    outs = []
    for head in range(2):
        mine = (row >= head * HEAD) & (row < (head + 1) * HEAD)
        q_t = jnp.where(mine, queries_t, jnp.zeros_like(queries_t))
        scores = (dot(ko_ref[...], q_t), dot(kt_ref[...], q_t))
        peak = jnp.maximum(
            jnp.max(scores[0], axis=0, keepdims=True), jnp.max(scores[1], axis=0, keepdims=True)
        )
        weights = tuple(jnp.exp(part - peak) for part in scores)
        total = jnp.sum(weights[0], axis=0, keepdims=True) + jnp.sum(weights[1], axis=0, keepdims=True)
        lse_ref[0, head : head + 1, :] = peak + jnp.log(total)
        at = slice(head * HEAD, (head + 1) * HEAD)
        out = dot(values_t[0][at], weights[0].astype(BF16)) + dot(values_t[1][at], weights[1].astype(BF16))
        outs.append(out / total)
    mixed_ref[...] = jnp.concatenate(outs, axis=0).T.astype(BF16)


def attend(queries, keys, keys_twin, values, values_twin, deps=()):
    rows, width = queries.shape
    pairs = width // (2 * HEAD)
    block = pl.BlockSpec((rows, 2 * HEAD), lambda pair: (0, pair))
    return call(
        attention_kernel,
        [queries, keys, keys_twin, values, values_twin],
        [block] * 5,
        (shaped((rows, width), BF16), shaped((pairs, 8, rows), F32)),
        (block, pl.BlockSpec((1, 8, rows), lambda pair: (pair, 0, 0))),
        deps,
        grid=(pairs,),
        cost_estimate=cost(32 * rows * rows * width, 12 * rows * width, 4 * pairs * rows * rows),
        name="attend",
    )


def up_kernel(layer, place_ref, stream_ref, mixed_ref, vectors_ref, up_bias_ref, *refs):
    shares, (attended_ref, activated_ref, slope_ref, out_w, up_w, sems) = refs[:-6], refs[-6:]
    width = stream_ref.shape[1]
    share = width // SHARDS
    out_copies = load_rows(shares, place_ref, OUT, out_w, sems.at[0], share)
    up_copies = load_rows(shares, place_ref, UP[layer], up_w, sems.at[1], share)
    start_all(out_copies)
    start_all(up_copies)
    wait_all(out_copies)
    attended_ref[...] = stream_ref[...] + dot(mixed_ref[...], out_w[0]) + vectors_ref[layer, 4:5]
    standard, _ = standardize(attended_ref[...])
    second = (standard * vectors_ref[layer, 5:6] + vectors_ref[layer, 6:7]).astype(BF16)
    wait_all(up_copies)
    for block in range(SHARDS):
        at = slice(block * width, (block + 1) * width)
        hidden = dot(second, up_w[block]) + up_bias_ref[layer : layer + 1, at]
        activated, slope = gelu_parts(hidden)
        activated_ref[:, at] = activated.astype(BF16)
        slope_ref[:, at] = slope.astype(BF16)


def feed_up(layer, place, stream, mixed, vectors, up_bias, shares, deps=()):
    rows, width = stream.shape
    wide = SHARDS * width
    return call(
        functools.partial(up_kernel, layer),
        [place, stream, mixed, vectors, up_bias, *shares],
        [smem_spec()] + [vmem_spec()] * 4 + [any_spec()] * len(shares),
        (shaped((rows, width), F32), shaped((rows, wide), BF16), shaped((rows, wide), BF16)),
        (vmem_spec(),) * 3,
        deps,
        scratch_shapes=[
            pltpu.VMEM((1, width, width), BF16),
            pltpu.VMEM((4, width, width), BF16),
            pltpu.SemaphoreType.DMA((2, 12)),
        ],
        cost_estimate=cost(10 * rows * width * width, 24 * rows * width + 10 * width * width, rows * wide),
        name="feed_up",
    )


def down_kernel(layer, place_ref, attended_ref, activated_ref, vectors_ref, *refs):
    shares, (next_ref, down_w, sems) = refs[:-3], refs[-3:]
    width = attended_ref.shape[1]
    copies = load_down(shares, place_ref, DOWN[layer], down_w, sems, width // SHARDS)
    start_all(copies)
    next_ref[...] = attended_ref[...] + vectors_ref[layer, 7:8]
    wait_all(copies)
    next_ref[...] += dot(activated_ref[...], down_w[...].reshape(SHARDS * width, width))


def last_down_kernel(layer, place_ref, attended_ref, activated_ref, vectors_ref, *refs):
    shares, (mine_ref, other_ref, down_w, sems) = refs[:-4], refs[-4:]
    width = attended_ref.shape[1]
    copies = load_down(shares, place_ref, DOWN[layer], down_w, sems, width // SHARDS)
    start_all(copies)
    total = attended_ref[...] + vectors_ref[layer, 7:8]
    wait_all(copies)
    total += dot(activated_ref[...], down_w[...].reshape(SHARDS * width, width))
    half = mine_ref.shape[0]
    mine_ref[...] = total[:half].astype(BF16)
    other_ref[...] = total[half:].astype(BF16)


def feed_down(layer, place, attended, activated, vectors, shares, deps=()):
    rows, width = attended.shape
    last = layer == LAYERS - 1
    return call(
        functools.partial(last_down_kernel if last else down_kernel, layer),
        [place, attended, activated, vectors, *shares],
        [smem_spec()] + [vmem_spec()] * 3 + [any_spec()] * len(shares),
        (shaped((rows // 2, width), BF16),) * 2 if last else shaped((rows, width), F32),
        (vmem_spec(),) * 2 if last else vmem_spec(),
        deps,
        scratch_shapes=[
            pltpu.VMEM((4 * SHARDS, width // SHARDS, width), BF16),
            pltpu.SemaphoreType.DMA((12,)),
        ],
        cost_estimate=cost(8 * rows * width * width, 16 * rows * width + 8 * width * width),
        name="feed_down",
    )


def feed_scratch(width):
    return [
        pltpu.VMEM((1, width, width), BF16),
        pltpu.VMEM((4, width, width), BF16),
        pltpu.VMEM((4 * SHARDS, width // SHARDS, width), BF16),
        pltpu.SemaphoreType.DMA((3, 12)),
    ]


def feed_back_kernel(layer, place_ref, grad_ref, slope_ref, attended_ref, vectors_ref, *refs):
    shares, refs = refs[:-9], refs[-9:]
    hidden_ref, attended_grad_ref, mixed_grad_ref, sums_ref, up_sums_ref, out_w, up_w, down_w, sems = refs
    width = grad_ref.shape[1]
    share = width // SHARDS
    down_copies = load_down(shares, place_ref, DOWN[layer], down_w, sems.at[2], share)
    up_copies = load_rows(shares, place_ref, UP[layer], up_w, sems.at[1], share)
    out_copies = load_rows(shares, place_ref, OUT, out_w, sems.at[0], share)
    start_all(down_copies)
    start_all(up_copies)
    start_all(out_copies)
    branch = grad_ref[...].astype(BF16)
    sums_ref[...] = jnp.zeros_like(sums_ref)
    sums_ref[7:8] = column_sum(branch)
    wait_all(down_copies)
    wait_all(up_copies)
    second_grad = None
    for block in range(SHARDS):
        at = slice(block * width, (block + 1) * width)
        down = down_w[block * SHARDS : (block + 1) * SHARDS].reshape(width, width)
        hidden_grad = (dot(branch, down, NT) * slope_ref[:, at].astype(F32)).astype(BF16)
        hidden_ref[:, at] = hidden_grad
        up_sums_ref[:, at] = column_sum(hidden_grad)
        part = dot(hidden_grad, up_w[block], NT)
        second_grad = part if second_grad is None else second_grad + part
    standard, inverse = standardize(attended_ref[...])
    sums_ref[5:6] = column_sum(second_grad * standard)
    sums_ref[6:7] = column_sum(second_grad)
    attended_grad = grad_ref[...] + norm_input_grad(second_grad, standard, inverse, vectors_ref[layer, 5:6])
    attended_grad_ref[...] = attended_grad
    out_grad = attended_grad.astype(BF16)
    sums_ref[4:5] = column_sum(out_grad)
    wait_all(out_copies)
    mixed_grad_ref[...] = dot(out_grad, out_w[0], NT).astype(BF16)


def feed_back(layer, place, grad, slope, attended, vectors, shares, deps=()):
    rows, width = grad.shape
    wide = SHARDS * width
    return call(
        functools.partial(feed_back_kernel, layer),
        [place, grad, slope, attended, vectors, *shares],
        [smem_spec()] + [vmem_spec()] * 4 + [any_spec()] * len(shares),
        (
            shaped((rows, wide), BF16),
            shaped((rows, width), F32),
            shaped((rows, width), BF16),
            shaped((8, width), F32),
            shaped((1, wide), F32),
        ),
        (vmem_spec(),) * 5,
        deps,
        scratch_shapes=feed_scratch(width),
        cost_estimate=cost(18 * rows * width * width, 30 * rows * width + 18 * width * width),
        name="feed_back",
    )


def owners(place_ref, keep_ref, send_refs):
    s = place_ref[0]
    return (
        (s ^ 3, send_refs[2:]),
        (s ^ 1, send_refs[:2]),
        (s ^ 2, (keep_ref.at[1, 0], keep_ref.at[1, 1])),
        (s, (keep_ref.at[0, 0], keep_ref.at[0, 1])),
    )


def quarters(place_ref, split, rows):
    size = rows // 4
    near, inner = (place_ref[1], place_ref[3]) if split else (0, 0)
    for y in range(2):
        for z in range(2):
            start = (near ^ y) * (2 * size) + (inner ^ z) * size
            yield y, z, pl.ds(pl.multiple_of(start, size), size)


def run_steps(steps, work, sems):
    pending = [None, None]
    for index, (make, targets) in enumerate(steps):
        slot = index % 2
        if pending[slot] is not None:
            wait_all(pending[slot])
        work[slot] = make().astype(BF16).reshape(work.shape[1:])
        copies = [
            pltpu.make_async_copy(source, target, sems.at[slot, number])
            for number, (source, target) in enumerate(targets(work.at[slot]))
        ]
        start_all(copies)
        pending[slot] = copies
    for copies in pending:
        if copies is not None:
            wait_all(copies)


def by_rows(place_ref, split, keep_ref, send_refs, block):
    def targets(work):
        return [
            (work.at[shard, rows], target[y].at[z, block])
            for shard, target in owners(place_ref, keep_ref, send_refs)
            for y, z, rows in quarters(place_ref, split, work.shape[1])
        ]

    return targets


def whole_share(place_ref, split, target):
    def targets(work):
        return [
            (work.at[:, rows], target[y].at[z]) for y, z, rows in quarters(place_ref, split, work.shape[1])
        ]

    return targets


def down_grad_kernel(split, place_ref, activated_ref, grad_ref, keep_ref, *refs):
    send_refs, (work, sems) = refs[:4], refs[4:]
    width = grad_ref.shape[1]
    branch = grad_ref[...].astype(BF16)
    steps = []
    for shard, target in owners(place_ref, keep_ref, send_refs):
        at = pl.ds(pl.multiple_of(shard * width, width), width)
        steps.append(
            (lambda at=at: dot(activated_ref[:, at], branch, TN), whole_share(place_ref, split, target))
        )
    run_steps(steps, work, sems)


def grad_shapes(count, width):
    part = (2, count, width // SHARDS // 4, width)
    return (shaped((2, 2) + part, BF16),) + (shaped(part, BF16),) * 4


def grad_scratch(width):
    return [pltpu.VMEM((2, SHARDS, width // SHARDS, width), BF16), pltpu.SemaphoreType.DMA((2, 16))]


def down_weight_grad(place, split, activated, grad, deps=()):
    rows, width = grad.shape
    return call(
        functools.partial(down_grad_kernel, split),
        [place, activated, grad],
        [smem_spec()] + [vmem_spec()] * 2,
        grad_shapes(SHARDS, width),
        (any_spec(),) * 5,
        deps,
        scratch_shapes=grad_scratch(width),
        cost_estimate=cost(8 * rows * width * width, 12 * rows * width + 8 * width * width),
        name="down_weight_grad",
    )


def feed_grad_kernel(
    layer,
    split,
    place_ref,
    hidden_ref,
    attended_ref,
    attended_grad_ref,
    mixed_ref,
    vectors_ref,
    keep_ref,
    *refs,
):
    send_refs, (work, sems) = refs[:4], refs[4:]
    width = attended_ref.shape[1]
    standard, _ = standardize(attended_ref[...])
    second_t = (standard * vectors_ref[layer, 5:6] + vectors_ref[layer, 6:7]).astype(BF16).T
    steps = [
        (
            lambda: dot(mixed_ref[...], attended_grad_ref[...].astype(BF16), TN),
            by_rows(place_ref, split, keep_ref, send_refs, 0),
        )
    ]
    for block in range(SHARDS):
        at = slice(block * width, (block + 1) * width)
        steps.append(
            (lambda at=at: dot(second_t, hidden_ref[:, at]), by_rows(place_ref, split, keep_ref, send_refs, 1 + block))
        )
    run_steps(steps, work, sems)


def feed_weight_grads(layer, split, place, hidden_grad, attended, attended_grad, mixed, vectors, deps=()):
    rows, width = attended.shape
    return call(
        functools.partial(feed_grad_kernel, layer, split),
        [place, hidden_grad, attended, attended_grad, mixed, vectors],
        [smem_spec()] + [vmem_spec()] * 5,
        grad_shapes(1 + SHARDS, width),
        (any_spec(),) * 5,
        deps,
        scratch_shapes=grad_scratch(width),
        cost_estimate=cost(10 * rows * width * width, 20 * rows * width + 10 * width * width),
        name="feed_weight_grads",
    )


def qkv_grad_kernel(
    layer,
    split,
    place_ref,
    stream_ref,
    vectors_ref,
    dq_ref,
    dk_ref,
    dv_ref,
    dk_back_ref,
    dv_back_ref,
    sums_ref,
    total_ref,
    keep_ref,
    *refs,
):
    send_refs, (work, sems) = refs[:4], refs[4:]
    standard, _ = standardize(stream_ref[...])
    normed_t = (standard * vectors_ref[layer, 0:1] + vectors_ref[layer, 1:2]).astype(BF16).T
    total_ref[0] = (dk_ref[...].astype(F32) + dk_back_ref[...].astype(F32)).astype(BF16)
    total_ref[1] = (dv_ref[...].astype(F32) + dv_back_ref[...].astype(F32)).astype(BF16)
    sums_ref[...] = jnp.zeros_like(sums_ref)
    sums_ref[2:3] = column_sum(dq_ref[...])
    sums_ref[3:4] = column_sum(total_ref[1])
    makers = (
        lambda: dot(normed_t, dq_ref[...]),
        lambda: dot(normed_t, total_ref[0]),
        lambda: dot(normed_t, total_ref[1]),
    )
    run_steps(
        [(make, by_rows(place_ref, split, keep_ref, send_refs, block)) for block, make in enumerate(makers)],
        work,
        sems,
    )


def qkv_weight_grads(layer, split, place, stream, vectors, dq, dk, dv, dk_back, dv_back, deps=()):
    rows, width = stream.shape
    return call(
        functools.partial(qkv_grad_kernel, layer, split),
        [place, stream, vectors, dq, dk, dv, dk_back, dv_back],
        [smem_spec()] + [vmem_spec()] * 7,
        (shaped((8, width), F32), shaped((2, rows, width), BF16)) + grad_shapes(3, width),
        (vmem_spec(),) * 2 + (any_spec(),) * 5,
        deps,
        scratch_shapes=grad_scratch(width),
        cost_estimate=cost(6 * rows * width * width, 10 * rows * width + 6 * width * width),
        name="qkv_weight_grads",
    )


def attention_back_kernel(
    q_ref,
    ko_ref,
    kt_ref,
    vo_ref,
    vt_ref,
    lse_ref,
    out_grad_ref,
    dq_ref,
    dk_ref,
    dv_ref,
    dk_twin_ref,
    dv_twin_ref,
):
    queries = q_ref[...]
    out_grad = out_grad_ref[...]
    queries_t, out_grad_t = queries.T, out_grad.T
    row = lax.broadcasted_iota(jnp.int32, queries_t.shape, 0)
    lane = lax.broadcasted_iota(jnp.int32, queries.shape, 1)
    keys, values = (ko_ref, kt_ref), (vo_ref, vt_ref)
    keys_t = tuple(part[...].T for part in keys)
    key_grads, value_grads, query_grads = [None, None], [None, None], []
    for head in range(2):
        low, high = head * HEAD, (head + 1) * HEAD
        mine_t = (row >= low) & (row < high)
        mine = (lane >= low) & (lane < high)
        q_t = jnp.where(mine_t, queries_t, jnp.zeros_like(queries_t))
        o_t = jnp.where(mine_t, out_grad_t, jnp.zeros_like(queries_t))
        q_h = jnp.where(mine, queries, jnp.zeros_like(queries))
        o_h = jnp.where(mine, out_grad, jnp.zeros_like(queries))
        lse = lse_ref[0, head : head + 1, :]
        probability = [jnp.exp(dot(part[...], q_t) - lse) for part in keys]
        probability_grad = [dot(part[...], o_t) for part in values]
        inner = sum(
            jnp.sum(left * right, axis=0, keepdims=True)
            for left, right in zip(probability, probability_grad)
        )
        query_grad = None
        for index in range(2):
            score_grad = (probability[index] * (probability_grad[index] - inner)).astype(BF16)
            value_part = dot(probability[index].astype(BF16), o_h)
            key_part = dot(score_grad, q_h)
            query_part = dot(keys_t[index][low:high], score_grad)
            if head == 0:
                key_grads[index], value_grads[index] = key_part, value_part
            else:
                key_grads[index] += key_part
                value_grads[index] += value_part
            query_grad = query_part if index == 0 else query_grad + query_part
        query_grads.append(query_grad)
    dq_ref[...] = (jnp.concatenate(query_grads, axis=0).T * HEAD ** (-0.5)).astype(BF16)
    for ref, value in zip((dk_ref, dk_twin_ref, dv_ref, dv_twin_ref), key_grads + value_grads):
        ref[...] = value.astype(BF16)


def attend_back(queries, keys, keys_twin, values, values_twin, lse, out_grad, deps=()):
    rows, width = queries.shape
    pairs = width // (2 * HEAD)
    block = pl.BlockSpec((rows, 2 * HEAD), lambda pair: (0, pair))
    return call(
        attention_back_kernel,
        [queries, keys, keys_twin, values, values_twin, lse, out_grad],
        [block] * 5 + [pl.BlockSpec((1, 8, rows), lambda pair: (pair, 0, 0)), block],
        (shaped((rows, width), BF16),) * 5,
        (block,) * 5,
        deps,
        grid=(pairs,),
        cost_estimate=cost(80 * rows * rows * width, 24 * rows * width),
        name="attend_back",
    )


def norm_back_kernel(layer, place_ref, stream_ref, vectors_ref, attended_grad_ref, dq_ref, dkv_ref, *refs):
    shares, (grad_ref, sums_ref, weights, sems) = refs[:-4], refs[-4:]
    copies = load_rows(shares, place_ref, QKV, weights, sems, weights.shape[1] // SHARDS)
    start_all(copies)
    standard, inverse = standardize(stream_ref[...])
    wait_all(copies)
    normed_grad = (
        dot(dq_ref[...], weights[0], NT) + dot(dkv_ref[0], weights[1], NT) + dot(dkv_ref[1], weights[2], NT)
    )
    sums_ref[...] = jnp.zeros_like(sums_ref)
    sums_ref[0:1] = column_sum(normed_grad * standard)
    sums_ref[1:2] = column_sum(normed_grad)
    grad_ref[...] = attended_grad_ref[...] + norm_input_grad(
        normed_grad, standard, inverse, vectors_ref[layer, 0:1]
    )


def norm_back(layer, place, stream, vectors, attended_grad, dq, dkv, shares, deps=()):
    rows, width = stream.shape
    return call(
        functools.partial(norm_back_kernel, layer),
        [place, stream, vectors, attended_grad, dq, dkv, *shares],
        [smem_spec()] + [vmem_spec()] * 5 + [any_spec()] * len(shares),
        (shaped((rows, width), F32), shaped((8, width), F32)),
        (vmem_spec(),) * 2,
        deps,
        scratch_shapes=[pltpu.VMEM((3, width, width), BF16), pltpu.SemaphoreType.DMA((8,))],
        cost_estimate=cost(6 * rows * width * width, 18 * rows * width + 6 * width * width),
        name="norm_back",
    )


def finish_kernel(layer, split, pieces, places, place_ref, *refs):
    sources, refs = refs[: len(pieces)], refs[len(pieces) :]
    outs, (arrived, work, sems) = refs[:-3], refs[-3:]
    count = len(places)
    near, inner = (place_ref[1], place_ref[3]) if split else (0, 0)
    size, width = work.shape[1:]
    loads = []
    for index, (source, (start, _, _)) in enumerate(zip(sources, pieces)):
        at = pl.ds(index * count, count)
        loads.append(pltpu.make_async_copy(source.at[pl.ds(start, count)], arrived.at[at], sems.at[0, index]))
    start_all(loads)
    stores = []
    for number, (load, (_, y, z)) in enumerate(zip(loads, pieces)):
        load.wait()
        for block, (out, row, column) in enumerate(places):
            index = number * count + block
            work[index] = arrived[index].astype(F32)
            start = row + (near ^ y) * (2 * size) + (inner ^ z) * size
            target = outs[out].at[layer, aligned(start, size), pl.ds(column, width)]
            stores.append(pltpu.make_async_copy(work.at[index], target, sems.at[1, index]))
            stores[-1].start()
    wait_all(stores)


def finish(layer, split, sources, places, out_shapes, place, buffers=None, deps=()):
    size, width = sources[0][0].shape[-2:]
    count = 4 * len(places)
    operands = [place, *(source[0] for source in sources)]
    aliases = {}
    if buffers is not None:
        aliases = {len(operands) + index: index for index in range(len(buffers))}
        operands += list(buffers)
    first = 1 + len(sources)
    pieces = [source[1:] for source in sources]

    def kernel(*refs):
        finish_kernel(layer, split, pieces, places, *refs[:first], *refs[len(operands) :])

    return call(
        kernel,
        operands,
        [smem_spec()] + [any_spec()] * (len(operands) - 1),
        tuple(shaped(shape, F32) for shape in out_shapes),
        (any_spec(),) * len(out_shapes),
        deps,
        input_output_aliases=aliases,
        scratch_shapes=[
            pltpu.VMEM((count, size, width), BF16),
            pltpu.VMEM((count, size, width), F32),
            pltpu.SemaphoreType.DMA((2, count)),
        ],
        cost_estimate=cost(0, 6 * count * size * width),
        name="finish",
    )


def combine_kernel(plan, *refs):
    arrays = 1 + max(operand for segments in plan for _, terms in segments for operand, _ in terms)
    operands, outs, (work, sems, out_sems) = refs[:arrays], refs[arrays:-3], refs[-3:]
    jobs, copies, at = [], [], 0
    for out, segments in zip(outs, plan):
        place = 0
        for count, terms in segments:
            places = []
            for operand, start in terms:
                source = operands[operand].at[pl.ds(start, count)]
                copies.append(
                    pltpu.make_async_copy(source, work.at[pl.ds(at, count)], sems.at[len(copies)])
                )
                places.append((copies[-1], at))
                at += count
            jobs.append((out, place, count, places))
            place += count
    start_all(copies)
    stores = []
    for out, place, count, places in jobs:
        for copy, _ in places:
            copy.wait()
        first = places[0][1]
        if len(places) == 2:
            for index in range(count):
                work[first + index] += work[places[1][1] + index]
        elif len(places) > 2:
            for index in range(count):
                total = work[first + index].astype(F32)
                for _, start in places[1:]:
                    total += work[start + index].astype(F32)
                work[first + index] = total.astype(BF16)
        stores.append(
            pltpu.make_async_copy(
                work.at[pl.ds(first, count)], out.at[pl.ds(place, count)], out_sems.at[len(stores)]
            )
        )
        stores[-1].start()
    wait_all(stores)


def combine(outputs, deps=()):
    arrays, plan = [], []
    for segments in outputs:
        plan.append([])
        for count, terms in segments:
            named = []
            for array, start in terms:
                index = next((i for i, known in enumerate(arrays) if known is array), len(arrays))
                if index == len(arrays):
                    arrays.append(array)
                named.append((index, start))
            plan[-1].append((count, named))
    size, width = arrays[0].shape[1:]
    moves = [len(terms) for segments in plan for _, terms in segments]
    rows = sum(count * len(terms) for segments in plan for count, terms in segments)
    return call(
        functools.partial(combine_kernel, plan),
        arrays,
        [any_spec()] * len(arrays),
        tuple(shaped((sum(count for count, _ in segments), size, width), BF16) for segments in plan),
        (any_spec(),) * len(plan),
        deps,
        scratch_shapes=[
            pltpu.VMEM((rows, size, width), BF16),
            pltpu.SemaphoreType.DMA((sum(moves),)),
            pltpu.SemaphoreType.DMA((len(moves),)),
        ],
        cost_estimate=cost(0, 0),
        name="combine",
    )


PAIRS, MIRROR = [(0, 1), (1, 0), (2, 3), (3, 2)], [(0, 3), (3, 0), (1, 2), (2, 1)]


class Flow:
    def __init__(self, split, parts, *pins, last="spread"):
        keep, *send = parts
        self.split, self.count, self.last = split, keep.shape[3], last
        self.keep = keep.reshape((-1,) + keep.shape[-2:])
        send = after(tuple(send), *pins)
        self.back = [swap(part.reshape((-1,) + part.shape[-2:]), "core") for part in send]

    def sums(self, x, y, z, *arrivals):
        n = self.count
        terms = [(self.keep, (4 * x + 2 * y + z) * n), (self.back[2 * x + y], z * n)]
        return (n, terms + [(array, start + offset * n) for (array, start), offset in arrivals])

    def segments(self, stage):
        n = self.count
        if stage == "x":
            return {"x": [self.sums(1, y, z) for y in range(2) for z in range(2)]}
        if stage == "y":
            return {"y": [self.sums(0, 1, z, (self.x, 2 + z)) for z in range(2)]}
        if stage == "pair":
            if not self.split:
                return {"sum": [self.sums(0, 0, z, (self.x, z), (self.y, z)) for z in range(2)]}
            return {"pair": [self.sums(0, 0, 1, (self.x, 1), (self.y, 1))]}
        if stage == "mirror":
            if not self.split:
                return {}
            return {"mirror": [self.sums(0, 0, 0, (self.x, 0), (self.y, 0), (self.pair, 0))]}
        if stage == "after":
            if not self.split:
                return {"near": [(2 * n, [self.sum])]}
            whole = (n, [self.mirror_sent, self.mirror])
            return {"near": [whole], "spread": [whole]}
        if not self.split:
            return {}
        return {self.last: [(n, [self.rest if self.last == "spread" else self.part_z])]}

    def record(self, stage, channel, sent, arrived):
        if stage == "after":
            if channel == "near":
                self.part, self.rest = sent, arrived
            else:
                self.part_z = arrived
        elif stage == "last":
            self.rest_z = arrived
        else:
            setattr(self, channel, arrived)
            setattr(self, channel + "_sent", sent)

    def finish(self, layer, places, out_shapes, place, buffers=None, deps=()):
        n = self.count
        if self.split:
            sources = [(*self.part, 0, 0), (*self.part_z, 0, 1), (*self.rest, 1, 0), (*self.rest_z, 1, 1)]
        else:
            sources = [
                (array, start + z * n, y, z)
                for y, (array, start) in enumerate((self.part, self.rest))
                for z in range(2)
            ]
        return finish(layer, self.split, sources, places, out_shapes, place, buffers, deps)


class Totals:
    def __init__(self, split, values):
        self.split = split
        self.terms = [(values, 0), (swap(values, "core"), 0)]

    def segments(self, stage):
        if stage in ("pair", "mirror") and not self.split:
            return {"sum": [(1, self.terms)]} if stage == "pair" else {}
        return {stage: [(1, self.terms)]}

    def record(self, stage, channel, sent, arrived):
        self.terms = [arrived] if channel == "sum" else [sent, arrived]

    def done(self):
        return sum(array[start].astype(F32) for array, start in self.terms)


def exchange(steps, *pins):
    outputs, owners_of = {}, {}
    for flow, stage in steps:
        for channel, segments in flow.segments(stage).items():
            placed = outputs.setdefault(channel, [])
            start = sum(count for count, _ in placed)
            owners_of.setdefault(channel, []).append((flow, stage, start))
            placed += segments
    if not outputs:
        return pins[0], ()
    names, landed = list(outputs), []
    results = combine([outputs[name] for name in names], pins)
    for name, sent in zip(names, results):
        if name == "sum":
            arrived = lax.psum(sent, "z")
        elif name in ("pair", "spread", "mirror"):
            arrived = lax.ppermute(sent, "z", MIRROR if name == "mirror" else PAIRS)
        else:
            arrived = swap(sent, "y" if name == "near" else name)
        landed.append(arrived)
        for flow, stage, start in owners_of[name]:
            flow.record(stage, name, (sent, start), (arrived, start))
    return results[0], tuple(landed)


def body(
    frames,
    cotangent,
    first_gain,
    first_shift,
    query_weight,
    query_bias,
    key_weight,
    value_weight,
    value_bias,
    out_weight,
    out_bias,
    second_gain,
    second_shift,
    up_weight,
    up_bias,
    down_weight,
    down_bias,
):
    x, y, z, core = (lax.axis_index(axis) for axis in ("x", "y", "z", "core"))
    shard = 2 * x + core
    inner = jnp.where((z == 0) | (z == 3), 0, 1)
    place = jnp.stack([shard, y, x, inner]).astype(jnp.int32)
    quarter, width = frames.shape[1:]
    share = width // SHARDS
    split = lax.axis_size("z") == 4

    def blocks_of(layer):
        attention = [(source, layer, (0, 0)) for source in (0, 1, 2)]
        up = [(3, layer, (0, 0))] + [(4, layer, (0, block * width)) for block in range(SHARDS)]
        down = [(5, layer, (block * share, 0)) for block in range(SHARDS)]
        return attention, up, down

    sources = (query_weight, key_weight, value_weight, out_weight, up_weight, down_weight)
    (attention0, up0, down0), (attention1, up1, down1) = blocks_of(0), blocks_of(1)
    own0, half0, other_frames = pack_shares(
        place, sources[:3], [(True, attention0)], share, width, clips=(frames,)
    )
    near = {0: swap(half0, "x")}
    arrived_frames = swap(other_frames, "x")
    twin = {0: swap(own0, "core")}
    *packed, other_cotangent = pack_shares(
        place,
        sources,
        [
            (True, blocks)
            for blocks in (up0 + down0[:1], down0[1:], attention1, up1[:3], up1[3:], down1)
        ],
        share,
        width,
        clips=(cotangent,),
        deps=(half0,),
    )
    own, half = dict(enumerate([own0, *packed[0::2]])), dict(enumerate([half0, *packed[1::2]]))
    near[0] = after(near[0], half[1])
    far, near_twin, far_twin = {0: swap(near[0], "y")}, {0: swap(near[0], "core")}, {}

    small = jnp.stack(
        [first_gain, first_shift, query_bias, value_bias, out_bias, second_gain, second_shift, down_bias], axis=1
    )
    small = jnp.concatenate([small, up_bias.reshape(LAYERS, SHARDS, share)], axis=1)
    small = after(small, half0)
    pair = jnp.stack([small, swap(small, "core")])
    pieces = jnp.concatenate([pair, swap(pair, "x")], axis=0)
    small = jnp.stack(
        [lax.dynamic_index_in_dim(pieces, shard ^ index, 0, keepdims=False) for index in range(SHARDS)]
    ).astype(F32)
    vectors = jnp.transpose(small[:, :, :8], (1, 2, 0, 3)).reshape(LAYERS, 8, width)
    up_biases = jnp.transpose(small[:, :, 8:], (1, 0, 2, 3)).reshape(LAYERS, SHARDS * width)

    def fetch(chunk, *pins):
        near[chunk] = swap(after(half[chunk], *pins), "x")

    def spread(chunk, *pins):
        far[chunk] = swap(after(near[chunk], *pins), "y")

    def trade(chunk, *pins):
        twin[chunk] = swap(after(own[chunk], *pins), "core")

    def trade_near(chunk, *pins):
        near_twin[chunk] = swap(after(near[chunk], *pins), "core")

    def trade_far(chunk, *pins):
        far_twin[chunk] = swap(after(far[chunk], *pins), "core")

    def shares(chunk):
        return own[chunk], twin[chunk], near[chunk], far[chunk], near_twin[chunk], far_twin[chunk]

    trade_far(0)
    fetch(1, arrived_frames)
    for chunk in range(1, 7):
        trade(chunk, arrived_frames)
    stream0, queries0, keys0, values0 = first_qkv(
        place, frames, arrived_frames, vectors, shares(0), deps=tuple(twin[chunk] for chunk in range(1, 7))
    )
    qkv0 = shares(0)
    keys0, values0 = after((keys0, values0), near[1])
    keys_twin0, values_twin0 = swap(keys0, "core"), swap(values0, "core")
    fetch(2, keys0)
    spread(1, keys0)
    trade_near(1, keys0)
    mixed0, lse0 = attend(queries0, keys0, keys_twin0, values0, values_twin0, deps=(near_twin[1],))
    trade_far(1, mixed0)
    fetch(3, near[2], mixed0)
    spread(2, mixed0)
    trade_near(2, mixed0)
    attended0, activated0, slope0 = feed_up(
        0, place, stream0, mixed0, vectors, up_biases, shares(1), deps=(near_twin[2],)
    )
    trade_far(2, activated0)
    fetch(4, near[3], activated0)
    spread(3, activated0)
    trade_near(3, activated0)
    second0 = shares(1) + shares(2)
    stream1 = feed_down(0, place, attended0, activated0, vectors, second0, deps=(near_twin[3],))
    trade_far(3, stream1)
    fetch(5, near[4], stream1)
    spread(4, stream1)
    trade_near(4, stream1)
    qkv1 = shares(3)
    queries1, keys1, values1 = next_qkv(1, place, stream1, vectors, qkv1, deps=(near_twin[4],))
    keys1, values1 = after((keys1, values1), near[5], far[4])
    keys_twin1, values_twin1 = swap(keys1, "core"), swap(values1, "core")
    fetch(6, near[5], keys1)
    spread(5, keys1)
    trade_near(5, keys1)
    trade_far(4, keys1)
    mixed1, lse1 = attend(
        queries1, keys1, keys_twin1, values1, values_twin1, deps=(near_twin[5], far_twin[4])
    )
    trade_far(5, mixed1)
    spread(6, mixed1)
    trade_near(6, mixed1)
    arrived_cotangent = swap(after(other_cotangent, near[6]), "x")
    late = shares(4) + shares(5)
    attended1, activated1, slope1 = feed_up(
        1, place, stream1, mixed1, vectors, up_biases, late, deps=(near_twin[6],)
    )
    mine_cotangent = lax.dynamic_index_in_dim(cotangent, x, 0, keepdims=False)
    pieces = after((mine_cotangent, arrived_cotangent), attended1)
    gradient = jnp.concatenate(pieces, axis=0).astype(F32)
    down1 = Flow(split, down_weight_grad(place, split, activated1, gradient), far[6])
    trade_far(6, down1.keep)
    output_mine, output_other = feed_down(1, place, attended1, activated1, vectors, shares(6))
    late += shares(6)

    def by_clip(mine, other):
        return jnp.where(x == 0, jnp.stack([mine, other]), jnp.stack([other, mine]))

    output_other = swap(output_other, "x")

    def square(row_blocks, column_blocks):
        return (LAYERS, row_blocks * share, column_blocks * width)

    down_places, down_shapes = [(0, block * share, 0) for block in range(SHARDS)], [square(SHARDS, 1)]
    feed_places = [(0, 0, 0)] + [(1, 0, block * width) for block in range(SHARDS)]
    feed_shapes = [square(1, 1), square(1, SHARDS)]
    qkv_places, qkv_shapes = [(block, 0, 0) for block in range(3)], [square(1, 1)] * 3

    pin, landed = exchange([(down1, "x")], output_mine, *down1.back)
    hidden_grad, attended_grad, mixed_grad, feed_sums1, up_sums1 = feed_back(
        1, place, gradient, slope1, attended1, vectors, late, deps=(pin,)
    )
    parts = feed_weight_grads(1, split, place, hidden_grad, attended1, attended_grad, mixed1, vectors)
    feed1 = Flow(split, parts, *landed, output_other)
    output = by_clip(output_mine, output_other)
    pin, (near, far) = exchange([(down1, "y"), (feed1, "x")], *feed1.back)
    dq, dk, dv, dk_twin, dv_twin = attend_back(
        queries1, keys1, keys_twin1, values1, values_twin1, lse1, mixed_grad, deps=(pin,)
    )
    dk_twin, dv_twin = after((dk_twin, dv_twin), near)
    dk_back, dv_back = swap(dk_twin, "core"), swap(dv_twin, "core")
    pin, landed = exchange([(down1, "pair")], dq)
    qkv_sums1, dkv, *parts = qkv_weight_grads(
        1, split, place, stream1, vectors, dq, dk, dv, dk_back, dv_back, deps=(pin,)
    )
    gradient, norm_sums1 = norm_back(
        1, place, stream1, vectors, attended_grad, dq, dkv, qkv1, deps=(parts[0],)
    )
    qkv_1 = Flow(split, parts, far, *landed)
    pin, landed = exchange([(qkv_1, "x"), (feed1, "y"), (down1, "mirror")], gradient, *qkv_1.back)

    parts = down_weight_grad(place, split, activated0, gradient, deps=(pin,))
    hidden_grad, attended_grad, mixed_grad, feed_sums0, up_sums0 = feed_back(
        0, place, gradient, slope0, attended0, vectors, second0, deps=(parts[0],)
    )
    down0 = Flow(split, parts, mixed_grad, *landed, last="near")
    steps = [(down0, "x"), (qkv_1, "y"), (down1, "after"), (feed1, "pair")]
    pin, landed = exchange(steps, mixed_grad, *down0.back)
    parts = feed_weight_grads(
        0, split, place, hidden_grad, attended0, attended_grad, mixed0, vectors, deps=(pin,)
    )
    dq, dk, dv, dk_twin, dv_twin = attend_back(
        queries0, keys0, keys_twin0, values0, values_twin0, lse0, mixed_grad, deps=(parts[0],)
    )
    dk_twin, dv_twin = after((dk_twin, dv_twin), *landed)
    dk_back, dv_back = swap(dk_twin, "core"), swap(dv_twin, "core")
    feed0 = Flow(split, parts, dq, *landed, last="near")
    steps = [(feed0, "x"), (down0, "y"), (down1, "last"), (qkv_1, "pair"), (feed1, "mirror")]
    pin, (far, *landed) = exchange(steps, dq, *feed0.back)
    qkv_sums0, dkv, *parts = qkv_weight_grads(
        0, split, place, stream0, vectors, dq, dk, dv, dk_back, dv_back, deps=(pin,)
    )
    gradient, norm_sums0 = norm_back(
        0, place, stream0, vectors, attended_grad, dq, dkv, qkv0, deps=(parts[0],)
    )
    qkv_0 = Flow(split, parts, gradient, *landed, last="near")
    sums = jnp.concatenate(
        [
            part
            for feed, qkv, norm, up in (
                (feed_sums0, qkv_sums0, norm_sums0, up_sums0),
                (feed_sums1, qkv_sums1, norm_sums1, up_sums1),
            )
            for part in (feed + qkv + norm, up.reshape(SHARDS, width))
        ]
    ).astype(BF16)
    sums = jnp.pad(sums, ((0, share // 4 - sums.shape[0]), (0, 0)))
    totals = Totals(split, sums[None])
    steps = [(qkv_0, "x"), (totals, "x"), (down0, "pair"), (feed1, "after")]
    pin, landed = exchange(steps, gradient, *qkv_0.back)
    down_out = down1.finish(1, down_places, down_shapes, place, deps=(pin,))
    pin, landed = exchange([(feed0, "y"), (down0, "mirror"), (feed1, "last")], down_out[0])
    input_other = swap(after(gradient[quarter:].astype(BF16), pin), "x")
    steps = [(qkv_0, "y"), (totals, "y"), (feed0, "pair"), (down0, "after"), (qkv_1, "mirror")]
    pin, landed = exchange(steps, pin)
    feed_out = feed1.finish(1, feed_places, feed_shapes, place, deps=(pin, input_other))
    input_grad = by_clip(gradient[:quarter], input_other.astype(F32))
    steps = [(qkv_0, "pair"), (totals, "pair"), (feed0, "mirror"), (down0, "last"), (qkv_1, "after")]
    pin, landed = exchange(steps, feed_out[0])
    steps = [(qkv_0, "mirror"), (totals, "mirror"), (feed0, "after"), (qkv_1, "last")]
    pin, landed = exchange(steps, pin)
    (down_out,) = down0.finish(0, down_places, down_shapes, place, down_out, deps=(pin,))
    pin, landed = exchange([(qkv_0, "after"), (feed0, "last")], down_out)
    totals = totals.done()[: LAYERS * (8 + SHARDS)].reshape(LAYERS, 8 + SHARDS, width)
    qkv_out = qkv_1.finish(1, qkv_places, qkv_shapes, place, deps=(pin,))
    pin, landed = exchange([(qkv_0, "last")], qkv_out[0])
    out_out, up_out = feed0.finish(0, feed_places, feed_shapes, place, feed_out, deps=(pin,))
    query_out, key_out, value_out = qkv_0.finish(0, qkv_places, qkv_shapes, place, qkv_out, deps=(out_out,))

    own_vectors = lax.dynamic_slice_in_dim(totals[:, :8], shard * share, share, axis=2)
    own_up = lax.dynamic_slice_in_dim(
        totals[:, 8:].reshape(LAYERS, SHARDS * width), shard * width, width, axis=1
    )
    vector = [own_vectors[:, index] for index in range(8)]
    return (
        output,
        input_grad,
        vector[0],
        vector[1],
        query_out,
        vector[2],
        key_out,
        value_out,
        vector[3],
        out_out,
        vector[4],
        vector[5],
        vector[6],
        up_out,
        own_up,
        down_out,
        vector[7],
    )


def solution(mesh):
    groups = mesh.shape["rep"]
    finer = Mesh(mesh.devices.reshape(groups // 2, 2, 2, 2), ("z", "y", "x", "core"))
    rep, shard = ("z", "y"), ("x", "core")
    rows = P(rep, shard, None)
    vector, matrix = P(None, shard), P(None, shard, None)
    parameters = (
        vector,
        vector,
        matrix,
        vector,
        matrix,
        matrix,
        vector,
        matrix,
        vector,
        vector,
        vector,
        matrix,
        vector,
        matrix,
        vector,
    )
    return jax.shard_map(
        body,
        mesh=finer,
        in_specs=(rows, rows) + parameters,
        out_specs=(rows, rows) + parameters,
        check_vma=False,
    )
```

time: 833 us -> 565 us (0.68)
  waiting for transfers between devices: 414 us -> 123 us
  Pallas kernels: 217 us -> 306 us
  other arithmetic: 52.5 us -> 5.94 us
  starting transfers between devices: 36 us -> 81.2 us
  local copies, waits for them, and re-layouts: 85.2 us -> 40.3 us
  between operations: 15.1 us -> 2.78 us
    ppermute x44 -> x93, waiting for transfers between devices: 297 us -> 73.6 us  [swap(): return lax.ppermute(values, axis, SWAP)]
    psum x2 -> x0, waiting for transfers between devices: 117 us -> none  [the longest x1 117 us: reduce_grads(): part = lax.psum(part, 'z')]
    pallas_call x18 -> x41, Pallas kernels: 217 us -> 306 us  [call(): pl.pallas_call(ordered, in_specs=list(in_specs) + [any_spec()] * len(deps...]
    ppermute x0 -> x20, waiting for transfers between devices: none -> 49.8 us  [exchange(): arrived = lax.ppermute(sent, 'z', MIRROR if name == 'mirror' else PAIRS)]
    convert_element_type x30 -> x2, other arithmetic: 39.2 us -> 1.3 us  [the longest x1 1.27 us: body(): gradient = jnp.concatenate(pieces, axis=0).astype(F32)]
    ppermute x0 -> x20, starting transfers between devices: none -> 24.2 us  [exchange(): arrived = lax.ppermute(sent, 'z', MIRROR if name == 'mirror' else PAIRS)]
    ppermute x44 -> x93, starting transfers between devices: 35.7 us -> 57 us  [swap(): return lax.ppermute(values, axis, SWAP)]
    another operation x6 -> x1, local copies, waits for them, and re-layouts: 14.1 us -> 0.05 us  [by_clip(): return jnp.where(x == 0, jnp.stack([mine, other]), jnp.stack([other, mine]))]
  transfers between devices with their start and end apart: 46 -> 113, of which waited for: 18 -> 47; matrix products, arithmetic and copies ran while one was open for 11% -> 3% of each run, Pallas kernels for 17% -> 50%
where the time goes in v2:
time: 565 us; the launch traced here: 559 us
  Pallas kernels  306 us (54%)
  waiting for transfers between devices  123 us (22%)
  starting transfers between devices  81.2 us (14%)
  local copies, waits for them, and re-layouts  40.3 us (7%)
  other arithmetic  5.94 us (1%)
    pallas_call x41, Pallas kernels, call(): pl.pallas_call(ordered, in_specs=list(in_specs) + [any_spec()] * len(deps...  306 us
    ppermute x93, waiting for transfers between devices, swap(): return lax.ppermute(values, axis, SWAP)  73.6 us
    ppermute x93, starting transfers between devices, swap(): return lax.ppermute(values, axis, SWAP)  57 us
    ppermute x20, waiting for transfers between devices, exchange(): arrived = lax.ppermute(sent, 'z', MIRROR if name == 'mirror' else PAIRS)  49.8 us
    unnamed x304, local copies, waits for them, and re-layouts  32.8 us
    ppermute x20, starting transfers between devices, exchange(): arrived = lax.ppermute(sent, 'z', MIRROR if name == 'mirror' else PAIRS)  24.2 us
  transfers between devices with their start and end apart: 113, of which 47 were waited for; matrix products, arithmetic and copies ran while one was open for 3% of the time, Pallas kernels for 50%

profile of v2, /device:TPU:0, one launch (start us, length us, event | category | flops | bytes accessed | tf_op | source)
XLA Modules:
  0.0 559.3 jit_solution(5957964264166900177)
XLA Ops:
  7.5 7.3 %pack_shares.3 = (bf16[6,192,768]{2,1,0:T(8,128)(2,1)}, bf16[6,96,768]{2,1,0:T(8,128)(2,1)}, bf16[3,192,768]{2,1,0:T(8,128)(2,1)}, bf16[3,96,768]{2,1,0:T(8,128)...) custom-call(s32[4]{0:T(128)} %pad_add_fusion.refs_0_, ...), custom_call_target="tpu_custom_call" | custom-call | tf_op jit(solution)/shard_map/pack_shares/pallas_call | solution.py:66
  14.8 3.7 collective-permute-done.4.refs_6_.refs_8_
  29.8 3.5 collective-permute-done.12.refs_14_.refs_12_
  41.3 6.2 %first_qkv.1 = (f32[512,768]{1,0:T(8,128)}, bf16[512,768]{1,0:T(8,128)(2,1)}, bf16[512,768]{1,0:T(8,128)(2,1)}, bf16[512,768]{1,0:T(8,128)(2,1)}) custom-call(s32[4]{0:T(128)} %pad_add_fusion.refs_0_, bf16[2,256,768]{2,1,0:T(8,128)(2,1)} %refs_1_.5, bf16[256,768]{1,0:T(8,128)(2,1)} %copy-done.82, f32[2,8,768]{2,1,0:T(8,128)} %reshape.153.refs_3_.refs_2_.refs_4_.refs_5_, ...), custom_call_target="tpu_custom_call" | custom-call | tf_op jit(solution)/shard_map/first_qkv/pallas_call | solution.py:66
  47.5 8.2 %collective-permute-done.14.refs_7_.refs_6_ = bf16[6,96,768]{2,1,0:T(8,128)(2,1)} collective-permute-done((bf16[6,96,768]{2,1,0:T(8,128)(2,1)}, bf16[6,96,768]{2,1,0:T(8,128)(2,1)}, u32[]{:S(2)}, u32[]{:S(2)}) %collective-permute-start.14) | collective-permute-done | bytes 884768 | tf_op jit(solution)/shard_map/ppermute | solution.py:35
  62.2 13.8 %attend.2 = (bf16[512,768]{1,0:T(8,128)(2,1)}, f32[6,8,512]{2,1,0:T(8,128)}) custom-call(bf16[512,768]{1,0:T(8,128)(2,1)} %get-tuple-element.237.refs_0_, bf16[512,768]{1,0:T(8,128)(2,1)} %get-tuple-element.241.refs_1_, bf16[512,768]{1,0:T(8,128)(2,1)} %copy-done.26, bf16[512,768]{1,0:T(8,128)(2,1)} %get-tuple-element.242.refs_3_, ...), custom_call_target="tpu_custom_call" | custom-call | tf_op jit(solution)/shard_map/attend/pallas_call | solution.py:66
  84.9 14.5 %feed_up.2 = (f32[512,768]{1,0:T(8,128)}, bf16[512,3072]{1,0:T(8,128)(2,1)}, bf16[512,3072]{1,0:T(8,128)(2,1)}) custom-call(s32[4]{0:T(128)} %pad_add_fusion.refs_0_, f32[512,768]{1,0:T(8,128)} %get-tuple-element.236.refs_1_, bf16[512,768]{1,0:T(8,128)(2,1)} %get-tuple-element.244.refs_2_.refs_4_, f32[2,8,768]{2,1,0:T(8,128)} %reshape.153.refs_3_.refs_2_.refs_4_.refs_5_, ...), custom_call_target="tpu_custom_call" | custom-call | tf_op jit(solution)/shard_map/feed_up/pallas_call | solution.py:66
  102.7 8.6 %feed_down.2.refs_1_ = f32[512,768]{1,0:T(8,128)} custom-call(s32[4]{0:T(128)} %pad_add_fusion.refs_0_, f32[512,768]{1,0:T(8,128)} %get-tuple-element.249.refs_1_.refs_3_.refs_2_, bf16[512,3072]{1,0:T(8,128)(2,1)} %get-tuple-element.250.refs_2_.refs_1_, f32[2,8,768]{2,1,0:T(8,128)} %reshape.153.refs_3_.refs_2_.refs_4_.refs_5_, ...), custom_call_target="tpu_custom_call" | custom-call | tf_op jit(solution)/shard_map/feed_down/pallas_call | solution.py:66
  116.0 6.7 %next_qkv.1 = (bf16[512,768]{1,0:T(8,128)(2,1)}, bf16[512,768]{1,0:T(8,128)(2,1)}, bf16[512,768]{1,0:T(8,128)(2,1)}) custom-call(s32[4]{0:T(128)} %pad_add_fusion.refs_0_, f32[512,768]{1,0:T(8,128)} %feed_down.2.refs_1_, f32[2,8,768]{2,1,0:T(8,128)} %reshape.153.refs_3_.refs_2_.refs_4_.refs_5_, bf16[3,192,768]{2,1,0:T(8,128)(2,1)} %get-tuple-element.229.refs_3_.refs_6_, ...), custom_call_target="tpu_custom_call" | custom-call | tf_op jit(solution)/shard_map/next_qkv/pallas_call | solution.py:66
  131.2 13.7 %attend.3 = (bf16[512,768]{1,0:T(8,128)(2,1)}, f32[6,8,512]{2,1,0:T(8,128)}) custom-call(bf16[512,768]{1,0:T(8,128)(2,1)} %get-tuple-element.259.refs_0_, bf16[512,768]{1,0:T(8,128)(2,1)} %get-tuple-element.264.refs_1_, bf16[512,768]{1,0:T(8,128)(2,1)} %copy-done.28, bf16[512,768]{1,0:T(8,128)(2,1)} %get-tuple-element.265.refs_3_, ...), custom_call_target="tpu_custom_call" | custom-call | tf_op jit(solution)/shard_map/attend/pallas_call | solution.py:66
  151.3 14.4 %feed_up.3 = (f32[512,768]{1,0:T(8,128)}, bf16[512,3072]{1,0:T(8,128)(2,1)}, bf16[512,3072]{1,0:T(8,128)(2,1)}) custom-call(s32[4]{0:T(128)} %pad_add_fusion.refs_0_, f32[512,768]{1,0:T(8,128)} %feed_down.2.refs_1_, bf16[512,768]{1,0:T(8,128)(2,1)} %get-tuple-element.268.refs_2_.refs_4_, f32[2,8,768]{2,1,0:T(8,128)} %reshape.153.refs_3_.refs_2_.refs_4_.refs_5_, ...), custom_call_target="tpu_custom_call" | custom-call | tf_op jit(solution)/shard_map/feed_up/pallas_call | solution.py:66
  167.0 7.8 %down_weight_grad.2 = (bf16[2,2,2,4,48,768]{5,4,3,2,1,0:T(8,128)(2,1)}, bf16[2,4,48,768]{3,2,1,0:T(8,128)(2,1)}, bf16[2,4,48,768]{3,2,1,0:T(8,128)(2,1)}, bf16[2...) custom-call(s32[4]{0:T(128)} %pad_add_fusion.refs_0_, bf16[512,3072]{1,0:T(8,128)(2,1)} %get-tuple-element.274.refs_1_.refs_2_, ...), custom_call_target="tpu_custom_call" | custom-call | tf_op jit(solution)/shard_map/down_weight_grad/pallas_call | solution.py:66
  179.4 8.4 %feed_down.3 = (bf16[256,768]{1,0:T(8,128)(2,1)}, bf16[256,768]{1,0:T(8,128)(2,1)}) custom-call(s32[4]{0:T(128)} %pad_add_fusion.refs_0_, f32[512,768]{1,0:T(8,128)} %get-tuple-element.273.refs_1_.refs_3_.refs_2_, bf16[512,3072]{1,0:T(8,128)(2,1)} %get-tuple-element.274.refs_1_.refs_2_, f32[2,8,768]{2,1,0:T(8,128)} %reshape.153.refs_3_.refs_2_.refs_4_.refs_5_, ...), custom_call_target="tpu_custom_call" | custom-call | tf_op jit(solution)/shard_map/feed_down/pallas_call | solution.py:66
  193.8 15.3 %feed_back.2 = (bf16[512,3072]{1,0:T(8,128)(2,1)}, f32[512,768]{1,0:T(8,128)}, bf16[512,768]{1,0:T(8,128)(2,1)}, f32[8,768]{1,0:T(8,128)}, f32[1,3072]{1,0:T(1,128)}) custom-call(s32[4]{0:T(128)} %pad_add_fusion.refs_0_, f32[512,768]{1,0:T(8,128)} %maximum_convert_fusion.refs_2_.refs_1_, bf16[512,3072]{1,0:T(8,128)(2,1)} %get-tuple-element.283.refs_2_, ...), custom_call_target="tpu_custom_call" | custom-call | tf_op jit(solution)/shard_map/feed_back/pallas_call | solution.py:66
  209.2 9.4 %feed_weight_grads.2 = (bf16[2,2,2,5,48,768]{5,4,3,2,1,0:T(8,128)(2,1)}, bf16[2,5,48,768]{3,2,1,0:T(8,128)(2,1)}, bf16[2,5,48,768]{3,2,1,0:T(8,128)(2,1)}, bf16[...) custom-call(s32[4]{0:T(128)} %pad_add_fusion.refs_0_, bf16[512,3072]{1,0:T(8,128)(2,1)} %get-tuple-element.295.refs_1_, ...), custom_call_target="tpu_custom_call" | custom-call | tf_op jit(solution)/shard_map/feed_weight_grads/pallas_call | solution.py:66
  218.6 9.8 %collective-permute-done.43 = bf16[256,768]{1,0:T(8,128)(2,1)S(1)} collective-permute-done((bf16[256,768]{1,0:T(8,128)(2,1)S(1)}, bf16[256,768]{1,0:T(8,128)(2,1)S(1)}, u32[]{:S(2)}, u32[]{:S(2)}) %collective-permute-start.43) | collective-permute-done | bytes 393248 | tf_op jit(solution)/shard_map/ppermute | solution.py:35
  235.7 3.4 combine.14
  240.1 22.6 %attend_back.2 = (bf16[512,768]{1,0:T(8,128)(2,1)}, bf16[512,768]{1,0:T(8,128)(2,1)}, bf16[512,768]{1,0:T(8,128)(2,1)}, bf16[512,768]{1,0:T(8,128)(2,1)}, bf16[512,768]{1,0:T(8,128)(2,1)}) custom-call(bf16[512,768]{1,0:T(8,128)(2,1)} %get-tuple-element.259.refs_0_, bf16[512,768]{1,0:T(8,128)(2,1)} %get-tuple-element.264.refs_1_, ...), custom_call_target="tpu_custom_call" | custom-call | tf_op jit(solution)/shard_map/attend_back/pallas_call | solution.py:66
  268.6 9.2 %qkv_weight_grads.2 = (f32[8,768]{1,0:T(8,128)}, bf16[2,512,768]{2,1,0:T(8,128)(2,1)}, bf16[2,2,2,3,48,768]{5,4,3,2,1,0:T(8,128)(2,1)}, bf16[2,3,48,768]{3,2,1,0...) custom-call(s32[4]{0:T(128)} %pad_add_fusion.refs_0_, ...), custom_call_target="tpu_custom_call" | custom-call | tf_op jit(solution)/shard_map/qkv_weight_grads/pallas_call | solution.py:66
  278.9 8.4 %norm_back.2 = (f32[512,768]{1,0:T(8,128)}, f32[8,768]{1,0:T(8,128)}) custom-call(s32[4]{0:T(128)} %pad_add_fusion.refs_0_, f32[512,768]{1,0:T(8,128)} %feed_down.2.refs_1_, f32[2,8,768]{2,1,0:T(8,128)} %reshape.153.refs_3_.refs_2_.refs_4_.refs_5_, f32[512,768]{1,0:T(8,128)} %get-tuple-element.292.refs_3_, ...), custom_call_target="tpu_custom_call" | custom-call | tf_op jit(solution)/shard_map/norm_back/pallas_call | solution.py:66
  288.6 4.2 combine.16
  298.3 7.8 %down_weight_grad.3 = (bf16[2,2,2,4,48,768]{5,4,3,2,1,0:T(8,128)(2,1)}, bf16[2,4,48,768]{3,2,1,0:T(8,128)(2,1)}, bf16[2,4,48,768]{3,2,1,0:T(8,128)(2,1)}, bf16[2...) custom-call(s32[4]{0:T(128)} %pad_add_fusion.refs_0_, bf16[512,3072]{1,0:T(8,128)(2,1)} %get-tuple-element.250.refs_2_.refs_1_, ...), custom_call_target="tpu_custom_call" | custom-call | tf_op jit(solution)/shard_map/down_weight_grad/pallas_call | solution.py:66
  306.1 15.7 %feed_back.3 = (bf16[512,3072]{1,0:T(8,128)(2,1)}, f32[512,768]{1,0:T(8,128)}, bf16[512,768]{1,0:T(8,128)(2,1)}, f32[8,768]{1,0:T(8,128)}, f32[1,3072]{1,0:T(1,128)}) custom-call(s32[4]{0:T(128)} %pad_add_fusion.refs_0_, f32[512,768]{1,0:T(8,128)} %get-tuple-element.315.refs_11_.refs_2_.refs_1_, bf16[512,3072]{1,0:T(8,128)(2,1)} %get-tuple-element.316.refs_2_, ...), custom_call_target="tpu_custom_call" | custom-call | tf_op jit(solution)/shard_map/feed_back/pallas_call | solution.py:66
  327.4 4.6 combine.17
  336.6 9.6 %feed_weight_grads.3 = (bf16[2,2,2,5,48,768]{5,4,3,2,1,0:T(8,128)(2,1)}, bf16[2,5,48,768]{3,2,1,0:T(8,128)(2,1)}, bf16[2,5,48,768]{3,2,1,0:T(8,128)(2,1)}, bf16[...) custom-call(s32[4]{0:T(128)} %pad_add_fusion.refs_0_, bf16[512,3072]{1,0:T(8,128)(2,1)} %get-tuple-element.331.refs_1_, ...), custom_call_target="tpu_custom_call" | custom-call | tf_op jit(solution)/shard_map/feed_weight_grads/pallas_call | solution.py:66
  346.3 22.8 %attend_back.3 = (bf16[512,768]{1,0:T(8,128)(2,1)}, bf16[512,768]{1,0:T(8,128)(2,1)}, bf16[512,768]{1,0:T(8,128)(2,1)}, bf16[512,768]{1,0:T(8,128)(2,1)}, bf16[512,768]{1,0:T(8,128)(2,1)}) custom-call(bf16[512,768]{1,0:T(8,128)(2,1)} %get-tuple-element.237.refs_0_, bf16[512,768]{1,0:T(8,128)(2,1)} %get-tuple-element.241.refs_1_, ...), custom_call_target="tpu_custom_call" | custom-call | tf_op jit(solution)/shard_map/attend_back/pallas_call | solution.py:66
  376.6 5.3 combine.18
  387.5 9.0 %qkv_weight_grads.3 = (f32[8,768]{1,0:T(8,128)}, bf16[2,512,768]{2,1,0:T(8,128)(2,1)}, bf16[2,2,2,3,48,768]{5,4,3,2,1,0:T(8,128)(2,1)}, bf16[2,3,48,768]{3,2,1,0...) custom-call(s32[4]{0:T(128)} %pad_add_fusion.refs_0_, ...), custom_call_target="tpu_custom_call" | custom-call | tf_op jit(solution)/shard_map/qkv_weight_grads/pallas_call | solution.py:66
  396.6 8.4 %norm_back.3 = (f32[512,768]{1,0:T(8,128)}, f32[8,768]{1,0:T(8,128)}) custom-call(s32[4]{0:T(128)} %pad_add_fusion.refs_0_, f32[512,768]{1,0:T(8,128)} %get-tuple-element.236.refs_1_, f32[2,8,768]{2,1,0:T(8,128)} %reshape.153.refs_3_.refs_2_.refs_4_.refs_5_, f32[512,768]{1,0:T(8,128)} %get-tuple-element.328.refs_3_, ...), custom_call_target="tpu_custom_call" | custom-call | tf_op jit(solution)/shard_map/norm_back/pallas_call | solution.py:66
  411.3 3.7 combine.19
  417.7 3.3 finish.6.refs_9_.refs_5_
  421.0 4.9 collective-permute-done.90.refs_7_
  428.1 3.1 combine.20
  437.1 7.8 %collective-permute-done.95.refs_9_ = bf16[4,48,768]{2,1,0:T(8,128)(2,1)S(1)} collective-permute-done((bf16[4,48,768]{2,1,0:T(8,128)(2,1)}, bf16[4,48,768]{2,1,0:T(8,128)(2,1)S(1)}, u32[]{:S(2)}, u32[]{:S(2)}) %collective-permute-start.95) | collective-permute-done | bytes 294944 | tf_op jit(solution)/shard_map/ppermute | solution.py:989
  444.8 4.7 collective-permute-done.94.refs_7_.refs_8_
  450.4 3.9 combine.21
  462.0 4.6 collective-permute-done.92.refs_6_
  467.3 3.6 finish.7
  470.9 7.5 %collective-permute-done.99.refs_12_ = bf16[3,48,768]{2,1,0:T(8,128)(2,1)S(1)} collective-permute-done((bf16[3,48,768]{2,1,0:T(8,128)(2,1)}, bf16[3,48,768]{2,1,0:T(8,128)(2,1)S(1)}, u32[]{:S(2)}, u32[]{:S(2)}) %collective-permute-start.99) | collective-permute-done | bytes 221216 | tf_op jit(solution)/shard_map/ppermute | solution.py:989
  479.5 3.4 combine.22
  487.8 10.9 %collective-permute-done.102.refs_4_ = bf16[4,48,768]{2,1,0:T(8,128)(2,1)S(1)} collective-permute-done((bf16[4,48,768]{2,1,0:T(8,128)(2,1)}, bf16[4,48,768]{2,1,0:T(8,128)(2,1)S(1)}, u32[]{:S(2)}, u32[]{:S(2)}) %collective-permute-start.102) | collective-permute-done | bytes 294944 | tf_op jit(solution)/shard_map/ppermute | solution.py:989
  500.3 3.0 combine.23
  511.8 3.3 finish.8.refs_3_
  516.2 15.3 %collective-permute-done.106.refs_2_.refs_4_ = bf16[8,48,768]{2,1,0:T(8,128)(2,1)S(1)} collective-permute-done((bf16[8,48,768]{2,1,0:T(8,128)(2,1)S(1)}, bf16[8,48,768]{2,1,0:T(8,128)(2,1)S(1)}, u32[]{:S(2)}, u32[]{:S(2)}) %collective-permute-start.106) | collective-permute-done | bytes 589856 | tf_op jit(solution)/shard_map/ppermute | solution.py:989
  538.5 3.0 finish.9
  547.4 3.5 collective-permute-done.109.refs_4_.refs_3_
  551.7 3.6 finish.10
  556.0 3.0 finish.11
  (565 shorter events, 177.9 us)
Async XLA Ops:
  4.3 14.2 %collective-permute-start.4 = (bf16[3,96,768]{2,1,0:T(8,128)(2,1)}, bf16[3,96,768]{2,1,0:T(8,128)(2,1)S(1)}, u32[]{:S(2)}, u32[]{:S(2)}) collective-permute-start(bf16[3,96,768]{2,1,0:T(8,128)(2,1)} %get-tuple-element.219.refs_8_), channel_id=1, source_target_pairs={{0,2},{2,0},{1,3},{3,1},{4,6},{6,4},{5,7},{7,5},{8,10},{10,8},{9,1... | collective-permute-start | bytes 1327112 | tf_op jit(solution)/shard_map/ppermute | solution.py:35
  7.3 19.2 %collective-permute-start = (bf16[256,768]{1,0:T(8,128)(2,1)}, bf16[256,768]{1,0:T(8,128)(2,1)S(1)}, u32[]{:S(2)}, u32[]{:S(2)}) collective-permute-start(bf16[256,768]{1,0:T(8,128)(2,1)} %get-tuple-element.218), channel_id=1, source_target_pairs={{0,2},{2,0},{1,3},{3,1},{4,6},{6,4},{5,7},{7,5},{8,10},{10,8},{9,1... | collective-permute-start | bytes 1179656 | tf_op jit(solution)/shard_map/ppermute | solution.py:35
  7.4 22.2 %collective-permute-start.3 = (bf16[3,192,768]{2,1,0:T(8,128)(2,1)}, bf16[3,192,768]{2,1,0:T(8,128)(2,1)}, u32[]{:S(2)}, u32[]{:S(2)}) collective-permute-start(bf16[3,192,768]{2,1,0:T(8,128)(2,1)} %get-tuple-element.221.refs_4_.refs_6_), channel_id=1, source_target_pairs={{0,1},{1,0},{2,3},{3,2},{4,5},{5,4},{6,7},{7,6},{8,9},{9,8},{10,11... | collective-permute-start | bytes 2654216 | tf_op jit(solution)/shard_map/ppermute | solution.py:35
  33.4 22.2 %collective-permute-start.14 = (bf16[6,96,768]{2,1,0:T(8,128)(2,1)}, bf16[6,96,768]{2,1,0:T(8,128)(2,1)}, u32[]{:S(2)}, u32[]{:S(2)}) collective-permute-start(bf16[6,96,768]{2,1,0:T(8,128)(2,1)} %get-tuple-element.240), channel_id=1, source_target_pairs={{0,2},{2,0},{1,3},{3,1},{4,6},{6,4},{5,7},{7,5},{8,10},{10,8},{9,1... | collective-permute-start | bytes 2654216 | tf_op jit(solution)/shard_map/ppermute | solution.py:35
  55.7 22.3 %collective-permute-start.18 = (bf16[6,96,768]{2,1,0:T(8,128)(2,1)}, bf16[6,96,768]{2,1,0:T(8,128)(2,1)S(1)}, u32[]{:S(2)}, u32[]{:S(2)}) collective-permute-start(bf16[6,96,768]{2,1,0:T(8,128)(2,1)} %collective-permute-done.14.refs_7_.refs_6_), channel_id=1, source_target_pairs={{0,4},{4,0},{1,5},{5,1},{2,6},{6,2},{3,7},{7,3},{8,12},{12,8},{9,1... | collective-permute-start | bytes 2654216 | tf_op jit(solution)/shard_map/ppermute | solution.py:35
  58.0 20.0 %collective-permute-start.20 = (bf16[3,96,768]{2,1,0:T(8,128)(2,1)S(1)}, bf16[3,96,768]{2,1,0:T(8,128)(2,1)S(1)}, u32[]{:S(2)}, u32[]{:S(2)}) collective-permute-start(bf16[3,96,768]{2,1,0:T(8,128)(2,1)S(1)} %copy-done.140), channel_id=1, source_target_pairs={{0,2},{2,0},{1,3},{3,1},{4,6},{6,4},{5,7},{7,5},{8,10},{10,8},{9,1... | collective-permute-start | bytes 1327112 | tf_op jit(solution)/shard_map/ppermute | solution.py:35
  78.5 20.9 %collective-permute-start.24 = (bf16[3,96,768]{2,1,0:T(8,128)(2,1)}, bf16[3,96,768]{2,1,0:T(8,128)(2,1)S(1)}, u32[]{:S(2)}, u32[]{:S(2)}) collective-permute-start(bf16[3,96,768]{2,1,0:T(8,128)(2,1)} %get-tuple-element.253), channel_id=1, source_target_pairs={{0,2},{2,0},{1,3},{3,1},{4,6},{6,4},{5,7},{7,5},{8,10},{10,8},{9,1... | collective-permute-start | bytes 1327112 | tf_op jit(solution)/shard_map/ppermute | solution.py:35
  80.2 19.3 %collective-permute-start.22 = (bf16[3,96,768]{2,1,0:T(8,128)(2,1)S(1)}, bf16[3,96,768]{2,1,0:T(8,128)(2,1)S(1)}, u32[]{:S(2)}, u32[]{:S(2)}) collective-permute-start(bf16[3,96,768]{2,1,0:T(8,128)(2,1)S(1)} %collective-permute-done.20.refs_12_.refs_13_), channel_id=1, source_target_pairs={{0,4},{4,0},{1,5},{5,1},{2,6},{6,2},{3,7},{7,3},{8,12},{12,8},{9,1... | collective-permute-start | bytes 1327112 | tf_op jit(solution)/shard_map/ppermute | solution.py:35
  125.5 19.4 %collective-permute-start.38 = (bf16[4,96,768]{2,1,0:T(8,128)(2,1)S(1)}, bf16[4,96,768]{2,1,0:T(8,128)(2,1)S(1)}, u32[]{:S(2)}, u32[]{:S(2)}) collective-permute-start(bf16[4,96,768]{2,1,0:T(8,128)(2,1)S(1)} %copy-done.133), channel_id=1, source_target_pairs={{0,2},{2,0},{1,3},{3,1},{4,6},{6,4},{5,7},{7,5},{8,10},{10,8},{9,1... | collective-permute-start | bytes 1769480 | tf_op jit(solution)/shard_map/ppermute | solution.py:35
  129.4 18.7 %collective-permute-start.36 = (bf16[2,96,768]{2,1,0:T(8,128)(2,1)S(1)}, bf16[2,96,768]{2,1,0:T(8,128)(2,1)S(1)}, u32[]{:S(2)}, u32[]{:S(2)}) collective-permute-start(bf16[2,96,768]{2,1,0:T(8,128)(2,1)S(1)} %collective-permute-done.30.refs_13_), channel_id=1, source_target_pairs={{0,4},{4,0},{1,5},{5,1},{2,6},{6,2},{3,7},{7,3},{8,12},{12,8},{9,1... | collective-permute-start | bytes 884744 | tf_op jit(solution)/shard_map/ppermute | solution.py:35
  145.0 29.8 %collective-permute-start.40 = (bf16[4,96,768]{2,1,0:T(8,128)(2,1)S(1)}, bf16[4,96,768]{2,1,0:T(8,128)(2,1)S(1)}, u32[]{:S(2)}, u32[]{:S(2)}) collective-permute-start(bf16[4,96,768]{2,1,0:T(8,128)(2,1)S(1)} %collective-permute-done.38.refs_6_.refs_19_), channel_id=1, source_target_pairs={{0,4},{4,0},{1,5},{5,1},{2,6},{6,2},{3,7},{7,3},{8,12},{12,8},{9,1... | collective-permute-start | bytes 1769480 | tf_op jit(solution)/shard_map/ppermute | solution.py:35
  146.7 19.0 %collective-permute-start.41 = (bf16[256,768]{1,0:T(8,128)(2,1)}, bf16[256,768]{1,0:T(8,128)(2,1)S(1)}, u32[]{:S(2)}, u32[]{:S(2)}) collective-permute-start(bf16[256,768]{1,0:T(8,128)(2,1)} %get-tuple-element.276), channel_id=1, source_target_pairs={{0,2},{2,0},{1,3},{3,1},{4,6},{6,4},{5,7},{7,5},{8,10},{10,8},{9,1... | collective-permute-start | bytes 1179656 | tf_op jit(solution)/shard_map/ppermute | solution.py:35
  174.8 13.0 %collective-permute-start.44 = (bf16[8,48,768]{2,1,0:T(8,128)(2,1)}, bf16[8,48,768]{2,1,0:T(8,128)(2,1)S(1)}, u32[]{:S(2)}, u32[]{:S(2)}) collective-permute-start(bf16[8,48,768]{2,1,0:T(8,128)(2,1)} %bitcast.129), channel_id=1, source_target_pairs={{0,1},{1,0},{2,3},{3,2},{4,5},{5,4},{6,7},{7,6},{8,9},{9,8},{10,11... | collective-permute-start | bytes 1769480 | tf_op jit(solution)/shard_map/ppermute | solution.py:35
  191.7 36.7 %collective-permute-start.48 = (bf16[16,48,768]{2,1,0:T(8,128)(2,1)}, bf16[16,48,768]{2,1,0:T(8,128)(2,1)S(1)}, u32[]{:S(2)}, u32[]{:S(2)}) collective-permute-start(bf16[16,48,768]{2,1,0:T(8,128)(2,1)} %combine.13.refs_23_), channel_id=1, source_target_pairs={{0,2},{2,0},{1,3},{3,1},{4,6},{6,4},{5,7},{7,5},{8,10},{10,8},{9,1... | collective-permute-start | bytes 3538952 | tf_op jit(solution)/shard_map/ppermute | solution.py:35
  192.4 36.1 %collective-permute-start.43 = (bf16[256,768]{1,0:T(8,128)(2,1)S(1)}, bf16[256,768]{1,0:T(8,128)(2,1)S(1)}, u32[]{:S(2)}, u32[]{:S(2)}) collective-permute-start(bf16[256,768]{1,0:T(8,128)(2,1)S(1)} %copy-done.145), channel_id=1, source_target_pairs={{0,2},{2,0},{1,3},{3,1},{4,6},{6,4},{5,7},{7,5},{8,10},{10,8},{9,1... | collective-permute-start | bytes 1179656 | tf_op jit(solution)/shard_map/ppermute | solution.py:35
  239.1 38.7 %collective-permute-start.56 = (bf16[20,48,768]{2,1,0:T(8,128)(2,1)}, bf16[20,48,768]{2,1,0:T(8,128)(2,1)S(1)}, u32[]{:S(2)}, u32[]{:S(2)}) collective-permute-start(bf16[20,48,768]{2,1,0:T(8,128)(2,1)} %get-tuple-element.321), channel_id=1, source_target_pairs={{0,2},{2,0},{1,3},{3,1},{4,6},{6,4},{5,7},{7,5},{8,10},{10,8},{9,1... | collective-permute-start | bytes 4423688 | tf_op jit(solution)/shard_map/ppermute | solution.py:35
  239.7 22.9 %collective-permute-start.53 = (bf16[8,48,768]{2,1,0:T(8,128)(2,1)}, bf16[8,48,768]{2,1,0:T(8,128)(2,1)S(1)}, u32[]{:S(2)}, u32[]{:S(2)}) collective-permute-start(bf16[8,48,768]{2,1,0:T(8,128)(2,1)} %get-tuple-element.305.refs_7_), channel_id=1, source_target_pairs={{0,4},{4,0},{1,5},{5,1},{2,6},{6,2},{3,7},{7,3},{8,12},{12,8},{9,1... | collective-permute-start | bytes 1769480 | tf_op jit(solution)/shard_map/ppermute | solution.py:35
  292.8 29.1 %collective-permute-start.62 = (bf16[12,48,768]{2,1,0:T(8,128)(2,1)}, bf16[12,48,768]{2,1,0:T(8,128)(2,1)S(1)}, u32[]{:S(2)}, u32[]{:S(2)}) collective-permute-start(bf16[12,48,768]{2,1,0:T(8,128)(2,1)} %get-tuple-element.326.refs_3_), channel_id=1, source_target_pairs={{0,2},{2,0},{1,3},{3,1},{4,6},{6,4},{5,7},{7,5},{8,10},{10,8},{9,1... | collective-permute-start | bytes 2654216 | tf_op jit(solution)/shard_map/ppermute | solution.py:35
  294.3 27.6 %collective-permute-start.63 = (bf16[10,48,768]{2,1,0:T(8,128)(2,1)}, bf16[10,48,768]{2,1,0:T(8,128)(2,1)S(1)}, u32[]{:S(2)}, u32[]{:S(2)}) collective-permute-start(bf16[10,48,768]{2,1,0:T(8,128)(2,1)} %get-tuple-element.336), channel_id=1, source_target_pairs={{0,4},{4,0},{1,5},{5,1},{2,6},{6,2},{3,7},{7,3},{8,12},{12,8},{9,1... | collective-permute-start | bytes 2211848 | tf_op jit(solution)/shard_map/ppermute | solution.py:35
  295.8 26.0 %collective-permute-start.64 = (bf16[4,48,768]{2,1,0:T(8,128)(2,1)}, bf16[4,48,768]{2,1,0:T(8,128)(2,1)S(1)}, u32[]{:S(2)}, u32[]{:S(2)}) collective-permute-start(bf16[4,48,768]{2,1,0:T(8,128)(2,1)} %get-tuple-element.337.refs_6_), channel_id=1, source_target_pairs={{0,24},{24,0},{8,16},{16,8},{1,25},{25,1},{9,17},{17,9},{2,26},{26... | collective-permute-start | bytes 884744 | tf_op jit(solution)/shard_map/ppermute | solution.py:989
  331.9 37.3 %collective-permute-start.69 = (bf16[16,48,768]{2,1,0:T(8,128)(2,1)}, bf16[16,48,768]{2,1,0:T(8,128)(2,1)S(1)}, u32[]{:S(2)}, u32[]{:S(2)}) collective-permute-start(bf16[16,48,768]{2,1,0:T(8,128)(2,1)} %get-tuple-element.342.refs_6_), channel_id=1, source_target_pairs={{0,2},{2,0},{1,3},{3,1},{4,6},{6,4},{5,7},{7,5},{8,10},{10,8},{9,1... | collective-permute-start | bytes 3538952 | tf_op jit(solution)/shard_map/ppermute | solution.py:35
  332.6 36.6 %collective-permute-start.70 = (bf16[6,48,768]{2,1,0:T(8,128)(2,1)}, bf16[6,48,768]{2,1,0:T(8,128)(2,1)S(1)}, u32[]{:S(2)}, u32[]{:S(2)}) collective-permute-start(bf16[6,48,768]{2,1,0:T(8,128)(2,1)} %get-tuple-element.349), channel_id=1, source_target_pairs={{0,4},{4,0},{1,5},{5,1},{2,6},{6,2},{3,7},{7,3},{8,12},{12,8},{9,1... | collective-permute-start | bytes 1327112 | tf_op jit(solution)/shard_map/ppermute | solution.py:35
  333.1 36.1 %collective-permute-start.73 = (bf16[5,48,768]{2,1,0:T(8,128)(2,1)}, bf16[5,48,768]{2,1,0:T(8,128)(2,1)S(1)}, u32[]{:S(2)}, u32[]{:S(2)}) collective-permute-start(bf16[5,48,768]{2,1,0:T(8,128)(2,1)} %get-tuple-element.352), channel_id=1, source_target_pairs={{0,8},{8,0},{16,24},{24,16},{1,9},{9,1},{17,25},{25,17},{2,10},{10... | collective-permute-start | bytes 1105928 | tf_op jit(solution)/shard_map/ppermute | solution.py:989
  333.8 35.4 %collective-permute-start.71 = (bf16[4,48,768]{2,1,0:T(8,128)(2,1)}, bf16[4,48,768]{2,1,0:T(8,128)(2,1)S(1)}, u32[]{:S(2)}, u32[]{:S(2)}) collective-permute-start(bf16[4,48,768]{2,1,0:T(8,128)(2,1)} %get-tuple-element.350.refs_1_), channel_id=1, source_target_pairs={{0,4},{4,0},{1,5},{5,1},{2,6},{6,2},{3,7},{7,3},{8,12},{12,8},{9,1... | collective-permute-start | bytes 884744 | tf_op jit(solution)/shard_map/ppermute | solution.py:35
  335.3 33.9 %collective-permute-start.72 = (bf16[4,48,768]{2,1,0:T(8,128)(2,1)}, bf16[4,48,768]{2,1,0:T(8,128)(2,1)S(1)}, u32[]{:S(2)}, u32[]{:S(2)}) collective-permute-start(bf16[4,48,768]{2,1,0:T(8,128)(2,1)} %get-tuple-element.351), channel_id=1, source_target_pairs={{0,8},{8,0},{16,24},{24,16},{1,9},{9,1},{17,25},{25,17},{2,10},{10... | collective-permute-start | bytes 884744 | tf_op jit(solution)/shard_map/ppermute | solution.py:989
  370.3 15.1 %collective-permute-start.74 = (bf16[512,768]{1,0:T(8,128)(2,1)}, bf16[512,768]{1,0:T(8,128)(2,1)}, u32[]{:S(2)}, u32[]{:S(2)}) collective-permute-start(bf16[512,768]{1,0:T(8,128)(2,1)} %get-tuple-element.353), channel_id=1, source_target_pairs={{0,1},{1,0},{2,3},{3,2},{4,5},{5,4},{6,7},{7,6},{8,9},{9,8},{10,11... | collective-permute-start | bytes 2359304 | tf_op jit(solution)/shard_map/ppermute | solution.py:35
  371.8 13.6 %collective-permute-start.75 = (bf16[512,768]{1,0:T(8,128)(2,1)}, bf16[512,768]{1,0:T(8,128)(2,1)}, u32[]{:S(2)}, u32[]{:S(2)}) collective-permute-start(bf16[512,768]{1,0:T(8,128)(2,1)} %get-tuple-element.354), channel_id=1, source_target_pairs={{0,1},{1,0},{2,3},{3,2},{4,5},{5,4},{6,7},{7,6},{8,9},{9,8},{10,11... | collective-permute-start | bytes 2359304 | tf_op jit(solution)/shard_map/ppermute | solution.py:35
  381.9 24.7 %collective-permute-start.81 = (bf16[8,48,768]{2,1,0:T(8,128)(2,1)}, bf16[8,48,768]{2,1,0:T(8,128)(2,1)S(1)}, u32[]{:S(2)}, u32[]{:S(2)}) collective-permute-start(bf16[8,48,768]{2,1,0:T(8,128)(2,1)} %get-tuple-element.367), channel_id=1, source_target_pairs={{0,4},{4,0},{1,5},{5,1},{2,6},{6,2},{3,7},{7,3},{8,12},{12,8},{9,1... | collective-permute-start | bytes 1769480 | tf_op jit(solution)/shard_map/ppermute | solution.py:35
  382.5 43.8 %collective-permute-start.80 = (bf16[20,48,768]{2,1,0:T(8,128)(2,1)}, bf16[20,48,768]{2,1,0:T(8,128)(2,1)S(1)}, u32[]{:S(2)}, u32[]{:S(2)}) collective-permute-start(bf16[20,48,768]{2,1,0:T(8,128)(2,1)} %get-tuple-element.363.refs_8_), channel_id=1, source_target_pairs={{0,2},{2,0},{1,3},{3,1},{4,6},{6,4},{5,7},{7,5},{8,10},{10,8},{9,1... | collective-permute-start | bytes 4423688 | tf_op jit(solution)/shard_map/ppermute | solution.py:35
  384.0 22.6 %collective-permute-start.84 = (bf16[5,48,768]{2,1,0:T(8,128)(2,1)}, bf16[5,48,768]{2,1,0:T(8,128)(2,1)S(1)}, u32[]{:S(2)}, u32[]{:S(2)}) collective-permute-start(bf16[5,48,768]{2,1,0:T(8,128)(2,1)} %get-tuple-element.374.refs_9_), channel_id=1, source_target_pairs={{0,24},{24,0},{8,16},{16,8},{1,25},{25,1},{9,17},{17,9},{2,26},{26... | collective-permute-start | bytes 1105928 | tf_op jit(solution)/shard_map/ppermute | solution.py:989
  385.4 21.2 %collective-permute-start.82 = (bf16[4,48,768]{2,1,0:T(8,128)(2,1)}, bf16[4,48,768]{2,1,0:T(8,128)(2,1)S(1)}, u32[]{:S(2)}, u32[]{:S(2)}) collective-permute-start(bf16[4,48,768]{2,1,0:T(8,128)(2,1)} %get-tuple-element.372), channel_id=1, source_target_pairs={{0,8},{8,0},{16,24},{24,16},{1,9},{9,1},{17,25},{25,17},{2,10},{10... | collective-permute-start | bytes 884744 | tf_op jit(solution)/shard_map/ppermute | solution.py:989
  385.4 21.2 %collective-permute-start.83 = (bf16[3,48,768]{2,1,0:T(8,128)(2,1)}, bf16[3,48,768]{2,1,0:T(8,128)(2,1)S(1)}, u32[]{:S(2)}, u32[]{:S(2)}) collective-permute-start(bf16[3,48,768]{2,1,0:T(8,128)(2,1)} %get-tuple-element.373), channel_id=1, source_target_pairs={{0,8},{8,0},{16,24},{24,16},{1,9},{9,1},{17,25},{25,17},{2,10},{10... | collective-permute-start | bytes 663560 | tf_op jit(solution)/shard_map/ppermute | solution.py:989
  417.1 27.7 %collective-permute-start.93 = (bf16[13,48,768]{2,1,0:T(8,128)(2,1)}, bf16[13,48,768]{2,1,0:T(8,128)(2,1)S(1)}, u32[]{:S(2)}, u32[]{:S(2)}) collective-permute-start(bf16[13,48,768]{2,1,0:T(8,128)(2,1)} %get-tuple-element.389.refs_5_.refs_3_), channel_id=1, source_target_pairs={{0,2},{2,0},{1,3},{3,1},{4,6},{6,4},{5,7},{7,5},{8,10},{10,8},{9,1... | collective-permute-start | bytes 2875400 | tf_op jit(solution)/shard_map/ppermute | solution.py:35
  431.3 18.2 %collective-permute-start.94 = (bf16[10,48,768]{2,1,0:T(8,128)(2,1)}, bf16[10,48,768]{2,1,0:T(8,128)(2,1)S(1)}, u32[]{:S(2)}, u32[]{:S(2)}) collective-permute-start(bf16[10,48,768]{2,1,0:T(8,128)(2,1)} %get-tuple-element.390.refs_15_), channel_id=1, source_target_pairs={{0,4},{4,0},{1,5},{5,1},{2,6},{6,2},{3,7},{7,3},{8,12},{12,8},{9,1... | collective-permute-start | bytes 2211848 | tf_op jit(solution)/shard_map/ppermute | solution.py:35
  435.0 23.1 %collective-permute-start.100 = (bf16[5,48,768]{2,1,0:T(8,128)(2,1)S(1)}, bf16[5,48,768]{2,1,0:T(8,128)(2,1)S(1)}, u32[]{:S(2)}, u32[]{:S(2)}) collective-permute-start(bf16[5,48,768]{2,1,0:T(8,128)(2,1)S(1)} %copy-done.146), channel_id=1, source_target_pairs={{0,8},{8,0},{16,24},{24,16},{1,9},{9,1},{17,25},{25,17},{2,10},{10... | collective-permute-start | bytes 1105928 | tf_op jit(solution)/shard_map/ppermute | solution.py:989
  435.0 24.7 %collective-permute-start.101 = (bf16[5,48,768]{2,1,0:T(8,128)(2,1)}, bf16[5,48,768]{2,1,0:T(8,128)(2,1)S(1)}, u32[]{:S(2)}, u32[]{:S(2)}) collective-permute-start(bf16[5,48,768]{2,1,0:T(8,128)(2,1)} %get-tuple-element.398), channel_id=1, source_target_pairs={{0,8},{8,0},{16,24},{24,16},{1,9},{9,1},{17,25},{25,17},{2,10},{10... | collective-permute-start | bytes 1105928 | tf_op jit(solution)/shard_map/ppermute | solution.py:989
  454.3 24.1 %collective-permute-start.96 = (bf16[7,48,768]{2,1,0:T(8,128)(2,1)}, bf16[7,48,768]{2,1,0:T(8,128)(2,1)S(1)}, u32[]{:S(2)}, u32[]{:S(2)}) collective-permute-start(bf16[7,48,768]{2,1,0:T(8,128)(2,1)} %get-tuple-element.393.refs_5_.refs_4_), channel_id=1, source_target_pairs={{0,4},{4,0},{1,5},{5,1},{2,6},{6,2},{3,7},{7,3},{8,12},{12,8},{9,1... | collective-permute-start | bytes 1548296 | tf_op jit(solution)/shard_map/ppermute | solution.py:35
  457.7 20.7 %collective-permute-start.97 = (bf16[5,48,768]{2,1,0:T(8,128)(2,1)}, bf16[5,48,768]{2,1,0:T(8,128)(2,1)S(1)}, u32[]{:S(2)}, u32[]{:S(2)}) collective-permute-start(bf16[5,48,768]{2,1,0:T(8,128)(2,1)} %get-tuple-element.394), channel_id=1, source_target_pairs={{0,8},{8,0},{16,24},{24,16},{1,9},{9,1},{17,25},{25,17},{2,10},{10... | collective-permute-start | bytes 1105928 | tf_op jit(solution)/shard_map/ppermute | solution.py:989
  458.1 20.3 %collective-permute-start.98 = (bf16[4,48,768]{2,1,0:T(8,128)(2,1)}, bf16[4,48,768]{2,1,0:T(8,128)(2,1)S(1)}, u32[]{:S(2)}, u32[]{:S(2)}) collective-permute-start(bf16[4,48,768]{2,1,0:T(8,128)(2,1)} %get-tuple-element.395), channel_id=1, source_target_pairs={{0,8},{8,0},{16,24},{24,16},{1,9},{9,1},{17,25},{25,17},{2,10},{10... | collective-permute-start | bytes 884744 | tf_op jit(solution)/shard_map/ppermute | solution.py:989
  459.8 18.6 %collective-permute-start.99 = (bf16[3,48,768]{2,1,0:T(8,128)(2,1)}, bf16[3,48,768]{2,1,0:T(8,128)(2,1)S(1)}, u32[]{:S(2)}, u32[]{:S(2)}) collective-permute-start(bf16[3,48,768]{2,1,0:T(8,128)(2,1)} %get-tuple-element.396.refs_11_), channel_id=1, source_target_pairs={{0,24},{24,0},{8,16},{16,8},{1,25},{25,1},{9,17},{17,9},{2,26},{26... | collective-permute-start | bytes 663560 | tf_op jit(solution)/shard_map/ppermute | solution.py:989
  482.9 15.8 %collective-permute-start.104 = (bf16[7,48,768]{2,1,0:T(8,128)(2,1)}, bf16[7,48,768]{2,1,0:T(8,128)(2,1)S(1)}, u32[]{:S(2)}, u32[]{:S(2)}) collective-permute-start(bf16[7,48,768]{2,1,0:T(8,128)(2,1)} %get-tuple-element.402.refs_1_), channel_id=1, source_target_pairs={{0,4},{4,0},{1,5},{5,1},{2,6},{6,2},{3,7},{7,3},{8,12},{12,8},{9,1... | collective-permute-start | bytes 1548296 | tf_op jit(solution)/shard_map/ppermute | solution.py:35
  483.4 15.3 %collective-permute-start.103 = (bf16[5,48,768]{2,1,0:T(8,128)(2,1)}, bf16[5,48,768]{2,1,0:T(8,128)(2,1)S(1)}, u32[]{:S(2)}, u32[]{:S(2)}) collective-permute-start(bf16[5,48,768]{2,1,0:T(8,128)(2,1)} %get-tuple-element.401.refs_6_), channel_id=1, source_target_pairs={{0,24},{24,0},{8,16},{16,8},{1,25},{25,1},{9,17},{17,9},{2,26},{26... | collective-permute-start | bytes 1105928 | tf_op jit(solution)/shard_map/ppermute | solution.py:989
  485.1 13.6 %collective-permute-start.102 = (bf16[4,48,768]{2,1,0:T(8,128)(2,1)}, bf16[4,48,768]{2,1,0:T(8,128)(2,1)S(1)}, u32[]{:S(2)}, u32[]{:S(2)}) collective-permute-start(bf16[4,48,768]{2,1,0:T(8,128)(2,1)} %get-tuple-element.400.refs_5_.refs_9_), channel_id=1, source_target_pairs={{0,8},{8,0},{16,24},{24,16},{1,9},{9,1},{17,25},{25,17},{2,10},{10... | collective-permute-start | bytes 884744 | tf_op jit(solution)/shard_map/ppermute | solution.py:989
  486.2 24.9 %collective-permute-start.107 = (bf16[4,48,768]{2,1,0:T(8,128)(2,1)S(1)}, bf16[4,48,768]{2,1,0:T(8,128)(2,1)S(1)}, u32[]{:S(2)}, u32[]{:S(2)}) collective-permute-start(bf16[4,48,768]{2,1,0:T(8,128)(2,1)S(1)} %copy-done.94), channel_id=1, source_target_pairs={{0,4},{4,0},{1,5},{5,1},{2,6},{6,2},{3,7},{7,3},{8,12},{12,8},{9,1... | collective-permute-start | bytes 884744 | tf_op jit(solution)/shard_map/ppermute | solution.py:35
  506.6 31.2 %collective-permute-start.110 = (bf16[3,48,768]{2,1,0:T(8,128)(2,1)S(1)}, bf16[3,48,768]{2,1,0:T(8,128)(2,1)S(1)}, u32[]{:S(2)}, u32[]{:S(2)}) collective-permute-start(bf16[3,48,768]{2,1,0:T(8,128)(2,1)S(1)} %copy-done.148), channel_id=1, source_target_pairs={{0,8},{8,0},{16,24},{24,16},{1,9},{9,1},{17,25},{25,17},{2,10},{10... | collective-permute-start | bytes 663560 | tf_op jit(solution)/shard_map/ppermute | solution.py:989
  507.5 23.9 %collective-permute-start.106 = (bf16[8,48,768]{2,1,0:T(8,128)(2,1)S(1)}, bf16[8,48,768]{2,1,0:T(8,128)(2,1)S(1)}, u32[]{:S(2)}, u32[]{:S(2)}) collective-permute-start(bf16[8,48,768]{2,1,0:T(8,128)(2,1)S(1)} %copy-done.134), channel_id=1, source_target_pairs={{0,8},{8,0},{16,24},{24,16},{1,9},{9,1},{17,25},{25,17},{2,10},{10... | collective-permute-start | bytes 1769480 | tf_op jit(solution)/shard_map/ppermute | solution.py:989
  509.5 37.8 %collective-permute-start.112 = (bf16[5,48,768]{2,1,0:T(8,128)(2,1)S(1)}, bf16[5,48,768]{2,1,0:T(8,128)(2,1)S(1)}, u32[]{:S(2)}, u32[]{:S(2)}) collective-permute-start(bf16[5,48,768]{2,1,0:T(8,128)(2,1)S(1)} %copy-done.86), channel_id=1, source_target_pairs={{0,4},{4,0},{1,5},{5,1},{2,6},{6,2},{3,7},{7,3},{8,12},{12,8},{9,1... | collective-permute-start | bytes 1105928 | tf_op jit(solution)/shard_map/ppermute | solution.py:35
  534.4 16.5 %collective-permute-start.109 = (bf16[8,48,768]{2,1,0:T(8,128)(2,1)}, bf16[8,48,768]{2,1,0:T(8,128)(2,1)S(1)}, u32[]{:S(2)}, u32[]{:S(2)}) collective-permute-start(bf16[8,48,768]{2,1,0:T(8,128)(2,1)} %get-tuple-element.406.refs_5_.refs_1_), channel_id=1, source_target_pairs={{0,4},{4,0},{1,5},{5,1},{2,6},{6,2},{3,7},{7,3},{8,12},{12,8},{9,1... | collective-permute-start | bytes 1769480 | tf_op jit(solution)/shard_map/ppermute | solution.py:35
  (214 other events, 1272.8 us)

commit v3 on v2

--- a/solution.py
+++ b/solution.py
@@ -18,7 +18,7 @@
 NN = (((1,), (0,)), ((), ()))
 NT = (((1,), (1,)), ((), ()))
 TN = (((0,), (0,)), ((), ()))
-VMEM_LIMIT = 56 * 1024 * 1024
+VMEM_LIMIT = 40 * 1024 * 1024
 SCALE = 0.0
 
 QKV = ((0, slice(0, 3), 0),)
@@ -43,6 +43,10 @@
     return pl.BlockSpec(memory_space=pl.ANY)
 
 
+def hbm_spec():
+    return pl.BlockSpec(memory_space=pltpu.HBM)
+
+
 def smem_spec():
     return pl.BlockSpec(memory_space=pltpu.SMEM)
 
@@ -58,19 +62,26 @@
 
 
 def call(kernel, operands, in_specs, out_shape, out_specs, deps=(), **options):
-    first, last = len(operands), len(operands) + len(deps)
-
-    def ordered(*refs):
-        kernel(*refs[:first], *refs[last:])
-
+    def placed(array, spec):
+        if spec.memory_space == pltpu.HBM:
+            return pltpu.with_memory_space_constraint(array, pltpu.HBM)
+        return array
+
+    def result(shape, spec):
+        return pltpu.HBM(shape.shape, shape.dtype) if spec.memory_space == pltpu.HBM else shape
+
+    if isinstance(out_shape, tuple):
+        out_shape = tuple(map(result, out_shape, out_specs))
+    if deps:
+        operands = [after(operands[0], *deps), *operands[1:]]
     return pl.pallas_call(
-        ordered,
-        in_specs=list(in_specs) + [any_spec()] * len(deps),
+        kernel,
+        in_specs=list(in_specs),
         out_shape=out_shape,
         out_specs=out_specs,
         compiler_params=pltpu.CompilerParams(vmem_limit_bytes=VMEM_LIMIT),
         **options,
-    )(*operands, *deps)
+    )(*map(placed, operands, in_specs))
 
 
 def after(values, *deps):
@@ -202,9 +213,9 @@
     return call(
         functools.partial(pack_kernel, jobs, outs_of, len(clips)),
         [place, *sources, *clips],
-        [smem_spec()] + [any_spec()] * (len(sources) + len(clips)),
+        [smem_spec()] + [hbm_spec()] * (len(sources) + len(clips)),
         tuple(out_shape),
-        (any_spec(),) * len(out_shape),
+        (hbm_spec(),) * len(out_shape),
         deps,
         scratch_shapes=[
             pltpu.VMEM((len(jobs), share, width), BF16),
@@ -257,7 +268,7 @@
     return call(
         first_qkv_kernel,
         [place, frames, arrived, vectors, *shares],
-        [smem_spec()] + [vmem_spec()] * 3 + [any_spec()] * len(shares),
+        [smem_spec()] + [vmem_spec()] * 3 + [hbm_spec()] * len(shares),
         (shaped((rows, width), F32),) + (shaped((rows, width), BF16),) * 3,
         (vmem_spec(),) * 4,
         deps,
@@ -270,7 +281,7 @@
     return call(
         functools.partial(qkv_kernel, layer),
         [place, stream, vectors, *shares],
-        [smem_spec()] + [vmem_spec()] * 2 + [any_spec()] * len(shares),
+        [smem_spec()] + [vmem_spec()] * 2 + [hbm_spec()] * len(shares),
         (shaped((rows, width), BF16),) * 3,
         (vmem_spec(),) * 3,
         deps,
@@ -343,7 +354,7 @@
     return call(
         functools.partial(up_kernel, layer),
         [place, stream, mixed, vectors, up_bias, *shares],
-        [smem_spec()] + [vmem_spec()] * 4 + [any_spec()] * len(shares),
+        [smem_spec()] + [vmem_spec()] * 4 + [hbm_spec()] * len(shares),
         (shaped((rows, width), F32), shaped((rows, wide), BF16), shaped((rows, wide), BF16)),
         (vmem_spec(),) * 3,
         deps,
@@ -386,7 +397,7 @@
     return call(
         functools.partial(last_down_kernel if last else down_kernel, layer),
         [place, attended, activated, vectors, *shares],
-        [smem_spec()] + [vmem_spec()] * 3 + [any_spec()] * len(shares),
+        [smem_spec()] + [vmem_spec()] * 3 + [hbm_spec()] * len(shares),
         (shaped((rows // 2, width), BF16),) * 2 if last else shaped((rows, width), F32),
         (vmem_spec(),) * 2 if last else vmem_spec(),
         deps,
@@ -450,7 +461,7 @@
     return call(
         functools.partial(feed_back_kernel, layer),
         [place, grad, slope, attended, vectors, *shares],
-        [smem_spec()] + [vmem_spec()] * 4 + [any_spec()] * len(shares),
+        [smem_spec()] + [vmem_spec()] * 4 + [hbm_spec()] * len(shares),
         (
             shaped((rows, wide), BF16),
             shaped((rows, width), F32),
@@ -552,7 +563,7 @@
         [place, activated, grad],
         [smem_spec()] + [vmem_spec()] * 2,
         grad_shapes(SHARDS, width),
-        (any_spec(),) * 5,
+        (hbm_spec(),) * 5,
         deps,
         scratch_shapes=grad_scratch(width),
         cost_estimate=cost(8 * rows * width * width, 12 * rows * width + 8 * width * width),
@@ -597,7 +608,7 @@
         [place, hidden_grad, attended, attended_grad, mixed, vectors],
         [smem_spec()] + [vmem_spec()] * 5,
         grad_shapes(1 + SHARDS, width),
-        (any_spec(),) * 5,
+        (hbm_spec(),) * 5,
         deps,
         scratch_shapes=grad_scratch(width),
         cost_estimate=cost(10 * rows * width * width, 20 * rows * width + 10 * width * width),
@@ -648,7 +659,7 @@
         [place, stream, vectors, dq, dk, dv, dk_back, dv_back],
         [smem_spec()] + [vmem_spec()] * 7,
         (shaped((8, width), F32), shaped((2, rows, width), BF16)) + grad_shapes(3, width),
-        (vmem_spec(),) * 2 + (any_spec(),) * 5,
+        (vmem_spec(),) * 2 + (hbm_spec(),) * 5,
         deps,
         scratch_shapes=grad_scratch(width),
         cost_estimate=cost(6 * rows * width * width, 10 * rows * width + 6 * width * width),
@@ -750,7 +761,7 @@
     return call(
         functools.partial(norm_back_kernel, layer),
         [place, stream, vectors, attended_grad, dq, dkv, *shares],
-        [smem_spec()] + [vmem_spec()] * 5 + [any_spec()] * len(shares),
+        [smem_spec()] + [vmem_spec()] * 5 + [hbm_spec()] * len(shares),
         (shaped((rows, width), F32), shaped((8, width), F32)),
         (vmem_spec(),) * 2,
         deps,
@@ -801,9 +812,9 @@
     return call(
         kernel,
         operands,
-        [smem_spec()] + [any_spec()] * (len(operands) - 1),
+        [smem_spec()] + [hbm_spec()] * (len(operands) - 1),
         tuple(shaped(shape, F32) for shape in out_shapes),
-        (any_spec(),) * len(out_shapes),
+        (hbm_spec(),) * len(out_shapes),
         deps,
         input_output_aliases=aliases,
         scratch_shapes=[
@@ -875,9 +886,9 @@
     return call(
         functools.partial(combine_kernel, plan),
         arrays,
-        [any_spec()] * len(arrays),
+        [hbm_spec()] * len(arrays),
         tuple(shaped((sum(count for count, _ in segments), size, width), BF16) for segments in plan),
-        (any_spec(),) * len(plan),
+        (hbm_spec(),) * len(plan),
         deps,
         scratch_shapes=[
             pltpu.VMEM((rows, size, width), BF16),
@@ -923,8 +934,8 @@
             if not self.split:
                 return {"near": [(2 * n, [self.sum])]}
             whole = (n, [self.mirror_sent, self.mirror])
-            return {"near": [whole], "spread": [whole]}
-        if not self.split:
+            return {channel: [whole] for channel in ("near", "spread", "diagonal")[: 3 if self.last is None else 2]}
+        if not self.split or self.last is None:
             return {}
         return {self.last: [(n, [self.rest if self.last == "spread" else self.part_z])]}
 
@@ -932,8 +943,10 @@
         if stage == "after":
             if channel == "near":
                 self.part, self.rest = sent, arrived
+            elif channel == "spread":
+                self.part_z = arrived
             else:
-                self.part_z = arrived
+                self.rest_z = arrived
         elif stage == "last":
             self.rest_z = arrived
         else:
@@ -985,6 +998,9 @@
     for name, sent in zip(names, results):
         if name == "sum":
             arrived = lax.psum(sent, "z")
+        elif name == "diagonal":
+            both = [(2 * left + y, 2 * right + 1 - y) for left, right in PAIRS for y in range(2)]
+            arrived = lax.ppermute(sent, ("z", "y"), both)
         elif name in ("pair", "spread", "mirror"):
             arrived = lax.ppermute(sent, "z", MIRROR if name == "mirror" else PAIRS)
         else:
@@ -1144,8 +1160,6 @@
     def by_clip(mine, other):
         return jnp.where(x == 0, jnp.stack([mine, other]), jnp.stack([other, mine]))
 
-    output_other = swap(output_other, "x")
-
     def square(row_blocks, column_blocks):
         return (LAYERS, row_blocks * share, column_blocks * width)
 
@@ -1159,8 +1173,7 @@
         1, place, gradient, slope1, attended1, vectors, late, deps=(pin,)
     )
     parts = feed_weight_grads(1, split, place, hidden_grad, attended1, attended_grad, mixed1, vectors)
-    feed1 = Flow(split, parts, *landed, output_other)
-    output = by_clip(output_mine, output_other)
+    feed1 = Flow(split, parts, *landed)
     pin, (near, far) = exchange([(down1, "y"), (feed1, "x")], *feed1.back)
     dq, dk, dv, dk_twin, dv_twin = attend_back(
         queries1, keys1, keys_twin1, values1, values_twin1, lse1, mixed_grad, deps=(pin,)
@@ -1174,7 +1187,7 @@
     gradient, norm_sums1 = norm_back(
         1, place, stream1, vectors, attended_grad, dq, dkv, qkv1, deps=(parts[0],)
     )
-    qkv_1 = Flow(split, parts, far, *landed)
+    qkv_1 = Flow(split, parts, far, *landed, last=None)
     pin, landed = exchange([(qkv_1, "x"), (feed1, "y"), (down1, "mirror")], gradient, *qkv_1.back)
 
     parts = down_weight_grad(place, split, activated0, gradient, deps=(pin,))
@@ -1192,7 +1205,7 @@
     )
     dk_twin, dv_twin = after((dk_twin, dv_twin), *landed)
     dk_back, dv_back = swap(dk_twin, "core"), swap(dv_twin, "core")
-    feed0 = Flow(split, parts, dq, *landed, last="near")
+    feed0 = Flow(split, parts, dq, *landed, last=None)
     steps = [(feed0, "x"), (down0, "y"), (down1, "last"), (qkv_1, "pair"), (feed1, "mirror")]
     pin, (far, *landed) = exchange(steps, dq, *feed0.back)
     qkv_sums0, dkv, *parts = qkv_weight_grads(
@@ -1201,7 +1214,7 @@
     gradient, norm_sums0 = norm_back(
         0, place, stream0, vectors, attended_grad, dq, dkv, qkv0, deps=(parts[0],)
     )
-    qkv_0 = Flow(split, parts, gradient, *landed, last="near")
+    qkv_0 = Flow(split, parts, gradient, *landed, last=None)
     sums = jnp.concatenate(
         [
             part
@@ -1219,21 +1232,22 @@
     down_out = down1.finish(1, down_places, down_shapes, place, deps=(pin,))
     pin, landed = exchange([(feed0, "y"), (down0, "mirror"), (feed1, "last")], down_out[0])
     input_other = swap(after(gradient[quarter:].astype(BF16), pin), "x")
-    steps = [(qkv_0, "y"), (totals, "y"), (feed0, "pair"), (down0, "after"), (qkv_1, "mirror")]
+    steps = [(qkv_0, "y"), (totals, "y"), (feed0, "pair"), (down0, "after")]
     pin, landed = exchange(steps, pin)
+    output_other = swap(after(output_other, pin), "x")
     feed_out = feed1.finish(1, feed_places, feed_shapes, place, deps=(pin, input_other))
     input_grad = by_clip(gradient[:quarter], input_other.astype(F32))
-    steps = [(qkv_0, "pair"), (totals, "pair"), (feed0, "mirror"), (down0, "last"), (qkv_1, "after")]
-    pin, landed = exchange(steps, feed_out[0])
-    steps = [(qkv_0, "mirror"), (totals, "mirror"), (feed0, "after"), (qkv_1, "last")]
+    steps = [(qkv_0, "pair"), (totals, "pair"), (feed0, "mirror"), (down0, "last")]
+    pin, landed = exchange(steps, feed_out[0], output_other)
+    output = by_clip(output_mine, output_other)
+    steps = [(qkv_0, "mirror"), (totals, "mirror"), (feed0, "after"), (qkv_1, "mirror")]
     pin, landed = exchange(steps, pin)
     (down_out,) = down0.finish(0, down_places, down_shapes, place, down_out, deps=(pin,))
-    pin, landed = exchange([(qkv_0, "after"), (feed0, "last")], down_out)
+    pin, landed = exchange([(qkv_0, "after"), (qkv_1, "after")], down_out)
     totals = totals.done()[: LAYERS * (8 + SHARDS)].reshape(LAYERS, 8 + SHARDS, width)
-    qkv_out = qkv_1.finish(1, qkv_places, qkv_shapes, place, deps=(pin,))
-    pin, landed = exchange([(qkv_0, "last")], qkv_out[0])
     out_out, up_out = feed0.finish(0, feed_places, feed_shapes, place, feed_out, deps=(pin,))
-    query_out, key_out, value_out = qkv_0.finish(0, qkv_places, qkv_shapes, place, qkv_out, deps=(out_out,))
+    qkv_out = qkv_1.finish(1, qkv_places, qkv_shapes, place, deps=(out_out,))
+    query_out, key_out, value_out = qkv_0.finish(0, qkv_places, qkv_shapes, place, qkv_out)
 
     own_vectors = lax.dynamic_slice_in_dim(totals[:, :8], shard * share, share, axis=2)
     own_up = lax.dynamic_slice_in_dim(

time: 565 us -> 535 us (0.947)
  Pallas kernels: 306 us -> 258 us
  waiting for transfers between devices: 123 us -> 139 us
    pallas_call x41 -> x40, Pallas kernels: 306 us -> 258 us  [call(): pl.pallas_call(kernel, in_specs=list(in_specs), out_shape=out_shape, out_...]
    ppermute x0 -> x2, waiting for transfers between devices: none -> 10.4 us  [exchange(): arrived = lax.ppermute(sent, ('z', 'y'), both)]
    ppermute x93 -> x92, waiting for transfers between devices: 73.6 us -> 81.4 us  [swap(): return lax.ppermute(values, axis, SWAP)]
    unnamed x304 -> x324, local copies, waits for them, and re-layouts: 32.8 us -> 38.5 us
    ppermute x93 -> x92, starting transfers between devices: 57 us -> 54.1 us  [swap(): return lax.ppermute(values, axis, SWAP)]
    ppermute x20 -> x18, waiting for transfers between devices: 49.8 us -> 47.3 us  [exchange(): arrived = lax.ppermute(sent, 'z', MIRROR if name == 'mirror' else PAIRS)]
    ppermute x20 -> x18, starting transfers between devices: 24.2 us -> 26.2 us  [exchange(): arrived = lax.ppermute(sent, 'z', MIRROR if name == 'mirror' else PAIRS)]
  transfers between devices with their start and end apart: 113 -> 112, of which waited for: 47 -> 53; matrix products, arithmetic and copies ran while one was open for 3% -> 2% of each run, Pallas kernels for 50% -> 44%
where the time goes in v3:
time: 535 us; the launch traced here: 529 us
  Pallas kernels  258 us (48%)
  waiting for transfers between devices  139 us (26%)
  starting transfers between devices  83.1 us (16%)
  local copies, waits for them, and re-layouts  42.6 us (8%)
    pallas_call x40, Pallas kernels, call(): pl.pallas_call(kernel, in_specs=list(in_specs), out_shape=out_shape, out_...  258 us
    ppermute x92, waiting for transfers between devices, swap(): return lax.ppermute(values, axis, SWAP)  81.4 us
    ppermute x92, starting transfers between devices, swap(): return lax.ppermute(values, axis, SWAP)  54.1 us
    ppermute x18, waiting for transfers between devices, exchange(): arrived = lax.ppermute(sent, 'z', MIRROR if name == 'mirror' else PAIRS)  47.3 us
    unnamed x324, local copies, waits for them, and re-layouts  38.5 us
    ppermute x18, starting transfers between devices, exchange(): arrived = lax.ppermute(sent, 'z', MIRROR if name == 'mirror' else PAIRS)  26.2 us
  transfers between devices with their start and end apart: 112, of which 53 were waited for; matrix products, arithmetic and copies ran while one was open for 2% of the time, Pallas kernels for 44%

profile of v3, /device:TPU:0, one launch (start us, length us, event | category | flops | bytes accessed | tf_op | source)
XLA Modules:
  0.0 529.5 jit_solution(11108820521409878453)
XLA Ops:
  6.7 7.2 %pack_shares.3 = (bf16[6,192,768]{2,1,0:T(8,128)(2,1)}, bf16[6,96,768]{2,1,0:T(8,128)(2,1)}, bf16[3,192,768]{2,1,0:T(8,128)(2,1)}, bf16[3,96,768]{2,1,0:T(8,128)...) custom-call(s32[4]{0:T(128)S(1)} %pad_add_fusion.place_ref.refs_0_, ...), custom_call_target="tpu_custom_call" | custom-call | tf_op jit(solution)/shard_map/pack_shares/pallas_call | solution.py:77
  13.9 3.9 collective-permute-done.10.refs_2_
  19.9 5.4 %collective-permute-done.arrived_ref = bf16[256,768]{1,0:T(8,128)(2,1)S(1)} collective-permute-done((bf16[256,768]{1,0:T(8,128)(2,1)}, bf16[256,768]{1,0:T(8,128)(2,1)S(1)}, u32[]{:S(2)}, u32[]{:S(2)}) %collective-permute-start) | collective-permute-done | bytes 393248 | tf_op jit(solution)/shard_map/ppermute | solution.py:35
  32.7 3.8 collective-permute-done.2.refs_7_
  43.2 4.9 first_qkv.1
  48.2 12.0 %collective-permute-done.14.refs_2_ = bf16[6,96,768]{2,1,0:T(8,128)(2,1)} collective-permute-done((bf16[6,96,768]{2,1,0:T(8,128)(2,1)}, bf16[6,96,768]{2,1,0:T(8,128)(2,1)}, u32[]{:S(2)}, u32[]{:S(2)}) %collective-permute-start.14) | collective-permute-done | bytes 884768 | tf_op jit(solution)/shard_map/ppermute | solution.py:35
  65.1 13.0 %attend.2 = (bf16[512,768]{1,0:T(8,128)(2,1)S(1)}, f32[6,8,512]{2,1,0:T(8,128)S(1)}) custom-call(bf16[512,768]{1,0:T(8,128)(2,1)S(1)} %get-tuple-element.399.q_ref, bf16[512,768]{1,0:T(8,128)(2,1)S(1)} %get-tuple-element.282.ko_ref, bf16[512,768]{1,0:T(8,128)(2,1)S(1)} %collective-permute-done.17.kt_ref, bf16[512,768]{1,0:T(8,128)(2,1)S(1)} %get-tuple-element.287.vo_ref, ...), custom_call_target="tpu_custom_call" | custom-call | tf_op jit(solution)/shard_map/attend/pallas_call | solution.py:77
  88.7 10.6 %feed_up.2 = (f32[512,768]{1,0:T(8,128)S(1)}, bf16[512,3072]{1,0:T(8,128)(2,1)S(1)}, bf16[512,3072]{1,0:T(8,128)(2,1)S(1)}) custom-call(s32[4]{0:T(128)S(1)} %pad_add_fusion.place_ref.refs_0_, f32[512,768]{1,0:T(8,128)S(1)} %get-tuple-element.292.stream_ref, bf16[512,768]{1,0:T(8,128)(2,1)S(1)} %copy-done.35, f32[2,8,768]{2,1,0:T(8,128)S(1)} %reshape.153.vectors_ref, ...), custom_call_target="tpu_custom_call" | custom-call | tf_op jit(solution)/shard_map/feed_up/pallas_call | solution.py:77
  102.8 5.6 %feed_down.2.stream_ref = f32[512,768]{1,0:T(8,128)S(1)} custom-call(s32[4]{0:T(128)S(1)} %pad_add_fusion.place_ref.refs_0_, f32[512,768]{1,0:T(8,128)S(1)} %get-tuple-element.298.attended_ref, bf16[512,3072]{1,0:T(8,128)(2,1)S(1)} %get-tuple-element.294.activated_ref, f32[2,8,768]{2,1,0:T(8,128)S(1)} %reshape.153.vectors_ref, ...), custom_call_target="tpu_custom_call" | custom-call | tf_op jit(solution)/shard_map/feed_down/pallas_call | solution.py:77
  108.4 3.7 collective-permute-done.23.refs_2_
  116.5 5.3 next_qkv.1
  131.0 12.9 %attend.3 = (bf16[512,768]{1,0:T(8,128)(2,1)S(1)}, f32[6,8,512]{2,1,0:T(8,128)S(1)}) custom-call(bf16[512,768]{1,0:T(8,128)(2,1)S(1)} %get-tuple-element.351.q_ref, bf16[512,768]{1,0:T(8,128)(2,1)S(1)} %get-tuple-element.306.ko_ref, bf16[512,768]{1,0:T(8,128)(2,1)S(1)} %collective-permute-done.35.kt_ref, bf16[512,768]{1,0:T(8,128)(2,1)S(1)} %get-tuple-element.312.vo_ref, ...), custom_call_target="tpu_custom_call" | custom-call | tf_op jit(solution)/shard_map/attend/pallas_call | solution.py:77
  150.5 10.6 %feed_up.3 = (f32[512,768]{1,0:T(8,128)S(1)}, bf16[512,3072]{1,0:T(8,128)(2,1)S(1)}, bf16[512,3072]{1,0:T(8,128)(2,1)S(1)}) custom-call(s32[4]{0:T(128)S(1)} %pad_add_fusion.place_ref.refs_0_, f32[512,768]{1,0:T(8,128)S(1)} %feed_down.2.stream_ref, bf16[512,768]{1,0:T(8,128)(2,1)S(1)} %copy-done.9, f32[2,8,768]{2,1,0:T(8,128)S(1)} %reshape.153.vectors_ref, ...), custom_call_target="tpu_custom_call" | custom-call | tf_op jit(solution)/shard_map/feed_up/pallas_call | solution.py:77
  162.2 6.0 %down_weight_grad.2 = (bf16[2,2,2,4,48,768]{5,4,3,2,1,0:T(8,128)(2,1)}, bf16[2,4,48,768]{3,2,1,0:T(8,128)(2,1)}, bf16[2,4,48,768]{3,2,1,0:T(8,128)(2,1)}, bf16[2...) custom-call(s32[4]{0:T(128)S(1)} %pad_add_fusion.place_ref.refs_0_, ...), custom_call_target="tpu_custom_call" | custom-call | tf_op jit(solution)/shard_map/down_weight_grad/pallas_call | solution.py:77
  171.4 5.8 %feed_down.3 = (bf16[256,768]{1,0:T(8,128)(2,1)S(1)}, bf16[256,768]{1,0:T(8,128)(2,1)S(1)}) custom-call(s32[4]{0:T(128)S(1)} %pad_add_fusion.place_ref.refs_0_, f32[512,768]{1,0:T(8,128)S(1)} %get-tuple-element.317.attended_ref, bf16[512,3072]{1,0:T(8,128)(2,1)S(1)} %get-tuple-element.318.activated_ref, f32[2,8,768]{2,1,0:T(8,128)S(1)} %reshape.153.vectors_ref, ...), custom_call_target="tpu_custom_call" | custom-call | tf_op jit(solution)/shard_map/feed_down/pallas_call | solution.py:77
  181.6 11.7 %feed_back.2 = (bf16[512,3072]{1,0:T(8,128)(2,1)S(1)}, f32[512,768]{1,0:T(8,128)S(1)}, bf16[512,768]{1,0:T(8,128)(2,1)S(1)}, f32[8,768]{1,0:T(8,128)S(1)}, f32[1,3072]{1,0:T(1,128)S(1)}) custom-call(s32[4]{0:T(128)S(1)} %pad_add_fusion.place_ref.refs_0_, f32[512,768]{1,0:T(8,128)S(1)} %maximum_convert_fusion.grad_ref, ...), custom_call_target="tpu_custom_call" | custom-call | tf_op jit(solution)/shard_map/feed_back/pallas_call | solution.py:77
  193.3 7.0 %feed_weight_grads.2 = (bf16[2,2,2,5,48,768]{5,4,3,2,1,0:T(8,128)(2,1)}, bf16[2,5,48,768]{3,2,1,0:T(8,128)(2,1)}, bf16[2,5,48,768]{3,2,1,0:T(8,128)(2,1)}, bf16[...) custom-call(s32[4]{0:T(128)S(1)} %pad_add_fusion.place_ref.refs_0_, ...), custom_call_target="tpu_custom_call" | custom-call | tf_op jit(solution)/shard_map/feed_weight_grads/pallas_call | solution.py:77
  200.3 8.8 %collective-permute-done.47.refs_2_.refs_8_ = bf16[16,48,768]{2,1,0:T(8,128)(2,1)S(1)} collective-permute-done((bf16[16,48,768]{2,1,0:T(8,128)(2,1)}, bf16[16,48,768]{2,1,0:T(8,128)(2,1)S(1)}, u32[]{:S(2)}, u32[]{:S(2)}) %collective-permute-start.47) | collective-permute-done | bytes 1179680 | tf_op jit(solution)/shard_map/ppermute | solution.py:35
  215.6 3.4 combine.13
  220.7 22.1 %attend_back.2 = (bf16[512,768]{1,0:T(8,128)(2,1)S(1)}, bf16[512,768]{1,0:T(8,128)(2,1)S(1)}, bf16[512,768]{1,0:T(8,128)(2,1)S(1)}, bf16[512,768]{1,0:T(8,128)(2,1)S(1)}, bf16[512,768]{1,0:T(8,128)(2,1)S(1)}) custom-call(bf16[512,768]{1,0:T(8,128)(2,1)S(1)} %copy-done.23, bf16[512,768]{1,0:T(8,128)(2,1)S(1)} %copy-done.25, bf16[512,768]{1,0:T(8,128)(2,1)S(1)} %copy-done.29, ...), custom_call_target="tpu_custom_call" | custom-call | tf_op jit(solution)/shard_map/attend_back/pallas_call | solution.py:77
  247.4 5.9 %qkv_weight_grads.2 = (f32[8,768]{1,0:T(8,128)S(1)}, bf16[2,512,768]{2,1,0:T(8,128)(2,1)S(1)}, bf16[2,2,2,3,48,768]{5,4,3,2,1,0:T(8,128)(2,1)}, bf16[2,3,48,768]...) custom-call(s32[4]{0:T(128)S(1)} %pad_add_fusion.place_ref.refs_0_, ...), custom_call_target="tpu_custom_call" | custom-call | tf_op jit(solution)/shard_map/qkv_weight_grads/pallas_call | solution.py:77
  255.9 5.4 %norm_back.2 = (f32[512,768]{1,0:T(8,128)S(1)}, f32[8,768]{1,0:T(8,128)S(1)}) custom-call(s32[4]{0:T(128)S(1)} %pad_add_fusion.place_ref.refs_0_, f32[512,768]{1,0:T(8,128)S(1)} %feed_down.2.stream_ref, f32[2,8,768]{2,1,0:T(8,128)S(1)} %reshape.153.vectors_ref, f32[512,768]{1,0:T(8,128)S(1)} %get-tuple-element.339.attended_grad_ref, ...), custom_call_target="tpu_custom_call" | custom-call | tf_op jit(solution)/shard_map/norm_back/pallas_call | solution.py:77
  262.4 4.4 combine.15
  269.3 3.6 collective-permute-start.63
  272.9 6.0 %down_weight_grad.3 = (bf16[2,2,2,4,48,768]{5,4,3,2,1,0:T(8,128)(2,1)}, bf16[2,4,48,768]{3,2,1,0:T(8,128)(2,1)}, bf16[2,4,48,768]{3,2,1,0:T(8,128)(2,1)}, bf16[2...) custom-call(s32[4]{0:T(128)S(1)} %pad_add_fusion.place_ref.refs_0_, bf16[512,3072]{1,0:T(8,128)(2,1)S(1)} %copy-done.3, ...), custom_call_target="tpu_custom_call" | custom-call | tf_op jit(solution)/shard_map/down_weight_grad/pallas_call | solution.py:77
  279.0 11.9 %feed_back.3 = (bf16[512,3072]{1,0:T(8,128)(2,1)S(1)}, f32[512,768]{1,0:T(8,128)S(1)}, bf16[512,768]{1,0:T(8,128)(2,1)S(1)}, f32[8,768]{1,0:T(8,128)S(1)}, f32[1,3072]{1,0:T(1,128)S(1)}) custom-call(s32[4]{0:T(128)S(1)} %pad_add_fusion.place_ref.refs_0_, f32[512,768]{1,0:T(8,128)S(1)} %get-tuple-element.366.grad_ref, bf16[512,3072]{1,0:T(8,128)(2,1)S(1)} %copy-done.7, ...), custom_call_target="tpu_custom_call" | custom-call | tf_op jit(solution)/shard_map/feed_back/pallas_call | solution.py:77
  296.4 4.6 combine.16
  305.9 7.2 %feed_weight_grads.3 = (bf16[2,2,2,5,48,768]{5,4,3,2,1,0:T(8,128)(2,1)}, bf16[2,5,48,768]{3,2,1,0:T(8,128)(2,1)}, bf16[2,5,48,768]{3,2,1,0:T(8,128)(2,1)}, bf16[...) custom-call(s32[4]{0:T(128)S(1)} %pad_add_fusion.place_ref.refs_0_, ...), custom_call_target="tpu_custom_call" | custom-call | tf_op jit(solution)/shard_map/feed_weight_grads/pallas_call | solution.py:77
  313.2 22.8 %attend_back.3 = (bf16[512,768]{1,0:T(8,128)(2,1)S(1)}, bf16[512,768]{1,0:T(8,128)(2,1)S(1)}, bf16[512,768]{1,0:T(8,128)(2,1)S(1)}, bf16[512,768]{1,0:T(8,128)(2,1)S(1)}, bf16[512,768]{1,0:T(8,128)(2,1)}) custom-call(bf16[512,768]{1,0:T(8,128)(2,1)S(1)} %copy-done.13, bf16[512,768]{1,0:T(8,128)(2,1)S(1)} %copy-done.15, bf16[512,768]{1,0:T(8,128)(2,1)S(1)} %copy-done.19, ...), custom_call_target="tpu_custom_call" | custom-call | tf_op jit(solution)/shard_map/attend_back/pallas_call | solution.py:77
  343.6 5.4 %combine.17 = (bf16[20,48,768]{2,1,0:T(8,128)(2,1)}, bf16[8,48,768]{2,1,0:T(8,128)(2,1)}, bf16[4,48,768]{2,1,0:T(8,128)(2,1)}, bf16[3,48,768]{2,1,0:T(8,128)(2,1)}, bf16[5,48,768]{2,1,0:T(8,128)(2,1)}) custom-call(bf16[40,48,768]{2,1,0:T(8,128)(2,1)} %bitcast.83, bf16[10,48,768]{2,1,0:T(8,128)(2,1)} %copy-done.94, bf16[10,48,768]{2,1,0:T(8,128)(2,1)} %copy-done.95, ...), custom_call_target="tpu_custom_call" | custom-call | tf_op jit(solution)/shard_map/combine/pallas_call | solution.py:77
  362.4 5.8 %qkv_weight_grads.3 = (f32[8,768]{1,0:T(8,128)S(1)}, bf16[2,512,768]{2,1,0:T(8,128)(2,1)S(1)}, bf16[2,2,2,3,48,768]{5,4,3,2,1,0:T(8,128)(2,1)}, bf16[2,3,48,768]...) custom-call(s32[4]{0:T(128)S(1)} %pad_add_fusion.place_ref.refs_0_, ...), custom_call_target="tpu_custom_call" | custom-call | tf_op jit(solution)/shard_map/qkv_weight_grads/pallas_call | solution.py:77
  368.2 5.4 %norm_back.3 = (f32[512,768]{1,0:T(8,128)S(1)}, f32[8,768]{1,0:T(8,128)S(1)}) custom-call(s32[4]{0:T(128)S(1)} %pad_add_fusion.place_ref.refs_0_, f32[512,768]{1,0:T(8,128)S(1)} %copy-done.1, f32[2,8,768]{2,1,0:T(8,128)S(1)} %reshape.153.vectors_ref, f32[512,768]{1,0:T(8,128)S(1)} %copy-done.5, bf16[512,768]{1,0:T(8,128)(2,1)S(1)} %copy-done.33, ...), custom_call_target="tpu_custom_call" | custom-call | tf_op jit(solution)/shard_map/norm_back/pallas_call | solution.py:77
  380.2 3.7 combine.18
  386.6 3.2 finish.6.refs_5_
  389.9 4.0 collective-permute-done.89.refs_7_
  403.1 8.6 %collective-permute-done.93.refs_9_ = bf16[4,48,768]{2,1,0:T(8,128)(2,1)S(1)} collective-permute-done((bf16[4,48,768]{2,1,0:T(8,128)(2,1)}, bf16[4,48,768]{2,1,0:T(8,128)(2,1)S(1)}, u32[]{:S(2)}, u32[]{:S(2)}) %collective-permute-start.93) | collective-permute-done | bytes 294944 | tf_op jit(solution)/shard_map/ppermute | solution.py:1005
  411.7 5.0 collective-permute-done.92.refs_7_.refs_8_
  417.6 3.4 combine.20
  425.9 9.4 %collective-permute-done.97.refs_4_ = bf16[5,48,768]{2,1,0:T(8,128)(2,1)S(1)} collective-permute-done((bf16[5,48,768]{2,1,0:T(8,128)(2,1)S(1)}, bf16[5,48,768]{2,1,0:T(8,128)(2,1)S(1)}, u32[]{:S(2)}, u32[]{:S(2)}) %collective-permute-start.97) | collective-permute-done | bytes 368672 | tf_op jit(solution)/shard_map/ppermute | solution.py:1005
  436.0 3.5 finish.7
  439.5 6.8 %collective-permute-done.100.refs_10_.refs_2_ = bf16[4,48,768]{2,1,0:T(8,128)(2,1)S(1)} collective-permute-done((bf16[4,48,768]{2,1,0:T(8,128)(2,1)}, bf16[4,48,768]{2,1,0:T(8,128)(2,1)S(1)}, u32[]{:S(2)}, u32[]{:S(2)}) %collective-permute-start.100) | collective-permute-done | bytes 294944 | tf_op jit(solution)/shard_map/ppermute | solution.py:1005
  447.9 3.3 combine.21
  455.0 11.5 %collective-permute-done.101.refs_4_ = bf16[4,48,768]{2,1,0:T(8,128)(2,1)S(1)} collective-permute-done((bf16[4,48,768]{2,1,0:T(8,128)(2,1)}, bf16[4,48,768]{2,1,0:T(8,128)(2,1)S(1)}, u32[]{:S(2)}, u32[]{:S(2)}) %collective-permute-start.101) | collective-permute-done | bytes 294944 | tf_op jit(solution)/shard_map/ppermute | solution.py:1005
  467.9 3.9 combine.22
  478.8 3.2 finish.8
  494.5 7.6 %collective-permute-start.106 = (bf16[6,48,768]{2,1,0:T(8,128)(2,1)}, bf16[6,48,768]{2,1,0:T(8,128)(2,1)S(1)}, u32[]{:S(2)}, u32[]{:S(2)}) collective-permute-start(bf16[6,48,768]{2,1,0:T(8,128)(2,1)} %get-tuple-element.475), channel_id=1, source_target_pairs={{0,8},{8,0},{16,24},{24,16},{1,9},{9,1},{17,25},{25,17},{2,10},{10... | collective-permute-start | bytes 1327112 | tf_op jit(solution)/shard_map/ppermute | solution.py:1005
  504.4 3.5 finish.9
  513.4 9.1 %collective-permute-done.108.refs_4_ = bf16[6,48,768]{2,1,0:T(8,128)(2,1)S(1)} collective-permute-done((bf16[6,48,768]{2,1,0:T(8,128)(2,1)}, bf16[6,48,768]{2,1,0:T(8,128)(2,1)S(1)}, u32[]{:S(2)}, u32[]{:S(2)}) %collective-permute-start.108) | collective-permute-done | bytes 442400 | tf_op jit(solution)/shard_map/ppermute | solution.py:1003
  (582 shorter events, 184.8 us)
Async XLA Ops:
  3.5 14.3 %collective-permute-start.10 = (bf16[3,96,768]{2,1,0:T(8,128)(2,1)}, bf16[3,96,768]{2,1,0:T(8,128)(2,1)}, u32[]{:S(2)}, u32[]{:S(2)}) collective-permute-start(bf16[3,96,768]{2,1,0:T(8,128)(2,1)} %get-tuple-element.254), channel_id=1, source_target_pairs={{0,2},{2,0},{1,3},{3,1},{4,6},{6,4},{5,7},{7,5},{8,10},{10,8},{9,1... | collective-permute-start | bytes 1327112 | tf_op jit(solution)/shard_map/ppermute | solution.py:35
  6.6 18.7 %collective-permute-start = (bf16[256,768]{1,0:T(8,128)(2,1)}, bf16[256,768]{1,0:T(8,128)(2,1)S(1)}, u32[]{:S(2)}, u32[]{:S(2)}) collective-permute-start(bf16[256,768]{1,0:T(8,128)(2,1)} %get-tuple-element.262), channel_id=1, source_target_pairs={{0,2},{2,0},{1,3},{3,1},{4,6},{6,4},{5,7},{7,5},{8,10},{10,8},{9,1... | collective-permute-start | bytes 1179656 | tf_op jit(solution)/shard_map/ppermute | solution.py:35
  17.9 14.3 %collective-permute-start.11 = (bf16[3,96,768]{2,1,0:T(8,128)(2,1)}, bf16[3,96,768]{2,1,0:T(8,128)(2,1)}, u32[]{:S(2)}, u32[]{:S(2)}) collective-permute-start(bf16[3,96,768]{2,1,0:T(8,128)(2,1)} %collective-permute-done.10.refs_2_), channel_id=1, source_target_pairs={{0,4},{4,0},{1,5},{5,1},{2,6},{6,2},{3,7},{7,3},{8,12},{12,8},{9,1... | collective-permute-start | bytes 1327112 | tf_op jit(solution)/shard_map/ppermute | solution.py:35
  38.2 22.0 %collective-permute-start.14 = (bf16[6,96,768]{2,1,0:T(8,128)(2,1)}, bf16[6,96,768]{2,1,0:T(8,128)(2,1)}, u32[]{:S(2)}, u32[]{:S(2)}) collective-permute-start(bf16[6,96,768]{2,1,0:T(8,128)(2,1)} %get-tuple-element.281), channel_id=1, source_target_pairs={{0,2},{2,0},{1,3},{3,1},{4,6},{6,4},{5,7},{7,5},{8,10},{10,8},{9,1... | collective-permute-start | bytes 2654216 | tf_op jit(solution)/shard_map/ppermute | solution.py:35
  60.2 22.4 %collective-permute-start.21 = (bf16[6,96,768]{2,1,0:T(8,128)(2,1)}, bf16[6,96,768]{2,1,0:T(8,128)(2,1)}, u32[]{:S(2)}, u32[]{:S(2)}) collective-permute-start(bf16[6,96,768]{2,1,0:T(8,128)(2,1)} %collective-permute-done.14.refs_2_), channel_id=1, source_target_pairs={{0,4},{4,0},{1,5},{5,1},{2,6},{6,2},{3,7},{7,3},{8,12},{12,8},{9,1... | collective-permute-start | bytes 2654216 | tf_op jit(solution)/shard_map/ppermute | solution.py:35
  62.2 20.3 %collective-permute-start.15 = (bf16[3,96,768]{2,1,0:T(8,128)(2,1)S(1)}, bf16[3,96,768]{2,1,0:T(8,128)(2,1)}, u32[]{:S(2)}, u32[]{:S(2)}) collective-permute-start(bf16[3,96,768]{2,1,0:T(8,128)(2,1)S(1)} %copy-done.153), channel_id=1, source_target_pairs={{0,2},{2,0},{1,3},{3,1},{4,6},{6,4},{5,7},{7,5},{8,10},{10,8},{9,1... | collective-permute-start | bytes 1327112 | tf_op jit(solution)/shard_map/ppermute | solution.py:35
  83.1 16.2 %collective-permute-start.19 = (bf16[3,96,768]{2,1,0:T(8,128)(2,1)}, bf16[3,96,768]{2,1,0:T(8,128)(2,1)}, u32[]{:S(2)}, u32[]{:S(2)}) collective-permute-start(bf16[3,96,768]{2,1,0:T(8,128)(2,1)} %get-tuple-element.289), channel_id=1, source_target_pairs={{0,2},{2,0},{1,3},{3,1},{4,6},{6,4},{5,7},{7,5},{8,10},{10,8},{9,1... | collective-permute-start | bytes 1327112 | tf_op jit(solution)/shard_map/ppermute | solution.py:35
  83.4 16.1 %collective-permute-start.25 = (bf16[3,96,768]{2,1,0:T(8,128)(2,1)}, bf16[3,96,768]{2,1,0:T(8,128)(2,1)}, u32[]{:S(2)}, u32[]{:S(2)}) collective-permute-start(bf16[3,96,768]{2,1,0:T(8,128)(2,1)} %collective-permute-done.15.refs_8_), channel_id=1, source_target_pairs={{0,4},{4,0},{1,5},{5,1},{2,6},{6,2},{3,7},{7,3},{8,12},{12,8},{9,1... | collective-permute-start | bytes 1327112 | tf_op jit(solution)/shard_map/ppermute | solution.py:35
  126.1 18.8 %collective-permute-start.32 = (bf16[4,96,768]{2,1,0:T(8,128)(2,1)S(1)}, bf16[4,96,768]{2,1,0:T(8,128)(2,1)}, u32[]{:S(2)}, u32[]{:S(2)}) collective-permute-start(bf16[4,96,768]{2,1,0:T(8,128)(2,1)S(1)} %copy-done.147), channel_id=1, source_target_pairs={{0,2},{2,0},{1,3},{3,1},{4,6},{6,4},{5,7},{7,5},{8,10},{10,8},{9,1... | collective-permute-start | bytes 1769480 | tf_op jit(solution)/shard_map/ppermute | solution.py:35
  130.0 17.4 %collective-permute-start.38 = (bf16[2,96,768]{2,1,0:T(8,128)(2,1)S(1)}, bf16[2,96,768]{2,1,0:T(8,128)(2,1)}, u32[]{:S(2)}, u32[]{:S(2)}) collective-permute-start(bf16[2,96,768]{2,1,0:T(8,128)(2,1)S(1)} %collective-permute-done.27.refs_8_), channel_id=1, source_target_pairs={{0,4},{4,0},{1,5},{5,1},{2,6},{6,2},{3,7},{7,3},{8,12},{12,8},{9,1... | collective-permute-start | bytes 884744 | tf_op jit(solution)/shard_map/ppermute | solution.py:35
  144.9 23.3 %collective-permute-start.40 = (bf16[4,96,768]{2,1,0:T(8,128)(2,1)}, bf16[4,96,768]{2,1,0:T(8,128)(2,1)}, u32[]{:S(2)}, u32[]{:S(2)}) collective-permute-start(bf16[4,96,768]{2,1,0:T(8,128)(2,1)} %collective-permute-done.32.refs_2_.refs_14_), channel_id=1, source_target_pairs={{0,4},{4,0},{1,5},{5,1},{2,6},{6,2},{3,7},{7,3},{8,12},{12,8},{9,1... | collective-permute-start | bytes 1769480 | tf_op jit(solution)/shard_map/ppermute | solution.py:35
  146.1 15.0 %collective-permute-start.41 = (bf16[256,768]{1,0:T(8,128)(2,1)}, bf16[256,768]{1,0:T(8,128)(2,1)}, u32[]{:S(2)}, u32[]{:S(2)}) collective-permute-start(bf16[256,768]{1,0:T(8,128)(2,1)} %get-tuple-element.320), channel_id=1, source_target_pairs={{0,2},{2,0},{1,3},{3,1},{4,6},{6,4},{5,7},{7,5},{8,10},{10,8},{9,1... | collective-permute-start | bytes 1179656 | tf_op jit(solution)/shard_map/ppermute | solution.py:35
  180.8 28.3 %collective-permute-start.47 = (bf16[16,48,768]{2,1,0:T(8,128)(2,1)}, bf16[16,48,768]{2,1,0:T(8,128)(2,1)S(1)}, u32[]{:S(2)}, u32[]{:S(2)}) collective-permute-start(bf16[16,48,768]{2,1,0:T(8,128)(2,1)} %combine.12), channel_id=1, source_target_pairs={{0,2},{2,0},{1,3},{3,1},{4,6},{6,4},{5,7},{7,5},{8,10},{10,8},{9,1... | collective-permute-start | bytes 3538952 | tf_op jit(solution)/shard_map/ppermute | solution.py:35
  219.0 35.8 %collective-permute-start.55 = (bf16[20,48,768]{2,1,0:T(8,128)(2,1)}, bf16[20,48,768]{2,1,0:T(8,128)(2,1)S(1)}, u32[]{:S(2)}, u32[]{:S(2)}) collective-permute-start(bf16[20,48,768]{2,1,0:T(8,128)(2,1)} %get-tuple-element.371), channel_id=1, source_target_pairs={{0,2},{2,0},{1,3},{3,1},{4,6},{6,4},{5,7},{7,5},{8,10},{10,8},{9,1... | collective-permute-start | bytes 4423688 | tf_op jit(solution)/shard_map/ppermute | solution.py:35
  219.7 23.0 %collective-permute-start.52 = (bf16[8,48,768]{2,1,0:T(8,128)(2,1)}, bf16[8,48,768]{2,1,0:T(8,128)(2,1)S(1)}, u32[]{:S(2)}, u32[]{:S(2)}) collective-permute-start(bf16[8,48,768]{2,1,0:T(8,128)(2,1)} %get-tuple-element.350), channel_id=1, source_target_pairs={{0,4},{4,0},{1,5},{5,1},{2,6},{6,2},{3,7},{7,3},{8,12},{12,8},{9,1... | collective-permute-start | bytes 1769480 | tf_op jit(solution)/shard_map/ppermute | solution.py:35
  266.8 24.2 %collective-permute-start.61 = (bf16[12,48,768]{2,1,0:T(8,128)(2,1)}, bf16[12,48,768]{2,1,0:T(8,128)(2,1)S(1)}, u32[]{:S(2)}, u32[]{:S(2)}) collective-permute-start(bf16[12,48,768]{2,1,0:T(8,128)(2,1)} %get-tuple-element.377), channel_id=1, source_target_pairs={{0,2},{2,0},{1,3},{3,1},{4,6},{6,4},{5,7},{7,5},{8,10},{10,8},{9,1... | collective-permute-start | bytes 2654216 | tf_op jit(solution)/shard_map/ppermute | solution.py:35
  268.6 22.3 %collective-permute-start.62 = (bf16[10,48,768]{2,1,0:T(8,128)(2,1)}, bf16[10,48,768]{2,1,0:T(8,128)(2,1)S(1)}, u32[]{:S(2)}, u32[]{:S(2)}) collective-permute-start(bf16[10,48,768]{2,1,0:T(8,128)(2,1)} %get-tuple-element.387), channel_id=1, source_target_pairs={{0,4},{4,0},{1,5},{5,1},{2,6},{6,2},{3,7},{7,3},{8,12},{12,8},{9,1... | collective-permute-start | bytes 2211848 | tf_op jit(solution)/shard_map/ppermute | solution.py:35
  269.3 21.6 %collective-permute-start.63 = (bf16[4,48,768]{2,1,0:T(8,128)(2,1)}, bf16[4,48,768]{2,1,0:T(8,128)(2,1)S(1)}, u32[]{:S(2)}, u32[]{:S(2)}) collective-permute-start(bf16[4,48,768]{2,1,0:T(8,128)(2,1)} %get-tuple-element.388.refs_6_), channel_id=1, source_target_pairs={{0,24},{24,0},{8,16},{16,8},{1,25},{25,1},{9,17},{17,9},{2,26},{26... | collective-permute-start | bytes 884744 | tf_op jit(solution)/shard_map/ppermute | solution.py:1005
  301.1 35.1 %collective-permute-start.68 = (bf16[16,48,768]{2,1,0:T(8,128)(2,1)}, bf16[16,48,768]{2,1,0:T(8,128)(2,1)S(1)}, u32[]{:S(2)}, u32[]{:S(2)}) collective-permute-start(bf16[16,48,768]{2,1,0:T(8,128)(2,1)} %get-tuple-element.394), channel_id=1, source_target_pairs={{0,2},{2,0},{1,3},{3,1},{4,6},{6,4},{5,7},{7,5},{8,10},{10,8},{9,1... | collective-permute-start | bytes 3538952 | tf_op jit(solution)/shard_map/ppermute | solution.py:35
  301.8 34.3 %collective-permute-start.69 = (bf16[6,48,768]{2,1,0:T(8,128)(2,1)}, bf16[6,48,768]{2,1,0:T(8,128)(2,1)S(1)}, u32[]{:S(2)}, u32[]{:S(2)}) collective-permute-start(bf16[6,48,768]{2,1,0:T(8,128)(2,1)} %get-tuple-element.406), channel_id=1, source_target_pairs={{0,4},{4,0},{1,5},{5,1},{2,6},{6,2},{3,7},{7,3},{8,12},{12,8},{9,1... | collective-permute-start | bytes 1327112 | tf_op jit(solution)/shard_map/ppermute | solution.py:35
  302.8 33.4 %collective-permute-start.72 = (bf16[5,48,768]{2,1,0:T(8,128)(2,1)}, bf16[5,48,768]{2,1,0:T(8,128)(2,1)S(1)}, u32[]{:S(2)}, u32[]{:S(2)}) collective-permute-start(bf16[5,48,768]{2,1,0:T(8,128)(2,1)} %get-tuple-element.409), channel_id=1, source_target_pairs={{0,8},{8,0},{16,24},{24,16},{1,9},{9,1},{17,25},{25,17},{2,10},{10... | collective-permute-start | bytes 1105928 | tf_op jit(solution)/shard_map/ppermute | solution.py:1005
  302.8 33.2 %collective-permute-start.70 = (bf16[4,48,768]{2,1,0:T(8,128)(2,1)}, bf16[4,48,768]{2,1,0:T(8,128)(2,1)S(1)}, u32[]{:S(2)}, u32[]{:S(2)}) collective-permute-start(bf16[4,48,768]{2,1,0:T(8,128)(2,1)} %get-tuple-element.407.refs_1_), channel_id=1, source_target_pairs={{0,4},{4,0},{1,5},{5,1},{2,6},{6,2},{3,7},{7,3},{8,12},{12,8},{9,1... | collective-permute-start | bytes 884744 | tf_op jit(solution)/shard_map/ppermute | solution.py:35
  304.1 32.0 %collective-permute-start.71 = (bf16[4,48,768]{2,1,0:T(8,128)(2,1)}, bf16[4,48,768]{2,1,0:T(8,128)(2,1)S(1)}, u32[]{:S(2)}, u32[]{:S(2)}) collective-permute-start(bf16[4,48,768]{2,1,0:T(8,128)(2,1)} %get-tuple-element.408), channel_id=1, source_target_pairs={{0,8},{8,0},{16,24},{24,16},{1,9},{9,1},{17,25},{25,17},{2,10},{10... | collective-permute-start | bytes 884744 | tf_op jit(solution)/shard_map/ppermute | solution.py:1005
  337.3 15.5 %collective-permute-start.77 = (bf16[512,768]{1,0:T(8,128)(2,1)S(1)}, bf16[512,768]{1,0:T(8,128)(2,1)S(1)}, u32[]{:S(2)}, u32[]{:S(2)}) collective-permute-start(bf16[512,768]{1,0:T(8,128)(2,1)S(1)} %get-tuple-element.421), channel_id=1, source_target_pairs={{0,1},{1,0},{2,3},{3,2},{4,5},{5,4},{6,7},{7,6},{8,9},{9,8},{10,11... | collective-permute-start | bytes 2359304 | tf_op jit(solution)/shard_map/ppermute | solution.py:35
  338.8 15.0 %collective-permute-start.78 = (bf16[512,768]{1,0:T(8,128)(2,1)}, bf16[512,768]{1,0:T(8,128)(2,1)S(1)}, u32[]{:S(2)}, u32[]{:S(2)}) collective-permute-start(bf16[512,768]{1,0:T(8,128)(2,1)} %get-tuple-element.422), channel_id=1, source_target_pairs={{0,1},{1,0},{2,3},{3,2},{4,5},{5,4},{6,7},{7,6},{8,9},{9,8},{10,11... | collective-permute-start | bytes 2359304 | tf_op jit(solution)/shard_map/ppermute | solution.py:35
  349.1 25.7 %collective-permute-start.79 = (bf16[8,48,768]{2,1,0:T(8,128)(2,1)}, bf16[8,48,768]{2,1,0:T(8,128)(2,1)}, u32[]{:S(2)}, u32[]{:S(2)}) collective-permute-start(bf16[8,48,768]{2,1,0:T(8,128)(2,1)} %get-tuple-element.431), channel_id=1, source_target_pairs={{0,4},{4,0},{1,5},{5,1},{2,6},{6,2},{3,7},{7,3},{8,12},{12,8},{9,1... | collective-permute-start | bytes 1769480 | tf_op jit(solution)/shard_map/ppermute | solution.py:35
  350.0 44.8 %collective-permute-start.88 = (bf16[20,48,768]{2,1,0:T(8,128)(2,1)}, bf16[20,48,768]{2,1,0:T(8,128)(2,1)}, u32[]{:S(2)}, u32[]{:S(2)}) collective-permute-start(bf16[20,48,768]{2,1,0:T(8,128)(2,1)} %get-tuple-element.415), channel_id=1, source_target_pairs={{0,2},{2,0},{1,3},{3,1},{4,6},{6,4},{5,7},{7,5},{8,10},{10,8},{9,1... | collective-permute-start | bytes 4423688 | tf_op jit(solution)/shard_map/ppermute | solution.py:35
  351.8 23.0 %collective-permute-start.82 = (bf16[5,48,768]{2,1,0:T(8,128)(2,1)}, bf16[5,48,768]{2,1,0:T(8,128)(2,1)}, u32[]{:S(2)}, u32[]{:S(2)}) collective-permute-start(bf16[5,48,768]{2,1,0:T(8,128)(2,1)} %get-tuple-element.434.refs_9_), channel_id=1, source_target_pairs={{0,24},{24,0},{8,16},{16,8},{1,25},{25,1},{9,17},{17,9},{2,26},{26... | collective-permute-start | bytes 1105928 | tf_op jit(solution)/shard_map/ppermute | solution.py:1005
  353.7 21.1 %collective-permute-start.80 = (bf16[4,48,768]{2,1,0:T(8,128)(2,1)}, bf16[4,48,768]{2,1,0:T(8,128)(2,1)}, u32[]{:S(2)}, u32[]{:S(2)}) collective-permute-start(bf16[4,48,768]{2,1,0:T(8,128)(2,1)} %get-tuple-element.432), channel_id=1, source_target_pairs={{0,8},{8,0},{16,24},{24,16},{1,9},{9,1},{17,25},{25,17},{2,10},{10... | collective-permute-start | bytes 884744 | tf_op jit(solution)/shard_map/ppermute | solution.py:1005
  354.6 20.1 %collective-permute-start.81 = (bf16[3,48,768]{2,1,0:T(8,128)(2,1)}, bf16[3,48,768]{2,1,0:T(8,128)(2,1)S(1)}, u32[]{:S(2)}, u32[]{:S(2)}) collective-permute-start(bf16[3,48,768]{2,1,0:T(8,128)(2,1)} %get-tuple-element.433), channel_id=1, source_target_pairs={{0,8},{8,0},{16,24},{24,16},{1,9},{9,1},{17,25},{25,17},{2,10},{10... | collective-permute-start | bytes 663560 | tf_op jit(solution)/shard_map/ppermute | solution.py:1005
  384.9 26.8 %collective-permute-start.91 = (bf16[13,48,768]{2,1,0:T(8,128)(2,1)}, bf16[13,48,768]{2,1,0:T(8,128)(2,1)S(1)}, u32[]{:S(2)}, u32[]{:S(2)}) collective-permute-start(bf16[13,48,768]{2,1,0:T(8,128)(2,1)} %get-tuple-element.448.refs_3_), channel_id=1, source_target_pairs={{0,2},{2,0},{1,3},{3,1},{4,6},{6,4},{5,7},{7,5},{8,10},{10,8},{9,1... | collective-permute-start | bytes 2875400 | tf_op jit(solution)/shard_map/ppermute | solution.py:35
  398.7 18.0 %collective-permute-start.92 = (bf16[10,48,768]{2,1,0:T(8,128)(2,1)}, bf16[10,48,768]{2,1,0:T(8,128)(2,1)S(1)}, u32[]{:S(2)}, u32[]{:S(2)}) collective-permute-start(bf16[10,48,768]{2,1,0:T(8,128)(2,1)} %get-tuple-element.453), channel_id=1, source_target_pairs={{0,4},{4,0},{1,5},{5,1},{2,6},{6,2},{3,7},{7,3},{8,12},{12,8},{9,1... | collective-permute-start | bytes 2211848 | tf_op jit(solution)/shard_map/ppermute | solution.py:35
  402.3 21.5 %collective-permute-start.96 = (bf16[5,48,768]{2,1,0:T(8,128)(2,1)S(1)}, bf16[5,48,768]{2,1,0:T(8,128)(2,1)S(1)}, u32[]{:S(2)}, u32[]{:S(2)}) collective-permute-start(bf16[5,48,768]{2,1,0:T(8,128)(2,1)S(1)} %copy-done.154), channel_id=1, source_target_pairs={{0,8},{8,0},{16,24},{24,16},{1,9},{9,1},{17,25},{25,17},{2,10},{10... | collective-permute-start | bytes 1105928 | tf_op jit(solution)/shard_map/ppermute | solution.py:1005
  402.3 23.4 %collective-permute-start.95 = (bf16[256,768]{1,0:T(8,128)(2,1)S(1)}, bf16[256,768]{1,0:T(8,128)(2,1)S(1)}, u32[]{:S(2)}, u32[]{:S(2)}) collective-permute-start(bf16[256,768]{1,0:T(8,128)(2,1)S(1)} %slice.83), channel_id=1, source_target_pairs={{0,2},{2,0},{1,3},{3,1},{4,6},{6,4},{5,7},{7,5},{8,10},{10,8},{9,1... | collective-permute-start | bytes 1179656 | tf_op jit(solution)/shard_map/ppermute | solution.py:35
  421.0 25.3 %collective-permute-start.98 = (bf16[7,48,768]{2,1,0:T(8,128)(2,1)}, bf16[7,48,768]{2,1,0:T(8,128)(2,1)S(1)}, u32[]{:S(2)}, u32[]{:S(2)}) collective-permute-start(bf16[7,48,768]{2,1,0:T(8,128)(2,1)} %get-tuple-element.456.refs_4_), channel_id=1, source_target_pairs={{0,4},{4,0},{1,5},{5,1},{2,6},{6,2},{3,7},{7,3},{8,12},{12,8},{9,1... | collective-permute-start | bytes 1548296 | tf_op jit(solution)/shard_map/ppermute | solution.py:35
  422.0 17.5 %collective-permute-start.94 = (bf16[256,768]{1,0:T(8,128)(2,1)S(1)}, bf16[256,768]{1,0:T(8,128)(2,1)S(1)}, u32[]{:S(2)}, u32[]{:S(2)}) collective-permute-start(bf16[256,768]{1,0:T(8,128)(2,1)S(1)} %copy-done.52), channel_id=1, source_target_pairs={{0,2},{2,0},{1,3},{3,1},{4,6},{6,4},{5,7},{7,5},{8,10},{10,8},{9,1... | collective-permute-start | bytes 1179656 | tf_op jit(solution)/shard_map/ppermute | solution.py:35
  423.8 22.5 %collective-permute-start.99 = (bf16[5,48,768]{2,1,0:T(8,128)(2,1)}, bf16[5,48,768]{2,1,0:T(8,128)(2,1)S(1)}, u32[]{:S(2)}, u32[]{:S(2)}) collective-permute-start(bf16[5,48,768]{2,1,0:T(8,128)(2,1)} %get-tuple-element.464), channel_id=1, source_target_pairs={{0,8},{8,0},{16,24},{24,16},{1,9},{9,1},{17,25},{25,17},{2,10},{10... | collective-permute-start | bytes 1105928 | tf_op jit(solution)/shard_map/ppermute | solution.py:1005
  425.8 20.5 %collective-permute-start.100 = (bf16[4,48,768]{2,1,0:T(8,128)(2,1)}, bf16[4,48,768]{2,1,0:T(8,128)(2,1)S(1)}, u32[]{:S(2)}, u32[]{:S(2)}) collective-permute-start(bf16[4,48,768]{2,1,0:T(8,128)(2,1)} %get-tuple-element.465), channel_id=1, source_target_pairs={{0,8},{8,0},{16,24},{24,16},{1,9},{9,1},{17,25},{25,17},{2,10},{10... | collective-permute-start | bytes 884744 | tf_op jit(solution)/shard_map/ppermute | solution.py:1005
  451.3 15.2 %collective-permute-start.102 = (bf16[5,48,768]{2,1,0:T(8,128)(2,1)}, bf16[5,48,768]{2,1,0:T(8,128)(2,1)S(1)}, u32[]{:S(2)}, u32[]{:S(2)}) collective-permute-start(bf16[5,48,768]{2,1,0:T(8,128)(2,1)} %get-tuple-element.468.refs_11_), channel_id=1, source_target_pairs={{0,24},{24,0},{8,16},{16,8},{1,25},{25,1},{9,17},{17,9},{2,26},{26... | collective-permute-start | bytes 1105928 | tf_op jit(solution)/shard_map/ppermute | solution.py:1005
  452.9 24.5 %collective-permute-start.104 = (bf16[4,48,768]{2,1,0:T(8,128)(2,1)S(1)}, bf16[4,48,768]{2,1,0:T(8,128)(2,1)S(1)}, u32[]{:S(2)}, u32[]{:S(2)}) collective-permute-start(bf16[4,48,768]{2,1,0:T(8,128)(2,1)S(1)} %copy-done.123), channel_id=1, source_target_pairs={{0,4},{4,0},{1,5},{5,1},{2,6},{6,2},{3,7},{7,3},{8,12},{12,8},{9,1... | collective-permute-start | bytes 884744 | tf_op jit(solution)/shard_map/ppermute | solution.py:35
  454.0 23.4 %collective-permute-start.105 = (bf16[4,48,768]{2,1,0:T(8,128)(2,1)S(1)}, bf16[4,48,768]{2,1,0:T(8,128)(2,1)S(1)}, u32[]{:S(2)}, u32[]{:S(2)}) collective-permute-start(bf16[4,48,768]{2,1,0:T(8,128)(2,1)S(1)} %copy-done.158), channel_id=1, source_target_pairs={{0,4},{4,0},{1,5},{5,1},{2,6},{6,2},{3,7},{7,3},{8,12},{12,8},{9,1... | collective-permute-start | bytes 884744 | tf_op jit(solution)/shard_map/ppermute | solution.py:35
  471.8 16.8 %collective-permute-start.103 = (bf16[7,48,768]{2,1,0:T(8,128)(2,1)}, bf16[7,48,768]{2,1,0:T(8,128)(2,1)S(1)}, u32[]{:S(2)}, u32[]{:S(2)}) collective-permute-start(bf16[7,48,768]{2,1,0:T(8,128)(2,1)} %get-tuple-element.473.refs_0_), channel_id=1, source_target_pairs={{0,24},{24,0},{8,16},{16,8},{1,25},{25,1},{9,17},{17,9},{2,26},{26... | collective-permute-start | bytes 1548296 | tf_op jit(solution)/shard_map/ppermute | solution.py:1005
  482.0 20.1 %collective-permute-start.109 = (bf16[5,48,768]{2,1,0:T(8,128)(2,1)S(1)}, bf16[5,48,768]{2,1,0:T(8,128)(2,1)S(1)}, u32[]{:S(2)}, u32[]{:S(2)}) collective-permute-start(bf16[5,48,768]{2,1,0:T(8,128)(2,1)S(1)} %copy-done.155), channel_id=1, source_target_pairs={{0,8},{8,0},{16,24},{24,16},{1,9},{9,1},{17,25},{25,17},{2,10},{10... | collective-permute-start | bytes 1105928 | tf_op jit(solution)/shard_map/ppermute | solution.py:1005
  482.1 20.3 %collective-permute-start.110 = (bf16[5,48,768]{2,1,0:T(8,128)(2,1)S(1)}, bf16[5,48,768]{2,1,0:T(8,128)(2,1)S(1)}, u32[]{:S(2)}, u32[]{:S(2)}) collective-permute-start(bf16[5,48,768]{2,1,0:T(8,128)(2,1)S(1)} %copy-done.117), channel_id=1, source_target_pairs={{0,4},{4,0},{1,5},{5,1},{2,6},{6,2},{3,7},{7,3},{8,12},{12,8},{9,1... | collective-permute-start | bytes 1105928 | tf_op jit(solution)/shard_map/ppermute | solution.py:35
  483.0 20.7 %collective-permute-start.111 = (bf16[5,48,768]{2,1,0:T(8,128)(2,1)}, bf16[5,48,768]{2,1,0:T(8,128)(2,1)S(1)}, u32[]{:S(2)}, u32[]{:S(2)}) collective-permute-start(bf16[5,48,768]{2,1,0:T(8,128)(2,1)} %get-tuple-element.480), channel_id=1, source_target_pairs={{0,12},{4,8},{8,4},{12,0},{16,28},{20,24},{24,20},{28,16},{1,13},{... | collective-permute-start | bytes 1105928 | tf_op jit(solution)/shard_map/ppermute | solution.py:1003
  492.5 20.9 %collective-permute-start.107 = (bf16[6,48,768]{2,1,0:T(8,128)(2,1)}, bf16[6,48,768]{2,1,0:T(8,128)(2,1)S(1)}, u32[]{:S(2)}, u32[]{:S(2)}) collective-permute-start(bf16[6,48,768]{2,1,0:T(8,128)(2,1)} %get-tuple-element.474.refs_1_), channel_id=1, source_target_pairs={{0,4},{4,0},{1,5},{5,1},{2,6},{6,2},{3,7},{7,3},{8,12},{12,8},{9,1... | collective-permute-start | bytes 1327112 | tf_op jit(solution)/shard_map/ppermute | solution.py:35
  494.5 18.9 %collective-permute-start.106 = (bf16[6,48,768]{2,1,0:T(8,128)(2,1)}, bf16[6,48,768]{2,1,0:T(8,128)(2,1)S(1)}, u32[]{:S(2)}, u32[]{:S(2)}) collective-permute-start(bf16[6,48,768]{2,1,0:T(8,128)(2,1)} %get-tuple-element.475), channel_id=1, source_target_pairs={{0,8},{8,0},{16,24},{24,16},{1,9},{9,1},{17,25},{25,17},{2,10},{10... | collective-permute-start | bytes 1327112 | tf_op jit(solution)/shard_map/ppermute | solution.py:1005
  502.1 20.4 %collective-permute-start.108 = (bf16[6,48,768]{2,1,0:T(8,128)(2,1)}, bf16[6,48,768]{2,1,0:T(8,128)(2,1)S(1)}, u32[]{:S(2)}, u32[]{:S(2)}) collective-permute-start(bf16[6,48,768]{2,1,0:T(8,128)(2,1)} %get-tuple-element.476), channel_id=1, source_target_pairs={{0,12},{4,8},{8,4},{12,0},{16,28},{20,24},{24,20},{28,16},{1,13},{... | collective-permute-start | bytes 1327112 | tf_op jit(solution)/shard_map/ppermute | solution.py:1003
  (223 other events, 1642.3 us)

commit v4 on v3

--- a/solution.py
+++ b/solution.py
@@ -1173,7 +1173,7 @@
         1, place, gradient, slope1, attended1, vectors, late, deps=(pin,)
     )
     parts = feed_weight_grads(1, split, place, hidden_grad, attended1, attended_grad, mixed1, vectors)
-    feed1 = Flow(split, parts, *landed)
+    feed1 = Flow(split, parts)
     pin, (near, far) = exchange([(down1, "y"), (feed1, "x")], *feed1.back)
     dq, dk, dv, dk_twin, dv_twin = attend_back(
         queries1, keys1, keys_twin1, values1, values_twin1, lse1, mixed_grad, deps=(pin,)

time: 535 us -> 530 us (level)
  waiting for transfers between devices: 139 us -> 133 us
    ppermute x92, waiting for transfers between devices: 81.4 us -> 75.7 us  [swap(): return lax.ppermute(values, axis, SWAP)]
where the time goes in v4:
time: 530 us; the launch traced here: 524 us
  Pallas kernels  258 us (49%)
  waiting for transfers between devices  133 us (25%)
  starting transfers between devices  83.3 us (16%)
  local copies, waits for them, and re-layouts  42.8 us (8%)
    pallas_call x40, Pallas kernels, call(): pl.pallas_call(kernel, in_specs=list(in_specs), out_shape=out_shape, out_...  258 us
    ppermute x92, waiting for transfers between devices, swap(): return lax.ppermute(values, axis, SWAP)  75.7 us
    ppermute x92, starting transfers between devices, swap(): return lax.ppermute(values, axis, SWAP)  54.1 us
    ppermute x18, waiting for transfers between devices, exchange(): arrived = lax.ppermute(sent, 'z', MIRROR if name == 'mirror' else PAIRS)  47.2 us
    unnamed x324, local copies, waits for them, and re-layouts  38.7 us
    ppermute x18, starting transfers between devices, exchange(): arrived = lax.ppermute(sent, 'z', MIRROR if name == 'mirror' else PAIRS)  26.4 us
  transfers between devices with their start and end apart: 112, of which 53 were waited for; matrix products, arithmetic and copies ran while one was open for 2% of the time, Pallas kernels for 44%

profile of v4, /device:TPU:0, one launch (start us, length us, event | category | flops | bytes accessed | tf_op | source)
XLA Modules:
  0.0 523.8 jit_solution(15092101736202617511)
XLA Ops:
  6.7 7.2 %pack_shares.3 = (bf16[6,192,768]{2,1,0:T(8,128)(2,1)}, bf16[6,96,768]{2,1,0:T(8,128)(2,1)}, bf16[3,192,768]{2,1,0:T(8,128)(2,1)}, bf16[3,96,768]{2,1,0:T(8,128)...) custom-call(s32[4]{0:T(128)S(1)} %pad_add_fusion.place_ref.refs_0_, ...), custom_call_target="tpu_custom_call" | custom-call | tf_op jit(solution)/shard_map/pack_shares/pallas_call | solution.py:77
  13.9 3.9 collective-permute-done.10.refs_2_
  19.9 5.4 %collective-permute-done.arrived_ref = bf16[256,768]{1,0:T(8,128)(2,1)S(1)} collective-permute-done((bf16[256,768]{1,0:T(8,128)(2,1)}, bf16[256,768]{1,0:T(8,128)(2,1)S(1)}, u32[]{:S(2)}, u32[]{:S(2)}) %collective-permute-start) | collective-permute-done | bytes 393248 | tf_op jit(solution)/shard_map/ppermute | solution.py:35
  32.7 3.8 collective-permute-done.2.refs_7_
  43.2 4.9 first_qkv.1
  48.2 12.0 %collective-permute-done.14.refs_2_ = bf16[6,96,768]{2,1,0:T(8,128)(2,1)} collective-permute-done((bf16[6,96,768]{2,1,0:T(8,128)(2,1)}, bf16[6,96,768]{2,1,0:T(8,128)(2,1)}, u32[]{:S(2)}, u32[]{:S(2)}) %collective-permute-start.14) | collective-permute-done | bytes 884768 | tf_op jit(solution)/shard_map/ppermute | solution.py:35
  65.1 13.0 %attend.2 = (bf16[512,768]{1,0:T(8,128)(2,1)S(1)}, f32[6,8,512]{2,1,0:T(8,128)S(1)}) custom-call(bf16[512,768]{1,0:T(8,128)(2,1)S(1)} %get-tuple-element.399.q_ref, bf16[512,768]{1,0:T(8,128)(2,1)S(1)} %get-tuple-element.282.ko_ref, bf16[512,768]{1,0:T(8,128)(2,1)S(1)} %collective-permute-done.17.kt_ref, bf16[512,768]{1,0:T(8,128)(2,1)S(1)} %get-tuple-element.287.vo_ref, ...), custom_call_target="tpu_custom_call" | custom-call | tf_op jit(solution)/shard_map/attend/pallas_call | solution.py:77
  88.7 10.6 %feed_up.2 = (f32[512,768]{1,0:T(8,128)S(1)}, bf16[512,3072]{1,0:T(8,128)(2,1)S(1)}, bf16[512,3072]{1,0:T(8,128)(2,1)S(1)}) custom-call(s32[4]{0:T(128)S(1)} %pad_add_fusion.place_ref.refs_0_, f32[512,768]{1,0:T(8,128)S(1)} %get-tuple-element.292.stream_ref, bf16[512,768]{1,0:T(8,128)(2,1)S(1)} %copy-done.35, f32[2,8,768]{2,1,0:T(8,128)S(1)} %reshape.153.vectors_ref, ...), custom_call_target="tpu_custom_call" | custom-call | tf_op jit(solution)/shard_map/feed_up/pallas_call | solution.py:77
  102.8 5.6 %feed_down.2.stream_ref = f32[512,768]{1,0:T(8,128)S(1)} custom-call(s32[4]{0:T(128)S(1)} %pad_add_fusion.place_ref.refs_0_, f32[512,768]{1,0:T(8,128)S(1)} %get-tuple-element.298.attended_ref, bf16[512,3072]{1,0:T(8,128)(2,1)S(1)} %get-tuple-element.294.activated_ref, f32[2,8,768]{2,1,0:T(8,128)S(1)} %reshape.153.vectors_ref, ...), custom_call_target="tpu_custom_call" | custom-call | tf_op jit(solution)/shard_map/feed_down/pallas_call | solution.py:77
  108.4 3.7 collective-permute-done.23.refs_2_
  116.4 5.3 %next_qkv.1 = (bf16[512,768]{1,0:T(8,128)(2,1)S(1)}, bf16[512,768]{1,0:T(8,128)(2,1)S(1)}, bf16[512,768]{1,0:T(8,128)(2,1)S(1)}) custom-call(s32[4]{0:T(128)S(1)} %pad_add_fusion.place_ref.refs_0_, f32[512,768]{1,0:T(8,128)S(1)} %feed_down.2.stream_ref, f32[2,8,768]{2,1,0:T(8,128)S(1)} %reshape.153.vectors_ref, ...), custom_call_target="tpu_custom_call" | custom-call | tf_op jit(solution)/shard_map/next_qkv/pallas_call | solution.py:77
  131.0 12.9 %attend.3 = (bf16[512,768]{1,0:T(8,128)(2,1)S(1)}, f32[6,8,512]{2,1,0:T(8,128)S(1)}) custom-call(bf16[512,768]{1,0:T(8,128)(2,1)S(1)} %get-tuple-element.351.q_ref, bf16[512,768]{1,0:T(8,128)(2,1)S(1)} %get-tuple-element.306.ko_ref, bf16[512,768]{1,0:T(8,128)(2,1)S(1)} %collective-permute-done.35.kt_ref, bf16[512,768]{1,0:T(8,128)(2,1)S(1)} %get-tuple-element.312.vo_ref, ...), custom_call_target="tpu_custom_call" | custom-call | tf_op jit(solution)/shard_map/attend/pallas_call | solution.py:77
  150.5 10.6 %feed_up.3 = (f32[512,768]{1,0:T(8,128)S(1)}, bf16[512,3072]{1,0:T(8,128)(2,1)S(1)}, bf16[512,3072]{1,0:T(8,128)(2,1)S(1)}) custom-call(s32[4]{0:T(128)S(1)} %pad_add_fusion.place_ref.refs_0_, f32[512,768]{1,0:T(8,128)S(1)} %feed_down.2.stream_ref, bf16[512,768]{1,0:T(8,128)(2,1)S(1)} %copy-done.9, f32[2,8,768]{2,1,0:T(8,128)S(1)} %reshape.153.vectors_ref, ...), custom_call_target="tpu_custom_call" | custom-call | tf_op jit(solution)/shard_map/feed_up/pallas_call | solution.py:77
  162.2 6.0 %down_weight_grad.2 = (bf16[2,2,2,4,48,768]{5,4,3,2,1,0:T(8,128)(2,1)}, bf16[2,4,48,768]{3,2,1,0:T(8,128)(2,1)}, bf16[2,4,48,768]{3,2,1,0:T(8,128)(2,1)}, bf16[2...) custom-call(s32[4]{0:T(128)S(1)} %pad_add_fusion.place_ref.refs_0_, ...), custom_call_target="tpu_custom_call" | custom-call | tf_op jit(solution)/shard_map/down_weight_grad/pallas_call | solution.py:77
  171.4 5.8 %feed_down.3 = (bf16[256,768]{1,0:T(8,128)(2,1)S(1)}, bf16[256,768]{1,0:T(8,128)(2,1)S(1)}) custom-call(s32[4]{0:T(128)S(1)} %pad_add_fusion.place_ref.refs_0_, f32[512,768]{1,0:T(8,128)S(1)} %get-tuple-element.317.attended_ref, bf16[512,3072]{1,0:T(8,128)(2,1)S(1)} %get-tuple-element.318.activated_ref, f32[2,8,768]{2,1,0:T(8,128)S(1)} %reshape.153.vectors_ref, ...), custom_call_target="tpu_custom_call" | custom-call | tf_op jit(solution)/shard_map/feed_down/pallas_call | solution.py:77
  181.5 11.7 %feed_back.2 = (bf16[512,3072]{1,0:T(8,128)(2,1)S(1)}, f32[512,768]{1,0:T(8,128)S(1)}, bf16[512,768]{1,0:T(8,128)(2,1)S(1)}, f32[8,768]{1,0:T(8,128)S(1)}, f32[1,3072]{1,0:T(1,128)S(1)}) custom-call(s32[4]{0:T(128)S(1)} %pad_add_fusion.place_ref.refs_0_, f32[512,768]{1,0:T(8,128)S(1)} %maximum_convert_fusion.grad_ref, ...), custom_call_target="tpu_custom_call" | custom-call | tf_op jit(solution)/shard_map/feed_back/pallas_call | solution.py:77
  193.3 7.0 %feed_weight_grads.2 = (bf16[2,2,2,5,48,768]{5,4,3,2,1,0:T(8,128)(2,1)}, bf16[2,5,48,768]{3,2,1,0:T(8,128)(2,1)}, bf16[2,5,48,768]{3,2,1,0:T(8,128)(2,1)}, bf16[...) custom-call(s32[4]{0:T(128)S(1)} %pad_add_fusion.place_ref.refs_0_, ...), custom_call_target="tpu_custom_call" | custom-call | tf_op jit(solution)/shard_map/feed_weight_grads/pallas_call | solution.py:77
  210.1 3.4 combine.13
  215.2 22.1 %attend_back.2 = (bf16[512,768]{1,0:T(8,128)(2,1)S(1)}, bf16[512,768]{1,0:T(8,128)(2,1)S(1)}, bf16[512,768]{1,0:T(8,128)(2,1)S(1)}, bf16[512,768]{1,0:T(8,128)(2,1)S(1)}, bf16[512,768]{1,0:T(8,128)(2,1)S(1)}) custom-call(bf16[512,768]{1,0:T(8,128)(2,1)S(1)} %copy-done.23, bf16[512,768]{1,0:T(8,128)(2,1)S(1)} %copy-done.25, bf16[512,768]{1,0:T(8,128)(2,1)S(1)} %copy-done.29, ...), custom_call_target="tpu_custom_call" | custom-call | tf_op jit(solution)/shard_map/attend_back/pallas_call | solution.py:77
  241.9 5.9 %qkv_weight_grads.2 = (f32[8,768]{1,0:T(8,128)S(1)}, bf16[2,512,768]{2,1,0:T(8,128)(2,1)S(1)}, bf16[2,2,2,3,48,768]{5,4,3,2,1,0:T(8,128)(2,1)}, bf16[2,3,48,768]...) custom-call(s32[4]{0:T(128)S(1)} %pad_add_fusion.place_ref.refs_0_, ...), custom_call_target="tpu_custom_call" | custom-call | tf_op jit(solution)/shard_map/qkv_weight_grads/pallas_call | solution.py:77
  250.4 5.4 %norm_back.2 = (f32[512,768]{1,0:T(8,128)S(1)}, f32[8,768]{1,0:T(8,128)S(1)}) custom-call(s32[4]{0:T(128)S(1)} %pad_add_fusion.place_ref.refs_0_, f32[512,768]{1,0:T(8,128)S(1)} %feed_down.2.stream_ref, f32[2,8,768]{2,1,0:T(8,128)S(1)} %reshape.153.vectors_ref, f32[512,768]{1,0:T(8,128)S(1)} %get-tuple-element.339.attended_grad_ref, ...), custom_call_target="tpu_custom_call" | custom-call | tf_op jit(solution)/shard_map/norm_back/pallas_call | solution.py:77
  256.9 4.4 combine.15
  263.8 3.6 collective-permute-start.63
  267.4 6.0 %down_weight_grad.3 = (bf16[2,2,2,4,48,768]{5,4,3,2,1,0:T(8,128)(2,1)}, bf16[2,4,48,768]{3,2,1,0:T(8,128)(2,1)}, bf16[2,4,48,768]{3,2,1,0:T(8,128)(2,1)}, bf16[2...) custom-call(s32[4]{0:T(128)S(1)} %pad_add_fusion.place_ref.refs_0_, bf16[512,3072]{1,0:T(8,128)(2,1)S(1)} %copy-done.3, ...), custom_call_target="tpu_custom_call" | custom-call | tf_op jit(solution)/shard_map/down_weight_grad/pallas_call | solution.py:77
  273.5 11.9 %feed_back.3 = (bf16[512,3072]{1,0:T(8,128)(2,1)S(1)}, f32[512,768]{1,0:T(8,128)S(1)}, bf16[512,768]{1,0:T(8,128)(2,1)S(1)}, f32[8,768]{1,0:T(8,128)S(1)}, f32[1,3072]{1,0:T(1,128)S(1)}) custom-call(s32[4]{0:T(128)S(1)} %pad_add_fusion.place_ref.refs_0_, f32[512,768]{1,0:T(8,128)S(1)} %get-tuple-element.366.grad_ref, bf16[512,3072]{1,0:T(8,128)(2,1)S(1)} %copy-done.7, ...), custom_call_target="tpu_custom_call" | custom-call | tf_op jit(solution)/shard_map/feed_back/pallas_call | solution.py:77
  290.9 4.7 combine.16
  300.5 7.1 %feed_weight_grads.3 = (bf16[2,2,2,5,48,768]{5,4,3,2,1,0:T(8,128)(2,1)}, bf16[2,5,48,768]{3,2,1,0:T(8,128)(2,1)}, bf16[2,5,48,768]{3,2,1,0:T(8,128)(2,1)}, bf16[...) custom-call(s32[4]{0:T(128)S(1)} %pad_add_fusion.place_ref.refs_0_, ...), custom_call_target="tpu_custom_call" | custom-call | tf_op jit(solution)/shard_map/feed_weight_grads/pallas_call | solution.py:77
  307.7 22.8 %attend_back.3 = (bf16[512,768]{1,0:T(8,128)(2,1)S(1)}, bf16[512,768]{1,0:T(8,128)(2,1)S(1)}, bf16[512,768]{1,0:T(8,128)(2,1)S(1)}, bf16[512,768]{1,0:T(8,128)(2,1)S(1)}, bf16[512,768]{1,0:T(8,128)(2,1)}) custom-call(bf16[512,768]{1,0:T(8,128)(2,1)S(1)} %copy-done.13, bf16[512,768]{1,0:T(8,128)(2,1)S(1)} %copy-done.15, bf16[512,768]{1,0:T(8,128)(2,1)S(1)} %copy-done.19, ...), custom_call_target="tpu_custom_call" | custom-call | tf_op jit(solution)/shard_map/attend_back/pallas_call | solution.py:77
  338.0 5.4 %combine.17 = (bf16[20,48,768]{2,1,0:T(8,128)(2,1)}, bf16[8,48,768]{2,1,0:T(8,128)(2,1)}, bf16[4,48,768]{2,1,0:T(8,128)(2,1)}, bf16[3,48,768]{2,1,0:T(8,128)(2,1)}, bf16[5,48,768]{2,1,0:T(8,128)(2,1)}) custom-call(bf16[40,48,768]{2,1,0:T(8,128)(2,1)} %bitcast.83, bf16[10,48,768]{2,1,0:T(8,128)(2,1)} %copy-done.94, bf16[10,48,768]{2,1,0:T(8,128)(2,1)} %copy-done.95, ...), custom_call_target="tpu_custom_call" | custom-call | tf_op jit(solution)/shard_map/combine/pallas_call | solution.py:77
  356.8 5.8 %qkv_weight_grads.3 = (f32[8,768]{1,0:T(8,128)S(1)}, bf16[2,512,768]{2,1,0:T(8,128)(2,1)S(1)}, bf16[2,2,2,3,48,768]{5,4,3,2,1,0:T(8,128)(2,1)}, bf16[2,3,48,768]...) custom-call(s32[4]{0:T(128)S(1)} %pad_add_fusion.place_ref.refs_0_, ...), custom_call_target="tpu_custom_call" | custom-call | tf_op jit(solution)/shard_map/qkv_weight_grads/pallas_call | solution.py:77
  362.6 5.4 %norm_back.3 = (f32[512,768]{1,0:T(8,128)S(1)}, f32[8,768]{1,0:T(8,128)S(1)}) custom-call(s32[4]{0:T(128)S(1)} %pad_add_fusion.place_ref.refs_0_, f32[512,768]{1,0:T(8,128)S(1)} %copy-done.1, f32[2,8,768]{2,1,0:T(8,128)S(1)} %reshape.153.vectors_ref, f32[512,768]{1,0:T(8,128)S(1)} %copy-done.5, bf16[512,768]{1,0:T(8,128)(2,1)S(1)} %copy-done.33, ...), custom_call_target="tpu_custom_call" | custom-call | tf_op jit(solution)/shard_map/norm_back/pallas_call | solution.py:77
  374.5 3.7 combine.18
  381.0 3.2 finish.6.refs_5_
  384.3 4.0 collective-permute-done.89.refs_7_
  397.5 8.6 %collective-permute-done.93.refs_9_ = bf16[4,48,768]{2,1,0:T(8,128)(2,1)S(1)} collective-permute-done((bf16[4,48,768]{2,1,0:T(8,128)(2,1)}, bf16[4,48,768]{2,1,0:T(8,128)(2,1)S(1)}, u32[]{:S(2)}, u32[]{:S(2)}) %collective-permute-start.93) | collective-permute-done | bytes 294944 | tf_op jit(solution)/shard_map/ppermute | solution.py:1005
  406.1 5.0 collective-permute-done.92.refs_7_.refs_8_
  411.9 3.3 combine.20
  420.1 9.4 %collective-permute-done.97.refs_4_ = bf16[5,48,768]{2,1,0:T(8,128)(2,1)S(1)} collective-permute-done((bf16[5,48,768]{2,1,0:T(8,128)(2,1)S(1)}, bf16[5,48,768]{2,1,0:T(8,128)(2,1)S(1)}, u32[]{:S(2)}, u32[]{:S(2)}) %collective-permute-start.97) | collective-permute-done | bytes 368672 | tf_op jit(solution)/shard_map/ppermute | solution.py:1005
  430.2 3.5 finish.7
  433.7 6.8 %collective-permute-done.100.refs_10_.refs_2_ = bf16[4,48,768]{2,1,0:T(8,128)(2,1)S(1)} collective-permute-done((bf16[4,48,768]{2,1,0:T(8,128)(2,1)}, bf16[4,48,768]{2,1,0:T(8,128)(2,1)S(1)}, u32[]{:S(2)}, u32[]{:S(2)}) %collective-permute-start.100) | collective-permute-done | bytes 294944 | tf_op jit(solution)/shard_map/ppermute | solution.py:1005
  442.2 3.4 combine.21
  449.3 11.5 %collective-permute-done.101.refs_4_ = bf16[4,48,768]{2,1,0:T(8,128)(2,1)S(1)} collective-permute-done((bf16[4,48,768]{2,1,0:T(8,128)(2,1)}, bf16[4,48,768]{2,1,0:T(8,128)(2,1)S(1)}, u32[]{:S(2)}, u32[]{:S(2)}) %collective-permute-start.101) | collective-permute-done | bytes 294944 | tf_op jit(solution)/shard_map/ppermute | solution.py:1005
  462.3 3.8 combine.22
  473.1 3.2 finish.8
  483.7 3.2 combine.23
  488.8 7.7 %collective-permute-start.106 = (bf16[6,48,768]{2,1,0:T(8,128)(2,1)}, bf16[6,48,768]{2,1,0:T(8,128)(2,1)S(1)}, u32[]{:S(2)}, u32[]{:S(2)}) collective-permute-start(bf16[6,48,768]{2,1,0:T(8,128)(2,1)} %get-tuple-element.475), channel_id=1, source_target_pairs={{0,8},{8,0},{16,24},{24,16},{1,9},{9,1},{17,25},{25,17},{2,10},{10... | collective-permute-start | bytes 1327112 | tf_op jit(solution)/shard_map/ppermute | solution.py:1005
  498.8 3.5 finish.9
  507.8 9.1 %collective-permute-done.108.refs_4_ = bf16[6,48,768]{2,1,0:T(8,128)(2,1)S(1)} collective-permute-done((bf16[6,48,768]{2,1,0:T(8,128)(2,1)}, bf16[6,48,768]{2,1,0:T(8,128)(2,1)S(1)}, u32[]{:S(2)}, u32[]{:S(2)}) %collective-permute-start.108) | collective-permute-done | bytes 442400 | tf_op jit(solution)/shard_map/ppermute | solution.py:1003
  (582 shorter events, 184.9 us)
Async XLA Ops:
  3.5 14.3 %collective-permute-start.10 = (bf16[3,96,768]{2,1,0:T(8,128)(2,1)}, bf16[3,96,768]{2,1,0:T(8,128)(2,1)}, u32[]{:S(2)}, u32[]{:S(2)}) collective-permute-start(bf16[3,96,768]{2,1,0:T(8,128)(2,1)} %get-tuple-element.254), channel_id=1, source_target_pairs={{0,2},{2,0},{1,3},{3,1},{4,6},{6,4},{5,7},{7,5},{8,10},{10,8},{9,1... | collective-permute-start | bytes 1327112 | tf_op jit(solution)/shard_map/ppermute | solution.py:35
  6.6 18.7 %collective-permute-start = (bf16[256,768]{1,0:T(8,128)(2,1)}, bf16[256,768]{1,0:T(8,128)(2,1)S(1)}, u32[]{:S(2)}, u32[]{:S(2)}) collective-permute-start(bf16[256,768]{1,0:T(8,128)(2,1)} %get-tuple-element.262), channel_id=1, source_target_pairs={{0,2},{2,0},{1,3},{3,1},{4,6},{6,4},{5,7},{7,5},{8,10},{10,8},{9,1... | collective-permute-start | bytes 1179656 | tf_op jit(solution)/shard_map/ppermute | solution.py:35
  17.9 14.3 %collective-permute-start.11 = (bf16[3,96,768]{2,1,0:T(8,128)(2,1)}, bf16[3,96,768]{2,1,0:T(8,128)(2,1)}, u32[]{:S(2)}, u32[]{:S(2)}) collective-permute-start(bf16[3,96,768]{2,1,0:T(8,128)(2,1)} %collective-permute-done.10.refs_2_), channel_id=1, source_target_pairs={{0,4},{4,0},{1,5},{5,1},{2,6},{6,2},{3,7},{7,3},{8,12},{12,8},{9,1... | collective-permute-start | bytes 1327112 | tf_op jit(solution)/shard_map/ppermute | solution.py:35
  38.2 22.0 %collective-permute-start.14 = (bf16[6,96,768]{2,1,0:T(8,128)(2,1)}, bf16[6,96,768]{2,1,0:T(8,128)(2,1)}, u32[]{:S(2)}, u32[]{:S(2)}) collective-permute-start(bf16[6,96,768]{2,1,0:T(8,128)(2,1)} %get-tuple-element.281), channel_id=1, source_target_pairs={{0,2},{2,0},{1,3},{3,1},{4,6},{6,4},{5,7},{7,5},{8,10},{10,8},{9,1... | collective-permute-start | bytes 2654216 | tf_op jit(solution)/shard_map/ppermute | solution.py:35
  60.2 22.4 %collective-permute-start.21 = (bf16[6,96,768]{2,1,0:T(8,128)(2,1)}, bf16[6,96,768]{2,1,0:T(8,128)(2,1)}, u32[]{:S(2)}, u32[]{:S(2)}) collective-permute-start(bf16[6,96,768]{2,1,0:T(8,128)(2,1)} %collective-permute-done.14.refs_2_), channel_id=1, source_target_pairs={{0,4},{4,0},{1,5},{5,1},{2,6},{6,2},{3,7},{7,3},{8,12},{12,8},{9,1... | collective-permute-start | bytes 2654216 | tf_op jit(solution)/shard_map/ppermute | solution.py:35
  62.2 20.3 %collective-permute-start.15 = (bf16[3,96,768]{2,1,0:T(8,128)(2,1)S(1)}, bf16[3,96,768]{2,1,0:T(8,128)(2,1)}, u32[]{:S(2)}, u32[]{:S(2)}) collective-permute-start(bf16[3,96,768]{2,1,0:T(8,128)(2,1)S(1)} %copy-done.153), channel_id=1, source_target_pairs={{0,2},{2,0},{1,3},{3,1},{4,6},{6,4},{5,7},{7,5},{8,10},{10,8},{9,1... | collective-permute-start | bytes 1327112 | tf_op jit(solution)/shard_map/ppermute | solution.py:35
  83.1 16.2 %collective-permute-start.19 = (bf16[3,96,768]{2,1,0:T(8,128)(2,1)}, bf16[3,96,768]{2,1,0:T(8,128)(2,1)}, u32[]{:S(2)}, u32[]{:S(2)}) collective-permute-start(bf16[3,96,768]{2,1,0:T(8,128)(2,1)} %get-tuple-element.289), channel_id=1, source_target_pairs={{0,2},{2,0},{1,3},{3,1},{4,6},{6,4},{5,7},{7,5},{8,10},{10,8},{9,1... | collective-permute-start | bytes 1327112 | tf_op jit(solution)/shard_map/ppermute | solution.py:35
  83.4 16.1 %collective-permute-start.25 = (bf16[3,96,768]{2,1,0:T(8,128)(2,1)}, bf16[3,96,768]{2,1,0:T(8,128)(2,1)}, u32[]{:S(2)}, u32[]{:S(2)}) collective-permute-start(bf16[3,96,768]{2,1,0:T(8,128)(2,1)} %collective-permute-done.15.refs_8_), channel_id=1, source_target_pairs={{0,4},{4,0},{1,5},{5,1},{2,6},{6,2},{3,7},{7,3},{8,12},{12,8},{9,1... | collective-permute-start | bytes 1327112 | tf_op jit(solution)/shard_map/ppermute | solution.py:35
  126.1 18.7 %collective-permute-start.32 = (bf16[4,96,768]{2,1,0:T(8,128)(2,1)S(1)}, bf16[4,96,768]{2,1,0:T(8,128)(2,1)}, u32[]{:S(2)}, u32[]{:S(2)}) collective-permute-start(bf16[4,96,768]{2,1,0:T(8,128)(2,1)S(1)} %copy-done.147), channel_id=1, source_target_pairs={{0,2},{2,0},{1,3},{3,1},{4,6},{6,4},{5,7},{7,5},{8,10},{10,8},{9,1... | collective-permute-start | bytes 1769480 | tf_op jit(solution)/shard_map/ppermute | solution.py:35
  130.0 17.4 %collective-permute-start.38 = (bf16[2,96,768]{2,1,0:T(8,128)(2,1)S(1)}, bf16[2,96,768]{2,1,0:T(8,128)(2,1)}, u32[]{:S(2)}, u32[]{:S(2)}) collective-permute-start(bf16[2,96,768]{2,1,0:T(8,128)(2,1)S(1)} %collective-permute-done.27.refs_8_), channel_id=1, source_target_pairs={{0,4},{4,0},{1,5},{5,1},{2,6},{6,2},{3,7},{7,3},{8,12},{12,8},{9,1... | collective-permute-start | bytes 884744 | tf_op jit(solution)/shard_map/ppermute | solution.py:35
  144.9 23.3 %collective-permute-start.40 = (bf16[4,96,768]{2,1,0:T(8,128)(2,1)}, bf16[4,96,768]{2,1,0:T(8,128)(2,1)}, u32[]{:S(2)}, u32[]{:S(2)}) collective-permute-start(bf16[4,96,768]{2,1,0:T(8,128)(2,1)} %collective-permute-done.32.refs_2_.refs_14_), channel_id=1, source_target_pairs={{0,4},{4,0},{1,5},{5,1},{2,6},{6,2},{3,7},{7,3},{8,12},{12,8},{9,1... | collective-permute-start | bytes 1769480 | tf_op jit(solution)/shard_map/ppermute | solution.py:35
  146.1 15.0 %collective-permute-start.41 = (bf16[256,768]{1,0:T(8,128)(2,1)}, bf16[256,768]{1,0:T(8,128)(2,1)}, u32[]{:S(2)}, u32[]{:S(2)}) collective-permute-start(bf16[256,768]{1,0:T(8,128)(2,1)} %get-tuple-element.320), channel_id=1, source_target_pairs={{0,2},{2,0},{1,3},{3,1},{4,6},{6,4},{5,7},{7,5},{8,10},{10,8},{9,1... | collective-permute-start | bytes 1179656 | tf_op jit(solution)/shard_map/ppermute | solution.py:35
  180.8 28.3 %collective-permute-start.51 = (bf16[16,48,768]{2,1,0:T(8,128)(2,1)}, bf16[16,48,768]{2,1,0:T(8,128)(2,1)S(1)}, u32[]{:S(2)}, u32[]{:S(2)}) collective-permute-start(bf16[16,48,768]{2,1,0:T(8,128)(2,1)} %combine.12), channel_id=1, source_target_pairs={{0,2},{2,0},{1,3},{3,1},{4,6},{6,4},{5,7},{7,5},{8,10},{10,8},{9,1... | collective-permute-start | bytes 3538952 | tf_op jit(solution)/shard_map/ppermute | solution.py:35
  213.5 35.8 %collective-permute-start.55 = (bf16[20,48,768]{2,1,0:T(8,128)(2,1)}, bf16[20,48,768]{2,1,0:T(8,128)(2,1)S(1)}, u32[]{:S(2)}, u32[]{:S(2)}) collective-permute-start(bf16[20,48,768]{2,1,0:T(8,128)(2,1)} %get-tuple-element.371), channel_id=1, source_target_pairs={{0,2},{2,0},{1,3},{3,1},{4,6},{6,4},{5,7},{7,5},{8,10},{10,8},{9,1... | collective-permute-start | bytes 4423688 | tf_op jit(solution)/shard_map/ppermute | solution.py:35
  214.2 23.1 %collective-permute-start.52 = (bf16[8,48,768]{2,1,0:T(8,128)(2,1)}, bf16[8,48,768]{2,1,0:T(8,128)(2,1)S(1)}, u32[]{:S(2)}, u32[]{:S(2)}) collective-permute-start(bf16[8,48,768]{2,1,0:T(8,128)(2,1)} %get-tuple-element.350), channel_id=1, source_target_pairs={{0,4},{4,0},{1,5},{5,1},{2,6},{6,2},{3,7},{7,3},{8,12},{12,8},{9,1... | collective-permute-start | bytes 1769480 | tf_op jit(solution)/shard_map/ppermute | solution.py:35
  261.3 24.2 %collective-permute-start.61 = (bf16[12,48,768]{2,1,0:T(8,128)(2,1)}, bf16[12,48,768]{2,1,0:T(8,128)(2,1)S(1)}, u32[]{:S(2)}, u32[]{:S(2)}) collective-permute-start(bf16[12,48,768]{2,1,0:T(8,128)(2,1)} %get-tuple-element.377), channel_id=1, source_target_pairs={{0,2},{2,0},{1,3},{3,1},{4,6},{6,4},{5,7},{7,5},{8,10},{10,8},{9,1... | collective-permute-start | bytes 2654216 | tf_op jit(solution)/shard_map/ppermute | solution.py:35
  263.1 22.4 %collective-permute-start.62 = (bf16[10,48,768]{2,1,0:T(8,128)(2,1)}, bf16[10,48,768]{2,1,0:T(8,128)(2,1)S(1)}, u32[]{:S(2)}, u32[]{:S(2)}) collective-permute-start(bf16[10,48,768]{2,1,0:T(8,128)(2,1)} %get-tuple-element.387), channel_id=1, source_target_pairs={{0,4},{4,0},{1,5},{5,1},{2,6},{6,2},{3,7},{7,3},{8,12},{12,8},{9,1... | collective-permute-start | bytes 2211848 | tf_op jit(solution)/shard_map/ppermute | solution.py:35
  263.8 21.6 %collective-permute-start.63 = (bf16[4,48,768]{2,1,0:T(8,128)(2,1)}, bf16[4,48,768]{2,1,0:T(8,128)(2,1)S(1)}, u32[]{:S(2)}, u32[]{:S(2)}) collective-permute-start(bf16[4,48,768]{2,1,0:T(8,128)(2,1)} %get-tuple-element.388.refs_6_), channel_id=1, source_target_pairs={{0,24},{24,0},{8,16},{16,8},{1,25},{25,1},{9,17},{17,9},{2,26},{26... | collective-permute-start | bytes 884744 | tf_op jit(solution)/shard_map/ppermute | solution.py:1005
  295.6 35.0 %collective-permute-start.68 = (bf16[16,48,768]{2,1,0:T(8,128)(2,1)}, bf16[16,48,768]{2,1,0:T(8,128)(2,1)S(1)}, u32[]{:S(2)}, u32[]{:S(2)}) collective-permute-start(bf16[16,48,768]{2,1,0:T(8,128)(2,1)} %get-tuple-element.394), channel_id=1, source_target_pairs={{0,2},{2,0},{1,3},{3,1},{4,6},{6,4},{5,7},{7,5},{8,10},{10,8},{9,1... | collective-permute-start | bytes 3538952 | tf_op jit(solution)/shard_map/ppermute | solution.py:35
  296.4 34.2 %collective-permute-start.69 = (bf16[6,48,768]{2,1,0:T(8,128)(2,1)}, bf16[6,48,768]{2,1,0:T(8,128)(2,1)S(1)}, u32[]{:S(2)}, u32[]{:S(2)}) collective-permute-start(bf16[6,48,768]{2,1,0:T(8,128)(2,1)} %get-tuple-element.406), channel_id=1, source_target_pairs={{0,4},{4,0},{1,5},{5,1},{2,6},{6,2},{3,7},{7,3},{8,12},{12,8},{9,1... | collective-permute-start | bytes 1327112 | tf_op jit(solution)/shard_map/ppermute | solution.py:35
  297.3 33.3 %collective-permute-start.72 = (bf16[5,48,768]{2,1,0:T(8,128)(2,1)}, bf16[5,48,768]{2,1,0:T(8,128)(2,1)S(1)}, u32[]{:S(2)}, u32[]{:S(2)}) collective-permute-start(bf16[5,48,768]{2,1,0:T(8,128)(2,1)} %get-tuple-element.409), channel_id=1, source_target_pairs={{0,8},{8,0},{16,24},{24,16},{1,9},{9,1},{17,25},{25,17},{2,10},{10... | collective-permute-start | bytes 1105928 | tf_op jit(solution)/shard_map/ppermute | solution.py:1005
  297.3 33.2 %collective-permute-start.70 = (bf16[4,48,768]{2,1,0:T(8,128)(2,1)}, bf16[4,48,768]{2,1,0:T(8,128)(2,1)S(1)}, u32[]{:S(2)}, u32[]{:S(2)}) collective-permute-start(bf16[4,48,768]{2,1,0:T(8,128)(2,1)} %get-tuple-element.407.refs_1_), channel_id=1, source_target_pairs={{0,4},{4,0},{1,5},{5,1},{2,6},{6,2},{3,7},{7,3},{8,12},{12,8},{9,1... | collective-permute-start | bytes 884744 | tf_op jit(solution)/shard_map/ppermute | solution.py:35
  298.6 31.9 %collective-permute-start.71 = (bf16[4,48,768]{2,1,0:T(8,128)(2,1)}, bf16[4,48,768]{2,1,0:T(8,128)(2,1)S(1)}, u32[]{:S(2)}, u32[]{:S(2)}) collective-permute-start(bf16[4,48,768]{2,1,0:T(8,128)(2,1)} %get-tuple-element.408), channel_id=1, source_target_pairs={{0,8},{8,0},{16,24},{24,16},{1,9},{9,1},{17,25},{25,17},{2,10},{10... | collective-permute-start | bytes 884744 | tf_op jit(solution)/shard_map/ppermute | solution.py:1005
  331.7 15.5 %collective-permute-start.77 = (bf16[512,768]{1,0:T(8,128)(2,1)S(1)}, bf16[512,768]{1,0:T(8,128)(2,1)S(1)}, u32[]{:S(2)}, u32[]{:S(2)}) collective-permute-start(bf16[512,768]{1,0:T(8,128)(2,1)S(1)} %get-tuple-element.421), channel_id=1, source_target_pairs={{0,1},{1,0},{2,3},{3,2},{4,5},{5,4},{6,7},{7,6},{8,9},{9,8},{10,11... | collective-permute-start | bytes 2359304 | tf_op jit(solution)/shard_map/ppermute | solution.py:35
  333.2 15.0 %collective-permute-start.78 = (bf16[512,768]{1,0:T(8,128)(2,1)}, bf16[512,768]{1,0:T(8,128)(2,1)S(1)}, u32[]{:S(2)}, u32[]{:S(2)}) collective-permute-start(bf16[512,768]{1,0:T(8,128)(2,1)} %get-tuple-element.422), channel_id=1, source_target_pairs={{0,1},{1,0},{2,3},{3,2},{4,5},{5,4},{6,7},{7,6},{8,9},{9,8},{10,11... | collective-permute-start | bytes 2359304 | tf_op jit(solution)/shard_map/ppermute | solution.py:35
  343.5 25.7 %collective-permute-start.79 = (bf16[8,48,768]{2,1,0:T(8,128)(2,1)}, bf16[8,48,768]{2,1,0:T(8,128)(2,1)}, u32[]{:S(2)}, u32[]{:S(2)}) collective-permute-start(bf16[8,48,768]{2,1,0:T(8,128)(2,1)} %get-tuple-element.431), channel_id=1, source_target_pairs={{0,4},{4,0},{1,5},{5,1},{2,6},{6,2},{3,7},{7,3},{8,12},{12,8},{9,1... | collective-permute-start | bytes 1769480 | tf_op jit(solution)/shard_map/ppermute | solution.py:35
  344.5 44.7 %collective-permute-start.88 = (bf16[20,48,768]{2,1,0:T(8,128)(2,1)}, bf16[20,48,768]{2,1,0:T(8,128)(2,1)}, u32[]{:S(2)}, u32[]{:S(2)}) collective-permute-start(bf16[20,48,768]{2,1,0:T(8,128)(2,1)} %get-tuple-element.415), channel_id=1, source_target_pairs={{0,2},{2,0},{1,3},{3,1},{4,6},{6,4},{5,7},{7,5},{8,10},{10,8},{9,1... | collective-permute-start | bytes 4423688 | tf_op jit(solution)/shard_map/ppermute | solution.py:35
  346.2 23.0 %collective-permute-start.82 = (bf16[5,48,768]{2,1,0:T(8,128)(2,1)}, bf16[5,48,768]{2,1,0:T(8,128)(2,1)}, u32[]{:S(2)}, u32[]{:S(2)}) collective-permute-start(bf16[5,48,768]{2,1,0:T(8,128)(2,1)} %get-tuple-element.434.refs_9_), channel_id=1, source_target_pairs={{0,24},{24,0},{8,16},{16,8},{1,25},{25,1},{9,17},{17,9},{2,26},{26... | collective-permute-start | bytes 1105928 | tf_op jit(solution)/shard_map/ppermute | solution.py:1005
  348.1 21.1 %collective-permute-start.80 = (bf16[4,48,768]{2,1,0:T(8,128)(2,1)}, bf16[4,48,768]{2,1,0:T(8,128)(2,1)}, u32[]{:S(2)}, u32[]{:S(2)}) collective-permute-start(bf16[4,48,768]{2,1,0:T(8,128)(2,1)} %get-tuple-element.432), channel_id=1, source_target_pairs={{0,8},{8,0},{16,24},{24,16},{1,9},{9,1},{17,25},{25,17},{2,10},{10... | collective-permute-start | bytes 884744 | tf_op jit(solution)/shard_map/ppermute | solution.py:1005
  349.0 20.1 %collective-permute-start.81 = (bf16[3,48,768]{2,1,0:T(8,128)(2,1)}, bf16[3,48,768]{2,1,0:T(8,128)(2,1)S(1)}, u32[]{:S(2)}, u32[]{:S(2)}) collective-permute-start(bf16[3,48,768]{2,1,0:T(8,128)(2,1)} %get-tuple-element.433), channel_id=1, source_target_pairs={{0,8},{8,0},{16,24},{24,16},{1,9},{9,1},{17,25},{25,17},{2,10},{10... | collective-permute-start | bytes 663560 | tf_op jit(solution)/shard_map/ppermute | solution.py:1005
  379.3 26.8 %collective-permute-start.91 = (bf16[13,48,768]{2,1,0:T(8,128)(2,1)}, bf16[13,48,768]{2,1,0:T(8,128)(2,1)S(1)}, u32[]{:S(2)}, u32[]{:S(2)}) collective-permute-start(bf16[13,48,768]{2,1,0:T(8,128)(2,1)} %get-tuple-element.448.refs_3_), channel_id=1, source_target_pairs={{0,2},{2,0},{1,3},{3,1},{4,6},{6,4},{5,7},{7,5},{8,10},{10,8},{9,1... | collective-permute-start | bytes 2875400 | tf_op jit(solution)/shard_map/ppermute | solution.py:35
  393.1 18.0 %collective-permute-start.92 = (bf16[10,48,768]{2,1,0:T(8,128)(2,1)}, bf16[10,48,768]{2,1,0:T(8,128)(2,1)S(1)}, u32[]{:S(2)}, u32[]{:S(2)}) collective-permute-start(bf16[10,48,768]{2,1,0:T(8,128)(2,1)} %get-tuple-element.453), channel_id=1, source_target_pairs={{0,4},{4,0},{1,5},{5,1},{2,6},{6,2},{3,7},{7,3},{8,12},{12,8},{9,1... | collective-permute-start | bytes 2211848 | tf_op jit(solution)/shard_map/ppermute | solution.py:35
  396.7 21.3 %collective-permute-start.96 = (bf16[5,48,768]{2,1,0:T(8,128)(2,1)S(1)}, bf16[5,48,768]{2,1,0:T(8,128)(2,1)S(1)}, u32[]{:S(2)}, u32[]{:S(2)}) collective-permute-start(bf16[5,48,768]{2,1,0:T(8,128)(2,1)S(1)} %copy-done.154), channel_id=1, source_target_pairs={{0,8},{8,0},{16,24},{24,16},{1,9},{9,1},{17,25},{25,17},{2,10},{10... | collective-permute-start | bytes 1105928 | tf_op jit(solution)/shard_map/ppermute | solution.py:1005
  396.8 23.2 %collective-permute-start.95 = (bf16[256,768]{1,0:T(8,128)(2,1)S(1)}, bf16[256,768]{1,0:T(8,128)(2,1)S(1)}, u32[]{:S(2)}, u32[]{:S(2)}) collective-permute-start(bf16[256,768]{1,0:T(8,128)(2,1)S(1)} %slice.83), channel_id=1, source_target_pairs={{0,2},{2,0},{1,3},{3,1},{4,6},{6,4},{5,7},{7,5},{8,10},{10,8},{9,1... | collective-permute-start | bytes 1179656 | tf_op jit(solution)/shard_map/ppermute | solution.py:35
  415.2 25.3 %collective-permute-start.98 = (bf16[7,48,768]{2,1,0:T(8,128)(2,1)}, bf16[7,48,768]{2,1,0:T(8,128)(2,1)S(1)}, u32[]{:S(2)}, u32[]{:S(2)}) collective-permute-start(bf16[7,48,768]{2,1,0:T(8,128)(2,1)} %get-tuple-element.456.refs_4_), channel_id=1, source_target_pairs={{0,4},{4,0},{1,5},{5,1},{2,6},{6,2},{3,7},{7,3},{8,12},{12,8},{9,1... | collective-permute-start | bytes 1548296 | tf_op jit(solution)/shard_map/ppermute | solution.py:35
  416.2 17.5 %collective-permute-start.94 = (bf16[256,768]{1,0:T(8,128)(2,1)S(1)}, bf16[256,768]{1,0:T(8,128)(2,1)S(1)}, u32[]{:S(2)}, u32[]{:S(2)}) collective-permute-start(bf16[256,768]{1,0:T(8,128)(2,1)S(1)} %copy-done.52), channel_id=1, source_target_pairs={{0,2},{2,0},{1,3},{3,1},{4,6},{6,4},{5,7},{7,5},{8,10},{10,8},{9,1... | collective-permute-start | bytes 1179656 | tf_op jit(solution)/shard_map/ppermute | solution.py:35
  418.0 22.5 %collective-permute-start.99 = (bf16[5,48,768]{2,1,0:T(8,128)(2,1)}, bf16[5,48,768]{2,1,0:T(8,128)(2,1)S(1)}, u32[]{:S(2)}, u32[]{:S(2)}) collective-permute-start(bf16[5,48,768]{2,1,0:T(8,128)(2,1)} %get-tuple-element.464), channel_id=1, source_target_pairs={{0,8},{8,0},{16,24},{24,16},{1,9},{9,1},{17,25},{25,17},{2,10},{10... | collective-permute-start | bytes 1105928 | tf_op jit(solution)/shard_map/ppermute | solution.py:1005
  420.0 20.5 %collective-permute-start.100 = (bf16[4,48,768]{2,1,0:T(8,128)(2,1)}, bf16[4,48,768]{2,1,0:T(8,128)(2,1)S(1)}, u32[]{:S(2)}, u32[]{:S(2)}) collective-permute-start(bf16[4,48,768]{2,1,0:T(8,128)(2,1)} %get-tuple-element.465), channel_id=1, source_target_pairs={{0,8},{8,0},{16,24},{24,16},{1,9},{9,1},{17,25},{25,17},{2,10},{10... | collective-permute-start | bytes 884744 | tf_op jit(solution)/shard_map/ppermute | solution.py:1005
  445.6 15.3 %collective-permute-start.102 = (bf16[5,48,768]{2,1,0:T(8,128)(2,1)}, bf16[5,48,768]{2,1,0:T(8,128)(2,1)S(1)}, u32[]{:S(2)}, u32[]{:S(2)}) collective-permute-start(bf16[5,48,768]{2,1,0:T(8,128)(2,1)} %get-tuple-element.468.refs_11_), channel_id=1, source_target_pairs={{0,24},{24,0},{8,16},{16,8},{1,25},{25,1},{9,17},{17,9},{2,26},{26... | collective-permute-start | bytes 1105928 | tf_op jit(solution)/shard_map/ppermute | solution.py:1005
  447.2 24.4 %collective-permute-start.104 = (bf16[4,48,768]{2,1,0:T(8,128)(2,1)S(1)}, bf16[4,48,768]{2,1,0:T(8,128)(2,1)S(1)}, u32[]{:S(2)}, u32[]{:S(2)}) collective-permute-start(bf16[4,48,768]{2,1,0:T(8,128)(2,1)S(1)} %copy-done.123), channel_id=1, source_target_pairs={{0,4},{4,0},{1,5},{5,1},{2,6},{6,2},{3,7},{7,3},{8,12},{12,8},{9,1... | collective-permute-start | bytes 884744 | tf_op jit(solution)/shard_map/ppermute | solution.py:35
  448.3 23.4 %collective-permute-start.105 = (bf16[4,48,768]{2,1,0:T(8,128)(2,1)S(1)}, bf16[4,48,768]{2,1,0:T(8,128)(2,1)S(1)}, u32[]{:S(2)}, u32[]{:S(2)}) collective-permute-start(bf16[4,48,768]{2,1,0:T(8,128)(2,1)S(1)} %copy-done.158), channel_id=1, source_target_pairs={{0,4},{4,0},{1,5},{5,1},{2,6},{6,2},{3,7},{7,3},{8,12},{12,8},{9,1... | collective-permute-start | bytes 884744 | tf_op jit(solution)/shard_map/ppermute | solution.py:35
  466.1 16.8 %collective-permute-start.103 = (bf16[7,48,768]{2,1,0:T(8,128)(2,1)}, bf16[7,48,768]{2,1,0:T(8,128)(2,1)S(1)}, u32[]{:S(2)}, u32[]{:S(2)}) collective-permute-start(bf16[7,48,768]{2,1,0:T(8,128)(2,1)} %get-tuple-element.473.refs_0_), channel_id=1, source_target_pairs={{0,24},{24,0},{8,16},{16,8},{1,25},{25,1},{9,17},{17,9},{2,26},{26... | collective-permute-start | bytes 1548296 | tf_op jit(solution)/shard_map/ppermute | solution.py:1005
  476.3 20.2 %collective-permute-start.109 = (bf16[5,48,768]{2,1,0:T(8,128)(2,1)S(1)}, bf16[5,48,768]{2,1,0:T(8,128)(2,1)S(1)}, u32[]{:S(2)}, u32[]{:S(2)}) collective-permute-start(bf16[5,48,768]{2,1,0:T(8,128)(2,1)S(1)} %copy-done.155), channel_id=1, source_target_pairs={{0,8},{8,0},{16,24},{24,16},{1,9},{9,1},{17,25},{25,17},{2,10},{10... | collective-permute-start | bytes 1105928 | tf_op jit(solution)/shard_map/ppermute | solution.py:1005
  476.4 20.3 %collective-permute-start.110 = (bf16[5,48,768]{2,1,0:T(8,128)(2,1)S(1)}, bf16[5,48,768]{2,1,0:T(8,128)(2,1)S(1)}, u32[]{:S(2)}, u32[]{:S(2)}) collective-permute-start(bf16[5,48,768]{2,1,0:T(8,128)(2,1)S(1)} %copy-done.117), channel_id=1, source_target_pairs={{0,4},{4,0},{1,5},{5,1},{2,6},{6,2},{3,7},{7,3},{8,12},{12,8},{9,1... | collective-permute-start | bytes 1105928 | tf_op jit(solution)/shard_map/ppermute | solution.py:35
  477.3 20.8 %collective-permute-start.111 = (bf16[5,48,768]{2,1,0:T(8,128)(2,1)}, bf16[5,48,768]{2,1,0:T(8,128)(2,1)S(1)}, u32[]{:S(2)}, u32[]{:S(2)}) collective-permute-start(bf16[5,48,768]{2,1,0:T(8,128)(2,1)} %get-tuple-element.480), channel_id=1, source_target_pairs={{0,12},{4,8},{8,4},{12,0},{16,28},{20,24},{24,20},{28,16},{1,13},{... | collective-permute-start | bytes 1105928 | tf_op jit(solution)/shard_map/ppermute | solution.py:1003
  486.8 21.0 %collective-permute-start.107 = (bf16[6,48,768]{2,1,0:T(8,128)(2,1)}, bf16[6,48,768]{2,1,0:T(8,128)(2,1)S(1)}, u32[]{:S(2)}, u32[]{:S(2)}) collective-permute-start(bf16[6,48,768]{2,1,0:T(8,128)(2,1)} %get-tuple-element.474.refs_1_), channel_id=1, source_target_pairs={{0,4},{4,0},{1,5},{5,1},{2,6},{6,2},{3,7},{7,3},{8,12},{12,8},{9,1... | collective-permute-start | bytes 1327112 | tf_op jit(solution)/shard_map/ppermute | solution.py:35
  488.8 18.9 %collective-permute-start.106 = (bf16[6,48,768]{2,1,0:T(8,128)(2,1)}, bf16[6,48,768]{2,1,0:T(8,128)(2,1)S(1)}, u32[]{:S(2)}, u32[]{:S(2)}) collective-permute-start(bf16[6,48,768]{2,1,0:T(8,128)(2,1)} %get-tuple-element.475), channel_id=1, source_target_pairs={{0,8},{8,0},{16,24},{24,16},{1,9},{9,1},{17,25},{25,17},{2,10},{10... | collective-permute-start | bytes 1327112 | tf_op jit(solution)/shard_map/ppermute | solution.py:1005
  496.5 20.4 %collective-permute-start.108 = (bf16[6,48,768]{2,1,0:T(8,128)(2,1)}, bf16[6,48,768]{2,1,0:T(8,128)(2,1)S(1)}, u32[]{:S(2)}, u32[]{:S(2)}) collective-permute-start(bf16[6,48,768]{2,1,0:T(8,128)(2,1)} %get-tuple-element.476), channel_id=1, source_target_pairs={{0,12},{4,8},{8,4},{12,0},{16,28},{20,24},{24,20},{28,16},{1,13},{... | collective-permute-start | bytes 1327112 | tf_op jit(solution)/shard_map/ppermute | solution.py:1003
  (223 other events, 1696.3 us)

commit v5 on v4

--- a/solution.py
+++ b/solution.py
@@ -1187,7 +1187,7 @@
     gradient, norm_sums1 = norm_back(
         1, place, stream1, vectors, attended_grad, dq, dkv, qkv1, deps=(parts[0],)
     )
-    qkv_1 = Flow(split, parts, far, *landed, last=None)
+    qkv_1 = Flow(split, parts, far, *landed, last="near")
     pin, landed = exchange([(qkv_1, "x"), (feed1, "y"), (down1, "mirror")], gradient, *qkv_1.back)
 
     parts = down_weight_grad(place, split, activated0, gradient, deps=(pin,))
@@ -1230,24 +1230,26 @@
     steps = [(qkv_0, "x"), (totals, "x"), (down0, "pair"), (feed1, "after")]
     pin, landed = exchange(steps, gradient, *qkv_0.back)
     down_out = down1.finish(1, down_places, down_shapes, place, deps=(pin,))
-    pin, landed = exchange([(feed0, "y"), (down0, "mirror"), (feed1, "last")], down_out[0])
+    pin, landed = exchange([(feed0, "y"), (down0, "mirror"), (qkv_1, "mirror"), (feed1, "last")], down_out[0])
     input_other = swap(after(gradient[quarter:].astype(BF16), pin), "x")
-    steps = [(qkv_0, "y"), (totals, "y"), (feed0, "pair"), (down0, "after")]
+    steps = [(qkv_0, "y"), (totals, "y"), (feed0, "pair"), (down0, "after"), (qkv_1, "after")]
     pin, landed = exchange(steps, pin)
     output_other = swap(after(output_other, pin), "x")
     feed_out = feed1.finish(1, feed_places, feed_shapes, place, deps=(pin, input_other))
     input_grad = by_clip(gradient[:quarter], input_other.astype(F32))
-    steps = [(qkv_0, "pair"), (totals, "pair"), (feed0, "mirror"), (down0, "last")]
+    steps = [(qkv_0, "pair"), (totals, "pair"), (feed0, "mirror"), (down0, "last"), (qkv_1, "last")]
     pin, landed = exchange(steps, feed_out[0], output_other)
     output = by_clip(output_mine, output_other)
-    steps = [(qkv_0, "mirror"), (totals, "mirror"), (feed0, "after"), (qkv_1, "mirror")]
+    steps = [(qkv_0, "mirror"), (totals, "mirror"), (feed0, "after")]
     pin, landed = exchange(steps, pin)
     (down_out,) = down0.finish(0, down_places, down_shapes, place, down_out, deps=(pin,))
-    pin, landed = exchange([(qkv_0, "after"), (qkv_1, "after")], down_out)
+    qkv_out = qkv_1.finish(1, qkv_places, qkv_shapes, place, deps=(down_out,))
+    pin, landed = exchange([(qkv_0, "after")], qkv_out[0])
     totals = totals.done()[: LAYERS * (8 + SHARDS)].reshape(LAYERS, 8 + SHARDS, width)
     out_out, up_out = feed0.finish(0, feed_places, feed_shapes, place, feed_out, deps=(pin,))
-    qkv_out = qkv_1.finish(1, qkv_places, qkv_shapes, place, deps=(out_out,))
-    query_out, key_out, value_out = qkv_0.finish(0, qkv_places, qkv_shapes, place, qkv_out)
+    query_out, key_out, value_out = qkv_0.finish(
+        0, qkv_places, qkv_shapes, place, qkv_out, deps=(out_out,)
+    )
 
     own_vectors = lax.dynamic_slice_in_dim(totals[:, :8], shard * share, share, axis=2)
     own_up = lax.dynamic_slice_in_dim(

time: 530 us -> 523 us (0.987)
  waiting for transfers between devices: 133 us -> 126 us
    unnamed x324 -> x322, local copies, waits for them, and re-layouts: 38.7 us -> 38.6 us
  transfers between devices with their start and end apart: 112 -> 112, of which waited for: 53 -> 53; matrix products, arithmetic and copies ran while one was open for 2% -> 2% of each run, Pallas kernels for 44% -> 45%
where the time goes in v5:
time: 523 us; the launch traced here: 517 us
  Pallas kernels  257 us (49%)
  waiting for transfers between devices  126 us (24%)
  starting transfers between devices  85.9 us (16%)
  local copies, waits for them, and re-layouts  41.8 us (8%)
    pallas_call x40, Pallas kernels, call(): pl.pallas_call(kernel, in_specs=list(in_specs), out_shape=out_shape, out_...  257 us
    ppermute x92, waiting for transfers between devices, swap(): return lax.ppermute(values, axis, SWAP)  76.8 us
    ppermute x92, starting transfers between devices, swap(): return lax.ppermute(values, axis, SWAP)  52.6 us
    ppermute x18, waiting for transfers between devices, exchange(): arrived = lax.ppermute(sent, 'z', MIRROR if name == 'mirror' else PAIRS)  43.4 us
    unnamed x322, local copies, waits for them, and re-layouts  38.6 us
    ppermute x18, starting transfers between devices, exchange(): arrived = lax.ppermute(sent, 'z', MIRROR if name == 'mirror' else PAIRS)  28.3 us
  transfers between devices with their start and end apart: 112, of which 53 were waited for; matrix products, arithmetic and copies ran while one was open for 2% of the time, Pallas kernels for 45%

profile of v5, /device:TPU:0, one launch (start us, length us, event | category | flops | bytes accessed | tf_op | source)
XLA Modules:
  0.0 517.4 jit_solution(6153047114156066008)
XLA Ops:
  6.7 7.2 %pack_shares.3 = (bf16[6,192,768]{2,1,0:T(8,128)(2,1)}, bf16[6,96,768]{2,1,0:T(8,128)(2,1)}, bf16[3,192,768]{2,1,0:T(8,128)(2,1)}, bf16[3,96,768]{2,1,0:T(8,128)...) custom-call(s32[4]{0:T(128)S(1)} %pad_add_fusion.place_ref.refs_0_, ...), custom_call_target="tpu_custom_call" | custom-call | tf_op jit(solution)/shard_map/pack_shares/pallas_call | solution.py:77
  13.9 3.9 collective-permute-done.10.refs_2_
  19.9 5.4 %collective-permute-done.arrived_ref = bf16[256,768]{1,0:T(8,128)(2,1)S(1)} collective-permute-done((bf16[256,768]{1,0:T(8,128)(2,1)}, bf16[256,768]{1,0:T(8,128)(2,1)S(1)}, u32[]{:S(2)}, u32[]{:S(2)}) %collective-permute-start) | collective-permute-done | bytes 393248 | tf_op jit(solution)/shard_map/ppermute | solution.py:35
  32.7 3.8 collective-permute-done.2.refs_7_
  43.2 4.9 first_qkv.1
  48.2 12.0 %collective-permute-done.14.refs_2_ = bf16[6,96,768]{2,1,0:T(8,128)(2,1)} collective-permute-done((bf16[6,96,768]{2,1,0:T(8,128)(2,1)}, bf16[6,96,768]{2,1,0:T(8,128)(2,1)}, u32[]{:S(2)}, u32[]{:S(2)}) %collective-permute-start.14) | collective-permute-done | bytes 884768 | tf_op jit(solution)/shard_map/ppermute | solution.py:35
  65.1 13.0 %attend.2 = (bf16[512,768]{1,0:T(8,128)(2,1)S(1)}, f32[6,8,512]{2,1,0:T(8,128)S(1)}) custom-call(bf16[512,768]{1,0:T(8,128)(2,1)S(1)} %get-tuple-element.400.q_ref, bf16[512,768]{1,0:T(8,128)(2,1)S(1)} %get-tuple-element.283.ko_ref, bf16[512,768]{1,0:T(8,128)(2,1)S(1)} %collective-permute-done.17.kt_ref, bf16[512,768]{1,0:T(8,128)(2,1)S(1)} %get-tuple-element.288.vo_ref, ...), custom_call_target="tpu_custom_call" | custom-call | tf_op jit(solution)/shard_map/attend/pallas_call | solution.py:77
  88.7 10.6 %feed_up.2 = (f32[512,768]{1,0:T(8,128)S(1)}, bf16[512,3072]{1,0:T(8,128)(2,1)S(1)}, bf16[512,3072]{1,0:T(8,128)(2,1)S(1)}) custom-call(s32[4]{0:T(128)S(1)} %pad_add_fusion.place_ref.refs_0_, f32[512,768]{1,0:T(8,128)S(1)} %get-tuple-element.293.stream_ref, bf16[512,768]{1,0:T(8,128)(2,1)S(1)} %copy-done.35, f32[2,8,768]{2,1,0:T(8,128)S(1)} %reshape.153.vectors_ref, ...), custom_call_target="tpu_custom_call" | custom-call | tf_op jit(solution)/shard_map/feed_up/pallas_call | solution.py:77
  102.8 5.6 %feed_down.2.stream_ref = f32[512,768]{1,0:T(8,128)S(1)} custom-call(s32[4]{0:T(128)S(1)} %pad_add_fusion.place_ref.refs_0_, f32[512,768]{1,0:T(8,128)S(1)} %get-tuple-element.299.attended_ref, bf16[512,3072]{1,0:T(8,128)(2,1)S(1)} %get-tuple-element.295.activated_ref, f32[2,8,768]{2,1,0:T(8,128)S(1)} %reshape.153.vectors_ref, ...), custom_call_target="tpu_custom_call" | custom-call | tf_op jit(solution)/shard_map/feed_down/pallas_call | solution.py:77
  108.4 3.7 collective-permute-done.23.refs_2_
  116.4 5.3 %next_qkv.1 = (bf16[512,768]{1,0:T(8,128)(2,1)S(1)}, bf16[512,768]{1,0:T(8,128)(2,1)S(1)}, bf16[512,768]{1,0:T(8,128)(2,1)S(1)}) custom-call(s32[4]{0:T(128)S(1)} %pad_add_fusion.place_ref.refs_0_, f32[512,768]{1,0:T(8,128)S(1)} %feed_down.2.stream_ref, f32[2,8,768]{2,1,0:T(8,128)S(1)} %reshape.153.vectors_ref, ...), custom_call_target="tpu_custom_call" | custom-call | tf_op jit(solution)/shard_map/next_qkv/pallas_call | solution.py:77
  131.0 12.9 %attend.3 = (bf16[512,768]{1,0:T(8,128)(2,1)S(1)}, f32[6,8,512]{2,1,0:T(8,128)S(1)}) custom-call(bf16[512,768]{1,0:T(8,128)(2,1)S(1)} %get-tuple-element.352.q_ref, bf16[512,768]{1,0:T(8,128)(2,1)S(1)} %get-tuple-element.307.ko_ref, bf16[512,768]{1,0:T(8,128)(2,1)S(1)} %collective-permute-done.35.kt_ref, bf16[512,768]{1,0:T(8,128)(2,1)S(1)} %get-tuple-element.313.vo_ref, ...), custom_call_target="tpu_custom_call" | custom-call | tf_op jit(solution)/shard_map/attend/pallas_call | solution.py:77
  150.6 10.6 %feed_up.3 = (f32[512,768]{1,0:T(8,128)S(1)}, bf16[512,3072]{1,0:T(8,128)(2,1)S(1)}, bf16[512,3072]{1,0:T(8,128)(2,1)S(1)}) custom-call(s32[4]{0:T(128)S(1)} %pad_add_fusion.place_ref.refs_0_, f32[512,768]{1,0:T(8,128)S(1)} %feed_down.2.stream_ref, bf16[512,768]{1,0:T(8,128)(2,1)S(1)} %copy-done.9, f32[2,8,768]{2,1,0:T(8,128)S(1)} %reshape.153.vectors_ref, ...), custom_call_target="tpu_custom_call" | custom-call | tf_op jit(solution)/shard_map/feed_up/pallas_call | solution.py:77
  162.3 6.0 %down_weight_grad.2 = (bf16[2,2,2,4,48,768]{5,4,3,2,1,0:T(8,128)(2,1)}, bf16[2,4,48,768]{3,2,1,0:T(8,128)(2,1)}, bf16[2,4,48,768]{3,2,1,0:T(8,128)(2,1)}, bf16[2...) custom-call(s32[4]{0:T(128)S(1)} %pad_add_fusion.place_ref.refs_0_, ...), custom_call_target="tpu_custom_call" | custom-call | tf_op jit(solution)/shard_map/down_weight_grad/pallas_call | solution.py:77
  171.4 5.8 %feed_down.3 = (bf16[256,768]{1,0:T(8,128)(2,1)S(1)}, bf16[256,768]{1,0:T(8,128)(2,1)S(1)}) custom-call(s32[4]{0:T(128)S(1)} %pad_add_fusion.place_ref.refs_0_, f32[512,768]{1,0:T(8,128)S(1)} %get-tuple-element.318.attended_ref, bf16[512,3072]{1,0:T(8,128)(2,1)S(1)} %get-tuple-element.319.activated_ref, f32[2,8,768]{2,1,0:T(8,128)S(1)} %reshape.153.vectors_ref, ...), custom_call_target="tpu_custom_call" | custom-call | tf_op jit(solution)/shard_map/feed_down/pallas_call | solution.py:77
  181.6 11.7 %feed_back.2 = (bf16[512,3072]{1,0:T(8,128)(2,1)S(1)}, f32[512,768]{1,0:T(8,128)S(1)}, bf16[512,768]{1,0:T(8,128)(2,1)S(1)}, f32[8,768]{1,0:T(8,128)S(1)}, f32[1,3072]{1,0:T(1,128)S(1)}) custom-call(s32[4]{0:T(128)S(1)} %pad_add_fusion.place_ref.refs_0_, f32[512,768]{1,0:T(8,128)S(1)} %maximum_convert_fusion.grad_ref, ...), custom_call_target="tpu_custom_call" | custom-call | tf_op jit(solution)/shard_map/feed_back/pallas_call | solution.py:77
  193.3 7.1 %feed_weight_grads.2 = (bf16[2,2,2,5,48,768]{5,4,3,2,1,0:T(8,128)(2,1)}, bf16[2,5,48,768]{3,2,1,0:T(8,128)(2,1)}, bf16[2,5,48,768]{3,2,1,0:T(8,128)(2,1)}, bf16[...) custom-call(s32[4]{0:T(128)S(1)} %pad_add_fusion.place_ref.refs_0_, ...), custom_call_target="tpu_custom_call" | custom-call | tf_op jit(solution)/shard_map/feed_weight_grads/pallas_call | solution.py:77
  206.0 3.1 collective-permute-done.51.refs_2_.refs_8_
  210.2 3.4 combine.13
  215.3 22.1 %attend_back.2 = (bf16[512,768]{1,0:T(8,128)(2,1)S(1)}, bf16[512,768]{1,0:T(8,128)(2,1)S(1)}, bf16[512,768]{1,0:T(8,128)(2,1)S(1)}, bf16[512,768]{1,0:T(8,128)(2,1)S(1)}, bf16[512,768]{1,0:T(8,128)(2,1)S(1)}) custom-call(bf16[512,768]{1,0:T(8,128)(2,1)S(1)} %copy-done.23, bf16[512,768]{1,0:T(8,128)(2,1)S(1)} %copy-done.25, bf16[512,768]{1,0:T(8,128)(2,1)S(1)} %copy-done.29, ...), custom_call_target="tpu_custom_call" | custom-call | tf_op jit(solution)/shard_map/attend_back/pallas_call | solution.py:77
  242.0 5.9 %qkv_weight_grads.2 = (f32[8,768]{1,0:T(8,128)S(1)}, bf16[2,512,768]{2,1,0:T(8,128)(2,1)S(1)}, bf16[2,2,2,3,48,768]{5,4,3,2,1,0:T(8,128)(2,1)}, bf16[2,3,48,768]...) custom-call(s32[4]{0:T(128)S(1)} %pad_add_fusion.place_ref.refs_0_, ...), custom_call_target="tpu_custom_call" | custom-call | tf_op jit(solution)/shard_map/qkv_weight_grads/pallas_call | solution.py:77
  250.5 5.4 %norm_back.2 = (f32[512,768]{1,0:T(8,128)S(1)}, f32[8,768]{1,0:T(8,128)S(1)}) custom-call(s32[4]{0:T(128)S(1)} %pad_add_fusion.place_ref.refs_0_, f32[512,768]{1,0:T(8,128)S(1)} %feed_down.2.stream_ref, f32[2,8,768]{2,1,0:T(8,128)S(1)} %reshape.153.vectors_ref, f32[512,768]{1,0:T(8,128)S(1)} %get-tuple-element.340.attended_grad_ref, ...), custom_call_target="tpu_custom_call" | custom-call | tf_op jit(solution)/shard_map/norm_back/pallas_call | solution.py:77
  256.9 4.4 combine.15
  263.8 3.6 collective-permute-start.63
  267.4 6.0 %down_weight_grad.3 = (bf16[2,2,2,4,48,768]{5,4,3,2,1,0:T(8,128)(2,1)}, bf16[2,4,48,768]{3,2,1,0:T(8,128)(2,1)}, bf16[2,4,48,768]{3,2,1,0:T(8,128)(2,1)}, bf16[2...) custom-call(s32[4]{0:T(128)S(1)} %pad_add_fusion.place_ref.refs_0_, bf16[512,3072]{1,0:T(8,128)(2,1)S(1)} %copy-done.3, ...), custom_call_target="tpu_custom_call" | custom-call | tf_op jit(solution)/shard_map/down_weight_grad/pallas_call | solution.py:77
  273.5 11.9 %feed_back.3 = (bf16[512,3072]{1,0:T(8,128)(2,1)S(1)}, f32[512,768]{1,0:T(8,128)S(1)}, bf16[512,768]{1,0:T(8,128)(2,1)S(1)}, f32[8,768]{1,0:T(8,128)S(1)}, f32[1,3072]{1,0:T(1,128)S(1)}) custom-call(s32[4]{0:T(128)S(1)} %pad_add_fusion.place_ref.refs_0_, f32[512,768]{1,0:T(8,128)S(1)} %get-tuple-element.367.grad_ref, bf16[512,3072]{1,0:T(8,128)(2,1)S(1)} %copy-done.7, ...), custom_call_target="tpu_custom_call" | custom-call | tf_op jit(solution)/shard_map/feed_back/pallas_call | solution.py:77
  291.0 4.6 combine.16
  300.5 7.2 %feed_weight_grads.3 = (bf16[2,2,2,5,48,768]{5,4,3,2,1,0:T(8,128)(2,1)}, bf16[2,5,48,768]{3,2,1,0:T(8,128)(2,1)}, bf16[2,5,48,768]{3,2,1,0:T(8,128)(2,1)}, bf16[...) custom-call(s32[4]{0:T(128)S(1)} %pad_add_fusion.place_ref.refs_0_, ...), custom_call_target="tpu_custom_call" | custom-call | tf_op jit(solution)/shard_map/feed_weight_grads/pallas_call | solution.py:77
  307.8 22.8 %attend_back.3 = (bf16[512,768]{1,0:T(8,128)(2,1)S(1)}, bf16[512,768]{1,0:T(8,128)(2,1)S(1)}, bf16[512,768]{1,0:T(8,128)(2,1)S(1)}, bf16[512,768]{1,0:T(8,128)(2,1)S(1)}, bf16[512,768]{1,0:T(8,128)(2,1)}) custom-call(bf16[512,768]{1,0:T(8,128)(2,1)S(1)} %copy-done.13, bf16[512,768]{1,0:T(8,128)(2,1)S(1)} %copy-done.15, bf16[512,768]{1,0:T(8,128)(2,1)S(1)} %copy-done.19, ...), custom_call_target="tpu_custom_call" | custom-call | tf_op jit(solution)/shard_map/attend_back/pallas_call | solution.py:77
  338.2 5.4 %combine.17 = (bf16[20,48,768]{2,1,0:T(8,128)(2,1)}, bf16[8,48,768]{2,1,0:T(8,128)(2,1)}, bf16[4,48,768]{2,1,0:T(8,128)(2,1)}, bf16[3,48,768]{2,1,0:T(8,128)(2,1)}, bf16[5,48,768]{2,1,0:T(8,128)(2,1)}) custom-call(bf16[40,48,768]{2,1,0:T(8,128)(2,1)} %bitcast.79, bf16[10,48,768]{2,1,0:T(8,128)(2,1)} %copy-done.93, bf16[10,48,768]{2,1,0:T(8,128)(2,1)} %copy-done.94, ...), custom_call_target="tpu_custom_call" | custom-call | tf_op jit(solution)/shard_map/combine/pallas_call | solution.py:77
  356.9 5.9 %qkv_weight_grads.3 = (f32[8,768]{1,0:T(8,128)S(1)}, bf16[2,512,768]{2,1,0:T(8,128)(2,1)S(1)}, bf16[2,2,2,3,48,768]{5,4,3,2,1,0:T(8,128)(2,1)}, bf16[2,3,48,768]...) custom-call(s32[4]{0:T(128)S(1)} %pad_add_fusion.place_ref.refs_0_, ...), custom_call_target="tpu_custom_call" | custom-call | tf_op jit(solution)/shard_map/qkv_weight_grads/pallas_call | solution.py:77
  362.8 5.4 %norm_back.3 = (f32[512,768]{1,0:T(8,128)S(1)}, f32[8,768]{1,0:T(8,128)S(1)}) custom-call(s32[4]{0:T(128)S(1)} %pad_add_fusion.place_ref.refs_0_, f32[512,768]{1,0:T(8,128)S(1)} %copy-done.1, f32[2,8,768]{2,1,0:T(8,128)S(1)} %reshape.153.vectors_ref, f32[512,768]{1,0:T(8,128)S(1)} %copy-done.5, bf16[512,768]{1,0:T(8,128)(2,1)S(1)} %copy-done.33, ...), custom_call_target="tpu_custom_call" | custom-call | tf_op jit(solution)/shard_map/norm_back/pallas_call | solution.py:77
  374.7 3.7 combine.18
  381.2 3.2 finish.6.refs_5_
  384.4 4.0 collective-permute-done.89.refs_7_
  390.1 3.6 combine.19
  398.1 5.7 %collective-permute-done.91.refs_2_ = bf16[13,48,768]{2,1,0:T(8,128)(2,1)S(1)} collective-permute-done((bf16[13,48,768]{2,1,0:T(8,128)(2,1)}, bf16[13,48,768]{2,1,0:T(8,128)(2,1)S(1)}, u32[]{:S(2)}, u32[]{:S(2)}) %collective-permute-start.91) | collective-permute-done | bytes 958496 | tf_op jit(solution)/shard_map/ppermute | solution.py:35
  403.8 7.6 %collective-permute-done.93.refs_9_ = bf16[7,48,768]{2,1,0:T(8,128)(2,1)S(1)} collective-permute-done((bf16[7,48,768]{2,1,0:T(8,128)(2,1)}, bf16[7,48,768]{2,1,0:T(8,128)(2,1)S(1)}, u32[]{:S(2)}, u32[]{:S(2)}) %collective-permute-start.93) | collective-permute-done | bytes 516128 | tf_op jit(solution)/shard_map/ppermute | solution.py:1005
  413.1 3.8 combine.20
  418.1 7.4 %collective-permute-start.100 = (bf16[7,48,768]{2,1,0:T(8,128)(2,1)}, bf16[7,48,768]{2,1,0:T(8,128)(2,1)S(1)}, u32[]{:S(2)}, u32[]{:S(2)}) collective-permute-start(bf16[7,48,768]{2,1,0:T(8,128)(2,1)} %get-tuple-element.466), channel_id=1, source_target_pairs={{0,8},{8,0},{16,24},{24,16},{1,9},{9,1},{17,25},{25,17},{2,10},{10... | collective-permute-start | bytes 1548296 | tf_op jit(solution)/shard_map/ppermute | solution.py:1005
  428.7 17.5 %collective-permute-done.97.refs_4_ = bf16[5,48,768]{2,1,0:T(8,128)(2,1)S(1)} collective-permute-done((bf16[5,48,768]{2,1,0:T(8,128)(2,1)S(1)}, bf16[5,48,768]{2,1,0:T(8,128)(2,1)S(1)}, u32[]{:S(2)}, u32[]{:S(2)}) %collective-permute-start.97) | collective-permute-done | bytes 368672 | tf_op jit(solution)/shard_map/ppermute | solution.py:1005
  447.0 3.5 finish.7
  453.1 3.2 combine.21
  461.8 10.9 %collective-permute-done.101.refs_4_ = bf16[4,48,768]{2,1,0:T(8,128)(2,1)S(1)} collective-permute-done((bf16[4,48,768]{2,1,0:T(8,128)(2,1)}, bf16[4,48,768]{2,1,0:T(8,128)(2,1)S(1)}, u32[]{:S(2)}, u32[]{:S(2)}) %collective-permute-start.101) | collective-permute-done | bytes 294944 | tf_op jit(solution)/shard_map/ppermute | solution.py:1005
  474.2 3.2 combine.22
  486.8 3.2 finish.8
  504.8 3.5 finish.10
  509.1 4.3 collective-permute-done.111.refs_4_
  (580 shorter events, 179.7 us)
Async XLA Ops:
  3.5 14.3 %collective-permute-start.10 = (bf16[3,96,768]{2,1,0:T(8,128)(2,1)}, bf16[3,96,768]{2,1,0:T(8,128)(2,1)}, u32[]{:S(2)}, u32[]{:S(2)}) collective-permute-start(bf16[3,96,768]{2,1,0:T(8,128)(2,1)} %get-tuple-element.255), channel_id=1, source_target_pairs={{0,2},{2,0},{1,3},{3,1},{4,6},{6,4},{5,7},{7,5},{8,10},{10,8},{9,1... | collective-permute-start | bytes 1327112 | tf_op jit(solution)/shard_map/ppermute | solution.py:35
  6.6 18.7 %collective-permute-start = (bf16[256,768]{1,0:T(8,128)(2,1)}, bf16[256,768]{1,0:T(8,128)(2,1)S(1)}, u32[]{:S(2)}, u32[]{:S(2)}) collective-permute-start(bf16[256,768]{1,0:T(8,128)(2,1)} %get-tuple-element.263), channel_id=1, source_target_pairs={{0,2},{2,0},{1,3},{3,1},{4,6},{6,4},{5,7},{7,5},{8,10},{10,8},{9,1... | collective-permute-start | bytes 1179656 | tf_op jit(solution)/shard_map/ppermute | solution.py:35
  17.9 14.3 %collective-permute-start.11 = (bf16[3,96,768]{2,1,0:T(8,128)(2,1)}, bf16[3,96,768]{2,1,0:T(8,128)(2,1)}, u32[]{:S(2)}, u32[]{:S(2)}) collective-permute-start(bf16[3,96,768]{2,1,0:T(8,128)(2,1)} %collective-permute-done.10.refs_2_), channel_id=1, source_target_pairs={{0,4},{4,0},{1,5},{5,1},{2,6},{6,2},{3,7},{7,3},{8,12},{12,8},{9,1... | collective-permute-start | bytes 1327112 | tf_op jit(solution)/shard_map/ppermute | solution.py:35
  38.2 22.0 %collective-permute-start.14 = (bf16[6,96,768]{2,1,0:T(8,128)(2,1)}, bf16[6,96,768]{2,1,0:T(8,128)(2,1)}, u32[]{:S(2)}, u32[]{:S(2)}) collective-permute-start(bf16[6,96,768]{2,1,0:T(8,128)(2,1)} %get-tuple-element.282), channel_id=1, source_target_pairs={{0,2},{2,0},{1,3},{3,1},{4,6},{6,4},{5,7},{7,5},{8,10},{10,8},{9,1... | collective-permute-start | bytes 2654216 | tf_op jit(solution)/shard_map/ppermute | solution.py:35
  60.2 22.4 %collective-permute-start.21 = (bf16[6,96,768]{2,1,0:T(8,128)(2,1)}, bf16[6,96,768]{2,1,0:T(8,128)(2,1)}, u32[]{:S(2)}, u32[]{:S(2)}) collective-permute-start(bf16[6,96,768]{2,1,0:T(8,128)(2,1)} %collective-permute-done.14.refs_2_), channel_id=1, source_target_pairs={{0,4},{4,0},{1,5},{5,1},{2,6},{6,2},{3,7},{7,3},{8,12},{12,8},{9,1... | collective-permute-start | bytes 2654216 | tf_op jit(solution)/shard_map/ppermute | solution.py:35
  62.2 20.3 %collective-permute-start.15 = (bf16[3,96,768]{2,1,0:T(8,128)(2,1)S(1)}, bf16[3,96,768]{2,1,0:T(8,128)(2,1)}, u32[]{:S(2)}, u32[]{:S(2)}) collective-permute-start(bf16[3,96,768]{2,1,0:T(8,128)(2,1)S(1)} %copy-done.153), channel_id=1, source_target_pairs={{0,2},{2,0},{1,3},{3,1},{4,6},{6,4},{5,7},{7,5},{8,10},{10,8},{9,1... | collective-permute-start | bytes 1327112 | tf_op jit(solution)/shard_map/ppermute | solution.py:35
  83.1 16.2 %collective-permute-start.19 = (bf16[3,96,768]{2,1,0:T(8,128)(2,1)}, bf16[3,96,768]{2,1,0:T(8,128)(2,1)}, u32[]{:S(2)}, u32[]{:S(2)}) collective-permute-start(bf16[3,96,768]{2,1,0:T(8,128)(2,1)} %get-tuple-element.290), channel_id=1, source_target_pairs={{0,2},{2,0},{1,3},{3,1},{4,6},{6,4},{5,7},{7,5},{8,10},{10,8},{9,1... | collective-permute-start | bytes 1327112 | tf_op jit(solution)/shard_map/ppermute | solution.py:35
  83.4 16.2 %collective-permute-start.25 = (bf16[3,96,768]{2,1,0:T(8,128)(2,1)}, bf16[3,96,768]{2,1,0:T(8,128)(2,1)}, u32[]{:S(2)}, u32[]{:S(2)}) collective-permute-start(bf16[3,96,768]{2,1,0:T(8,128)(2,1)} %collective-permute-done.15.refs_8_), channel_id=1, source_target_pairs={{0,4},{4,0},{1,5},{5,1},{2,6},{6,2},{3,7},{7,3},{8,12},{12,8},{9,1... | collective-permute-start | bytes 1327112 | tf_op jit(solution)/shard_map/ppermute | solution.py:35
  126.1 18.8 %collective-permute-start.32 = (bf16[4,96,768]{2,1,0:T(8,128)(2,1)S(1)}, bf16[4,96,768]{2,1,0:T(8,128)(2,1)}, u32[]{:S(2)}, u32[]{:S(2)}) collective-permute-start(bf16[4,96,768]{2,1,0:T(8,128)(2,1)S(1)} %copy-done.146), channel_id=1, source_target_pairs={{0,2},{2,0},{1,3},{3,1},{4,6},{6,4},{5,7},{7,5},{8,10},{10,8},{9,1... | collective-permute-start | bytes 1769480 | tf_op jit(solution)/shard_map/ppermute | solution.py:35
  130.1 17.4 %collective-permute-start.38 = (bf16[2,96,768]{2,1,0:T(8,128)(2,1)S(1)}, bf16[2,96,768]{2,1,0:T(8,128)(2,1)}, u32[]{:S(2)}, u32[]{:S(2)}) collective-permute-start(bf16[2,96,768]{2,1,0:T(8,128)(2,1)S(1)} %collective-permute-done.27.refs_8_), channel_id=1, source_target_pairs={{0,4},{4,0},{1,5},{5,1},{2,6},{6,2},{3,7},{7,3},{8,12},{12,8},{9,1... | collective-permute-start | bytes 884744 | tf_op jit(solution)/shard_map/ppermute | solution.py:35
  145.0 23.3 %collective-permute-start.40 = (bf16[4,96,768]{2,1,0:T(8,128)(2,1)}, bf16[4,96,768]{2,1,0:T(8,128)(2,1)}, u32[]{:S(2)}, u32[]{:S(2)}) collective-permute-start(bf16[4,96,768]{2,1,0:T(8,128)(2,1)} %collective-permute-done.32.refs_2_.refs_14_), channel_id=1, source_target_pairs={{0,4},{4,0},{1,5},{5,1},{2,6},{6,2},{3,7},{7,3},{8,12},{12,8},{9,1... | collective-permute-start | bytes 1769480 | tf_op jit(solution)/shard_map/ppermute | solution.py:35
  146.1 15.0 %collective-permute-start.41 = (bf16[256,768]{1,0:T(8,128)(2,1)}, bf16[256,768]{1,0:T(8,128)(2,1)}, u32[]{:S(2)}, u32[]{:S(2)}) collective-permute-start(bf16[256,768]{1,0:T(8,128)(2,1)} %get-tuple-element.321), channel_id=1, source_target_pairs={{0,2},{2,0},{1,3},{3,1},{4,6},{6,4},{5,7},{7,5},{8,10},{10,8},{9,1... | collective-permute-start | bytes 1179656 | tf_op jit(solution)/shard_map/ppermute | solution.py:35
  180.9 28.3 %collective-permute-start.51 = (bf16[16,48,768]{2,1,0:T(8,128)(2,1)}, bf16[16,48,768]{2,1,0:T(8,128)(2,1)S(1)}, u32[]{:S(2)}, u32[]{:S(2)}) collective-permute-start(bf16[16,48,768]{2,1,0:T(8,128)(2,1)} %combine.12), channel_id=1, source_target_pairs={{0,2},{2,0},{1,3},{3,1},{4,6},{6,4},{5,7},{7,5},{8,10},{10,8},{9,1... | collective-permute-start | bytes 3538952 | tf_op jit(solution)/shard_map/ppermute | solution.py:35
  213.6 35.8 %collective-permute-start.55 = (bf16[20,48,768]{2,1,0:T(8,128)(2,1)}, bf16[20,48,768]{2,1,0:T(8,128)(2,1)S(1)}, u32[]{:S(2)}, u32[]{:S(2)}) collective-permute-start(bf16[20,48,768]{2,1,0:T(8,128)(2,1)} %get-tuple-element.372), channel_id=1, source_target_pairs={{0,2},{2,0},{1,3},{3,1},{4,6},{6,4},{5,7},{7,5},{8,10},{10,8},{9,1... | collective-permute-start | bytes 4423688 | tf_op jit(solution)/shard_map/ppermute | solution.py:35
  214.3 23.1 %collective-permute-start.52 = (bf16[8,48,768]{2,1,0:T(8,128)(2,1)}, bf16[8,48,768]{2,1,0:T(8,128)(2,1)S(1)}, u32[]{:S(2)}, u32[]{:S(2)}) collective-permute-start(bf16[8,48,768]{2,1,0:T(8,128)(2,1)} %get-tuple-element.351), channel_id=1, source_target_pairs={{0,4},{4,0},{1,5},{5,1},{2,6},{6,2},{3,7},{7,3},{8,12},{12,8},{9,1... | collective-permute-start | bytes 1769480 | tf_op jit(solution)/shard_map/ppermute | solution.py:35
  261.3 24.2 %collective-permute-start.61 = (bf16[12,48,768]{2,1,0:T(8,128)(2,1)}, bf16[12,48,768]{2,1,0:T(8,128)(2,1)S(1)}, u32[]{:S(2)}, u32[]{:S(2)}) collective-permute-start(bf16[12,48,768]{2,1,0:T(8,128)(2,1)} %get-tuple-element.378), channel_id=1, source_target_pairs={{0,2},{2,0},{1,3},{3,1},{4,6},{6,4},{5,7},{7,5},{8,10},{10,8},{9,1... | collective-permute-start | bytes 2654216 | tf_op jit(solution)/shard_map/ppermute | solution.py:35
  263.1 22.4 %collective-permute-start.62 = (bf16[10,48,768]{2,1,0:T(8,128)(2,1)}, bf16[10,48,768]{2,1,0:T(8,128)(2,1)S(1)}, u32[]{:S(2)}, u32[]{:S(2)}) collective-permute-start(bf16[10,48,768]{2,1,0:T(8,128)(2,1)} %get-tuple-element.388), channel_id=1, source_target_pairs={{0,4},{4,0},{1,5},{5,1},{2,6},{6,2},{3,7},{7,3},{8,12},{12,8},{9,1... | collective-permute-start | bytes 2211848 | tf_op jit(solution)/shard_map/ppermute | solution.py:35
  263.8 21.7 %collective-permute-start.63 = (bf16[4,48,768]{2,1,0:T(8,128)(2,1)}, bf16[4,48,768]{2,1,0:T(8,128)(2,1)S(1)}, u32[]{:S(2)}, u32[]{:S(2)}) collective-permute-start(bf16[4,48,768]{2,1,0:T(8,128)(2,1)} %get-tuple-element.389.refs_6_), channel_id=1, source_target_pairs={{0,24},{24,0},{8,16},{16,8},{1,25},{25,1},{9,17},{17,9},{2,26},{26... | collective-permute-start | bytes 884744 | tf_op jit(solution)/shard_map/ppermute | solution.py:1005
  295.7 35.1 %collective-permute-start.68 = (bf16[16,48,768]{2,1,0:T(8,128)(2,1)}, bf16[16,48,768]{2,1,0:T(8,128)(2,1)S(1)}, u32[]{:S(2)}, u32[]{:S(2)}) collective-permute-start(bf16[16,48,768]{2,1,0:T(8,128)(2,1)} %get-tuple-element.395), channel_id=1, source_target_pairs={{0,2},{2,0},{1,3},{3,1},{4,6},{6,4},{5,7},{7,5},{8,10},{10,8},{9,1... | collective-permute-start | bytes 3538952 | tf_op jit(solution)/shard_map/ppermute | solution.py:35
  296.4 34.3 %collective-permute-start.69 = (bf16[6,48,768]{2,1,0:T(8,128)(2,1)}, bf16[6,48,768]{2,1,0:T(8,128)(2,1)S(1)}, u32[]{:S(2)}, u32[]{:S(2)}) collective-permute-start(bf16[6,48,768]{2,1,0:T(8,128)(2,1)} %get-tuple-element.407), channel_id=1, source_target_pairs={{0,4},{4,0},{1,5},{5,1},{2,6},{6,2},{3,7},{7,3},{8,12},{12,8},{9,1... | collective-permute-start | bytes 1327112 | tf_op jit(solution)/shard_map/ppermute | solution.py:35
  297.4 33.4 %collective-permute-start.72 = (bf16[5,48,768]{2,1,0:T(8,128)(2,1)}, bf16[5,48,768]{2,1,0:T(8,128)(2,1)S(1)}, u32[]{:S(2)}, u32[]{:S(2)}) collective-permute-start(bf16[5,48,768]{2,1,0:T(8,128)(2,1)} %get-tuple-element.410), channel_id=1, source_target_pairs={{0,8},{8,0},{16,24},{24,16},{1,9},{9,1},{17,25},{25,17},{2,10},{10... | collective-permute-start | bytes 1105928 | tf_op jit(solution)/shard_map/ppermute | solution.py:1005
  297.4 33.3 %collective-permute-start.70 = (bf16[4,48,768]{2,1,0:T(8,128)(2,1)}, bf16[4,48,768]{2,1,0:T(8,128)(2,1)S(1)}, u32[]{:S(2)}, u32[]{:S(2)}) collective-permute-start(bf16[4,48,768]{2,1,0:T(8,128)(2,1)} %get-tuple-element.408.refs_1_), channel_id=1, source_target_pairs={{0,4},{4,0},{1,5},{5,1},{2,6},{6,2},{3,7},{7,3},{8,12},{12,8},{9,1... | collective-permute-start | bytes 884744 | tf_op jit(solution)/shard_map/ppermute | solution.py:35
  298.7 32.0 %collective-permute-start.71 = (bf16[4,48,768]{2,1,0:T(8,128)(2,1)}, bf16[4,48,768]{2,1,0:T(8,128)(2,1)S(1)}, u32[]{:S(2)}, u32[]{:S(2)}) collective-permute-start(bf16[4,48,768]{2,1,0:T(8,128)(2,1)} %get-tuple-element.409), channel_id=1, source_target_pairs={{0,8},{8,0},{16,24},{24,16},{1,9},{9,1},{17,25},{25,17},{2,10},{10... | collective-permute-start | bytes 884744 | tf_op jit(solution)/shard_map/ppermute | solution.py:1005
  331.9 15.5 %collective-permute-start.77 = (bf16[512,768]{1,0:T(8,128)(2,1)S(1)}, bf16[512,768]{1,0:T(8,128)(2,1)S(1)}, u32[]{:S(2)}, u32[]{:S(2)}) collective-permute-start(bf16[512,768]{1,0:T(8,128)(2,1)S(1)} %get-tuple-element.422), channel_id=1, source_target_pairs={{0,1},{1,0},{2,3},{3,2},{4,5},{5,4},{6,7},{7,6},{8,9},{9,8},{10,11... | collective-permute-start | bytes 2359304 | tf_op jit(solution)/shard_map/ppermute | solution.py:35
  333.4 15.0 %collective-permute-start.78 = (bf16[512,768]{1,0:T(8,128)(2,1)}, bf16[512,768]{1,0:T(8,128)(2,1)S(1)}, u32[]{:S(2)}, u32[]{:S(2)}) collective-permute-start(bf16[512,768]{1,0:T(8,128)(2,1)} %get-tuple-element.423), channel_id=1, source_target_pairs={{0,1},{1,0},{2,3},{3,2},{4,5},{5,4},{6,7},{7,6},{8,9},{9,8},{10,11... | collective-permute-start | bytes 2359304 | tf_op jit(solution)/shard_map/ppermute | solution.py:35
  343.7 25.7 %collective-permute-start.79 = (bf16[8,48,768]{2,1,0:T(8,128)(2,1)}, bf16[8,48,768]{2,1,0:T(8,128)(2,1)}, u32[]{:S(2)}, u32[]{:S(2)}) collective-permute-start(bf16[8,48,768]{2,1,0:T(8,128)(2,1)} %get-tuple-element.432), channel_id=1, source_target_pairs={{0,4},{4,0},{1,5},{5,1},{2,6},{6,2},{3,7},{7,3},{8,12},{12,8},{9,1... | collective-permute-start | bytes 1769480 | tf_op jit(solution)/shard_map/ppermute | solution.py:35
  344.7 44.7 %collective-permute-start.88 = (bf16[20,48,768]{2,1,0:T(8,128)(2,1)}, bf16[20,48,768]{2,1,0:T(8,128)(2,1)}, u32[]{:S(2)}, u32[]{:S(2)}) collective-permute-start(bf16[20,48,768]{2,1,0:T(8,128)(2,1)} %get-tuple-element.416), channel_id=1, source_target_pairs={{0,2},{2,0},{1,3},{3,1},{4,6},{6,4},{5,7},{7,5},{8,10},{10,8},{9,1... | collective-permute-start | bytes 4423688 | tf_op jit(solution)/shard_map/ppermute | solution.py:35
  346.4 22.9 %collective-permute-start.82 = (bf16[5,48,768]{2,1,0:T(8,128)(2,1)}, bf16[5,48,768]{2,1,0:T(8,128)(2,1)}, u32[]{:S(2)}, u32[]{:S(2)}) collective-permute-start(bf16[5,48,768]{2,1,0:T(8,128)(2,1)} %get-tuple-element.435.refs_9_), channel_id=1, source_target_pairs={{0,24},{24,0},{8,16},{16,8},{1,25},{25,1},{9,17},{17,9},{2,26},{26... | collective-permute-start | bytes 1105928 | tf_op jit(solution)/shard_map/ppermute | solution.py:1005
  348.3 21.1 %collective-permute-start.80 = (bf16[4,48,768]{2,1,0:T(8,128)(2,1)}, bf16[4,48,768]{2,1,0:T(8,128)(2,1)}, u32[]{:S(2)}, u32[]{:S(2)}) collective-permute-start(bf16[4,48,768]{2,1,0:T(8,128)(2,1)} %get-tuple-element.433), channel_id=1, source_target_pairs={{0,8},{8,0},{16,24},{24,16},{1,9},{9,1},{17,25},{25,17},{2,10},{10... | collective-permute-start | bytes 884744 | tf_op jit(solution)/shard_map/ppermute | solution.py:1005
  349.2 20.1 %collective-permute-start.81 = (bf16[3,48,768]{2,1,0:T(8,128)(2,1)}, bf16[3,48,768]{2,1,0:T(8,128)(2,1)S(1)}, u32[]{:S(2)}, u32[]{:S(2)}) collective-permute-start(bf16[3,48,768]{2,1,0:T(8,128)(2,1)} %get-tuple-element.434), channel_id=1, source_target_pairs={{0,8},{8,0},{16,24},{24,16},{1,9},{9,1},{17,25},{25,17},{2,10},{10... | collective-permute-start | bytes 663560 | tf_op jit(solution)/shard_map/ppermute | solution.py:1005
  379.5 24.3 %collective-permute-start.91 = (bf16[13,48,768]{2,1,0:T(8,128)(2,1)}, bf16[13,48,768]{2,1,0:T(8,128)(2,1)S(1)}, u32[]{:S(2)}, u32[]{:S(2)}) collective-permute-start(bf16[13,48,768]{2,1,0:T(8,128)(2,1)} %get-tuple-element.449.refs_3_), channel_id=1, source_target_pairs={{0,2},{2,0},{1,3},{3,1},{4,6},{6,4},{5,7},{7,5},{8,10},{10,8},{9,1... | collective-permute-start | bytes 2875400 | tf_op jit(solution)/shard_map/ppermute | solution.py:35
  393.7 18.0 %collective-permute-start.92 = (bf16[10,48,768]{2,1,0:T(8,128)(2,1)}, bf16[10,48,768]{2,1,0:T(8,128)(2,1)S(1)}, u32[]{:S(2)}, u32[]{:S(2)}) collective-permute-start(bf16[10,48,768]{2,1,0:T(8,128)(2,1)} %get-tuple-element.454), channel_id=1, source_target_pairs={{0,4},{4,0},{1,5},{5,1},{2,6},{6,2},{3,7},{7,3},{8,12},{12,8},{9,1... | collective-permute-start | bytes 2211848 | tf_op jit(solution)/shard_map/ppermute | solution.py:35
  394.7 16.7 %collective-permute-start.93 = (bf16[7,48,768]{2,1,0:T(8,128)(2,1)}, bf16[7,48,768]{2,1,0:T(8,128)(2,1)S(1)}, u32[]{:S(2)}, u32[]{:S(2)}) collective-permute-start(bf16[7,48,768]{2,1,0:T(8,128)(2,1)} %get-tuple-element.456.refs_8_), channel_id=1, source_target_pairs={{0,24},{24,0},{8,16},{16,8},{1,25},{25,1},{9,17},{17,9},{2,26},{26... | collective-permute-start | bytes 1548296 | tf_op jit(solution)/shard_map/ppermute | solution.py:1005
  397.4 29.3 %collective-permute-start.95 = (bf16[256,768]{1,0:T(8,128)(2,1)S(1)}, bf16[256,768]{1,0:T(8,128)(2,1)S(1)}, u32[]{:S(2)}, u32[]{:S(2)}) collective-permute-start(bf16[256,768]{1,0:T(8,128)(2,1)S(1)} %slice.83), channel_id=1, source_target_pairs={{0,2},{2,0},{1,3},{3,1},{4,6},{6,4},{5,7},{7,5},{8,10},{10,8},{9,1... | collective-permute-start | bytes 1179656 | tf_op jit(solution)/shard_map/ppermute | solution.py:35
  398.1 28.5 %collective-permute-start.96 = (bf16[5,48,768]{2,1,0:T(8,128)(2,1)S(1)}, bf16[5,48,768]{2,1,0:T(8,128)(2,1)S(1)}, u32[]{:S(2)}, u32[]{:S(2)}) collective-permute-start(bf16[5,48,768]{2,1,0:T(8,128)(2,1)S(1)} %copy-done.155), channel_id=1, source_target_pairs={{0,8},{8,0},{16,24},{24,16},{1,9},{9,1},{17,25},{25,17},{2,10},{10... | collective-permute-start | bytes 1105928 | tf_op jit(solution)/shard_map/ppermute | solution.py:1005
  416.9 34.5 %collective-permute-start.98 = (bf16[7,48,768]{2,1,0:T(8,128)(2,1)}, bf16[7,48,768]{2,1,0:T(8,128)(2,1)S(1)}, u32[]{:S(2)}, u32[]{:S(2)}) collective-permute-start(bf16[7,48,768]{2,1,0:T(8,128)(2,1)} %get-tuple-element.457.refs_4_), channel_id=1, source_target_pairs={{0,4},{4,0},{1,5},{5,1},{2,6},{6,2},{3,7},{7,3},{8,12},{12,8},{9,1... | collective-permute-start | bytes 1548296 | tf_op jit(solution)/shard_map/ppermute | solution.py:35
  418.1 33.4 %collective-permute-start.100 = (bf16[7,48,768]{2,1,0:T(8,128)(2,1)}, bf16[7,48,768]{2,1,0:T(8,128)(2,1)S(1)}, u32[]{:S(2)}, u32[]{:S(2)}) collective-permute-start(bf16[7,48,768]{2,1,0:T(8,128)(2,1)} %get-tuple-element.466), channel_id=1, source_target_pairs={{0,8},{8,0},{16,24},{24,16},{1,9},{9,1},{17,25},{25,17},{2,10},{10... | collective-permute-start | bytes 1548296 | tf_op jit(solution)/shard_map/ppermute | solution.py:1005
  425.5 25.0 %collective-permute-start.94 = (bf16[256,768]{1,0:T(8,128)(2,1)S(1)}, bf16[256,768]{1,0:T(8,128)(2,1)S(1)}, u32[]{:S(2)}, u32[]{:S(2)}) collective-permute-start(bf16[256,768]{1,0:T(8,128)(2,1)S(1)} %copy-done.52), channel_id=1, source_target_pairs={{0,2},{2,0},{1,3},{3,1},{4,6},{6,4},{5,7},{7,5},{8,10},{10,8},{9,1... | collective-permute-start | bytes 1179656 | tf_op jit(solution)/shard_map/ppermute | solution.py:35
  426.6 19.6 %collective-permute-start.97 = (bf16[5,48,768]{2,1,0:T(8,128)(2,1)S(1)}, bf16[5,48,768]{2,1,0:T(8,128)(2,1)S(1)}, u32[]{:S(2)}, u32[]{:S(2)}) collective-permute-start(bf16[5,48,768]{2,1,0:T(8,128)(2,1)S(1)} %copy-done.156), channel_id=1, source_target_pairs={{0,8},{8,0},{16,24},{24,16},{1,9},{9,1},{17,25},{25,17},{2,10},{10... | collective-permute-start | bytes 1105928 | tf_op jit(solution)/shard_map/ppermute | solution.py:1005
  426.7 24.7 %collective-permute-start.99 = (bf16[5,48,768]{2,1,0:T(8,128)(2,1)}, bf16[5,48,768]{2,1,0:T(8,128)(2,1)S(1)}, u32[]{:S(2)}, u32[]{:S(2)}) collective-permute-start(bf16[5,48,768]{2,1,0:T(8,128)(2,1)} %get-tuple-element.465), channel_id=1, source_target_pairs={{0,8},{8,0},{16,24},{24,16},{1,9},{9,1},{17,25},{25,17},{2,10},{10... | collective-permute-start | bytes 1105928 | tf_op jit(solution)/shard_map/ppermute | solution.py:1005
  456.3 16.4 %collective-permute-start.102 = (bf16[5,48,768]{2,1,0:T(8,128)(2,1)}, bf16[5,48,768]{2,1,0:T(8,128)(2,1)S(1)}, u32[]{:S(2)}, u32[]{:S(2)}) collective-permute-start(bf16[5,48,768]{2,1,0:T(8,128)(2,1)} %get-tuple-element.469.refs_6_), channel_id=1, source_target_pairs={{0,24},{24,0},{8,16},{16,8},{1,25},{25,1},{9,17},{17,9},{2,26},{26... | collective-permute-start | bytes 1105928 | tf_op jit(solution)/shard_map/ppermute | solution.py:1005
  458.8 13.9 %collective-permute-start.101 = (bf16[4,48,768]{2,1,0:T(8,128)(2,1)}, bf16[4,48,768]{2,1,0:T(8,128)(2,1)S(1)}, u32[]{:S(2)}, u32[]{:S(2)}) collective-permute-start(bf16[4,48,768]{2,1,0:T(8,128)(2,1)} %get-tuple-element.467.refs_5_), channel_id=1, source_target_pairs={{0,8},{8,0},{16,24},{24,16},{1,9},{9,1},{17,25},{25,17},{2,10},{10... | collective-permute-start | bytes 884744 | tf_op jit(solution)/shard_map/ppermute | solution.py:1005
  459.7 23.5 %collective-permute-start.104 = (bf16[7,48,768]{2,1,0:T(8,128)(2,1)}, bf16[7,48,768]{2,1,0:T(8,128)(2,1)S(1)}, u32[]{:S(2)}, u32[]{:S(2)}) collective-permute-start(bf16[7,48,768]{2,1,0:T(8,128)(2,1)} %get-tuple-element.472.refs_1_), channel_id=1, source_target_pairs={{0,4},{4,0},{1,5},{5,1},{2,6},{6,2},{3,7},{7,3},{8,12},{12,8},{9,1... | collective-permute-start | bytes 1548296 | tf_op jit(solution)/shard_map/ppermute | solution.py:35
  460.7 25.2 %collective-permute-start.105 = (bf16[7,48,768]{2,1,0:T(8,128)(2,1)S(1)}, bf16[7,48,768]{2,1,0:T(8,128)(2,1)S(1)}, u32[]{:S(2)}, u32[]{:S(2)}) collective-permute-start(bf16[7,48,768]{2,1,0:T(8,128)(2,1)S(1)} %copy-done.151), channel_id=1, source_target_pairs={{0,4},{4,0},{1,5},{5,1},{2,6},{6,2},{3,7},{7,3},{8,12},{12,8},{9,1... | collective-permute-start | bytes 1548296 | tf_op jit(solution)/shard_map/ppermute | solution.py:35
  477.3 15.5 %collective-permute-start.103 = (bf16[4,48,768]{2,1,0:T(8,128)(2,1)}, bf16[4,48,768]{2,1,0:T(8,128)(2,1)S(1)}, u32[]{:S(2)}, u32[]{:S(2)}) collective-permute-start(bf16[4,48,768]{2,1,0:T(8,128)(2,1)} %get-tuple-element.476.refs_0_), channel_id=1, source_target_pairs={{0,24},{24,0},{8,16},{16,8},{1,25},{25,1},{9,17},{17,9},{2,26},{26... | collective-permute-start | bytes 884744 | tf_op jit(solution)/shard_map/ppermute | solution.py:1005
  482.4 17.3 %collective-permute-start.106 = (bf16[5,48,768]{2,1,0:T(8,128)(2,1)}, bf16[5,48,768]{2,1,0:T(8,128)(2,1)S(1)}, u32[]{:S(2)}, u32[]{:S(2)}) collective-permute-start(bf16[5,48,768]{2,1,0:T(8,128)(2,1)} %get-tuple-element.480), channel_id=1, source_target_pairs={{0,8},{8,0},{16,24},{24,16},{1,9},{9,1},{17,25},{25,17},{2,10},{10... | collective-permute-start | bytes 1105928 | tf_op jit(solution)/shard_map/ppermute | solution.py:1005
  482.5 20.0 %collective-permute-start.107 = (bf16[5,48,768]{2,1,0:T(8,128)(2,1)S(1)}, bf16[5,48,768]{2,1,0:T(8,128)(2,1)S(1)}, u32[]{:S(2)}, u32[]{:S(2)}) collective-permute-start(bf16[5,48,768]{2,1,0:T(8,128)(2,1)S(1)} %copy-done.117), channel_id=1, source_target_pairs={{0,4},{4,0},{1,5},{5,1},{2,6},{6,2},{3,7},{7,3},{8,12},{12,8},{9,1... | collective-permute-start | bytes 1105928 | tf_op jit(solution)/shard_map/ppermute | solution.py:35
  483.2 20.9 %collective-permute-start.108 = (bf16[5,48,768]{2,1,0:T(8,128)(2,1)S(1)}, bf16[5,48,768]{2,1,0:T(8,128)(2,1)S(1)}, u32[]{:S(2)}, u32[]{:S(2)}) collective-permute-start(bf16[5,48,768]{2,1,0:T(8,128)(2,1)S(1)} %copy-done.154), channel_id=1, source_target_pairs={{0,12},{4,8},{8,4},{12,0},{16,28},{20,24},{24,20},{28,16},{1,13},{... | collective-permute-start | bytes 1105928 | tf_op jit(solution)/shard_map/ppermute | solution.py:1003
  (222 other events, 1704.3 us)

commit v6 on v5

--- a/solution.py
+++ b/solution.py
@@ -433,8 +433,8 @@
     branch = grad_ref[...].astype(BF16)
     sums_ref[...] = jnp.zeros_like(sums_ref)
     sums_ref[7:8] = column_sum(branch)
+    standard, inverse = standardize(attended_ref[...])
     wait_all(down_copies)
-    wait_all(up_copies)
     second_grad = None
     for block in range(SHARDS):
         at = slice(block * width, (block + 1) * width)
@@ -442,9 +442,10 @@
         hidden_grad = (dot(branch, down, NT) * slope_ref[:, at].astype(F32)).astype(BF16)
         hidden_ref[:, at] = hidden_grad
         up_sums_ref[:, at] = column_sum(hidden_grad)
+        if block == 0:
+            wait_all(up_copies)
         part = dot(hidden_grad, up_w[block], NT)
         second_grad = part if second_grad is None else second_grad + part
-    standard, inverse = standardize(attended_ref[...])
     sums_ref[5:6] = column_sum(second_grad * standard)
     sums_ref[6:7] = column_sum(second_grad)
     attended_grad = grad_ref[...] + norm_input_grad(second_grad, standard, inverse, vectors_ref[layer, 5:6])

time: 523 us -> 523 us (level)
  transfers between devices with their start and end apart: 112 -> 112, of which waited for: 53 -> 54; matrix products, arithmetic and copies ran while one was open for 2% -> 2% of each run, Pallas kernels for 45% -> 45%
where the time goes in v6:
time: 523 us; the launch traced here: 517 us
  Pallas kernels  256 us (49%)
  waiting for transfers between devices  127 us (24%)
  starting transfers between devices  86.3 us (17%)
  local copies, waits for them, and re-layouts  41.8 us (8%)
    pallas_call x40, Pallas kernels, call(): pl.pallas_call(kernel, in_specs=list(in_specs), out_shape=out_shape, out_...  256 us
    ppermute x92, waiting for transfers between devices, swap(): return lax.ppermute(values, axis, SWAP)  77.6 us
    ppermute x92, starting transfers between devices, swap(): return lax.ppermute(values, axis, SWAP)  54 us
    ppermute x18, waiting for transfers between devices, exchange(): arrived = lax.ppermute(sent, 'z', MIRROR if name == 'mirror' else PAIRS)  42.3 us
    unnamed x322, local copies, waits for them, and re-layouts  38.6 us
    ppermute x18, starting transfers between devices, exchange(): arrived = lax.ppermute(sent, 'z', MIRROR if name == 'mirror' else PAIRS)  27.6 us
  transfers between devices with their start and end apart: 112, of which 54 were waited for; matrix products, arithmetic and copies ran while one was open for 2% of the time, Pallas kernels for 45%

profile of v6, /device:TPU:0, one launch (start us, length us, event | category | flops | bytes accessed | tf_op | source)
XLA Modules:
  0.0 517.4 jit_solution(17912497739738966669)
XLA Ops:
  6.7 7.2 %pack_shares.3 = (bf16[6,192,768]{2,1,0:T(8,128)(2,1)}, bf16[6,96,768]{2,1,0:T(8,128)(2,1)}, bf16[3,192,768]{2,1,0:T(8,128)(2,1)}, bf16[3,96,768]{2,1,0:T(8,128)...) custom-call(s32[4]{0:T(128)S(1)} %pad_add_fusion.place_ref.refs_0_, ...), custom_call_target="tpu_custom_call" | custom-call | tf_op jit(solution)/shard_map/pack_shares/pallas_call | solution.py:77
  13.9 3.9 collective-permute-done.10.refs_2_
  19.9 5.4 %collective-permute-done.arrived_ref = bf16[256,768]{1,0:T(8,128)(2,1)S(1)} collective-permute-done((bf16[256,768]{1,0:T(8,128)(2,1)}, bf16[256,768]{1,0:T(8,128)(2,1)S(1)}, u32[]{:S(2)}, u32[]{:S(2)}) %collective-permute-start) | collective-permute-done | bytes 393248 | tf_op jit(solution)/shard_map/ppermute | solution.py:35
  32.7 3.8 collective-permute-done.2.refs_7_
  43.2 4.9 first_qkv.1
  48.2 12.0 %collective-permute-done.14.refs_2_ = bf16[6,96,768]{2,1,0:T(8,128)(2,1)} collective-permute-done((bf16[6,96,768]{2,1,0:T(8,128)(2,1)}, bf16[6,96,768]{2,1,0:T(8,128)(2,1)}, u32[]{:S(2)}, u32[]{:S(2)}) %collective-permute-start.14) | collective-permute-done | bytes 884768 | tf_op jit(solution)/shard_map/ppermute | solution.py:35
  65.1 13.0 %attend.2 = (bf16[512,768]{1,0:T(8,128)(2,1)S(1)}, f32[6,8,512]{2,1,0:T(8,128)S(1)}) custom-call(bf16[512,768]{1,0:T(8,128)(2,1)S(1)} %get-tuple-element.400.q_ref, bf16[512,768]{1,0:T(8,128)(2,1)S(1)} %get-tuple-element.283.ko_ref, bf16[512,768]{1,0:T(8,128)(2,1)S(1)} %collective-permute-done.17.kt_ref, bf16[512,768]{1,0:T(8,128)(2,1)S(1)} %get-tuple-element.288.vo_ref, ...), custom_call_target="tpu_custom_call" | custom-call | tf_op jit(solution)/shard_map/attend/pallas_call | solution.py:77
  88.7 10.6 %feed_up.2 = (f32[512,768]{1,0:T(8,128)S(1)}, bf16[512,3072]{1,0:T(8,128)(2,1)S(1)}, bf16[512,3072]{1,0:T(8,128)(2,1)S(1)}) custom-call(s32[4]{0:T(128)S(1)} %pad_add_fusion.place_ref.refs_0_, f32[512,768]{1,0:T(8,128)S(1)} %get-tuple-element.293.stream_ref, bf16[512,768]{1,0:T(8,128)(2,1)S(1)} %copy-done.35, f32[2,8,768]{2,1,0:T(8,128)S(1)} %reshape.153.vectors_ref, ...), custom_call_target="tpu_custom_call" | custom-call | tf_op jit(solution)/shard_map/feed_up/pallas_call | solution.py:77
  102.8 5.6 %feed_down.2.stream_ref = f32[512,768]{1,0:T(8,128)S(1)} custom-call(s32[4]{0:T(128)S(1)} %pad_add_fusion.place_ref.refs_0_, f32[512,768]{1,0:T(8,128)S(1)} %get-tuple-element.299.attended_ref, bf16[512,3072]{1,0:T(8,128)(2,1)S(1)} %get-tuple-element.295.activated_ref, f32[2,8,768]{2,1,0:T(8,128)S(1)} %reshape.153.vectors_ref, ...), custom_call_target="tpu_custom_call" | custom-call | tf_op jit(solution)/shard_map/feed_down/pallas_call | solution.py:77
  108.4 3.7 collective-permute-done.23.refs_2_
  116.4 5.3 %next_qkv.1 = (bf16[512,768]{1,0:T(8,128)(2,1)S(1)}, bf16[512,768]{1,0:T(8,128)(2,1)S(1)}, bf16[512,768]{1,0:T(8,128)(2,1)S(1)}) custom-call(s32[4]{0:T(128)S(1)} %pad_add_fusion.place_ref.refs_0_, f32[512,768]{1,0:T(8,128)S(1)} %feed_down.2.stream_ref, f32[2,8,768]{2,1,0:T(8,128)S(1)} %reshape.153.vectors_ref, ...), custom_call_target="tpu_custom_call" | custom-call | tf_op jit(solution)/shard_map/next_qkv/pallas_call | solution.py:77
  131.0 12.9 %attend.3 = (bf16[512,768]{1,0:T(8,128)(2,1)S(1)}, f32[6,8,512]{2,1,0:T(8,128)S(1)}) custom-call(bf16[512,768]{1,0:T(8,128)(2,1)S(1)} %get-tuple-element.352.q_ref, bf16[512,768]{1,0:T(8,128)(2,1)S(1)} %get-tuple-element.307.ko_ref, bf16[512,768]{1,0:T(8,128)(2,1)S(1)} %collective-permute-done.35.kt_ref, bf16[512,768]{1,0:T(8,128)(2,1)S(1)} %get-tuple-element.313.vo_ref, ...), custom_call_target="tpu_custom_call" | custom-call | tf_op jit(solution)/shard_map/attend/pallas_call | solution.py:77
  150.6 10.6 %feed_up.3 = (f32[512,768]{1,0:T(8,128)S(1)}, bf16[512,3072]{1,0:T(8,128)(2,1)S(1)}, bf16[512,3072]{1,0:T(8,128)(2,1)S(1)}) custom-call(s32[4]{0:T(128)S(1)} %pad_add_fusion.place_ref.refs_0_, f32[512,768]{1,0:T(8,128)S(1)} %feed_down.2.stream_ref, bf16[512,768]{1,0:T(8,128)(2,1)S(1)} %copy-done.9, f32[2,8,768]{2,1,0:T(8,128)S(1)} %reshape.153.vectors_ref, ...), custom_call_target="tpu_custom_call" | custom-call | tf_op jit(solution)/shard_map/feed_up/pallas_call | solution.py:77
  162.3 6.0 %down_weight_grad.2 = (bf16[2,2,2,4,48,768]{5,4,3,2,1,0:T(8,128)(2,1)}, bf16[2,4,48,768]{3,2,1,0:T(8,128)(2,1)}, bf16[2,4,48,768]{3,2,1,0:T(8,128)(2,1)}, bf16[2...) custom-call(s32[4]{0:T(128)S(1)} %pad_add_fusion.place_ref.refs_0_, ...), custom_call_target="tpu_custom_call" | custom-call | tf_op jit(solution)/shard_map/down_weight_grad/pallas_call | solution.py:77
  171.4 5.8 %feed_down.3 = (bf16[256,768]{1,0:T(8,128)(2,1)S(1)}, bf16[256,768]{1,0:T(8,128)(2,1)S(1)}) custom-call(s32[4]{0:T(128)S(1)} %pad_add_fusion.place_ref.refs_0_, f32[512,768]{1,0:T(8,128)S(1)} %get-tuple-element.318.attended_ref, bf16[512,3072]{1,0:T(8,128)(2,1)S(1)} %get-tuple-element.319.activated_ref, f32[2,8,768]{2,1,0:T(8,128)S(1)} %reshape.153.vectors_ref, ...), custom_call_target="tpu_custom_call" | custom-call | tf_op jit(solution)/shard_map/feed_down/pallas_call | solution.py:77
  181.6 11.0 %feed_back.2 = (bf16[512,3072]{1,0:T(8,128)(2,1)S(1)}, f32[512,768]{1,0:T(8,128)S(1)}, bf16[512,768]{1,0:T(8,128)(2,1)S(1)}, f32[8,768]{1,0:T(8,128)S(1)}, f32[1,3072]{1,0:T(1,128)S(1)}) custom-call(s32[4]{0:T(128)S(1)} %pad_add_fusion.place_ref.refs_0_, f32[512,768]{1,0:T(8,128)S(1)} %maximum_convert_fusion.grad_ref, ...), custom_call_target="tpu_custom_call" | custom-call | tf_op jit(solution)/shard_map/feed_back/pallas_call | solution.py:77
  192.6 7.1 %feed_weight_grads.2 = (bf16[2,2,2,5,48,768]{5,4,3,2,1,0:T(8,128)(2,1)}, bf16[2,5,48,768]{3,2,1,0:T(8,128)(2,1)}, bf16[2,5,48,768]{3,2,1,0:T(8,128)(2,1)}, bf16[...) custom-call(s32[4]{0:T(128)S(1)} %pad_add_fusion.place_ref.refs_0_, ...), custom_call_target="tpu_custom_call" | custom-call | tf_op jit(solution)/shard_map/feed_weight_grads/pallas_call | solution.py:77
  205.4 3.8 collective-permute-done.51.refs_2_.refs_8_
  210.2 3.5 combine.13
  215.4 22.1 %attend_back.2 = (bf16[512,768]{1,0:T(8,128)(2,1)S(1)}, bf16[512,768]{1,0:T(8,128)(2,1)S(1)}, bf16[512,768]{1,0:T(8,128)(2,1)S(1)}, bf16[512,768]{1,0:T(8,128)(2,1)S(1)}, bf16[512,768]{1,0:T(8,128)(2,1)S(1)}) custom-call(bf16[512,768]{1,0:T(8,128)(2,1)S(1)} %copy-done.23, bf16[512,768]{1,0:T(8,128)(2,1)S(1)} %copy-done.25, bf16[512,768]{1,0:T(8,128)(2,1)S(1)} %copy-done.29, ...), custom_call_target="tpu_custom_call" | custom-call | tf_op jit(solution)/shard_map/attend_back/pallas_call | solution.py:77
  242.1 5.9 %qkv_weight_grads.2 = (f32[8,768]{1,0:T(8,128)S(1)}, bf16[2,512,768]{2,1,0:T(8,128)(2,1)S(1)}, bf16[2,2,2,3,48,768]{5,4,3,2,1,0:T(8,128)(2,1)}, bf16[2,3,48,768]...) custom-call(s32[4]{0:T(128)S(1)} %pad_add_fusion.place_ref.refs_0_, ...), custom_call_target="tpu_custom_call" | custom-call | tf_op jit(solution)/shard_map/qkv_weight_grads/pallas_call | solution.py:77
  250.6 5.4 %norm_back.2 = (f32[512,768]{1,0:T(8,128)S(1)}, f32[8,768]{1,0:T(8,128)S(1)}) custom-call(s32[4]{0:T(128)S(1)} %pad_add_fusion.place_ref.refs_0_, f32[512,768]{1,0:T(8,128)S(1)} %feed_down.2.stream_ref, f32[2,8,768]{2,1,0:T(8,128)S(1)} %reshape.153.vectors_ref, f32[512,768]{1,0:T(8,128)S(1)} %get-tuple-element.340.attended_grad_ref, ...), custom_call_target="tpu_custom_call" | custom-call | tf_op jit(solution)/shard_map/norm_back/pallas_call | solution.py:77
  257.1 4.4 combine.15
  263.9 3.6 collective-permute-start.63
  267.6 6.0 %down_weight_grad.3 = (bf16[2,2,2,4,48,768]{5,4,3,2,1,0:T(8,128)(2,1)}, bf16[2,4,48,768]{3,2,1,0:T(8,128)(2,1)}, bf16[2,4,48,768]{3,2,1,0:T(8,128)(2,1)}, bf16[2...) custom-call(s32[4]{0:T(128)S(1)} %pad_add_fusion.place_ref.refs_0_, bf16[512,3072]{1,0:T(8,128)(2,1)S(1)} %copy-done.3, ...), custom_call_target="tpu_custom_call" | custom-call | tf_op jit(solution)/shard_map/down_weight_grad/pallas_call | solution.py:77
  273.7 11.5 %feed_back.3 = (bf16[512,3072]{1,0:T(8,128)(2,1)S(1)}, f32[512,768]{1,0:T(8,128)S(1)}, bf16[512,768]{1,0:T(8,128)(2,1)S(1)}, f32[8,768]{1,0:T(8,128)S(1)}, f32[1,3072]{1,0:T(1,128)S(1)}) custom-call(s32[4]{0:T(128)S(1)} %pad_add_fusion.place_ref.refs_0_, f32[512,768]{1,0:T(8,128)S(1)} %get-tuple-element.367.grad_ref, bf16[512,3072]{1,0:T(8,128)(2,1)S(1)} %copy-done.7, ...), custom_call_target="tpu_custom_call" | custom-call | tf_op jit(solution)/shard_map/feed_back/pallas_call | solution.py:77
  290.7 4.6 combine.16
  300.2 7.2 %feed_weight_grads.3 = (bf16[2,2,2,5,48,768]{5,4,3,2,1,0:T(8,128)(2,1)}, bf16[2,5,48,768]{3,2,1,0:T(8,128)(2,1)}, bf16[2,5,48,768]{3,2,1,0:T(8,128)(2,1)}, bf16[...) custom-call(s32[4]{0:T(128)S(1)} %pad_add_fusion.place_ref.refs_0_, ...), custom_call_target="tpu_custom_call" | custom-call | tf_op jit(solution)/shard_map/feed_weight_grads/pallas_call | solution.py:77
  307.5 22.8 %attend_back.3 = (bf16[512,768]{1,0:T(8,128)(2,1)S(1)}, bf16[512,768]{1,0:T(8,128)(2,1)S(1)}, bf16[512,768]{1,0:T(8,128)(2,1)S(1)}, bf16[512,768]{1,0:T(8,128)(2,1)S(1)}, bf16[512,768]{1,0:T(8,128)(2,1)}) custom-call(bf16[512,768]{1,0:T(8,128)(2,1)S(1)} %copy-done.13, bf16[512,768]{1,0:T(8,128)(2,1)S(1)} %copy-done.15, bf16[512,768]{1,0:T(8,128)(2,1)S(1)} %copy-done.19, ...), custom_call_target="tpu_custom_call" | custom-call | tf_op jit(solution)/shard_map/attend_back/pallas_call | solution.py:77
  337.8 5.4 %combine.17 = (bf16[20,48,768]{2,1,0:T(8,128)(2,1)}, bf16[8,48,768]{2,1,0:T(8,128)(2,1)}, bf16[4,48,768]{2,1,0:T(8,128)(2,1)}, bf16[3,48,768]{2,1,0:T(8,128)(2,1)}, bf16[5,48,768]{2,1,0:T(8,128)(2,1)}) custom-call(bf16[40,48,768]{2,1,0:T(8,128)(2,1)} %bitcast.79, bf16[10,48,768]{2,1,0:T(8,128)(2,1)} %copy-done.93, bf16[10,48,768]{2,1,0:T(8,128)(2,1)} %copy-done.94, ...), custom_call_target="tpu_custom_call" | custom-call | tf_op jit(solution)/shard_map/combine/pallas_call | solution.py:77
  357.0 5.9 %qkv_weight_grads.3 = (f32[8,768]{1,0:T(8,128)S(1)}, bf16[2,512,768]{2,1,0:T(8,128)(2,1)S(1)}, bf16[2,2,2,3,48,768]{5,4,3,2,1,0:T(8,128)(2,1)}, bf16[2,3,48,768]...) custom-call(s32[4]{0:T(128)S(1)} %pad_add_fusion.place_ref.refs_0_, ...), custom_call_target="tpu_custom_call" | custom-call | tf_op jit(solution)/shard_map/qkv_weight_grads/pallas_call | solution.py:77
  362.9 5.4 %norm_back.3 = (f32[512,768]{1,0:T(8,128)S(1)}, f32[8,768]{1,0:T(8,128)S(1)}) custom-call(s32[4]{0:T(128)S(1)} %pad_add_fusion.place_ref.refs_0_, f32[512,768]{1,0:T(8,128)S(1)} %copy-done.1, f32[2,8,768]{2,1,0:T(8,128)S(1)} %reshape.153.vectors_ref, f32[512,768]{1,0:T(8,128)S(1)} %copy-done.5, bf16[512,768]{1,0:T(8,128)(2,1)S(1)} %copy-done.33, ...), custom_call_target="tpu_custom_call" | custom-call | tf_op jit(solution)/shard_map/norm_back/pallas_call | solution.py:77
  374.8 3.7 combine.18
  381.3 3.2 finish.6.refs_5_
  384.5 4.0 collective-permute-done.89.refs_7_
  390.2 3.6 combine.19
  397.8 6.2 %collective-permute-done.91.refs_2_ = bf16[13,48,768]{2,1,0:T(8,128)(2,1)S(1)} collective-permute-done((bf16[13,48,768]{2,1,0:T(8,128)(2,1)}, bf16[13,48,768]{2,1,0:T(8,128)(2,1)S(1)}, u32[]{:S(2)}, u32[]{:S(2)}) %collective-permute-start.91) | collective-permute-done | bytes 958496 | tf_op jit(solution)/shard_map/ppermute | solution.py:35
  403.9 7.6 %collective-permute-done.93.refs_9_ = bf16[7,48,768]{2,1,0:T(8,128)(2,1)S(1)} collective-permute-done((bf16[7,48,768]{2,1,0:T(8,128)(2,1)}, bf16[7,48,768]{2,1,0:T(8,128)(2,1)S(1)}, u32[]{:S(2)}, u32[]{:S(2)}) %collective-permute-start.93) | collective-permute-done | bytes 516128 | tf_op jit(solution)/shard_map/ppermute | solution.py:1006
  413.2 3.8 combine.20
  418.2 7.2 %collective-permute-start.100 = (bf16[7,48,768]{2,1,0:T(8,128)(2,1)}, bf16[7,48,768]{2,1,0:T(8,128)(2,1)S(1)}, u32[]{:S(2)}, u32[]{:S(2)}) collective-permute-start(bf16[7,48,768]{2,1,0:T(8,128)(2,1)} %get-tuple-element.466), channel_id=1, source_target_pairs={{0,8},{8,0},{16,24},{24,16},{1,9},{9,1},{17,25},{25,17},{2,10},{10... | collective-permute-start | bytes 1548296 | tf_op jit(solution)/shard_map/ppermute | solution.py:1006
  428.8 17.3 %collective-permute-done.97.refs_4_ = bf16[5,48,768]{2,1,0:T(8,128)(2,1)S(1)} collective-permute-done((bf16[5,48,768]{2,1,0:T(8,128)(2,1)S(1)}, bf16[5,48,768]{2,1,0:T(8,128)(2,1)S(1)}, u32[]{:S(2)}, u32[]{:S(2)}) %collective-permute-start.97) | collective-permute-done | bytes 368672 | tf_op jit(solution)/shard_map/ppermute | solution.py:1006
  446.9 3.5 finish.7
  452.8 3.2 combine.21
  461.5 10.7 %collective-permute-done.101.refs_4_ = bf16[4,48,768]{2,1,0:T(8,128)(2,1)S(1)} collective-permute-done((bf16[4,48,768]{2,1,0:T(8,128)(2,1)}, bf16[4,48,768]{2,1,0:T(8,128)(2,1)S(1)}, u32[]{:S(2)}, u32[]{:S(2)}) %collective-permute-start.101) | collective-permute-done | bytes 294944 | tf_op jit(solution)/shard_map/ppermute | solution.py:1006
  473.6 3.2 combine.22
  486.2 3.2 finish.8
  504.9 3.5 finish.10
  508.8 4.7 collective-permute-done.111.refs_4_
  (580 shorter events, 179.8 us)
Async XLA Ops:
  3.5 14.3 %collective-permute-start.10 = (bf16[3,96,768]{2,1,0:T(8,128)(2,1)}, bf16[3,96,768]{2,1,0:T(8,128)(2,1)}, u32[]{:S(2)}, u32[]{:S(2)}) collective-permute-start(bf16[3,96,768]{2,1,0:T(8,128)(2,1)} %get-tuple-element.255), channel_id=1, source_target_pairs={{0,2},{2,0},{1,3},{3,1},{4,6},{6,4},{5,7},{7,5},{8,10},{10,8},{9,1... | collective-permute-start | bytes 1327112 | tf_op jit(solution)/shard_map/ppermute | solution.py:35
  6.6 18.7 %collective-permute-start = (bf16[256,768]{1,0:T(8,128)(2,1)}, bf16[256,768]{1,0:T(8,128)(2,1)S(1)}, u32[]{:S(2)}, u32[]{:S(2)}) collective-permute-start(bf16[256,768]{1,0:T(8,128)(2,1)} %get-tuple-element.263), channel_id=1, source_target_pairs={{0,2},{2,0},{1,3},{3,1},{4,6},{6,4},{5,7},{7,5},{8,10},{10,8},{9,1... | collective-permute-start | bytes 1179656 | tf_op jit(solution)/shard_map/ppermute | solution.py:35
  17.9 14.3 %collective-permute-start.11 = (bf16[3,96,768]{2,1,0:T(8,128)(2,1)}, bf16[3,96,768]{2,1,0:T(8,128)(2,1)}, u32[]{:S(2)}, u32[]{:S(2)}) collective-permute-start(bf16[3,96,768]{2,1,0:T(8,128)(2,1)} %collective-permute-done.10.refs_2_), channel_id=1, source_target_pairs={{0,4},{4,0},{1,5},{5,1},{2,6},{6,2},{3,7},{7,3},{8,12},{12,8},{9,1... | collective-permute-start | bytes 1327112 | tf_op jit(solution)/shard_map/ppermute | solution.py:35
  38.2 22.0 %collective-permute-start.14 = (bf16[6,96,768]{2,1,0:T(8,128)(2,1)}, bf16[6,96,768]{2,1,0:T(8,128)(2,1)}, u32[]{:S(2)}, u32[]{:S(2)}) collective-permute-start(bf16[6,96,768]{2,1,0:T(8,128)(2,1)} %get-tuple-element.282), channel_id=1, source_target_pairs={{0,2},{2,0},{1,3},{3,1},{4,6},{6,4},{5,7},{7,5},{8,10},{10,8},{9,1... | collective-permute-start | bytes 2654216 | tf_op jit(solution)/shard_map/ppermute | solution.py:35
  60.2 22.4 %collective-permute-start.21 = (bf16[6,96,768]{2,1,0:T(8,128)(2,1)}, bf16[6,96,768]{2,1,0:T(8,128)(2,1)}, u32[]{:S(2)}, u32[]{:S(2)}) collective-permute-start(bf16[6,96,768]{2,1,0:T(8,128)(2,1)} %collective-permute-done.14.refs_2_), channel_id=1, source_target_pairs={{0,4},{4,0},{1,5},{5,1},{2,6},{6,2},{3,7},{7,3},{8,12},{12,8},{9,1... | collective-permute-start | bytes 2654216 | tf_op jit(solution)/shard_map/ppermute | solution.py:35
  62.2 20.3 %collective-permute-start.15 = (bf16[3,96,768]{2,1,0:T(8,128)(2,1)S(1)}, bf16[3,96,768]{2,1,0:T(8,128)(2,1)}, u32[]{:S(2)}, u32[]{:S(2)}) collective-permute-start(bf16[3,96,768]{2,1,0:T(8,128)(2,1)S(1)} %copy-done.153), channel_id=1, source_target_pairs={{0,2},{2,0},{1,3},{3,1},{4,6},{6,4},{5,7},{7,5},{8,10},{10,8},{9,1... | collective-permute-start | bytes 1327112 | tf_op jit(solution)/shard_map/ppermute | solution.py:35
  83.1 16.2 %collective-permute-start.19 = (bf16[3,96,768]{2,1,0:T(8,128)(2,1)}, bf16[3,96,768]{2,1,0:T(8,128)(2,1)}, u32[]{:S(2)}, u32[]{:S(2)}) collective-permute-start(bf16[3,96,768]{2,1,0:T(8,128)(2,1)} %get-tuple-element.290), channel_id=1, source_target_pairs={{0,2},{2,0},{1,3},{3,1},{4,6},{6,4},{5,7},{7,5},{8,10},{10,8},{9,1... | collective-permute-start | bytes 1327112 | tf_op jit(solution)/shard_map/ppermute | solution.py:35
  83.4 16.2 %collective-permute-start.25 = (bf16[3,96,768]{2,1,0:T(8,128)(2,1)}, bf16[3,96,768]{2,1,0:T(8,128)(2,1)}, u32[]{:S(2)}, u32[]{:S(2)}) collective-permute-start(bf16[3,96,768]{2,1,0:T(8,128)(2,1)} %collective-permute-done.15.refs_8_), channel_id=1, source_target_pairs={{0,4},{4,0},{1,5},{5,1},{2,6},{6,2},{3,7},{7,3},{8,12},{12,8},{9,1... | collective-permute-start | bytes 1327112 | tf_op jit(solution)/shard_map/ppermute | solution.py:35
  126.1 18.8 %collective-permute-start.32 = (bf16[4,96,768]{2,1,0:T(8,128)(2,1)S(1)}, bf16[4,96,768]{2,1,0:T(8,128)(2,1)}, u32[]{:S(2)}, u32[]{:S(2)}) collective-permute-start(bf16[4,96,768]{2,1,0:T(8,128)(2,1)S(1)} %copy-done.146), channel_id=1, source_target_pairs={{0,2},{2,0},{1,3},{3,1},{4,6},{6,4},{5,7},{7,5},{8,10},{10,8},{9,1... | collective-permute-start | bytes 1769480 | tf_op jit(solution)/shard_map/ppermute | solution.py:35
  130.1 17.4 %collective-permute-start.38 = (bf16[2,96,768]{2,1,0:T(8,128)(2,1)S(1)}, bf16[2,96,768]{2,1,0:T(8,128)(2,1)}, u32[]{:S(2)}, u32[]{:S(2)}) collective-permute-start(bf16[2,96,768]{2,1,0:T(8,128)(2,1)S(1)} %collective-permute-done.27.refs_8_), channel_id=1, source_target_pairs={{0,4},{4,0},{1,5},{5,1},{2,6},{6,2},{3,7},{7,3},{8,12},{12,8},{9,1... | collective-permute-start | bytes 884744 | tf_op jit(solution)/shard_map/ppermute | solution.py:35
  145.0 23.3 %collective-permute-start.40 = (bf16[4,96,768]{2,1,0:T(8,128)(2,1)}, bf16[4,96,768]{2,1,0:T(8,128)(2,1)}, u32[]{:S(2)}, u32[]{:S(2)}) collective-permute-start(bf16[4,96,768]{2,1,0:T(8,128)(2,1)} %collective-permute-done.32.refs_2_.refs_14_), channel_id=1, source_target_pairs={{0,4},{4,0},{1,5},{5,1},{2,6},{6,2},{3,7},{7,3},{8,12},{12,8},{9,1... | collective-permute-start | bytes 1769480 | tf_op jit(solution)/shard_map/ppermute | solution.py:35
  146.1 15.0 %collective-permute-start.41 = (bf16[256,768]{1,0:T(8,128)(2,1)}, bf16[256,768]{1,0:T(8,128)(2,1)}, u32[]{:S(2)}, u32[]{:S(2)}) collective-permute-start(bf16[256,768]{1,0:T(8,128)(2,1)} %get-tuple-element.321), channel_id=1, source_target_pairs={{0,2},{2,0},{1,3},{3,1},{4,6},{6,4},{5,7},{7,5},{8,10},{10,8},{9,1... | collective-permute-start | bytes 1179656 | tf_op jit(solution)/shard_map/ppermute | solution.py:35
  180.9 28.3 %collective-permute-start.51 = (bf16[16,48,768]{2,1,0:T(8,128)(2,1)}, bf16[16,48,768]{2,1,0:T(8,128)(2,1)S(1)}, u32[]{:S(2)}, u32[]{:S(2)}) collective-permute-start(bf16[16,48,768]{2,1,0:T(8,128)(2,1)} %combine.12), channel_id=1, source_target_pairs={{0,2},{2,0},{1,3},{3,1},{4,6},{6,4},{5,7},{7,5},{8,10},{10,8},{9,1... | collective-permute-start | bytes 3538952 | tf_op jit(solution)/shard_map/ppermute | solution.py:35
  213.7 35.8 %collective-permute-start.55 = (bf16[20,48,768]{2,1,0:T(8,128)(2,1)}, bf16[20,48,768]{2,1,0:T(8,128)(2,1)S(1)}, u32[]{:S(2)}, u32[]{:S(2)}) collective-permute-start(bf16[20,48,768]{2,1,0:T(8,128)(2,1)} %get-tuple-element.372), channel_id=1, source_target_pairs={{0,2},{2,0},{1,3},{3,1},{4,6},{6,4},{5,7},{7,5},{8,10},{10,8},{9,1... | collective-permute-start | bytes 4423688 | tf_op jit(solution)/shard_map/ppermute | solution.py:35
  214.4 23.1 %collective-permute-start.52 = (bf16[8,48,768]{2,1,0:T(8,128)(2,1)}, bf16[8,48,768]{2,1,0:T(8,128)(2,1)S(1)}, u32[]{:S(2)}, u32[]{:S(2)}) collective-permute-start(bf16[8,48,768]{2,1,0:T(8,128)(2,1)} %get-tuple-element.351), channel_id=1, source_target_pairs={{0,4},{4,0},{1,5},{5,1},{2,6},{6,2},{3,7},{7,3},{8,12},{12,8},{9,1... | collective-permute-start | bytes 1769480 | tf_op jit(solution)/shard_map/ppermute | solution.py:35
  261.4 23.7 %collective-permute-start.61 = (bf16[12,48,768]{2,1,0:T(8,128)(2,1)}, bf16[12,48,768]{2,1,0:T(8,128)(2,1)S(1)}, u32[]{:S(2)}, u32[]{:S(2)}) collective-permute-start(bf16[12,48,768]{2,1,0:T(8,128)(2,1)} %get-tuple-element.378), channel_id=1, source_target_pairs={{0,2},{2,0},{1,3},{3,1},{4,6},{6,4},{5,7},{7,5},{8,10},{10,8},{9,1... | collective-permute-start | bytes 2654216 | tf_op jit(solution)/shard_map/ppermute | solution.py:35
  263.2 21.9 %collective-permute-start.62 = (bf16[10,48,768]{2,1,0:T(8,128)(2,1)}, bf16[10,48,768]{2,1,0:T(8,128)(2,1)S(1)}, u32[]{:S(2)}, u32[]{:S(2)}) collective-permute-start(bf16[10,48,768]{2,1,0:T(8,128)(2,1)} %get-tuple-element.388), channel_id=1, source_target_pairs={{0,4},{4,0},{1,5},{5,1},{2,6},{6,2},{3,7},{7,3},{8,12},{12,8},{9,1... | collective-permute-start | bytes 2211848 | tf_op jit(solution)/shard_map/ppermute | solution.py:35
  263.9 21.2 %collective-permute-start.63 = (bf16[4,48,768]{2,1,0:T(8,128)(2,1)}, bf16[4,48,768]{2,1,0:T(8,128)(2,1)S(1)}, u32[]{:S(2)}, u32[]{:S(2)}) collective-permute-start(bf16[4,48,768]{2,1,0:T(8,128)(2,1)} %get-tuple-element.389.refs_6_), channel_id=1, source_target_pairs={{0,24},{24,0},{8,16},{16,8},{1,25},{25,1},{9,17},{17,9},{2,26},{26... | collective-permute-start | bytes 884744 | tf_op jit(solution)/shard_map/ppermute | solution.py:1006
  295.3 35.1 %collective-permute-start.68 = (bf16[16,48,768]{2,1,0:T(8,128)(2,1)}, bf16[16,48,768]{2,1,0:T(8,128)(2,1)S(1)}, u32[]{:S(2)}, u32[]{:S(2)}) collective-permute-start(bf16[16,48,768]{2,1,0:T(8,128)(2,1)} %get-tuple-element.395), channel_id=1, source_target_pairs={{0,2},{2,0},{1,3},{3,1},{4,6},{6,4},{5,7},{7,5},{8,10},{10,8},{9,1... | collective-permute-start | bytes 3538952 | tf_op jit(solution)/shard_map/ppermute | solution.py:35
  296.1 34.3 %collective-permute-start.69 = (bf16[6,48,768]{2,1,0:T(8,128)(2,1)}, bf16[6,48,768]{2,1,0:T(8,128)(2,1)S(1)}, u32[]{:S(2)}, u32[]{:S(2)}) collective-permute-start(bf16[6,48,768]{2,1,0:T(8,128)(2,1)} %get-tuple-element.407), channel_id=1, source_target_pairs={{0,4},{4,0},{1,5},{5,1},{2,6},{6,2},{3,7},{7,3},{8,12},{12,8},{9,1... | collective-permute-start | bytes 1327112 | tf_op jit(solution)/shard_map/ppermute | solution.py:35
  297.0 33.3 %collective-permute-start.72 = (bf16[5,48,768]{2,1,0:T(8,128)(2,1)}, bf16[5,48,768]{2,1,0:T(8,128)(2,1)S(1)}, u32[]{:S(2)}, u32[]{:S(2)}) collective-permute-start(bf16[5,48,768]{2,1,0:T(8,128)(2,1)} %get-tuple-element.410), channel_id=1, source_target_pairs={{0,8},{8,0},{16,24},{24,16},{1,9},{9,1},{17,25},{25,17},{2,10},{10... | collective-permute-start | bytes 1105928 | tf_op jit(solution)/shard_map/ppermute | solution.py:1006
  297.5 32.8 %collective-permute-start.70 = (bf16[4,48,768]{2,1,0:T(8,128)(2,1)}, bf16[4,48,768]{2,1,0:T(8,128)(2,1)S(1)}, u32[]{:S(2)}, u32[]{:S(2)}) collective-permute-start(bf16[4,48,768]{2,1,0:T(8,128)(2,1)} %get-tuple-element.408.refs_1_), channel_id=1, source_target_pairs={{0,4},{4,0},{1,5},{5,1},{2,6},{6,2},{3,7},{7,3},{8,12},{12,8},{9,1... | collective-permute-start | bytes 884744 | tf_op jit(solution)/shard_map/ppermute | solution.py:35
  298.8 31.5 %collective-permute-start.71 = (bf16[4,48,768]{2,1,0:T(8,128)(2,1)}, bf16[4,48,768]{2,1,0:T(8,128)(2,1)S(1)}, u32[]{:S(2)}, u32[]{:S(2)}) collective-permute-start(bf16[4,48,768]{2,1,0:T(8,128)(2,1)} %get-tuple-element.409), channel_id=1, source_target_pairs={{0,8},{8,0},{16,24},{24,16},{1,9},{9,1},{17,25},{25,17},{2,10},{10... | collective-permute-start | bytes 884744 | tf_op jit(solution)/shard_map/ppermute | solution.py:1006
  331.5 15.9 %collective-permute-start.77 = (bf16[512,768]{1,0:T(8,128)(2,1)S(1)}, bf16[512,768]{1,0:T(8,128)(2,1)S(1)}, u32[]{:S(2)}, u32[]{:S(2)}) collective-permute-start(bf16[512,768]{1,0:T(8,128)(2,1)S(1)} %get-tuple-element.422), channel_id=1, source_target_pairs={{0,1},{1,0},{2,3},{3,2},{4,5},{5,4},{6,7},{7,6},{8,9},{9,8},{10,11... | collective-permute-start | bytes 2359304 | tf_op jit(solution)/shard_map/ppermute | solution.py:35
  333.0 15.4 %collective-permute-start.78 = (bf16[512,768]{1,0:T(8,128)(2,1)}, bf16[512,768]{1,0:T(8,128)(2,1)S(1)}, u32[]{:S(2)}, u32[]{:S(2)}) collective-permute-start(bf16[512,768]{1,0:T(8,128)(2,1)} %get-tuple-element.423), channel_id=1, source_target_pairs={{0,1},{1,0},{2,3},{3,2},{4,5},{5,4},{6,7},{7,6},{8,9},{9,8},{10,11... | collective-permute-start | bytes 2359304 | tf_op jit(solution)/shard_map/ppermute | solution.py:35
  343.3 26.2 %collective-permute-start.79 = (bf16[8,48,768]{2,1,0:T(8,128)(2,1)}, bf16[8,48,768]{2,1,0:T(8,128)(2,1)}, u32[]{:S(2)}, u32[]{:S(2)}) collective-permute-start(bf16[8,48,768]{2,1,0:T(8,128)(2,1)} %get-tuple-element.432), channel_id=1, source_target_pairs={{0,4},{4,0},{1,5},{5,1},{2,6},{6,2},{3,7},{7,3},{8,12},{12,8},{9,1... | collective-permute-start | bytes 1769480 | tf_op jit(solution)/shard_map/ppermute | solution.py:35
  344.3 45.2 %collective-permute-start.88 = (bf16[20,48,768]{2,1,0:T(8,128)(2,1)}, bf16[20,48,768]{2,1,0:T(8,128)(2,1)}, u32[]{:S(2)}, u32[]{:S(2)}) collective-permute-start(bf16[20,48,768]{2,1,0:T(8,128)(2,1)} %get-tuple-element.416), channel_id=1, source_target_pairs={{0,2},{2,0},{1,3},{3,1},{4,6},{6,4},{5,7},{7,5},{8,10},{10,8},{9,1... | collective-permute-start | bytes 4423688 | tf_op jit(solution)/shard_map/ppermute | solution.py:35
  346.0 23.4 %collective-permute-start.82 = (bf16[5,48,768]{2,1,0:T(8,128)(2,1)}, bf16[5,48,768]{2,1,0:T(8,128)(2,1)}, u32[]{:S(2)}, u32[]{:S(2)}) collective-permute-start(bf16[5,48,768]{2,1,0:T(8,128)(2,1)} %get-tuple-element.435.refs_9_), channel_id=1, source_target_pairs={{0,24},{24,0},{8,16},{16,8},{1,25},{25,1},{9,17},{17,9},{2,26},{26... | collective-permute-start | bytes 1105928 | tf_op jit(solution)/shard_map/ppermute | solution.py:1006
  348.4 21.1 %collective-permute-start.80 = (bf16[4,48,768]{2,1,0:T(8,128)(2,1)}, bf16[4,48,768]{2,1,0:T(8,128)(2,1)}, u32[]{:S(2)}, u32[]{:S(2)}) collective-permute-start(bf16[4,48,768]{2,1,0:T(8,128)(2,1)} %get-tuple-element.433), channel_id=1, source_target_pairs={{0,8},{8,0},{16,24},{24,16},{1,9},{9,1},{17,25},{25,17},{2,10},{10... | collective-permute-start | bytes 884744 | tf_op jit(solution)/shard_map/ppermute | solution.py:1006
  349.3 20.1 %collective-permute-start.81 = (bf16[3,48,768]{2,1,0:T(8,128)(2,1)}, bf16[3,48,768]{2,1,0:T(8,128)(2,1)S(1)}, u32[]{:S(2)}, u32[]{:S(2)}) collective-permute-start(bf16[3,48,768]{2,1,0:T(8,128)(2,1)} %get-tuple-element.434), channel_id=1, source_target_pairs={{0,8},{8,0},{16,24},{24,16},{1,9},{9,1},{17,25},{25,17},{2,10},{10... | collective-permute-start | bytes 663560 | tf_op jit(solution)/shard_map/ppermute | solution.py:1006
  379.6 24.3 %collective-permute-start.91 = (bf16[13,48,768]{2,1,0:T(8,128)(2,1)}, bf16[13,48,768]{2,1,0:T(8,128)(2,1)S(1)}, u32[]{:S(2)}, u32[]{:S(2)}) collective-permute-start(bf16[13,48,768]{2,1,0:T(8,128)(2,1)} %get-tuple-element.449.refs_3_), channel_id=1, source_target_pairs={{0,2},{2,0},{1,3},{3,1},{4,6},{6,4},{5,7},{7,5},{8,10},{10,8},{9,1... | collective-permute-start | bytes 2875400 | tf_op jit(solution)/shard_map/ppermute | solution.py:35
  393.8 18.0 %collective-permute-start.92 = (bf16[10,48,768]{2,1,0:T(8,128)(2,1)}, bf16[10,48,768]{2,1,0:T(8,128)(2,1)S(1)}, u32[]{:S(2)}, u32[]{:S(2)}) collective-permute-start(bf16[10,48,768]{2,1,0:T(8,128)(2,1)} %get-tuple-element.454), channel_id=1, source_target_pairs={{0,4},{4,0},{1,5},{5,1},{2,6},{6,2},{3,7},{7,3},{8,12},{12,8},{9,1... | collective-permute-start | bytes 2211848 | tf_op jit(solution)/shard_map/ppermute | solution.py:35
  394.8 16.7 %collective-permute-start.93 = (bf16[7,48,768]{2,1,0:T(8,128)(2,1)}, bf16[7,48,768]{2,1,0:T(8,128)(2,1)S(1)}, u32[]{:S(2)}, u32[]{:S(2)}) collective-permute-start(bf16[7,48,768]{2,1,0:T(8,128)(2,1)} %get-tuple-element.456.refs_8_), channel_id=1, source_target_pairs={{0,24},{24,0},{8,16},{16,8},{1,25},{25,1},{9,17},{17,9},{2,26},{26... | collective-permute-start | bytes 1548296 | tf_op jit(solution)/shard_map/ppermute | solution.py:1006
  397.0 29.8 %collective-permute-start.95 = (bf16[256,768]{1,0:T(8,128)(2,1)S(1)}, bf16[256,768]{1,0:T(8,128)(2,1)S(1)}, u32[]{:S(2)}, u32[]{:S(2)}) collective-permute-start(bf16[256,768]{1,0:T(8,128)(2,1)S(1)} %slice.83), channel_id=1, source_target_pairs={{0,2},{2,0},{1,3},{3,1},{4,6},{6,4},{5,7},{7,5},{8,10},{10,8},{9,1... | collective-permute-start | bytes 1179656 | tf_op jit(solution)/shard_map/ppermute | solution.py:35
  397.8 29.0 %collective-permute-start.96 = (bf16[5,48,768]{2,1,0:T(8,128)(2,1)S(1)}, bf16[5,48,768]{2,1,0:T(8,128)(2,1)S(1)}, u32[]{:S(2)}, u32[]{:S(2)}) collective-permute-start(bf16[5,48,768]{2,1,0:T(8,128)(2,1)S(1)} %copy-done.155), channel_id=1, source_target_pairs={{0,8},{8,0},{16,24},{24,16},{1,9},{9,1},{17,25},{25,17},{2,10},{10... | collective-permute-start | bytes 1105928 | tf_op jit(solution)/shard_map/ppermute | solution.py:1006
  417.0 34.1 %collective-permute-start.98 = (bf16[7,48,768]{2,1,0:T(8,128)(2,1)}, bf16[7,48,768]{2,1,0:T(8,128)(2,1)S(1)}, u32[]{:S(2)}, u32[]{:S(2)}) collective-permute-start(bf16[7,48,768]{2,1,0:T(8,128)(2,1)} %get-tuple-element.457.refs_4_), channel_id=1, source_target_pairs={{0,4},{4,0},{1,5},{5,1},{2,6},{6,2},{3,7},{7,3},{8,12},{12,8},{9,1... | collective-permute-start | bytes 1548296 | tf_op jit(solution)/shard_map/ppermute | solution.py:35
  418.2 33.0 %collective-permute-start.100 = (bf16[7,48,768]{2,1,0:T(8,128)(2,1)}, bf16[7,48,768]{2,1,0:T(8,128)(2,1)S(1)}, u32[]{:S(2)}, u32[]{:S(2)}) collective-permute-start(bf16[7,48,768]{2,1,0:T(8,128)(2,1)} %get-tuple-element.466), channel_id=1, source_target_pairs={{0,8},{8,0},{16,24},{24,16},{1,9},{9,1},{17,25},{25,17},{2,10},{10... | collective-permute-start | bytes 1548296 | tf_op jit(solution)/shard_map/ppermute | solution.py:1006
  425.4 25.0 %collective-permute-start.94 = (bf16[256,768]{1,0:T(8,128)(2,1)S(1)}, bf16[256,768]{1,0:T(8,128)(2,1)S(1)}, u32[]{:S(2)}, u32[]{:S(2)}) collective-permute-start(bf16[256,768]{1,0:T(8,128)(2,1)S(1)} %copy-done.52), channel_id=1, source_target_pairs={{0,2},{2,0},{1,3},{3,1},{4,6},{6,4},{5,7},{7,5},{8,10},{10,8},{9,1... | collective-permute-start | bytes 1179656 | tf_op jit(solution)/shard_map/ppermute | solution.py:35
  426.8 19.4 %collective-permute-start.97 = (bf16[5,48,768]{2,1,0:T(8,128)(2,1)S(1)}, bf16[5,48,768]{2,1,0:T(8,128)(2,1)S(1)}, u32[]{:S(2)}, u32[]{:S(2)}) collective-permute-start(bf16[5,48,768]{2,1,0:T(8,128)(2,1)S(1)} %copy-done.156), channel_id=1, source_target_pairs={{0,8},{8,0},{16,24},{24,16},{1,9},{9,1},{17,25},{25,17},{2,10},{10... | collective-permute-start | bytes 1105928 | tf_op jit(solution)/shard_map/ppermute | solution.py:1006
  426.8 24.3 %collective-permute-start.99 = (bf16[5,48,768]{2,1,0:T(8,128)(2,1)}, bf16[5,48,768]{2,1,0:T(8,128)(2,1)S(1)}, u32[]{:S(2)}, u32[]{:S(2)}) collective-permute-start(bf16[5,48,768]{2,1,0:T(8,128)(2,1)} %get-tuple-element.465), channel_id=1, source_target_pairs={{0,8},{8,0},{16,24},{24,16},{1,9},{9,1},{17,25},{25,17},{2,10},{10... | collective-permute-start | bytes 1105928 | tf_op jit(solution)/shard_map/ppermute | solution.py:1006
  456.0 16.2 %collective-permute-start.102 = (bf16[5,48,768]{2,1,0:T(8,128)(2,1)}, bf16[5,48,768]{2,1,0:T(8,128)(2,1)S(1)}, u32[]{:S(2)}, u32[]{:S(2)}) collective-permute-start(bf16[5,48,768]{2,1,0:T(8,128)(2,1)} %get-tuple-element.469.refs_6_), channel_id=1, source_target_pairs={{0,24},{24,0},{8,16},{16,8},{1,25},{25,1},{9,17},{17,9},{2,26},{26... | collective-permute-start | bytes 1105928 | tf_op jit(solution)/shard_map/ppermute | solution.py:1006
  459.4 23.5 %collective-permute-start.104 = (bf16[7,48,768]{2,1,0:T(8,128)(2,1)}, bf16[7,48,768]{2,1,0:T(8,128)(2,1)S(1)}, u32[]{:S(2)}, u32[]{:S(2)}) collective-permute-start(bf16[7,48,768]{2,1,0:T(8,128)(2,1)} %get-tuple-element.472.refs_1_), channel_id=1, source_target_pairs={{0,4},{4,0},{1,5},{5,1},{2,6},{6,2},{3,7},{7,3},{8,12},{12,8},{9,1... | collective-permute-start | bytes 1548296 | tf_op jit(solution)/shard_map/ppermute | solution.py:35
  460.3 25.1 %collective-permute-start.105 = (bf16[7,48,768]{2,1,0:T(8,128)(2,1)S(1)}, bf16[7,48,768]{2,1,0:T(8,128)(2,1)S(1)}, u32[]{:S(2)}, u32[]{:S(2)}) collective-permute-start(bf16[7,48,768]{2,1,0:T(8,128)(2,1)S(1)} %copy-done.151), channel_id=1, source_target_pairs={{0,4},{4,0},{1,5},{5,1},{2,6},{6,2},{3,7},{7,3},{8,12},{12,8},{9,1... | collective-permute-start | bytes 1548296 | tf_op jit(solution)/shard_map/ppermute | solution.py:35
  476.8 15.5 %collective-permute-start.103 = (bf16[4,48,768]{2,1,0:T(8,128)(2,1)}, bf16[4,48,768]{2,1,0:T(8,128)(2,1)S(1)}, u32[]{:S(2)}, u32[]{:S(2)}) collective-permute-start(bf16[4,48,768]{2,1,0:T(8,128)(2,1)} %get-tuple-element.476.refs_0_), channel_id=1, source_target_pairs={{0,24},{24,0},{8,16},{16,8},{1,25},{25,1},{9,17},{17,9},{2,26},{26... | collective-permute-start | bytes 884744 | tf_op jit(solution)/shard_map/ppermute | solution.py:1006
  481.9 17.3 %collective-permute-start.106 = (bf16[5,48,768]{2,1,0:T(8,128)(2,1)}, bf16[5,48,768]{2,1,0:T(8,128)(2,1)S(1)}, u32[]{:S(2)}, u32[]{:S(2)}) collective-permute-start(bf16[5,48,768]{2,1,0:T(8,128)(2,1)} %get-tuple-element.480), channel_id=1, source_target_pairs={{0,8},{8,0},{16,24},{24,16},{1,9},{9,1},{17,25},{25,17},{2,10},{10... | collective-permute-start | bytes 1105928 | tf_op jit(solution)/shard_map/ppermute | solution.py:1006
  482.1 19.9 %collective-permute-start.107 = (bf16[5,48,768]{2,1,0:T(8,128)(2,1)S(1)}, bf16[5,48,768]{2,1,0:T(8,128)(2,1)S(1)}, u32[]{:S(2)}, u32[]{:S(2)}) collective-permute-start(bf16[5,48,768]{2,1,0:T(8,128)(2,1)S(1)} %copy-done.117), channel_id=1, source_target_pairs={{0,4},{4,0},{1,5},{5,1},{2,6},{6,2},{3,7},{7,3},{8,12},{12,8},{9,1... | collective-permute-start | bytes 1105928 | tf_op jit(solution)/shard_map/ppermute | solution.py:35
  482.9 21.2 %collective-permute-start.108 = (bf16[5,48,768]{2,1,0:T(8,128)(2,1)S(1)}, bf16[5,48,768]{2,1,0:T(8,128)(2,1)S(1)}, u32[]{:S(2)}, u32[]{:S(2)}) collective-permute-start(bf16[5,48,768]{2,1,0:T(8,128)(2,1)S(1)} %copy-done.154), channel_id=1, source_target_pairs={{0,12},{4,8},{8,4},{12,0},{16,28},{20,24},{24,20},{28,16},{1,13},{... | collective-permute-start | bytes 1105928 | tf_op jit(solution)/shard_map/ppermute | solution.py:1004
  499.2 14.3 %collective-permute-start.111 = (bf16[3,48,768]{2,1,0:T(8,128)(2,1)}, bf16[3,48,768]{2,1,0:T(8,128)(2,1)S(1)}, u32[]{:S(2)}, u32[]{:S(2)}) collective-permute-start(bf16[3,48,768]{2,1,0:T(8,128)(2,1)} %get-tuple-element.486), channel_id=1, source_target_pairs={{0,12},{4,8},{8,4},{12,0},{16,28},{20,24},{24,20},{28,16},{1,13},{... | collective-permute-start | bytes 663560 | tf_op jit(solution)/shard_map/ppermute | solution.py:1004
  (222 other events, 1705.8 us)
